TPU v7x, 32 devices: a whole 2x2x4 slice. The times are simulated.
32 devices in a mesh: stripe: 4 (over y, x), scan: 8 (over z, core).
Axes of the slice: x: 2, y: 2, z: 4, core: 2. Of those that a mesh axis runs over, the one named last changes fastest.
Arguments:
- dose: bfloat16 [800, 800], P('stripe', 'scan'), may hold values from 0 to 4
- target: int32 [800, 800], P('stripe', 'scan'), may hold values 0 or 1
- psf: bfloat16 [61, 61], replicated, may hold values from 0 to 0.025
Outputs:
- resist: float32 [800, 800], P('stripe', 'scan')
- dose_out: float32 [800, 800], P('stripe', 'scan')
All inputs are finite; a program needn't handle non-finite values. No bound on the sum of `target` on one device may be relied on, other than what follows from the above.
Results may differ from a plain program's by a relative error of at most 0.0003.
Values may be sent and summed in bfloat16 or wider, within the bound.
No kernel may reach another device: no remote copies, remote signals or barrier semaphores. Data moves between devices by JAX's collectives and lax.ppermute only.
A program may use at most 64 MiB of HBM per device.

v0:
```python
import functools
import math

import jax
import jax.numpy as jnp
from jax import lax
from jax.experimental import pallas as pl
from jax.experimental.pallas import tpu as pltpu
from jax.sharding import PartitionSpec as P

TAPS = 61
RIM = 30
COARSE = 25
SIGMA = 40
ITERS = 4

back_ratio = 0.6
resist_gain = 3.0
resist_level = 1.5
step_length = 0.5

PHASES = 8
SPAN = 32
LANES = 128
PER = LANES // SPAN
TAPS_PAD = 64
FIRST_SHIFT = -(-RIM // PHASES)
BEFORE = FIRST_SHIFT * PHASES - RIM + PER
SLOTS = (2 * FIRST_SHIFT + 1) * PHASES + PER
EDGE = 8
HALO = 2 * RIM

f32 = jnp.float32
bf16 = jnp.bfloat16
highest = lax.Precision.HIGHEST


def round_up(value, unit):
    return -(-value // unit) * unit


def iota2(shape, dim):
    return lax.broadcasted_iota(jnp.int32, shape, dim)


def dot(left, right, precision=None):
    return lax.dot_general(
        left, right, (((1,), (0,)), ((), ())), precision=precision, preferred_element_type=f32
    )


def dot_t(left, right):
    return lax.dot_general(left, right, (((1,), (1,)), ((), ())), preferred_element_type=f32)


def split(value, parts):
    pieces = []
    for _ in range(parts):
        piece = value.astype(bf16)
        pieces.append(piece)
        value = value - piece.astype(f32)
    return pieces


def one_side(value, axis):
    a, b, c = split(value, 3)
    return jnp.concatenate([a, b, c, a, b, a], axis=axis)


def other_side(value, axis):
    pieces = []
    for _ in range(3):
        piece = lax.reduce_precision(value, 8, 7)
        pieces.append(piece.astype(bf16))
        value = value - piece
    a, b, c = pieces
    return jnp.concatenate([a, a, a, b, b, c], axis=axis)


def roll(value, shift):
    shift %= LANES
    return pltpu.roll(value, shift, 1) if shift else value


def window(low, high, first, lane):
    if first == 0:
        return low
    if first == LANES:
        return high
    return jnp.where(lane < LANES - first, roll(low, -first), roll(high, -first))


def bands_kernel(taps_ref, fwd_ref, adj_ref, base_ref, rows_ref):
    lane = iota2((TAPS_PAD, LANES), 1)
    tap = iota2((TAPS_PAD, LANES), 0)
    place = iota2((LANES, LANES), 1)
    margin = PER - 1
    for which, out_ref in enumerate((fwd_ref, adj_ref)):
        taps = taps_ref[which]
        for k in range(8):
            hot = (((k - lane) & (LANES - 1)) == tap).astype(f32).astype(bf16)
            base_ref[pl.ds(k, TAPS_PAD, stride=8), :] = dot(taps, hot)
        for a in range(margin):
            rows_ref[pl.ds(a * LANES, LANES), :] = jnp.zeros((LANES, LANES), f32)

        def turn(step, carry):
            base = base_ref[pl.ds(pl.multiple_of(step * 8, 8), 8), :]
            first = pl.multiple_of((step + margin) * LANES, LANES)
            for g in range(LANES // 8):
                rows_ref[pl.ds(first + 8 * g, 8), :] = pltpu.roll(base, 8 * g, 1) if g else base
            return carry

        lax.fori_loop(0, TAPS_PAD, turn, 0, unroll=8)
        for a in list(range(BEFORE)) + list(range(BEFORE + TAPS_PAD, SLOTS)):
            out_ref[pl.ds(a * LANES, LANES), :] = jnp.zeros((LANES, LANES), bf16)

        def join(step, carry):
            value = None
            for k in reversed(range(PER)):
                first = pl.multiple_of((step + margin - k) * LANES, LANES)
                turned = jnp.concatenate(
                    [
                        rows_ref[pl.ds(first + SPAN * k, LANES - SPAN * k), :],
                        rows_ref[pl.ds(first, SPAN * k), :],
                    ],
                    axis=0,
                ) if k else rows_ref[pl.ds(first, LANES), :]
                value = turned if value is None else jnp.where(place < SPAN * (k + 1), turned, value)
            out_ref[pl.ds(pl.multiple_of((step + BEFORE) * LANES, LANES), LANES), :] = value.astype(bf16)
            return carry

        lax.fori_loop(0, TAPS_PAD, join, 0, unroll=4)


def bands(psf):
    taps = jnp.stack([psf, psf[::-1, ::-1]])
    extra = TAPS_PAD - TAPS
    taps = jnp.pad(taps, ((0, 0), (0, extra), (0, extra)))
    table = jax.ShapeDtypeStruct((SLOTS * LANES, LANES), bf16)
    return pl.pallas_call(
        bands_kernel,
        out_shape=[table, table],
        scratch_shapes=[
            pltpu.VMEM((TAPS_PAD * 8, LANES), f32),
            pltpu.VMEM(((TAPS_PAD + PER - 1) * LANES, LANES), f32),
        ],
        compiler_params=pltpu.CompilerParams(vmem_limit_bytes=32 * 1024 * 1024),
    )(taps)


def correlate(line_ref, blocks, depth, band_ref, acc_ref):
    acc_ref[...] = jnp.zeros_like(acc_ref)
    count = PHASES * LANES

    def one(m, carry):
        slot = m * PHASES * LANES
        table = jnp.concatenate(
            [
                band_ref[pl.ds(pl.multiple_of(slot + PER * LANES, LANES), count), :],
                band_ref[pl.ds(pl.multiple_of(slot, LANES), count), :],
            ],
            axis=1,
        )
        product = dot(line_ref[...], table)
        first = EDGE + FIRST_SHIFT - m
        for b in range(blocks):
            for n in range(2):
                acc_ref[n, b, pl.ds(first, depth), :] += product[
                    b * depth:(b + 1) * depth, n * LANES:(n + 1) * LANES
                ]
        return carry

    lax.fori_loop(0, 2 * FIRST_SHIFT + 1, one, 0)


def gather_plane(acc_ref, blocks, depth, r, lane):
    n, k = divmod(r, PER)
    tiles = []
    for first in range(0, blocks, PER):
        tile = None
        for b in reversed(range(first, min(first + PER, blocks))):
            part = roll(acc_ref[n, b, pl.ds(EDGE, depth), :], SPAN * (b - first - k))
            tile = part if tile is None else jnp.where(lane < SPAN * (b - first + 1), part, tile)
        tiles.append(tile)
    return tiles


def put_lines(line_ref, r, low, high, blocks, lane):
    wide = jnp.concatenate([window(low, high, SPAN * b, lane) for b in range(blocks)], axis=0)
    rest = line_ref.shape[0] - wide.shape[0]
    if rest:
        wide = jnp.concatenate([wide, jnp.zeros((rest, LANES), f32)], axis=0)
    line_ref[:, r * LANES:(r + 1) * LANES] = wide.astype(bf16)


def row_table(r, depth, half):
    row = iota2((depth, 2 * half), 0) * PHASES + r
    cell = iota2((depth, 2 * half), 1)
    cell = jnp.where(cell >= half, cell - half, cell)
    return ((row >= cell * COARSE) & (row < cell * COARSE + COARSE)).astype(f32).astype(bf16)


def cell_table(r, depth, half):
    row = iota2((half, depth), 1) * PHASES + r
    cell = iota2((half, depth), 0)
    return ((row >= cell * COARSE) & (row < cell * COARSE + COARSE)).astype(f32).astype(bf16)


def own_columns(width, first, crow):
    place = iota2((8, width), 1) - first
    owner = iota2((8, width), 0)
    hit = (place >= owner * COARSE) & (place < owner * COARSE + COARSE) & (owner < crow)
    return hit.astype(f32).astype(bf16)


def by_columns(first, crow, value):
    picked = own_columns(value.shape[1], first, crow)
    return dot_t(
        jnp.concatenate([picked] * 3, axis=1), jnp.concatenate(split(value, 3), axis=1)
    )


def coarse(red_ref, rows_ref, pull_ref, back_ref, half):
    red = red_ref[...].reshape(red_ref.shape[0] * 8, 2 * half)
    mixed = dot_t(rows_ref[...], one_side(red, 1))
    pull = dot(one_side(mixed[:half], 1), pull_ref[...])
    if back_ref is None:
        return pull
    levels = jnp.concatenate([mixed[half:2 * half], mixed[2 * half:]], axis=1)
    return pull, dot(one_side(levels, 1), back_ref[...])


def start_kernel(sizes, both_ref, own_out, left_out, right_out, red_out, wide_ref):
    planes, depth, half, cols, crow = sizes
    lane = iota2((depth, LANES), 1)
    cells = jnp.zeros((half, LANES), f32)
    for part in range(2):
        wide_ref[part] = both_ref[:, part * LANES:(part + 1) * LANES].astype(f32)
    for r in range(PHASES):
        pieces = []
        for part in range(2):
            value = wide_ref[part, pl.ds(r, planes, stride=PHASES), :]
            if depth > planes:
                value = jnp.concatenate([value, jnp.zeros((depth - planes, LANES), f32)], axis=0)
            pieces.append(value)
        dose, mask = pieces
        own_out[r, :, :LANES] = dose
        own_out[r, :, LANES:] = mask
        left_out[r] = jnp.where(lane < LANES // 2, dose, roll(mask, LANES // 2)).astype(bf16)
        right_out[r] = jnp.where(
            lane < LANES // 2, roll(dose, HALO - cols), roll(mask, LANES // 2 + RIM - cols)
        ).astype(bf16)
        cells += dot(cell_table(r, depth, half), dose.astype(bf16))
    red_out[...] = jnp.zeros_like(red_out)
    red_out[:, :half] = by_columns(0, crow, cells)


def step_kernel(sizes, first, last, *refs):
    planes, depth, half, cols, crow = sizes
    stripe_ref, own_ref, from_left_ref, from_right_ref, red_ref = refs[:5]
    refs = refs[5:]
    if not first:
        mask_ref, refs = refs[0], refs[1:]
    rows_ref, pull_ref, back_ref, inside_ref, fwd_ref, adj_ref = refs[:6]
    refs = refs[6:]
    if last:
        v_out, resist_out, red_out = refs[:3]
        refs = refs[3:]
        x_ref, e_ref, t_ref, acc_ref, row_ref = refs
    else:
        v_out, left_out, right_out, red_out = refs[:4]
        refs = refs[4:]
        if first:
            mask_ref, refs = refs[0], refs[1:]
        x_ref, e_ref, t_ref, acc_ref = refs
    lane = iota2((depth, LANES), 1)
    filled = iota2((depth, LANES), 0) < planes
    inner = cols + HALO - LANES

    pull, back = coarse(red_ref, rows_ref, pull_ref, back_ref, half)
    pull = jnp.concatenate(split(pull, 2), axis=0)
    back = jnp.concatenate(split(back, 2), axis=0)

    for r in range(PHASES):
        if first:
            own = roll(own_ref[r, :, :LANES], HALO)
            left = from_left_ref[r].astype(f32)
            right_raw = from_right_ref[r].astype(f32)
            right = roll(right_raw, inner)
            mask_own = roll(own_ref[r, :, LANES:], RIM)
            t0 = jnp.where(
                lane < RIM, roll(left, LANES // 2), mask_own
            )
            t1 = jnp.where(
                lane < cols + RIM - LANES, mask_own, roll(right_raw, cols + RIM - LANES - LANES // 2)
            )
            mask_ref[r, :, :LANES] = t0.astype(bf16)
            mask_ref[r, :, LANES:] = t1.astype(bf16)
        else:
            own = roll(own_ref[r], HALO)
            left = roll(from_left_ref[r // 2], LANES // 2 * (r % 2))
            right = roll(from_right_ref[r // 2], inner - LANES // 2 * (r % 2))
        t0 = jnp.where(lane < HALO, left, own)
        t1 = jnp.where(lane < inner, own, jnp.where(lane < inner + HALO, right, 0.0))
        pulled = dot(row_table(r, depth, half), pull)
        t0 = (t0 - pulled[:, :LANES]).astype(bf16).astype(f32)
        t1 = (t1 - pulled[:, LANES:]).astype(bf16).astype(f32)
        put_lines(x_ref, r, t0, t1, acc_ref.shape[1], lane)
        t_ref[r] = window(t0, t1, HALO, lane)

    blocks = acc_ref.shape[1]
    correlate(x_ref, blocks, depth, fwd_ref, acc_ref)

    inside = inside_ref[...]
    sums = jnp.zeros((half, 2 * LANES), f32)
    tile_blocks = e_ref.shape[0] // depth
    for r in range(PHASES):
        t0, t1 = gather_plane(acc_ref, blocks, depth, r, lane)
        exposure = jnp.concatenate([t0, t1], axis=1) + dot(row_table(r, depth, half), back)
        resist = 1.0 / (1.0 + jnp.exp(-resist_gain * (exposure - resist_level)))
        error = (resist - mask_ref[r].astype(f32)) * resist_gain * resist * (1.0 - resist)
        error = jnp.where(iota2((depth, 2 * LANES), 0) < planes, error * inside, 0.0)
        if last:
            row_ref[pl.ds(r, planes, stride=PHASES), :] = window(
                resist[:, :LANES], resist[:, LANES:], RIM, lane
            )[:planes]
        rounded = error.astype(bf16)
        sums += dot(cell_table(r, depth, half), rounded)
        rounded = rounded.astype(f32)
        put_lines(e_ref, r, rounded[:, :LANES], rounded[:, LANES:], tile_blocks, lane)
    red_out[:, half:] = by_columns(RIM, crow, sums)
    own_rows = planes * PHASES // sizes_stripes(planes, v_out, last)
    if last:
        start = pl.multiple_of(stripe_ref[0] * own_rows, 8)
        resist_out[...] = row_ref[pl.ds(start, own_rows), :][:, :cols]

    correlate(e_ref, tile_blocks, depth, adj_ref, acc_ref)

    cells = jnp.zeros((half, LANES), f32)
    before = None
    for r in range(PHASES):
        (t0,) = gather_plane(acc_ref, tile_blocks, depth, r, lane)
        value = jnp.where(filled, t_ref[r] - step_length * t0, 0.0)
        if last:
            row_ref[pl.ds(r, planes, stride=PHASES), :] = value[:planes]
            continue
        v_out[r] = value
        table = cell_table(r, depth, half)
        for piece in split(value, 2):
            cells += dot(table, piece)
        if r % 2:
            half_lane = lane < LANES // 2
            left_out[r // 2] = jnp.where(half_lane, before, roll(value, LANES // 2))
            right_out[r // 2] = jnp.where(
                half_lane, roll(before, HALO - cols), roll(value, HALO - cols + LANES // 2)
            )
        before = value
    if last:
        v_out[...] = row_ref[pl.ds(start, own_rows), :][:, :cols]
        red_out[:, :half] = jnp.zeros((8, half), f32)
    else:
        red_out[:, :half] = by_columns(0, crow, cells)


def sizes_stripes(planes, v_out, last):
    return planes * PHASES // v_out.shape[0] if last else 1


def end_kernel(sizes, stripe_ref, v_ref, red_ref, rows_ref, pull_ref, out_ref):
    planes, depth, half, cols, crow = sizes
    pull = coarse(red_ref, rows_ref, pull_ref, None, half)
    pull = jnp.concatenate(split(pull, 2), axis=0)
    rows = v_ref.shape[0]
    row = iota2((rows, 2 * half), 0) + stripe_ref[0] * rows
    cell = iota2((rows, 2 * half), 1)
    cell = jnp.where(cell >= half, cell - half, cell)
    table = ((row >= cell * COARSE) & (row < cell * COARSE + COARSE)).astype(f32).astype(bf16)
    pulled = dot(table, pull)
    out_ref[...] = v_ref[...] - pulled[:, :cols]


def gauss(rows_at, cols_at, rows_ok, cols_ok):
    dist = (rows_at[:, None] - cols_at[None, :]).astype(f32)
    table = jnp.exp(-dist * dist / (2.0 * SIGMA * SIGMA)) / (math.sqrt(2.0 * math.pi) * SIGMA)
    return jnp.where(rows_ok[:, None] & cols_ok[None, :], table, 0.0)


def per_device(dose, target, psf):
    rows, cols = dose.shape
    stripes = lax.axis_size("stripe")
    scans = lax.axis_size("scan")
    stripe = lax.axis_index("stripe").reshape(1)
    scan = lax.axis_index("scan")
    planes = rows * stripes // PHASES
    depth = round_up(planes, 8)
    ncx = rows * stripes // COARSE
    crow = cols // COARSE
    ncy = crow * scans
    half = round_up(ncx, LANES // 2)
    sizes = (planes, depth, half, cols, crow)

    forward = [(i, i + 1) for i in range(scans - 1)]
    backward = [(i + 1, i) for i in range(scans - 1)]

    def shift(to_right, to_left):
        return (
            lax.ppermute(to_right, "scan", forward),
            lax.ppermute(to_left, "scan", backward),
        )

    def share(red):
        return lax.all_to_all(jnp.broadcast_to(red, (scans,) + red.shape), "scan", 0, 0)

    vmem = pl.BlockSpec(memory_space=pltpu.VMEM)
    smem = pl.BlockSpec(memory_space=pltpu.SMEM)
    params = pltpu.CompilerParams(vmem_limit_bytes=48 * 1024 * 1024)

    def call(kernel, out_shape, args, scratch=()):
        return pl.pallas_call(
            kernel,
            out_shape=out_shape,
            in_specs=[smem if a is stripe else vmem for a in args],
            scratch_shapes=list(scratch),
            compiler_params=params,
        )(*args)

    def array(shape, dtype=f32):
        return jax.ShapeDtypeStruct(shape, dtype)

    row_at = jnp.arange(half, dtype=jnp.int32)
    lane_at = jnp.arange(2 * half, dtype=jnp.int32)
    row_ok = row_at < ncx
    gx = gauss(row_at, row_at, row_ok, row_ok)
    gxc = gauss(row_at, lane_at, row_ok, lane_at < ncx)
    gxs = gauss(row_at, lane_at - half, row_ok, (lane_at >= half) & (lane_at < half + ncx))
    rows_table = other_side(jnp.concatenate([gxs, gxc, dot(gx, gxs, highest)], axis=0), 1)
    held = jnp.arange(8 * scans, dtype=jnp.int32)
    held_ok = held % 8 < crow
    held_at = (held // 8) * crow + held % 8
    cell_at = jnp.arange(ncy, dtype=jnp.int32)
    cell_ok = cell_at < ncy

    def columns(rim):
        at = scan * cols - rim + jnp.arange(2 * LANES, dtype=jnp.int32)
        return at // COARSE, (at >= 0) & (at < cols * scans)

    pull_scale = step_length * back_ratio / (COARSE * COARSE)
    at2, ok2 = columns(HALO)
    at1, ok1 = columns(RIM)
    at0, ok0 = columns(0)
    pull_table = other_side(pull_scale * gauss(held_at, at2, held_ok, ok2), 0)
    end_table = other_side(pull_scale * gauss(held_at, at0, held_ok, ok0), 0)
    level_table = back_ratio / (COARSE * COARSE) * gauss(held_at, at1, held_ok, ok1)
    again = dot(
        gauss(held_at, cell_at, held_ok, cell_ok), gauss(cell_at, at1, cell_ok, ok1), highest
    )
    back_table = other_side(
        jnp.concatenate([level_table, -back_ratio * pull_scale * again], axis=0), 0
    )
    inside = ok1.astype(f32)[None, :]

    fill = ((0, 0), (0, LANES - cols))
    both = jnp.concatenate([jnp.pad(dose, fill), jnp.pad(target.astype(bf16), fill)], axis=1)
    both = lax.all_gather(both, "stripe", axis=0, tiled=True)
    few = array((8, 2 * half))
    halo = array((PHASES, depth, LANES), bf16)
    own, to_left, to_right, red = call(
        functools.partial(start_kernel, sizes),
        [array((PHASES, depth, 2 * LANES)), halo, halo, few],
        [both],
        [pltpu.VMEM((2, planes * PHASES, LANES), f32)],
    )
    fwd, adj = bands(psf)

    blocks2 = -(-(cols + 2 * RIM) // SPAN)
    blocks1 = -(-cols // SPAN)
    scratch = [
        pltpu.VMEM((round_up(blocks2 * depth, 16), PHASES * LANES), bf16),
        pltpu.VMEM((round_up(blocks1 * depth, 16), PHASES * LANES), bf16),
        pltpu.VMEM((PHASES, depth, LANES), f32),
        pltpu.VMEM((2, blocks2, depth + 2 * EDGE, LANES), f32),
    ]
    plane = array((PHASES, depth, LANES))
    packed = array((PHASES // 2, depth, LANES))
    tile = array((rows, cols))
    mask = None
    for step in range(ITERS):
        first = step == 0
        last = step == ITERS - 1
        from_left, from_right = shift(to_right, to_left)
        args = [stripe, own, from_left, from_right, share(red)]
        if not first:
            args.append(mask)
        args += [rows_table, pull_table, back_table, inside, fwd, adj]
        kernel = functools.partial(step_kernel, sizes, first, last)
        if last:
            row_scratch = pltpu.VMEM((planes * PHASES, LANES), f32)
            v, resist, red = call(kernel, [tile, tile, few], args, scratch + [row_scratch])
        elif first:
            shape = [plane, packed, packed, few, array((PHASES, depth, 2 * LANES), bf16)]
            own, to_left, to_right, red, mask = call(kernel, shape, args, scratch)
        else:
            shape = [plane, packed, packed, few]
            own, to_left, to_right, red = call(kernel, shape, args, scratch)

    updated = call(
        functools.partial(end_kernel, sizes),
        tile,
        [stripe, v, share(red), rows_table, end_table],
    )
    return resist, updated


def solution(mesh):
    in_specs = (P("stripe", "scan"), P("stripe", "scan"), P())
    out_specs = (P("stripe", "scan"), P("stripe", "scan"))
    return jax.shard_map(
        per_device, mesh=mesh, in_specs=in_specs, out_specs=out_specs, check_vma=False
    )
```

profile of v0, /device:TPU:0, one launch (start us, length us, event | category | flops | bytes accessed | tf_op | source)
XLA Modules:
  0.0 141.2 jit_solution(4694304792463249318)
XLA Ops:
  0.6 0.9 convert_element_type.80
  1.6 0.8 fusion.4
  2.4 11.1 %all_gather.3.both_ref = bf16[800,256]{1,0:T(8,128)(2,1)S(1)} all-gather(bf16[200,256]{1,0:T(8,128)(2,1)S(1)} %fusion.4), channel_id=1, replica_groups=mesh['stripe'=4,'scan'=8] {'stripe'}, dimensions={0}, use_global_device_ids=true | all-gather | bytes 512000 | tf_op jit(solution)/shard_map/all_gather | solution.py:464
  13.5 1.2 shard_map.50
  14.6 0.9 copy-done.1
  15.5 0.6 broadcast_in_dim.31
  16.2 4.9 %all-to-all-start = ((f32[8,8,128]{2,1,0:T(8,128)}), f32[8,8,128]{2,1,0:T(8,128)S(1)}, u32[]{:S(2)}, u32[]{:S(2)}) async-start(f32[8,8,128]{2,1,0:T(8,128)} %broadcast_in_dim.31), calls=%async_computation | async-start | bytes 65536 | tf_op jit(solution)/shard_map/all_to_all | solution.py:412
  21.0 3.1 %collective-permute-start = (bf16[8,104,128]{2,1,0:T(8,128)(2,1)}, bf16[8,104,128]{2,1,0:T(8,128)(2,1)}, u32[]{:S(2)}, u32[]{:S(2)}) collective-permute-start(bf16[8,104,128]{2,1,0:T(8,128)(2,1)} %get-tuple-element.25), channel_id=1, source_target_pairs={{0,1},{1,2},{2,3},{3,4},{4,5},{5,6},{6,7},{8,9},{9,10},{10,11},{11... | collective-permute-start | bytes 638984 | tf_op jit(solution)/shard_map/ppermute | solution.py:407
  24.1 1.3 collective-permute-start.1
  25.6 0.8 rev.3
  26.4 0.2 fusion.44
  26.9 0.3 convolution_multiply_fusion
  27.7 0.1 constant_dynamic-update-slice_fusion.17
  28.2 0.1 constant_dynamic-update-slice_fusion.6.refs_6_.refs_7_
  28.7 4.6 %shard_map.51 = (bf16[9728,128]{1,0:T(8,128)(2,1)S(1)}, bf16[9728,128]{1,0:T(8,128)(2,1)S(1)}) custom-call(bf16[2,64,64]{2,1,0:T(8,128)(2,1)S(1)} %fusion.56.taps_ref), custom_call_target="tpu_custom_call" | custom-call | tf_op jit(solution)/shard_map/pallas_call | solution.py:140
  33.3 1.4 %copy-done = bf16[9728,128]{1,0:T(8,128)(2,1)} copy-done((bf16[9728,128]{1,0:T(8,128)(2,1)}, bf16[9728,128]{1,0:T(8,128)(2,1)S(1)}, u32[]{:S(2)}) %copy-start) | copy-done | bytes 2490392
  34.8 1.1 copy-done.2
  35.9 13.5 %shard_map.52 = (f32[8,104,128]{2,1,0:T(8,128)S(1)}, f32[4,104,128]{2,1,0:T(8,128)S(1)}, f32[4,104,128]{2,1,0:T(8,128)S(1)}, f32[8,128]{1,0:T(8,128)S(1)}, bf16[8,104,256]{2,1,0:T(8,128)(2,1)S(1)}) custom-call(s32[1]{0:T(128)} %bitcast.refs_0_.stripe_ref, f32[8,104,256]{2,1,0:T(8,128)S(1)} %copy-done.2, bf16[8,104,128]{2,1,0:T(8,128)(2,1)} %collective-permute-done.refs_2_, ...), custom_call_target="tpu_custom_call" | custom-call | tf_op jit(solution)/shard_map/pallas_call | solution.py:419
  49.4 3.5 %collective-permute-start.2 = (f32[4,104,128]{2,1,0:T(8,128)S(1)}, f32[4,104,128]{2,1,0:T(8,128)S(1)}, u32[]{:S(2)}, u32[]{:S(2)}) collective-permute-start(f32[4,104,128]{2,1,0:T(8,128)S(1)} %get-tuple-element.31), channel_id=1, source_target_pairs={{0,1},{1,2},{2,3},{3,4},{4,5},{5,6},{6,7},{8,9},{9,10},{10,11},{11... | collective-permute-start | bytes 638984 | tf_op jit(solution)/shard_map/ppermute | solution.py:407
  53.0 1.3 collective-permute-start.3
  54.3 12.6 %all_to_all.25.refs_4_ = f32[8,8,128]{2,1,0:T(8,128)S(1)} all-to-all(f32[8,8,128]{2,1,0:T(8,128)S(1)} %broadcast_in_dim.38), channel_id=1, replica_groups=mesh['stripe'=4,'scan'=8] {'scan'}, dimensions={0} | all-to-all | bytes 65536 | tf_op jit(solution)/shard_map/all_to_all | solution.py:412
  66.9 12.8 %shard_map.53 = (f32[8,104,128]{2,1,0:T(8,128)S(1)}, f32[4,104,128]{2,1,0:T(8,128)S(1)}, f32[4,104,128]{2,1,0:T(8,128)S(1)}, f32[8,128]{1,0:T(8,128)S(1)}) custom-call(s32[1]{0:T(128)} %bitcast.refs_0_.stripe_ref, f32[8,104,128]{2,1,0:T(8,128)S(1)} %get-tuple-element.30.refs_1_, f32[4,104,128]{2,1,0:T(8,128)S(1)} %collective-permute-done.2.refs_2_, ...), custom_call_target="tpu_custom_call" | custom-call | tf_op jit(solution)/shard_map/pallas_call | solution.py:419
  79.6 1.7 %collective-permute-start.4 = (f32[4,104,128]{2,1,0:T(8,128)S(1)}, f32[4,104,128]{2,1,0:T(8,128)S(1)}, u32[]{:S(2)}, u32[]{:S(2)}) collective-permute-start(f32[4,104,128]{2,1,0:T(8,128)S(1)} %get-tuple-element.36), channel_id=1, source_target_pairs={{0,1},{1,2},{2,3},{3,4},{4,5},{5,6},{6,7},{8,9},{9,10},{10,11},{11... | collective-permute-start | bytes 638984 | tf_op jit(solution)/shard_map/ppermute | solution.py:407
  81.3 1.3 collective-permute-start.5
  82.6 10.1 %all_to_all.26.refs_4_ = f32[8,8,128]{2,1,0:T(8,128)S(1)} all-to-all(f32[8,8,128]{2,1,0:T(8,128)S(1)} %broadcast_in_dim.39), channel_id=1, replica_groups=mesh['stripe'=4,'scan'=8] {'scan'}, dimensions={0} | all-to-all | bytes 65536 | tf_op jit(solution)/shard_map/all_to_all | solution.py:412
  92.7 12.8 %shard_map.54 = (f32[8,104,128]{2,1,0:T(8,128)S(1)}, f32[4,104,128]{2,1,0:T(8,128)S(1)}, f32[4,104,128]{2,1,0:T(8,128)S(1)}, f32[8,128]{1,0:T(8,128)S(1)}) custom-call(s32[1]{0:T(128)} %bitcast.refs_0_.stripe_ref, f32[8,104,128]{2,1,0:T(8,128)S(1)} %get-tuple-element.35.refs_1_, f32[4,104,128]{2,1,0:T(8,128)S(1)} %collective-permute-done.4.refs_2_, ...), custom_call_target="tpu_custom_call" | custom-call | tf_op jit(solution)/shard_map/pallas_call | solution.py:419
  105.5 1.6 %collective-permute-start.6 = (f32[4,104,128]{2,1,0:T(8,128)S(1)}, f32[4,104,128]{2,1,0:T(8,128)S(1)}, u32[]{:S(2)}, u32[]{:S(2)}) collective-permute-start(f32[4,104,128]{2,1,0:T(8,128)S(1)} %get-tuple-element.40), channel_id=1, source_target_pairs={{0,1},{1,2},{2,3},{3,4},{4,5},{5,6},{6,7},{8,9},{9,10},{10,11},{11... | collective-permute-start | bytes 638984 | tf_op jit(solution)/shard_map/ppermute | solution.py:407
  107.1 1.3 collective-permute-start.7
  108.4 10.1 %all_to_all.27.refs_4_ = f32[8,8,128]{2,1,0:T(8,128)S(1)} all-to-all(f32[8,8,128]{2,1,0:T(8,128)S(1)} %broadcast_in_dim.40), channel_id=1, replica_groups=mesh['stripe'=4,'scan'=8] {'scan'}, dimensions={0} | all-to-all | bytes 65536 | tf_op jit(solution)/shard_map/all_to_all | solution.py:412
  118.5 13.3 %shard_map.55 = (f32[200,100]{1,0:T(8,128)S(1)}, f32[200,100]{1,0:T(8,128)}, f32[8,128]{1,0:T(8,128)S(1)}) custom-call(s32[1]{0:T(128)} %bitcast.refs_0_.stripe_ref, f32[8,104,128]{2,1,0:T(8,128)S(1)} %get-tuple-element.39.refs_1_, f32[4,104,128]{2,1,0:T(8,128)S(1)} %collective-permute-done.6.refs_2_, f32[4,104,128]{2,1,0:T(8,128)S(1)} %collective-permute-done.7.refs_3_, ...), custom_call_target="tpu_custom_call" | custom-call | tf_op jit(solution)/shard_map/pallas_call | solution.py:419
  131.9 8.1 %all_to_all.28.red_ref = f32[8,8,128]{2,1,0:T(8,128)S(1)} all-to-all(f32[8,8,128]{2,1,0:T(8,128)S(1)} %broadcast_in_dim.42), channel_id=1, replica_groups=mesh['stripe'=4,'scan'=8] {'scan'}, dimensions={0} | all-to-all | bytes 65536 | tf_op jit(solution)/shard_map/all_to_all | solution.py:412
  140.0 1.3 shard_map.56
  (59 shorter events, 1.5 us)
Async XLA Ops:
  0.6 28.0 %copy-start.5 = (bf16[61,61]{1,0:T(8,128)(2,1)S(1)}, bf16[61,61]{1,0:T(8,128)(2,1)}, u32[]{:S(2)}) copy-start(bf16[61,61]{1,0:T(8,128)(2,1)} %param.5) | copy-start | bytes 22330
  14.6 0.9 copy-start.1
  16.2 18.6 %all-to-all-start = ((f32[8,8,128]{2,1,0:T(8,128)}), f32[8,8,128]{2,1,0:T(8,128)S(1)}, u32[]{:S(2)}, u32[]{:S(2)}) async-start(f32[8,8,128]{2,1,0:T(8,128)} %broadcast_in_dim.31), calls=%async_computation | async-start | bytes 65536 | tf_op jit(solution)/shard_map/all_to_all | solution.py:412
  21.0 13.7 %collective-permute-start = (bf16[8,104,128]{2,1,0:T(8,128)(2,1)}, bf16[8,104,128]{2,1,0:T(8,128)(2,1)}, u32[]{:S(2)}, u32[]{:S(2)}) collective-permute-start(bf16[8,104,128]{2,1,0:T(8,128)(2,1)} %get-tuple-element.25), channel_id=1, source_target_pairs={{0,1},{1,2},{2,3},{3,4},{4,5},{5,6},{6,7},{8,9},{9,10},{10,11},{11... | collective-permute-start | bytes 638984 | tf_op jit(solution)/shard_map/ppermute | solution.py:407
  24.1 10.6 %collective-permute-start.1 = (bf16[8,104,128]{2,1,0:T(8,128)(2,1)}, bf16[8,104,128]{2,1,0:T(8,128)(2,1)}, u32[]{:S(2)}, u32[]{:S(2)}) collective-permute-start(bf16[8,104,128]{2,1,0:T(8,128)(2,1)} %get-tuple-element.26), channel_id=1, source_target_pairs={{1,0},{2,1},{3,2},{4,3},{5,4},{6,5},{7,6},{9,8},{10,9},{11,10},{12... | collective-permute-start | bytes 638984 | tf_op jit(solution)/shard_map/ppermute | solution.py:408
  27.8 0.8 copy-start.3
  33.2 1.5 %copy-start = (bf16[9728,128]{1,0:T(8,128)(2,1)}, bf16[9728,128]{1,0:T(8,128)(2,1)S(1)}, u32[]{:S(2)}) copy-start(bf16[9728,128]{1,0:T(8,128)(2,1)S(1)} %get-tuple-element.29.refs_10_.refs_11_) | copy-start | bytes 7471108
  34.8 1.2 copy-start.2
  49.4 17.4 %collective-permute-start.2 = (f32[4,104,128]{2,1,0:T(8,128)S(1)}, f32[4,104,128]{2,1,0:T(8,128)S(1)}, u32[]{:S(2)}, u32[]{:S(2)}) collective-permute-start(f32[4,104,128]{2,1,0:T(8,128)S(1)} %get-tuple-element.31), channel_id=1, source_target_pairs={{0,1},{1,2},{2,3},{3,4},{4,5},{5,6},{6,7},{8,9},{9,10},{10,11},{11... | collective-permute-start | bytes 638984 | tf_op jit(solution)/shard_map/ppermute | solution.py:407
  53.0 13.9 %collective-permute-start.3 = (f32[4,104,128]{2,1,0:T(8,128)S(1)}, f32[4,104,128]{2,1,0:T(8,128)S(1)}, u32[]{:S(2)}, u32[]{:S(2)}) collective-permute-start(f32[4,104,128]{2,1,0:T(8,128)S(1)} %get-tuple-element.32), channel_id=1, source_target_pairs={{1,0},{2,1},{3,2},{4,3},{5,4},{6,5},{7,6},{9,8},{10,9},{11,10},{12... | collective-permute-start | bytes 638984 | tf_op jit(solution)/shard_map/ppermute | solution.py:408
  79.6 13.1 %collective-permute-start.4 = (f32[4,104,128]{2,1,0:T(8,128)S(1)}, f32[4,104,128]{2,1,0:T(8,128)S(1)}, u32[]{:S(2)}, u32[]{:S(2)}) collective-permute-start(f32[4,104,128]{2,1,0:T(8,128)S(1)} %get-tuple-element.36), channel_id=1, source_target_pairs={{0,1},{1,2},{2,3},{3,4},{4,5},{5,6},{6,7},{8,9},{9,10},{10,11},{11... | collective-permute-start | bytes 638984 | tf_op jit(solution)/shard_map/ppermute | solution.py:407
  81.3 11.4 %collective-permute-start.5 = (f32[4,104,128]{2,1,0:T(8,128)S(1)}, f32[4,104,128]{2,1,0:T(8,128)S(1)}, u32[]{:S(2)}, u32[]{:S(2)}) collective-permute-start(f32[4,104,128]{2,1,0:T(8,128)S(1)} %get-tuple-element.37), channel_id=1, source_target_pairs={{1,0},{2,1},{3,2},{4,3},{5,4},{6,5},{7,6},{9,8},{10,9},{11,10},{12... | collective-permute-start | bytes 638984 | tf_op jit(solution)/shard_map/ppermute | solution.py:408
  105.5 13.1 %collective-permute-start.6 = (f32[4,104,128]{2,1,0:T(8,128)S(1)}, f32[4,104,128]{2,1,0:T(8,128)S(1)}, u32[]{:S(2)}, u32[]{:S(2)}) collective-permute-start(f32[4,104,128]{2,1,0:T(8,128)S(1)} %get-tuple-element.40), channel_id=1, source_target_pairs={{0,1},{1,2},{2,3},{3,4},{4,5},{5,6},{6,7},{8,9},{9,10},{10,11},{11... | collective-permute-start | bytes 638984 | tf_op jit(solution)/shard_map/ppermute | solution.py:407
  107.1 11.4 %collective-permute-start.7 = (f32[4,104,128]{2,1,0:T(8,128)S(1)}, f32[4,104,128]{2,1,0:T(8,128)S(1)}, u32[]{:S(2)}, u32[]{:S(2)}) collective-permute-start(f32[4,104,128]{2,1,0:T(8,128)S(1)} %get-tuple-element.41), channel_id=1, source_target_pairs={{1,0},{2,1},{3,2},{4,3},{5,4},{6,5},{7,6},{9,8},{10,9},{11,10},{12... | collective-permute-start | bytes 638984 | tf_op jit(solution)/shard_map/ppermute | solution.py:408
  118.5 21.4 %copy-start.4 = (bf16[384,256]{1,0:T(8,128)(2,1)S(1)}, bf16[384,256]{1,0:T(8,128)(2,1)}, u32[]{:S(2)}) copy-start(bf16[384,256]{1,0:T(8,128)(2,1)} %copy-done.3) | copy-start | bytes 589828
where the time goes:
time: 142 us; the launch traced here: 141 us
  Pallas kernels  59.4 us (42%)
  blocking collectives  52 us (37%)
  starting transfers between devices  19.9 us (14%)
  local copies, waits for them, and re-layouts  4.96 us (3%)
  other arithmetic  3.38 us (2%)
    pallas_call x6, Pallas kernels, call(): pl.pallas_call(kernel, out_shape=out_shape, in_specs=[smem if a is stripe...  54.8 us
    all_to_all x4, blocking collectives, share(): lax.all_to_all(jnp.broadcast_to(red, (scans,) + red.shape), 'scan', 0, 0)  40.9 us
    all_gather x1, blocking collectives, per_device(): both = lax.all_gather(both, 'stripe', axis=0, tiled=True)  11.1 us
    ppermute x4, starting transfers between devices, shift(): lax.ppermute(to_right, 'scan', forward)  9.9 us
    ppermute x4, starting transfers between devices, shift(): lax.ppermute(to_left, 'scan', backward)  5.16 us
    all_to_all x1, starting transfers between devices, share(): lax.all_to_all(jnp.broadcast_to(red, (scans,) + red.shape), 'scan', 0, 0)  4.88 us
    pallas_call x1, Pallas kernels, bands(): pl.pallas_call(bands_kernel, out_shape=[table, table], scratch_shapes=[pl...  4.58 us
    unnamed x12, local copies, waits for them, and re-layouts  3.51 us
  transfers between devices with their start and end apart: 9, of which 0 were waited for; matrix products, arithmetic and copies ran while one was open for 2% of the time, Pallas kernels for 3%

commit v1 on v0

--- a/solution.py
+++ b/solution.py
@@ -148,38 +148,34 @@
     )(taps)
 
 
-def correlate(line_ref, blocks, depth, band_ref, acc_ref):
-    acc_ref[...] = jnp.zeros_like(acc_ref)
+def correlate(line_ref, blocks, depth, band_ref, part_ref, acc_ref):
     count = PHASES * LANES
-
-    def one(m, carry):
+    height = line_ref.shape[0]
+    for m in range(2 * FIRST_SHIFT + 1):
         slot = m * PHASES * LANES
         table = jnp.concatenate(
-            [
-                band_ref[pl.ds(pl.multiple_of(slot + PER * LANES, LANES), count), :],
-                band_ref[pl.ds(pl.multiple_of(slot, LANES), count), :],
-            ],
-            axis=1,
+            [band_ref[pl.ds(slot + PER * LANES, count), :], band_ref[pl.ds(slot, count), :]], axis=1
         )
         product = dot(line_ref[...], table)
-        first = EDGE + FIRST_SHIFT - m
+        for n in range(2):
+            part_ref[n, m, pl.ds(EDGE, height), :] = product[:, n * LANES:(n + 1) * LANES]
+    for n in range(2):
         for b in range(blocks):
-            for n in range(2):
-                acc_ref[n, b, pl.ds(first, depth), :] += product[
-                    b * depth:(b + 1) * depth, n * LANES:(n + 1) * LANES
-                ]
-        return carry
-
-    lax.fori_loop(0, 2 * FIRST_SHIFT + 1, one, 0)
-
-
-def gather_plane(acc_ref, blocks, depth, r, lane):
+            total = None
+            for m in range(2 * FIRST_SHIFT + 1):
+                first = EDGE + b * depth + m - FIRST_SHIFT
+                piece = part_ref[n, m, pl.ds(first, depth), :]
+                total = piece if total is None else total + piece
+            acc_ref[n, b] = total
+
+
+def gather_plane(acc_ref, blocks, r, lane):
     n, k = divmod(r, PER)
     tiles = []
     for first in range(0, blocks, PER):
         tile = None
         for b in reversed(range(first, min(first + PER, blocks))):
-            part = roll(acc_ref[n, b, pl.ds(EDGE, depth), :], SPAN * (b - first - k))
+            part = roll(acc_ref[n, b], SPAN * (b - first - k))
             tile = part if tile is None else jnp.where(lane < SPAN * (b - first + 1), part, tile)
         tiles.append(tile)
     return tiles
@@ -230,7 +226,9 @@
     return pull, dot(one_side(levels, 1), back_ref[...])
 
 
-def start_kernel(sizes, both_ref, own_out, left_out, right_out, red_out, wide_ref):
+def start_kernel(
+    sizes, both_ref, own_out, left_out, right_out, red_out, in_row_out, in_cell_out, wide_ref
+):
     planes, depth, half, cols, crow = sizes
     lane = iota2((depth, LANES), 1)
     cells = jnp.zeros((half, LANES), f32)
@@ -250,7 +248,9 @@
         right_out[r] = jnp.where(
             lane < LANES // 2, roll(dose, HALO - cols), roll(mask, LANES // 2 + RIM - cols)
         ).astype(bf16)
-        cells += dot(cell_table(r, depth, half), dose.astype(bf16))
+        in_row_out[r] = row_table(r, depth, half)
+        in_cell_out[r] = cell_table(r, depth, half)
+        cells += dot(in_cell_out[r], dose.astype(bf16))
     red_out[...] = jnp.zeros_like(red_out)
     red_out[:, :half] = by_columns(0, crow, cells)
 
@@ -261,20 +261,25 @@
     refs = refs[5:]
     if not first:
         mask_ref, refs = refs[0], refs[1:]
-    rows_ref, pull_ref, back_ref, inside_ref, fwd_ref, adj_ref = refs[:6]
-    refs = refs[6:]
+    rows_ref, pull_ref, back_ref, inside_ref, in_row_ref, in_cell_ref, fwd_ref, adj_ref = refs[:8]
+    refs = refs[8:]
     if last:
         v_out, resist_out, red_out = refs[:3]
         refs = refs[3:]
-        x_ref, e_ref, t_ref, acc_ref, row_ref = refs
+        x_ref, e_ref, t_ref, acc_ref, part_ref, row_ref = refs
     else:
         v_out, left_out, right_out, red_out = refs[:4]
         refs = refs[4:]
         if first:
             mask_ref, refs = refs[0], refs[1:]
-        x_ref, e_ref, t_ref, acc_ref = refs
+        x_ref, e_ref, t_ref, acc_ref, part_ref = refs
     lane = iota2((depth, LANES), 1)
     filled = iota2((depth, LANES), 0) < planes
+    ends = part_ref.shape[2] - EDGE
+    for n in range(2):
+        for m in range(2 * FIRST_SHIFT + 1):
+            part_ref[n, m, pl.ds(0, EDGE), :] = jnp.zeros((EDGE, LANES), f32)
+            part_ref[n, m, pl.ds(ends, EDGE), :] = jnp.zeros((EDGE, LANES), f32)
     inner = cols + HALO - LANES
 
     pull, back = coarse(red_ref, rows_ref, pull_ref, back_ref, half)
@@ -302,21 +307,21 @@
             right = roll(from_right_ref[r // 2], inner - LANES // 2 * (r % 2))
         t0 = jnp.where(lane < HALO, left, own)
         t1 = jnp.where(lane < inner, own, jnp.where(lane < inner + HALO, right, 0.0))
-        pulled = dot(row_table(r, depth, half), pull)
+        pulled = dot(in_row_ref[r], pull)
         t0 = (t0 - pulled[:, :LANES]).astype(bf16).astype(f32)
         t1 = (t1 - pulled[:, LANES:]).astype(bf16).astype(f32)
         put_lines(x_ref, r, t0, t1, acc_ref.shape[1], lane)
         t_ref[r] = window(t0, t1, HALO, lane)
 
     blocks = acc_ref.shape[1]
-    correlate(x_ref, blocks, depth, fwd_ref, acc_ref)
+    correlate(x_ref, blocks, depth, fwd_ref, part_ref, acc_ref)
 
     inside = inside_ref[...]
     sums = jnp.zeros((half, 2 * LANES), f32)
     tile_blocks = e_ref.shape[0] // depth
     for r in range(PHASES):
-        t0, t1 = gather_plane(acc_ref, blocks, depth, r, lane)
-        exposure = jnp.concatenate([t0, t1], axis=1) + dot(row_table(r, depth, half), back)
+        t0, t1 = gather_plane(acc_ref, blocks, r, lane)
+        exposure = jnp.concatenate([t0, t1], axis=1) + dot(in_row_ref[r], back)
         resist = 1.0 / (1.0 + jnp.exp(-resist_gain * (exposure - resist_level)))
         error = (resist - mask_ref[r].astype(f32)) * resist_gain * resist * (1.0 - resist)
         error = jnp.where(iota2((depth, 2 * LANES), 0) < planes, error * inside, 0.0)
@@ -325,7 +330,7 @@
                 resist[:, :LANES], resist[:, LANES:], RIM, lane
             )[:planes]
         rounded = error.astype(bf16)
-        sums += dot(cell_table(r, depth, half), rounded)
+        sums += dot(in_cell_ref[r], rounded)
         rounded = rounded.astype(f32)
         put_lines(e_ref, r, rounded[:, :LANES], rounded[:, LANES:], tile_blocks, lane)
     red_out[:, half:] = by_columns(RIM, crow, sums)
@@ -334,18 +339,18 @@
         start = pl.multiple_of(stripe_ref[0] * own_rows, 8)
         resist_out[...] = row_ref[pl.ds(start, own_rows), :][:, :cols]
 
-    correlate(e_ref, tile_blocks, depth, adj_ref, acc_ref)
+    correlate(e_ref, tile_blocks, depth, adj_ref, part_ref, acc_ref)
 
     cells = jnp.zeros((half, LANES), f32)
     before = None
     for r in range(PHASES):
-        (t0,) = gather_plane(acc_ref, tile_blocks, depth, r, lane)
+        (t0,) = gather_plane(acc_ref, tile_blocks, r, lane)
         value = jnp.where(filled, t_ref[r] - step_length * t0, 0.0)
         if last:
             row_ref[pl.ds(r, planes, stride=PHASES), :] = value[:planes]
             continue
         v_out[r] = value
-        table = cell_table(r, depth, half)
+        table = in_cell_ref[r]
         for piece in split(value, 2):
             cells += dot(table, piece)
         if r % 2:
@@ -392,7 +397,7 @@
     stripe = lax.axis_index("stripe").reshape(1)
     scan = lax.axis_index("scan")
     planes = rows * stripes // PHASES
-    depth = round_up(planes, 8)
+    depth = round_up(planes + FIRST_SHIFT, 8)
     ncx = rows * stripes // COARSE
     crow = cols // COARSE
     ncy = crow * scans
@@ -464,9 +469,12 @@
     both = lax.all_gather(both, "stripe", axis=0, tiled=True)
     few = array((8, 2 * half))
     halo = array((PHASES, depth, LANES), bf16)
-    own, to_left, to_right, red = call(
+    own, to_left, to_right, red, in_row, in_cell = call(
         functools.partial(start_kernel, sizes),
-        [array((PHASES, depth, 2 * LANES)), halo, halo, few],
+        [
+            array((PHASES, depth, 2 * LANES)), halo, halo, few,
+            array((PHASES, depth, 2 * half), bf16), array((PHASES, half, depth), bf16),
+        ],
         [both],
         [pltpu.VMEM((2, planes * PHASES, LANES), f32)],
     )
@@ -478,7 +486,8 @@
         pltpu.VMEM((round_up(blocks2 * depth, 16), PHASES * LANES), bf16),
         pltpu.VMEM((round_up(blocks1 * depth, 16), PHASES * LANES), bf16),
         pltpu.VMEM((PHASES, depth, LANES), f32),
-        pltpu.VMEM((2, blocks2, depth + 2 * EDGE, LANES), f32),
+        pltpu.VMEM((2, blocks2, depth, LANES), f32),
+        pltpu.VMEM((2, 2 * FIRST_SHIFT + 1, round_up(blocks2 * depth, 16) + 2 * EDGE, LANES), f32),
     ]
     plane = array((PHASES, depth, LANES))
     packed = array((PHASES // 2, depth, LANES))
@@ -491,7 +500,7 @@
         args = [stripe, own, from_left, from_right, share(red)]
         if not first:
             args.append(mask)
-        args += [rows_table, pull_table, back_table, inside, fwd, adj]
+        args += [rows_table, pull_table, back_table, inside, in_row, in_cell, fwd, adj]
         kernel = functools.partial(step_kernel, sizes, first, last)
         if last:
             row_scratch = pltpu.VMEM((planes * PHASES, LANES), f32)

time: 142 us -> 131 us (0.923)
  Pallas kernels: 59.4 us -> 48.9 us
    pallas_call x6, Pallas kernels: 54.8 us -> 44.3 us  [call(): pl.pallas_call(kernel, out_shape=out_shape, in_specs=[smem if a is stripe...]
    unnamed x12 -> x8, local copies, waits for them, and re-layouts: 3.51 us -> 2.94 us
  transfers between devices with their start and end apart: 9 -> 9, of which waited for: 0 -> 0; matrix products, arithmetic and copies ran while one was open for 2% -> 2% of each run, Pallas kernels for 3% -> 4%
where the time goes in v1:
time: 131 us; the launch traced here: 130 us
  blocking collectives  52 us (40%)
  Pallas kernels  48.9 us (37%)
  starting transfers between devices  19.9 us (15%)
  local copies, waits for them, and re-layouts  4.4 us (3%)
  other arithmetic  3.38 us (3%)
    pallas_call x6, Pallas kernels, call(): pl.pallas_call(kernel, out_shape=out_shape, in_specs=[smem if a is stripe...  44.3 us
    all_to_all x4, blocking collectives, share(): lax.all_to_all(jnp.broadcast_to(red, (scans,) + red.shape), 'scan', 0, 0)  40.9 us
    all_gather x1, blocking collectives, per_device(): both = lax.all_gather(both, 'stripe', axis=0, tiled=True)  11.1 us
    ppermute x4, starting transfers between devices, shift(): lax.ppermute(to_right, 'scan', forward)  9.87 us
    ppermute x4, starting transfers between devices, shift(): lax.ppermute(to_left, 'scan', backward)  5.17 us
    all_to_all x1, starting transfers between devices, share(): lax.all_to_all(jnp.broadcast_to(red, (scans,) + red.shape), 'scan', 0, 0)  4.88 us
    pallas_call x1, Pallas kernels, bands(): pl.pallas_call(bands_kernel, out_shape=[table, table], scratch_shapes=[pl...  4.58 us
    unnamed x8, local copies, waits for them, and re-layouts  2.94 us
  transfers between devices with their start and end apart: 9, of which 0 were waited for; matrix products, arithmetic and copies ran while one was open for 2% of the time, Pallas kernels for 4%

profile of v1, /device:TPU:0, one launch (start us, length us, event | category | flops | bytes accessed | tf_op | source)
XLA Modules:
  0.0 130.2 jit_solution(8705549802939820983)
XLA Ops:
  0.6 0.9 convert_element_type.80
  1.6 0.8 fusion.4
  2.4 11.1 %all_gather.3.both_ref = bf16[800,256]{1,0:T(8,128)(2,1)S(1)} all-gather(bf16[200,256]{1,0:T(8,128)(2,1)S(1)} %fusion.4), channel_id=1, replica_groups=mesh['stripe'=4,'scan'=8] {'stripe'}, dimensions={0}, use_global_device_ids=true | all-gather | bytes 512000 | tf_op jit(solution)/shard_map/all_gather | solution.py:469
  13.5 0.5 shard_map.50
  14.0 0.6 broadcast_in_dim.31
  14.6 4.9 %all-to-all-start = ((f32[8,8,128]{2,1,0:T(8,128)}), f32[8,8,128]{2,1,0:T(8,128)S(1)}, u32[]{:S(2)}, u32[]{:S(2)}) async-start(f32[8,8,128]{2,1,0:T(8,128)} %broadcast_in_dim.31), calls=%async_computation | async-start | bytes 65536 | tf_op jit(solution)/shard_map/all_to_all | solution.py:417
  19.5 2.4 %collective-permute-start = (bf16[8,104,128]{2,1,0:T(8,128)(2,1)S(1)}, bf16[8,104,128]{2,1,0:T(8,128)(2,1)S(1)}, u32[]{:S(2)}, u32[]{:S(2)}) collective-permute-start(bf16[8,104,128]{2,1,0:T(8,128)(2,1)S(1)} %get-tuple-element.27), channel_id=1, source_target_pairs={{0,1},{1,2},{2,3},{3,4},{4,5},{5,6},{6,7},{8,9},{9,10},{10,11},{11... | collective-permute-start | bytes 638984 | tf_op jit(solution)/shard_map/ppermute | solution.py:412
  21.9 1.3 collective-permute-start.1
  23.4 0.8 rev.3
  24.3 0.2 fusion.44
  24.7 0.3 convolution_multiply_fusion
  25.3 0.1 constant_dynamic-update-slice_fusion.19
  25.5 0.1 constant_dynamic-update-slice_fusion.17
  26.1 0.1 constant_dynamic-update-slice_fusion.6.refs_6_.refs_7_
  26.5 4.6 %shard_map.51 = (bf16[9728,128]{1,0:T(8,128)(2,1)S(1)}, bf16[9728,128]{1,0:T(8,128)(2,1)S(1)}) custom-call(bf16[2,64,64]{2,1,0:T(8,128)(2,1)S(1)} %fusion.56.taps_ref), custom_call_target="tpu_custom_call" | custom-call | tf_op jit(solution)/shard_map/pallas_call | solution.py:140
  31.1 1.5 %copy-done = bf16[9728,128]{1,0:T(8,128)(2,1)} copy-done((bf16[9728,128]{1,0:T(8,128)(2,1)}, bf16[9728,128]{1,0:T(8,128)(2,1)S(1)}, u32[]{:S(2)}) %copy-start) | copy-done | bytes 2490392
  32.5 1.5 %copy-done.2 = bf16[9728,128]{1,0:T(8,128)(2,1)} copy-done((bf16[9728,128]{1,0:T(8,128)(2,1)}, bf16[9728,128]{1,0:T(8,128)(2,1)S(1)}, u32[]{:S(2)}) %copy-start.2) | copy-done | bytes 2490392
  34.1 11.3 %shard_map.52 = (f32[8,104,128]{2,1,0:T(8,128)S(1)}, f32[4,104,128]{2,1,0:T(8,128)S(1)}, f32[4,104,128]{2,1,0:T(8,128)S(1)}, f32[8,128]{1,0:T(8,128)S(1)}, bf16[8,104,256]{2,1,0:T(8,128)(2,1)S(1)}) custom-call(s32[1]{0:T(128)} %bitcast.refs_0_.stripe_ref, f32[8,104,256]{2,1,0:T(8,128)S(1)} %get-tuple-element.26.refs_1_, ...), custom_call_target="tpu_custom_call" | custom-call | tf_op jit(solution)/shard_map/pallas_call | solution.py:424
  45.4 4.2 %collective-permute-start.2 = (f32[4,104,128]{2,1,0:T(8,128)S(1)}, f32[4,104,128]{2,1,0:T(8,128)S(1)}, u32[]{:S(2)}, u32[]{:S(2)}) collective-permute-start(f32[4,104,128]{2,1,0:T(8,128)S(1)} %get-tuple-element.35), channel_id=1, source_target_pairs={{0,1},{1,2},{2,3},{3,4},{4,5},{5,6},{6,7},{8,9},{9,10},{10,11},{11... | collective-permute-start | bytes 638984 | tf_op jit(solution)/shard_map/ppermute | solution.py:412
  49.5 1.3 collective-permute-start.3
  50.9 12.6 %all_to_all.25.refs_4_ = f32[8,8,128]{2,1,0:T(8,128)S(1)} all-to-all(f32[8,8,128]{2,1,0:T(8,128)S(1)} %broadcast_in_dim.38), channel_id=1, replica_groups=mesh['stripe'=4,'scan'=8] {'scan'}, dimensions={0} | all-to-all | bytes 65536 | tf_op jit(solution)/shard_map/all_to_all | solution.py:417
  63.4 10.3 %shard_map.53 = (f32[8,104,128]{2,1,0:T(8,128)S(1)}, f32[4,104,128]{2,1,0:T(8,128)S(1)}, f32[4,104,128]{2,1,0:T(8,128)S(1)}, f32[8,128]{1,0:T(8,128)S(1)}) custom-call(s32[1]{0:T(128)} %bitcast.refs_0_.stripe_ref, f32[8,104,128]{2,1,0:T(8,128)S(1)} %get-tuple-element.34.refs_1_, f32[4,104,128]{2,1,0:T(8,128)S(1)} %collective-permute-done.2.refs_2_, ...), custom_call_target="tpu_custom_call" | custom-call | tf_op jit(solution)/shard_map/pallas_call | solution.py:424
  73.7 1.6 %collective-permute-start.4 = (f32[4,104,128]{2,1,0:T(8,128)S(1)}, f32[4,104,128]{2,1,0:T(8,128)S(1)}, u32[]{:S(2)}, u32[]{:S(2)}) collective-permute-start(f32[4,104,128]{2,1,0:T(8,128)S(1)} %get-tuple-element.40), channel_id=1, source_target_pairs={{0,1},{1,2},{2,3},{3,4},{4,5},{5,6},{6,7},{8,9},{9,10},{10,11},{11... | collective-permute-start | bytes 638984 | tf_op jit(solution)/shard_map/ppermute | solution.py:412
  75.4 1.3 collective-permute-start.5
  76.7 10.1 %all_to_all.26.refs_4_ = f32[8,8,128]{2,1,0:T(8,128)S(1)} all-to-all(f32[8,8,128]{2,1,0:T(8,128)S(1)} %broadcast_in_dim.39), channel_id=1, replica_groups=mesh['stripe'=4,'scan'=8] {'scan'}, dimensions={0} | all-to-all | bytes 65536 | tf_op jit(solution)/shard_map/all_to_all | solution.py:417
  86.8 10.3 %shard_map.54 = (f32[8,104,128]{2,1,0:T(8,128)S(1)}, f32[4,104,128]{2,1,0:T(8,128)S(1)}, f32[4,104,128]{2,1,0:T(8,128)S(1)}, f32[8,128]{1,0:T(8,128)S(1)}) custom-call(s32[1]{0:T(128)} %bitcast.refs_0_.stripe_ref, f32[8,104,128]{2,1,0:T(8,128)S(1)} %get-tuple-element.39.refs_1_, f32[4,104,128]{2,1,0:T(8,128)S(1)} %collective-permute-done.4.refs_2_, ...), custom_call_target="tpu_custom_call" | custom-call | tf_op jit(solution)/shard_map/pallas_call | solution.py:424
  97.1 1.6 %collective-permute-start.6 = (f32[4,104,128]{2,1,0:T(8,128)S(1)}, f32[4,104,128]{2,1,0:T(8,128)S(1)}, u32[]{:S(2)}, u32[]{:S(2)}) collective-permute-start(f32[4,104,128]{2,1,0:T(8,128)S(1)} %get-tuple-element.44), channel_id=1, source_target_pairs={{0,1},{1,2},{2,3},{3,4},{4,5},{5,6},{6,7},{8,9},{9,10},{10,11},{11... | collective-permute-start | bytes 638984 | tf_op jit(solution)/shard_map/ppermute | solution.py:412
  98.7 1.3 collective-permute-start.7
  100.0 10.1 %all_to_all.27.refs_4_ = f32[8,8,128]{2,1,0:T(8,128)S(1)} all-to-all(f32[8,8,128]{2,1,0:T(8,128)S(1)} %broadcast_in_dim.40), channel_id=1, replica_groups=mesh['stripe'=4,'scan'=8] {'scan'}, dimensions={0} | all-to-all | bytes 65536 | tf_op jit(solution)/shard_map/all_to_all | solution.py:417
  110.1 10.7 %shard_map.55 = (f32[200,100]{1,0:T(8,128)S(1)}, f32[200,100]{1,0:T(8,128)}, f32[8,128]{1,0:T(8,128)S(1)}) custom-call(s32[1]{0:T(128)} %bitcast.refs_0_.stripe_ref, f32[8,104,128]{2,1,0:T(8,128)S(1)} %get-tuple-element.43.refs_1_, f32[4,104,128]{2,1,0:T(8,128)S(1)} %collective-permute-done.6.refs_2_, f32[4,104,128]{2,1,0:T(8,128)S(1)} %collective-permute-done.7.refs_3_, ...), custom_call_target="tpu_custom_call" | custom-call | tf_op jit(solution)/shard_map/pallas_call | solution.py:424
  120.8 8.1 %all_to_all.28.red_ref = f32[8,8,128]{2,1,0:T(8,128)S(1)} all-to-all(f32[8,8,128]{2,1,0:T(8,128)S(1)} %broadcast_in_dim.42), channel_id=1, replica_groups=mesh['stripe'=4,'scan'=8] {'scan'}, dimensions={0} | all-to-all | bytes 65536 | tf_op jit(solution)/shard_map/all_to_all | solution.py:417
  128.9 1.3 shard_map.56
  (55 shorter events, 1.4 us)
Async XLA Ops:
  0.6 25.8 %copy-start.3 = (bf16[61,61]{1,0:T(8,128)(2,1)S(1)}, bf16[61,61]{1,0:T(8,128)(2,1)}, u32[]{:S(2)}) copy-start(bf16[61,61]{1,0:T(8,128)(2,1)} %param.5) | copy-start | bytes 22330
  14.6 19.4 %all-to-all-start = ((f32[8,8,128]{2,1,0:T(8,128)}), f32[8,8,128]{2,1,0:T(8,128)S(1)}, u32[]{:S(2)}, u32[]{:S(2)}) async-start(f32[8,8,128]{2,1,0:T(8,128)} %broadcast_in_dim.31), calls=%async_computation | async-start | bytes 65536 | tf_op jit(solution)/shard_map/all_to_all | solution.py:417
  19.5 14.5 %collective-permute-start = (bf16[8,104,128]{2,1,0:T(8,128)(2,1)S(1)}, bf16[8,104,128]{2,1,0:T(8,128)(2,1)S(1)}, u32[]{:S(2)}, u32[]{:S(2)}) collective-permute-start(bf16[8,104,128]{2,1,0:T(8,128)(2,1)S(1)} %get-tuple-element.27), channel_id=1, source_target_pairs={{0,1},{1,2},{2,3},{3,4},{4,5},{5,6},{6,7},{8,9},{9,10},{10,11},{11... | collective-permute-start | bytes 638984 | tf_op jit(solution)/shard_map/ppermute | solution.py:412
  21.9 12.1 %collective-permute-start.1 = (bf16[8,104,128]{2,1,0:T(8,128)(2,1)S(1)}, bf16[8,104,128]{2,1,0:T(8,128)(2,1)S(1)}, u32[]{:S(2)}, u32[]{:S(2)}) collective-permute-start(bf16[8,104,128]{2,1,0:T(8,128)(2,1)S(1)} %get-tuple-element.28), channel_id=1, source_target_pairs={{1,0},{2,1},{3,2},{4,3},{5,4},{6,5},{7,6},{9,8},{10,9},{11,10},{12... | collective-permute-start | bytes 638984 | tf_op jit(solution)/shard_map/ppermute | solution.py:413
  31.1 1.5 %copy-start = (bf16[9728,128]{1,0:T(8,128)(2,1)}, bf16[9728,128]{1,0:T(8,128)(2,1)S(1)}, u32[]{:S(2)}) copy-start(bf16[9728,128]{1,0:T(8,128)(2,1)S(1)} %get-tuple-element.32.refs_11_.refs_12_) | copy-start | bytes 7471108
  32.5 1.5 %copy-start.2 = (bf16[9728,128]{1,0:T(8,128)(2,1)}, bf16[9728,128]{1,0:T(8,128)(2,1)S(1)}, u32[]{:S(2)}) copy-start(bf16[9728,128]{1,0:T(8,128)(2,1)S(1)} %get-tuple-element.33.refs_12_.refs_13_) | copy-start | bytes 7471108
  34.1 29.4 %copy-start.1 = (bf16[9728,128]{1,0:T(8,128)(2,1)S(1)}, bf16[9728,128]{1,0:T(8,128)(2,1)}, u32[]{:S(2)}) copy-start(bf16[9728,128]{1,0:T(8,128)(2,1)} %copy-done) | copy-start | bytes 7471108
  45.4 18.1 %collective-permute-start.2 = (f32[4,104,128]{2,1,0:T(8,128)S(1)}, f32[4,104,128]{2,1,0:T(8,128)S(1)}, u32[]{:S(2)}, u32[]{:S(2)}) collective-permute-start(f32[4,104,128]{2,1,0:T(8,128)S(1)} %get-tuple-element.35), channel_id=1, source_target_pairs={{0,1},{1,2},{2,3},{3,4},{4,5},{5,6},{6,7},{8,9},{9,10},{10,11},{11... | collective-permute-start | bytes 638984 | tf_op jit(solution)/shard_map/ppermute | solution.py:412
  49.5 13.9 %collective-permute-start.3 = (f32[4,104,128]{2,1,0:T(8,128)S(1)}, f32[4,104,128]{2,1,0:T(8,128)S(1)}, u32[]{:S(2)}, u32[]{:S(2)}) collective-permute-start(f32[4,104,128]{2,1,0:T(8,128)S(1)} %get-tuple-element.36), channel_id=1, source_target_pairs={{1,0},{2,1},{3,2},{4,3},{5,4},{6,5},{7,6},{9,8},{10,9},{11,10},{12... | collective-permute-start | bytes 638984 | tf_op jit(solution)/shard_map/ppermute | solution.py:413
  73.7 13.1 %collective-permute-start.4 = (f32[4,104,128]{2,1,0:T(8,128)S(1)}, f32[4,104,128]{2,1,0:T(8,128)S(1)}, u32[]{:S(2)}, u32[]{:S(2)}) collective-permute-start(f32[4,104,128]{2,1,0:T(8,128)S(1)} %get-tuple-element.40), channel_id=1, source_target_pairs={{0,1},{1,2},{2,3},{3,4},{4,5},{5,6},{6,7},{8,9},{9,10},{10,11},{11... | collective-permute-start | bytes 638984 | tf_op jit(solution)/shard_map/ppermute | solution.py:412
  75.4 11.4 %collective-permute-start.5 = (f32[4,104,128]{2,1,0:T(8,128)S(1)}, f32[4,104,128]{2,1,0:T(8,128)S(1)}, u32[]{:S(2)}, u32[]{:S(2)}) collective-permute-start(f32[4,104,128]{2,1,0:T(8,128)S(1)} %get-tuple-element.41), channel_id=1, source_target_pairs={{1,0},{2,1},{3,2},{4,3},{5,4},{6,5},{7,6},{9,8},{10,9},{11,10},{12... | collective-permute-start | bytes 638984 | tf_op jit(solution)/shard_map/ppermute | solution.py:413
  97.1 13.1 %collective-permute-start.6 = (f32[4,104,128]{2,1,0:T(8,128)S(1)}, f32[4,104,128]{2,1,0:T(8,128)S(1)}, u32[]{:S(2)}, u32[]{:S(2)}) collective-permute-start(f32[4,104,128]{2,1,0:T(8,128)S(1)} %get-tuple-element.44), channel_id=1, source_target_pairs={{0,1},{1,2},{2,3},{3,4},{4,5},{5,6},{6,7},{8,9},{9,10},{10,11},{11... | collective-permute-start | bytes 638984 | tf_op jit(solution)/shard_map/ppermute | solution.py:412
  98.7 11.4 %collective-permute-start.7 = (f32[4,104,128]{2,1,0:T(8,128)S(1)}, f32[4,104,128]{2,1,0:T(8,128)S(1)}, u32[]{:S(2)}, u32[]{:S(2)}) collective-permute-start(f32[4,104,128]{2,1,0:T(8,128)S(1)} %get-tuple-element.45), channel_id=1, source_target_pairs={{1,0},{2,1},{3,2},{4,3},{5,4},{6,5},{7,6},{9,8},{10,9},{11,10},{12... | collective-permute-start | bytes 638984 | tf_op jit(solution)/shard_map/ppermute | solution.py:413

commit v2 on v1

v2 whole, which is shorter than its diff:
```python
import functools
import math

import jax
import jax.numpy as jnp
from jax import lax
from jax.experimental import pallas as pl
from jax.experimental.pallas import tpu as pltpu
from jax.sharding import PartitionSpec as P

TAPS = 61
RIM = 30
COARSE = 25
SIGMA = 40
ITERS = 4

back_ratio = 0.6
resist_gain = 3.0
resist_level = 1.5
step_length = 0.5

PHASES = 8
SPAN = 32
LANES = 128
PER = LANES // SPAN
PAIR = PHASES // PER
REACH = 3
TAPS_PAD = 64
FIRST_SHIFT = -(-RIM // PHASES)
SHIFTS = 2 * FIRST_SHIFT + 1
BEFORE = FIRST_SHIFT * PHASES - RIM + PER
SLOTS = SHIFTS * PHASES + PER
EDGE = 8
HALO = 2 * RIM
HALO_BLOCKS = 2
SPARE = HALO_BLOCKS * SPAN - HALO


f32 = jnp.float32
bf16 = jnp.bfloat16
highest = lax.Precision.HIGHEST


def round_up(value, unit):
    return -(-value // unit) * unit


def iota2(shape, dim):
    return lax.broadcasted_iota(jnp.int32, shape, dim)


def dot(left, right, precision=None):
    return lax.dot_general(
        left, right, (((1,), (0,)), ((), ())), precision=precision, preferred_element_type=f32
    )


def dot_t(left, right):
    return lax.dot_general(left, right, (((1,), (1,)), ((), ())), preferred_element_type=f32)


def split(value, parts):
    pieces = []
    for _ in range(parts):
        piece = value.astype(bf16)
        pieces.append(piece)
        value = value - piece.astype(f32)
    return pieces


def one_side(value, axis):
    a, b, c = split(value, 3)
    return jnp.concatenate([a, b, c, a, b, a], axis=axis)


def other_side(value, axis):
    pieces = []
    for _ in range(3):
        piece = lax.reduce_precision(value, 8, 7)
        pieces.append(piece.astype(bf16))
        value = value - piece
    a, b, c = pieces
    return jnp.concatenate([a, a, a, b, b, c], axis=axis)


def roll(value, shift):
    shift %= LANES
    return pltpu.roll(value, shift, 1) if shift else value


def place(shape):
    return iota2(shape, 1) % SPAN


def group(shape):
    return iota2(shape, 1) // SPAN


def bands_kernel(taps_ref, fwd_ref, adj_ref, base_ref, rows_ref):
    lane = iota2((TAPS_PAD, LANES), 1)
    tap = iota2((TAPS_PAD, LANES), 0)
    owner = group((SPAN, LANES))
    margin = PER - 1
    for which, (out_ref, offset) in enumerate(((fwd_ref, SPARE), (adj_ref, 0))):
        taps = taps_ref[which]
        for k in range(8):
            hot = (((k - offset - lane) & (LANES - 1)) == tap).astype(f32).astype(bf16)
            base_ref[pl.ds(k, TAPS_PAD, stride=8), :] = dot(taps, hot)
        for a in range(margin):
            rows_ref[pl.ds(a * LANES, LANES), :] = jnp.zeros((LANES, LANES), f32)

        def turn(step, carry):
            base = base_ref[pl.ds(pl.multiple_of(step * 8, 8), 8), :]
            first = pl.multiple_of((step + margin) * LANES, LANES)
            for g in range(LANES // 8):
                rows_ref[pl.ds(first + 8 * g, 8), :] = pltpu.roll(base, 8 * g, 1) if g else base
            return carry

        lax.fori_loop(0, TAPS_PAD, turn, 0, unroll=8)
        for g in range(REACH):
            for a in list(range(BEFORE)) + list(range(BEFORE + TAPS_PAD, SLOTS)):
                out_ref[g, pl.ds(a * SPAN, SPAN), :] = jnp.zeros((SPAN, LANES), bf16)

        def join(step, carry):
            for g in range(REACH):
                value = None
                for k in reversed(range(PER)):
                    first = pl.multiple_of((step + margin - k) * LANES, LANES)
                    part = rows_ref[pl.ds(first + SPAN * ((g + k) % PER), SPAN), :]
                    value = part if value is None else jnp.where(owner <= k, part, value)
                slot = pl.multiple_of((step + BEFORE) * SPAN, SPAN)
                out_ref[g, pl.ds(slot, SPAN), :] = value.astype(bf16)
            return carry

        lax.fori_loop(0, TAPS_PAD, join, 0, unroll=4)


def bands(psf):
    taps = jnp.stack([psf, psf[::-1, ::-1]])
    extra = TAPS_PAD - TAPS
    taps = jnp.pad(taps, ((0, 0), (0, extra), (0, extra)))
    table = jax.ShapeDtypeStruct((REACH, SLOTS * SPAN, LANES), bf16)
    return pl.pallas_call(
        bands_kernel,
        out_shape=[table, table],
        scratch_shapes=[
            pltpu.VMEM((TAPS_PAD * 8, LANES), f32),
            pltpu.VMEM(((TAPS_PAD + PER - 1) * LANES, LANES), f32),
        ],
        compiler_params=pltpu.CompilerParams(vmem_limit_bytes=32 * 1024 * 1024),
    )(taps)


def correlate(field_ref, blocks, depth, line_ref, band_ref, part_ref, acc_ref):
    height = blocks * depth
    for n in range(PAIR):
        for g in range(REACH):
            wide = field_ref[n, g:g + blocks].reshape(height, LANES)
            rest = line_ref.shape[0] - height
            if rest:
                wide = jnp.concatenate([wide, jnp.zeros((rest, LANES), f32)], axis=0)
            tile = n * REACH + g
            line_ref[:, tile * LANES:(tile + 1) * LANES] = wide.astype(bf16)
    for m in range(SHIFTS):
        table = jnp.concatenate(
            [
                jnp.concatenate(
                    [
                        band_ref[g, pl.ds((m * PHASES + PER * (1 + source - n)) * SPAN, LANES), :]
                        for source in range(PAIR) for g in range(REACH)
                    ],
                    axis=0,
                )
                for n in range(PAIR)
            ],
            axis=1,
        )
        product = dot(line_ref[...], table)
        for n in range(PAIR):
            part_ref[n, m, pl.ds(EDGE, line_ref.shape[0]), :] = product[:, n * LANES:(n + 1) * LANES]
    for n in range(PAIR):
        for b in range(blocks):
            total = None
            for m in range(SHIFTS):
                first = EDGE + b * depth + m - FIRST_SHIFT
                piece = part_ref[n, m, pl.ds(first, depth), :]
                total = piece if total is None else total + piece
            acc_ref[n, b] = total


def in_rows(n, depth, ncx):
    shape = (depth, PER * 2 * ncx)
    column = iota2(shape, 1)
    row = iota2(shape, 0) * PHASES + n * PER + column // (2 * ncx)
    cell = column % ncx
    return ((row >= cell * COARSE) & (row < cell * COARSE + COARSE)).astype(f32).astype(bf16)


def in_cells(n, depth, ncx):
    shape = (PER * ncx, depth)
    line = iota2(shape, 0)
    row = iota2(shape, 1) * PHASES + n * PER + line // ncx
    cell = line % ncx
    return ((row >= cell * COARSE) & (row < cell * COARSE + COARSE)).astype(f32).astype(bf16)


def over_rows(strips, ncx, blocks):
    owner = jnp.concatenate([group((ncx, LANES))] * blocks, axis=1)
    pieces = [piece.astype(f32) for piece in split(strips[:ncx], 2)]
    return jnp.concatenate(
        [jnp.where(owner == k, piece, 0.0).astype(bf16) for k in range(PER) for piece in pieces], axis=0
    )


def cell_rows(products, ncx, blocks):
    owner = jnp.concatenate([group((ncx, LANES))] * blocks, axis=1)
    value = products[:ncx]
    for k in range(1, PER):
        value = jnp.where(owner == k, products[k * ncx:(k + 1) * ncx], value)
    return value


def by_columns(first, crow, value, half):
    shape = (8, value.shape[1])
    lane = iota2(shape, 1)
    at = lane // LANES * SPAN + lane % SPAN - first
    owner = iota2(shape, 0)
    hit = (at >= owner * COARSE) & (at < owner * COARSE + COARSE) & (owner < crow)
    picked = hit.astype(f32).astype(bf16)
    rest = half - value.shape[0]
    if rest:
        value = jnp.concatenate([value, jnp.zeros((rest, value.shape[1]), f32)], axis=0)
    return dot_t(
        jnp.concatenate([picked] * 3, axis=1), jnp.concatenate(split(value, 3), axis=1)
    )


def coarse(red_ref, rows_ref, pull_ref, back_ref, half):
    red = red_ref[...].reshape(red_ref.shape[0] * 8, 2 * half)
    mixed = dot_t(rows_ref[...], one_side(red, 1))
    pull = dot(one_side(mixed[:half], 1), pull_ref[...])
    if back_ref is None:
        return pull
    levels = jnp.concatenate([mixed[half:2 * half], mixed[2 * half:]], axis=1)
    return pull, dot(one_side(levels, 1), back_ref[...])


def start_kernel(
    sizes, both_ref,
    own_out, mask_out, left_out, right_out, red_out, rows_out, cells_out, plane_ref, wide_ref,
):
    planes, depth, half, cols, crow, ncx = sizes
    owner = group((depth, LANES))
    for part in range(2):
        wide_ref[part] = both_ref[:, part * LANES:(part + 1) * LANES].astype(f32)
        for r in range(PHASES):
            value = wide_ref[part, pl.ds(r, planes, stride=PHASES), :]
            rest = jnp.zeros((depth - planes, LANES), f32)
            plane_ref[part, r] = jnp.concatenate([value, rest], axis=0)

    def tile(part, n, first):
        value = None
        for k in reversed(range(PER)):
            turned = roll(plane_ref[part, n * PER + k], SPAN * k - first)
            value = turned if value is None else jnp.where(owner <= k, turned, value)
        return value

    sums = None
    blocks = own_out.shape[1]
    for n in range(PAIR):
        rows_out[n] = in_rows(n, depth, ncx)
        cells_out[n] = in_cells(n, depth, ncx)
        tiles = []
        for b in range(blocks):
            tiles.append(tile(0, n, SPAN * b))
            own_out[n, b] = tiles[-1]
        for b in range(mask_out.shape[1]):
            mask_out[n, b] = tile(1, n, SPAN * b - RIM).astype(bf16)
        for t in range(HALO_BLOCKS):
            right_out[n, t] = tile(0, n, cols - (HALO_BLOCKS - t) * SPAN).astype(bf16)
            left_out[n, t] = tile(0, n, SPAN * (blocks - 1 + t) - cols).astype(bf16)
        right_out[n, HALO_BLOCKS] = tile(1, n, cols - RIM).astype(bf16)
        left_out[n, HALO_BLOCKS] = tile(1, n, SPAN * (mask_out.shape[1] - 1) - RIM - cols).astype(bf16)
        part = dot(cells_out[n], jnp.concatenate(tiles, axis=1).astype(bf16))
        sums = part if sums is None else sums + part
    red_out[...] = jnp.zeros_like(red_out)
    red_out[:, :half] = by_columns(0, crow, cell_rows(sums, ncx, blocks), half)


def step_kernel(sizes, first, last, *refs):
    planes, depth, half, cols, crow, ncx = sizes
    stripe_ref, own_ref, from_left_ref, from_right_ref, red_ref, mask_ref = refs[:6]
    rows_ref, pull_ref, back_ref, inside_ref, in_row_ref, in_cell_ref, fwd_ref, adj_ref = refs[6:14]
    refs = refs[14:]
    if last:
        v_out, resist_out, red_out = refs[:3]
        x_ref, e_ref, line_ref, tile_line_ref, acc_ref, part_ref, row_ref = refs[3:]
    else:
        v_out, left_out, right_out, red_out = refs[:4]
        refs = refs[4:]
        if first:
            mask_out, refs = refs[0], refs[1:]
        x_ref, e_ref, line_ref, tile_line_ref, acc_ref, part_ref = refs
    wide_blocks = x_ref.shape[1]
    blocks = acc_ref.shape[1]
    tile_blocks = own_ref.shape[1]
    at = place((depth, LANES))
    filled = iota2((depth, LANES), 0) < planes

    ends = part_ref.shape[2] - EDGE
    for n in range(PAIR):
        for m in range(SHIFTS):
            part_ref[n, m, pl.ds(0, EDGE), :] = jnp.zeros((EDGE, LANES), f32)
            part_ref[n, m, pl.ds(ends, EDGE), :] = jnp.zeros((EDGE, LANES), f32)
        e_ref[n, blocks] = jnp.zeros((depth, LANES), f32)

    pull, back = coarse(red_ref, rows_ref, pull_ref, back_ref, half)
    pull = over_rows(pull, ncx, wide_blocks)
    back = over_rows(back, ncx, blocks)

    tail = cols - SPAN * (tile_blocks - 1)
    for n in range(PAIR):
        pulled = dot(in_row_ref[n], pull)
        for b in range(wide_blocks):
            if b < HALO_BLOCKS:
                value = from_left_ref[n, b].astype(f32)
            elif b < HALO_BLOCKS + tile_blocks:
                value = own_ref[n, b - HALO_BLOCKS]
                if b == HALO_BLOCKS + tile_blocks - 1:
                    value = jnp.where(at < tail, value, from_right_ref[n, 0].astype(f32))
            else:
                value = from_right_ref[n, 1].astype(f32)
            value = value - pulled[:, b * LANES:(b + 1) * LANES]
            x_ref[n, b] = value.astype(bf16).astype(f32)

    correlate(x_ref, blocks, depth, line_ref, fwd_ref, part_ref, acc_ref)

    sums = None
    for n in range(PAIR):
        raised = dot(in_row_ref[n], back)
        rounded = []
        for b in range(blocks):
            mask = mask_ref[n, b]
            if first:
                mask = mask.astype(f32)
                if b == 0:
                    mask = jnp.where(at < RIM, from_left_ref[n, HALO_BLOCKS].astype(f32), mask)
                if b == blocks - 1:
                    edge = RIM + cols - SPAN * (blocks - 1)
                    mask = jnp.where(at < edge, mask, from_right_ref[n, HALO_BLOCKS].astype(f32))
                mask_out[n, b] = mask.astype(bf16)
            exposure = acc_ref[n, b] + raised[:, b * LANES:(b + 1) * LANES]
            resist = 1.0 / (1.0 + jnp.exp(-resist_gain * (exposure - resist_level)))
            error = (resist - mask.astype(f32)) * resist_gain * resist * (1.0 - resist)
            error = jnp.where(filled, error * inside_ref[b:b + 1, :], 0.0).astype(bf16)
            rounded.append(error)
            e_ref[n, b] = error.astype(f32)
            if last:
                acc_ref[n, b] = resist
        part = dot(in_cell_ref[n], jnp.concatenate(rounded, axis=1))
        sums = part if sums is None else sums + part
    red_out[:, half:] = by_columns(RIM, crow, cell_rows(sums, ncx, blocks), half)

    def to_rows(tiles, origin, count):
        lane = iota2((depth, LANES), 1)
        for r in range(PHASES):
            n, k = divmod(r, PER)
            value = None
            for b in reversed(range(count)):
                part = roll(tiles(n, b), SPAN * (b - k) - origin)
                value = part if value is None else jnp.where(lane < SPAN * (b + 1) - origin, part, value)
            row_ref[pl.ds(r, planes, stride=PHASES), :] = value[:planes]

    if last:
        own_rows = v_out.shape[0]
        start = pl.multiple_of(stripe_ref[0] * own_rows, 8)
        to_rows(lambda n, b: acc_ref[n, b], RIM, blocks)
        resist_out[...] = row_ref[pl.ds(start, own_rows), :][:, :cols]

    correlate(e_ref, tile_blocks, depth, tile_line_ref, adj_ref, part_ref, acc_ref)

    cells = None
    for n in range(PAIR):
        fresh = []
        for b in range(tile_blocks):
            value = x_ref[n, HALO_BLOCKS + b] - step_length * acc_ref[n, b]
            value = jnp.where(filled, value, 0.0)
            fresh.append(value)
            if last:
                acc_ref[n, b] = value
            else:
                v_out[n, b] = value
        if last:
            continue
        for piece in split(jnp.concatenate(fresh, axis=1), 2):
            part = dot(in_cell_ref[n], piece)
            cells = part if cells is None else cells + part

        def moved(begin):
            b, step = divmod(begin, SPAN)
            low = roll(fresh[b], -step) if 0 <= b < tile_blocks else None
            high = roll(fresh[b + 1], SPAN - step) if step and 0 <= b + 1 < tile_blocks else None
            if low is None or high is None:
                return high if low is None else low
            return jnp.where(at < SPAN - step, low, high)

        for t in range(HALO_BLOCKS):
            right_out[n, t] = moved(cols - (HALO_BLOCKS - t) * SPAN)
            left_out[n, t] = moved(SPAN * (tile_blocks - 1 + t) - cols)
    if last:
        to_rows(lambda n, b: acc_ref[n, b], 0, tile_blocks)
        v_out[...] = row_ref[pl.ds(start, own_rows), :][:, :cols]
        red_out[:, :half] = jnp.zeros((8, half), f32)
    else:
        red_out[:, :half] = by_columns(0, crow, cell_rows(cells, ncx, tile_blocks), half)


def end_kernel(sizes, stripe_ref, v_ref, red_ref, rows_ref, pull_ref, out_ref):
    planes, depth, half, cols, crow, ncx = sizes
    pull = coarse(red_ref, rows_ref, pull_ref, None, half)
    pull = jnp.concatenate(split(pull, 2), axis=0)
    rows = v_ref.shape[0]
    row = iota2((rows, 2 * half), 0) + stripe_ref[0] * rows
    cell = iota2((rows, 2 * half), 1)
    cell = jnp.where(cell >= half, cell - half, cell)
    table = ((row >= cell * COARSE) & (row < cell * COARSE + COARSE)).astype(f32).astype(bf16)
    pulled = dot(table, pull)
    out_ref[...] = v_ref[...] - pulled[:, :cols]


def gauss(rows_at, cols_at, rows_ok, cols_ok):
    dist = (rows_at[:, None] - cols_at[None, :]).astype(f32)
    table = jnp.exp(-dist * dist / (2.0 * SIGMA * SIGMA)) / (math.sqrt(2.0 * math.pi) * SIGMA)
    return jnp.where(rows_ok[:, None] & cols_ok[None, :], table, 0.0)


def per_device(dose, target, psf):
    rows, cols = dose.shape
    stripes = lax.axis_size("stripe")
    scans = lax.axis_size("scan")
    stripe = lax.axis_index("stripe").reshape(1)
    scan = lax.axis_index("scan")
    planes = rows * stripes // PHASES
    depth = round_up(planes + FIRST_SHIFT, 8)
    ncx = rows * stripes // COARSE
    crow = cols // COARSE
    ncy = crow * scans
    half = round_up(ncx, LANES // 2)
    sizes = (planes, depth, half, cols, crow, ncx)
    tile_blocks = -(-cols // SPAN)
    blocks = -(-(cols + 2 * RIM) // SPAN)
    wide_blocks = blocks + REACH - 1

    forward = [(i, i + 1) for i in range(scans - 1)]
    backward = [(i + 1, i) for i in range(scans - 1)]

    def shift(to_right, to_left):
        return (
            lax.ppermute(to_right, "scan", forward),
            lax.ppermute(to_left, "scan", backward),
        )

    def share(red):
        return lax.all_to_all(jnp.broadcast_to(red, (scans,) + red.shape), "scan", 0, 0)

    vmem = pl.BlockSpec(memory_space=pltpu.VMEM)
    smem = pl.BlockSpec(memory_space=pltpu.SMEM)
    params = pltpu.CompilerParams(vmem_limit_bytes=48 * 1024 * 1024)

    def call(kernel, out_shape, args, scratch=()):
        return pl.pallas_call(
            kernel,
            out_shape=out_shape,
            in_specs=[smem if a is stripe else vmem for a in args],
            scratch_shapes=list(scratch),
            compiler_params=params,
        )(*args)

    def array(shape, dtype=f32):
        return jax.ShapeDtypeStruct(shape, dtype)

    row_at = jnp.arange(half, dtype=jnp.int32)
    lane_at = jnp.arange(2 * half, dtype=jnp.int32)
    row_ok = row_at < ncx
    gx = gauss(row_at, row_at, row_ok, row_ok)
    gxc = gauss(row_at, lane_at, row_ok, lane_at < ncx)
    gxs = gauss(row_at, lane_at - half, row_ok, (lane_at >= half) & (lane_at < half + ncx))
    rows_table = other_side(jnp.concatenate([gxs, gxc, dot(gx, gxs, highest)], axis=0), 1)
    held = jnp.arange(8 * scans, dtype=jnp.int32)
    held_ok = held % 8 < crow
    held_at = (held // 8) * crow + held % 8
    cell_at = jnp.arange(ncy, dtype=jnp.int32)
    cell_ok = cell_at < ncy

    def columns(first, count):
        lane = jnp.arange(count * LANES, dtype=jnp.int32)
        at = scan * cols + first + lane // LANES * SPAN + lane % SPAN
        return at // COARSE, (at >= 0) & (at < cols * scans)

    pull_scale = step_length * back_ratio / (COARSE * COARSE)
    at2, ok2 = columns(-HALO_BLOCKS * SPAN, wide_blocks)
    at1, ok1 = columns(-RIM, blocks)
    at0 = scan * cols + jnp.arange(LANES, dtype=jnp.int32)
    ok0 = at0 < (scan + 1) * cols
    at0 = at0 // COARSE
    pull_table = other_side(pull_scale * gauss(held_at, at2, held_ok, ok2), 0)
    end_table = other_side(pull_scale * gauss(held_at, at0, held_ok, ok0), 0)
    level_table = back_ratio / (COARSE * COARSE) * gauss(held_at, at1, held_ok, ok1)
    again = dot(
        gauss(held_at, cell_at, held_ok, cell_ok), gauss(cell_at, at1, cell_ok, ok1), highest
    )
    back_table = other_side(
        jnp.concatenate([level_table, -back_ratio * pull_scale * again], axis=0), 0
    )
    inside = ok1.astype(f32).reshape(blocks, LANES)

    fill = ((0, 0), (0, LANES - cols))
    both = jnp.concatenate([jnp.pad(dose, fill), jnp.pad(target.astype(bf16), fill)], axis=1)
    both = lax.all_gather(both, "stripe", axis=0, tiled=True)
    few = array((8, 2 * half))
    halo = array((PAIR, HALO_BLOCKS + 1, depth, LANES), bf16)
    mask_tiles = array((PAIR, blocks, depth, LANES), bf16)
    tiles = array((PAIR, tile_blocks, depth, LANES))
    own, mask, to_left, to_right, red, in_row, in_cell = call(
        functools.partial(start_kernel, sizes),
        [
            tiles, mask_tiles, halo, halo, few,
            array((PAIR, depth, PER * 2 * ncx), bf16), array((PAIR, PER * ncx, depth), bf16),
        ],
        [both],
        [pltpu.VMEM((2, PHASES, depth, LANES), f32), pltpu.VMEM((2, planes * PHASES, LANES), f32)],
    )
    fwd, adj = bands(psf)

    height = round_up(blocks * depth, 16)
    scratch = [
        pltpu.VMEM((PAIR, wide_blocks, depth, LANES), f32),
        pltpu.VMEM((PAIR, blocks + 1, depth, LANES), f32),
        pltpu.VMEM((height, PAIR * REACH * LANES), bf16),
        pltpu.VMEM((round_up(tile_blocks * depth, 16), PAIR * REACH * LANES), bf16),
        pltpu.VMEM((PAIR, blocks, depth, LANES), f32),
        pltpu.VMEM((PAIR, SHIFTS, height + 2 * EDGE, LANES), f32),
    ]
    packed = array((PAIR, HALO_BLOCKS, depth, LANES))
    tile = array((rows, cols))
    for step in range(ITERS):
        first = step == 0
        last = step == ITERS - 1
        from_left, from_right = shift(to_right, to_left)
        args = [stripe, own, from_left, from_right, share(red), mask]
        args += [rows_table, pull_table, back_table, inside, in_row, in_cell, fwd, adj]
        kernel = functools.partial(step_kernel, sizes, first, last)
        if last:
            row_scratch = pltpu.VMEM((planes * PHASES, LANES), f32)
            v, resist, red = call(kernel, [tile, tile, few], args, scratch + [row_scratch])
        elif first:
            own, to_left, to_right, red, mask = call(
                kernel, [tiles, packed, packed, few, mask_tiles], args, scratch
            )
        else:
            own, to_left, to_right, red = call(kernel, [tiles, packed, packed, few], args, scratch)

    updated = call(
        functools.partial(end_kernel, sizes),
        tile,
        [stripe, v, share(red), rows_table, end_table],
    )
    return resist, updated


def solution(mesh):
    in_specs = (P("stripe", "scan"), P("stripe", "scan"), P())
    out_specs = (P("stripe", "scan"), P("stripe", "scan"))
    return jax.shard_map(
        per_device, mesh=mesh, in_specs=in_specs, out_specs=out_specs, check_vma=False
    )
```

time: 131 us -> 157 us (1.20)
  blocking collectives: 52 us -> 11.1 us
  local copies, waits for them, and re-layouts: 4.4 us -> 32.8 us
  starting transfers between devices: 19.9 us -> 39.9 us
  waiting for transfers between devices: 0.02 us -> 18 us
  Pallas kernels: 48.9 us -> 40.8 us
  other arithmetic: 3.38 us -> 10.7 us
    all_to_all x4 -> x0, blocking collectives: 40.9 us -> none  [share(): lax.all_to_all(jnp.broadcast_to(red, (scans,) + red.shape), 'scan', 0, 0)]
    unnamed x8 -> x72, local copies, waits for them, and re-layouts: 2.94 us -> 29.7 us
    all_to_all x1 -> x5, starting transfers between devices: 4.88 us -> 25.1 us  [share(): lax.all_to_all(jnp.broadcast_to(red, (scans,) + red.shape), 'scan', 0, 0)]
    all_to_all x1 -> x5, waiting for transfers between devices: 0.01 us -> 18 us  [share(): lax.all_to_all(jnp.broadcast_to(red, (scans,) + red.shape), 'scan', 0, 0)]
    pallas_call x6, Pallas kernels: 44.3 us -> 35.7 us  [call(): pl.pallas_call(kernel, out_shape=out_shape, in_specs=[smem if a is stripe...]
    unnamed x19 -> x20, other arithmetic: 1.05 us -> 6.44 us
    broadcast_in_dim x5, local copies, waits for them, and re-layouts: 0.64 us -> 3.07 us  [share(): jnp.broadcast_to(red, (scans,) + red.shape)]
  transfers between devices with their start and end apart: 9 -> 13, of which waited for: 0 -> 4; matrix products, arithmetic and copies ran while one was open for 2% -> 8% of each run, Pallas kernels for 4% -> 3%
where the time goes in v2:
time: 157 us; the launch traced here: 155 us
  Pallas kernels  40.8 us (26%)
  starting transfers between devices  39.9 us (25%)
  local copies, waits for them, and re-layouts  32.8 us (21%)
  waiting for transfers between devices  18 us (11%)
  blocking collectives  11.1 us (7%)
  other arithmetic  10.7 us (7%)
    pallas_call x6, Pallas kernels, call(): pl.pallas_call(kernel, out_shape=out_shape, in_specs=[smem if a is stripe...  35.7 us
    unnamed x72, local copies, waits for them, and re-layouts  29.7 us
    all_to_all x5, starting transfers between devices, share(): lax.all_to_all(jnp.broadcast_to(red, (scans,) + red.shape), 'scan', 0, 0)  25.1 us
    all_to_all x5, waiting for transfers between devices, share(): lax.all_to_all(jnp.broadcast_to(red, (scans,) + red.shape), 'scan', 0, 0)  18 us
    all_gather x1, blocking collectives, per_device(): both = lax.all_gather(both, 'stripe', axis=0, tiled=True)  11.1 us
    ppermute x4, starting transfers between devices, shift(): lax.ppermute(to_right, 'scan', forward)  9.66 us
    unnamed x20, other arithmetic  6.44 us
    ppermute x4, starting transfers between devices, shift(): lax.ppermute(to_left, 'scan', backward)  5.12 us
  transfers between devices with their start and end apart: 13, of which 4 were waited for; matrix products, arithmetic and copies ran while one was open for 8% of the time, Pallas kernels for 3%

profile of v2, /device:TPU:0, one launch (start us, length us, event | category | flops | bytes accessed | tf_op | source)
XLA Modules:
  0.0 155.0 jit_solution(1025224443372419569)
XLA Ops:
  2.4 11.1 %all_gather.3.both_ref = bf16[800,256]{1,0:T(8,128)(2,1)S(1)} all-gather(bf16[200,256]{1,0:T(8,128)(2,1)S(1)} %fusion.18), channel_id=1, replica_groups=mesh['stripe'=4,'scan'=8] {'stripe'}, dimensions={0}, use_global_device_ids=true | all-gather | bytes 512000 | tf_op jit(solution)/shard_map/all_gather | solution.py:519
  13.5 1.8 %shard_map.50 = (f32[2,4,104,128]{3,2,1,0:T(8,128)S(1)}, bf16[2,5,104,128]{3,2,1,0:T(8,128)(2,1)S(1)}, bf16[2,3,104,128]{3,2,1,0:T(8,128)(2,1)}, bf16[2,3,104,12...) custom-call(bf16[800,256]{1,0:T(8,128)(2,1)S(1)} %all_gather.3.both_ref), custom_call_target="tpu_custom_call" | custom-call | tf_op jit(solution)/shard_map/pallas_call | solution.py:471
  18.1 1.9 %collective-permute-start = (bf16[2,3,104,128]{3,2,1,0:T(8,128)(2,1)}, bf16[2,3,104,128]{3,2,1,0:T(8,128)(2,1)}, u32[]{:S(2)}, u32[]{:S(2)}) collective-permute-start(bf16[2,3,104,128]{3,2,1,0:T(8,128)(2,1)} %get-tuple-element.28), channel_id=1, source_target_pairs={{0,1},{1,2},{2,3},{3,4},{4,5},{5,6},{6,7},{8,9},{9,10},{10,11},{11... | collective-permute-start | bytes 479240 | tf_op jit(solution)/shard_map/ppermute | solution.py:459
  20.0 1.3 collective-permute-start.1
  21.9 7.2 %all-to-all-start = ((f32[8,8,128]{2,1,0:T(8,128)}), f32[8,8,128]{2,1,0:T(8,128)}, u32[]{:S(2)}, u32[]{:S(2)}) async-start(f32[8,8,128]{2,1,0:T(8,128)} %broadcast_in_dim.34), calls=%async_computation | async-start | bytes 65536 | tf_op jit(solution)/shard_map/all_to_all | solution.py:464
  35.4 5.0 %shard_map.51 = (bf16[3,2432,128]{2,1,0:T(8,128)(2,1)S(1)}, bf16[3,2432,128]{2,1,0:T(8,128)(2,1)S(1)}) custom-call(bf16[2,64,64]{2,1,0:T(8,128)(2,1)S(1)} %copy-done.31), custom_call_target="tpu_custom_call" | custom-call | tf_op jit(solution)/shard_map/pallas_call | solution.py:143
  40.4 1.3 copy-done
  46.4 7.9 %shard_map.52 = (f32[2,4,104,128]{3,2,1,0:T(8,128)S(1)}, f32[2,2,104,128]{3,2,1,0:T(8,128)}, f32[2,2,104,128]{3,2,1,0:T(8,128)}, f32[8,128]{1,0:T(8,128)S(1)}, bf16[2,5,104,128]{3,2,1,0:T(8,128)(2,1)S(1)}) custom-call(s32[1]{0:T(128)} %bitcast.refs_0_.stripe_ref, f32[2,4,104,128]{3,2,1,0:T(8,128)S(1)} %copy-done.28, ...), custom_call_target="tpu_custom_call" | custom-call | tf_op jit(solution)/shard_map/pallas_call | solution.py:471
  55.7 3.1 %collective-permute-start.2 = (f32[2,2,104,128]{3,2,1,0:T(8,128)}, f32[2,2,104,128]{3,2,1,0:T(8,128)}, u32[]{:S(2)}, u32[]{:S(2)}) collective-permute-start(f32[2,2,104,128]{3,2,1,0:T(8,128)} %get-tuple-element.37), channel_id=1, source_target_pairs={{0,1},{1,2},{2,3},{3,4},{4,5},{5,6},{6,7},{8,9},{9,10},{10,11},{11... | collective-permute-start | bytes 638984 | tf_op jit(solution)/shard_map/ppermute | solution.py:459
  58.8 1.3 collective-permute-start.3
  60.7 6.3 %all-to-all-start.1 = ((f32[8,8,128]{2,1,0:T(8,128)}), f32[8,8,128]{2,1,0:T(8,128)}, u32[]{:S(2)}, u32[]{:S(2)}) async-start(f32[8,8,128]{2,1,0:T(8,128)} %broadcast_in_dim.42), calls=%async_computation.1 | async-start | bytes 65536 | tf_op jit(solution)/shard_map/all_to_all | solution.py:464
  67.0 1.3 constant_dynamic-update-slice_fusion.14
  68.3 4.6 %all-to-all-done.1.refs_4_ = f32[8,8,128]{2,1,0:T(8,128)} async-done(((f32[8,8,128]{2,1,0:T(8,128)}), f32[8,8,128]{2,1,0:T(8,128)}, u32[]{:S(2)}, u32[]{:S(2)}) %all-to-all-start.1) | async-done | bytes 32800 | tf_op jit(solution)/shard_map/all_to_all | solution.py:464
  77.5 8.0 %shard_map.53 = (f32[2,4,104,128]{3,2,1,0:T(8,128)S(1)}, f32[2,2,104,128]{3,2,1,0:T(8,128)}, f32[2,2,104,128]{3,2,1,0:T(8,128)}, f32[8,128]{1,0:T(8,128)S(1)}) custom-call(s32[1]{0:T(128)} %bitcast.refs_0_.stripe_ref, f32[2,4,104,128]{3,2,1,0:T(8,128)S(1)} %copy-done.24, f32[2,2,104,128]{3,2,1,0:T(8,128)} %collective-permute-done.2.refs_2_, ...), custom_call_target="tpu_custom_call" | custom-call | tf_op jit(solution)/shard_map/pallas_call | solution.py:471
  86.3 2.3 %collective-permute-start.4 = (f32[2,2,104,128]{3,2,1,0:T(8,128)}, f32[2,2,104,128]{3,2,1,0:T(8,128)}, u32[]{:S(2)}, u32[]{:S(2)}) collective-permute-start(f32[2,2,104,128]{3,2,1,0:T(8,128)} %get-tuple-element.42), channel_id=1, source_target_pairs={{0,1},{1,2},{2,3},{3,4},{4,5},{5,6},{6,7},{8,9},{9,10},{10,11},{11... | collective-permute-start | bytes 638984 | tf_op jit(solution)/shard_map/ppermute | solution.py:459
  88.6 1.3 collective-permute-start.5
  90.5 3.9 %all-to-all-start.2 = ((f32[8,8,128]{2,1,0:T(8,128)}), f32[8,8,128]{2,1,0:T(8,128)}, u32[]{:S(2)}, u32[]{:S(2)}) async-start(f32[8,8,128]{2,1,0:T(8,128)} %broadcast_in_dim.44), calls=%async_computation.2 | async-start | bytes 65536 | tf_op jit(solution)/shard_map/all_to_all | solution.py:464
  94.4 1.3 constant_dynamic-update-slice_fusion.13
  95.7 4.5 %all-to-all-done.2.refs_4_ = f32[8,8,128]{2,1,0:T(8,128)} async-done(((f32[8,8,128]{2,1,0:T(8,128)}), f32[8,8,128]{2,1,0:T(8,128)}, u32[]{:S(2)}, u32[]{:S(2)}) %all-to-all-start.2) | async-done | bytes 32800 | tf_op jit(solution)/shard_map/all_to_all | solution.py:464
  103.9 1.0 copy-done.26
  104.9 8.0 %shard_map.54 = (f32[2,4,104,128]{3,2,1,0:T(8,128)S(1)}, f32[2,2,104,128]{3,2,1,0:T(8,128)}, f32[2,2,104,128]{3,2,1,0:T(8,128)}, f32[8,128]{1,0:T(8,128)S(1)}) custom-call(s32[1]{0:T(128)} %bitcast.refs_0_.stripe_ref, f32[2,4,104,128]{3,2,1,0:T(8,128)S(1)} %copy-done.26, f32[2,2,104,128]{3,2,1,0:T(8,128)} %collective-permute-done.4.refs_2_, ...), custom_call_target="tpu_custom_call" | custom-call | tf_op jit(solution)/shard_map/pallas_call | solution.py:471
  113.6 2.3 %collective-permute-start.6 = (f32[2,2,104,128]{3,2,1,0:T(8,128)}, f32[2,2,104,128]{3,2,1,0:T(8,128)}, u32[]{:S(2)}, u32[]{:S(2)}) collective-permute-start(f32[2,2,104,128]{3,2,1,0:T(8,128)} %get-tuple-element.46), channel_id=1, source_target_pairs={{0,1},{1,2},{2,3},{3,4},{4,5},{5,6},{6,7},{8,9},{9,10},{10,11},{11... | collective-permute-start | bytes 638984 | tf_op jit(solution)/shard_map/ppermute | solution.py:459
  115.9 1.3 collective-permute-start.7
  117.9 4.4 %all-to-all-start.3 = ((f32[8,8,128]{2,1,0:T(8,128)}), f32[8,8,128]{2,1,0:T(8,128)}, u32[]{:S(2)}, u32[]{:S(2)}) async-start(f32[8,8,128]{2,1,0:T(8,128)} %broadcast_in_dim.45), calls=%async_computation.3 | async-start | bytes 65536 | tf_op jit(solution)/shard_map/all_to_all | solution.py:464
  122.2 1.3 constant_dynamic-update-slice_fusion.12
  123.5 4.5 %all-to-all-done.3.refs_4_ = f32[8,8,128]{2,1,0:T(8,128)} async-done(((f32[8,8,128]{2,1,0:T(8,128)}), f32[8,8,128]{2,1,0:T(8,128)}, u32[]{:S(2)}, u32[]{:S(2)}) %all-to-all-start.3) | async-done | bytes 32800 | tf_op jit(solution)/shard_map/all_to_all | solution.py:464
  131.7 1.0 copy-done.22
  132.7 8.0 %shard_map.55 = (f32[200,100]{1,0:T(8,128)S(1)}, f32[200,100]{1,0:T(8,128)}, f32[8,128]{1,0:T(8,128)S(1)}) custom-call(s32[1]{0:T(128)} %bitcast.refs_0_.stripe_ref, f32[2,4,104,128]{3,2,1,0:T(8,128)S(1)} %copy-done.22, f32[2,2,104,128]{3,2,1,0:T(8,128)} %collective-permute-done.6.refs_2_, f32[2,2,104,128]{3,2,1,0:T(8,128)} %collective-permute-done.7.refs_3_, ...), custom_call_target="tpu_custom_call" | custom-call | tf_op jit(solution)/shard_map/pallas_call | solution.py:471
  141.9 3.3 %all-to-all-start.4 = ((f32[8,8,128]{2,1,0:T(8,128)}), f32[8,8,128]{2,1,0:T(8,128)S(1)}, u32[]{:S(2)}, u32[]{:S(2)}) async-start(f32[8,8,128]{2,1,0:T(8,128)} %broadcast_in_dim.46), calls=%async_computation.4 | async-start | bytes 65536 | tf_op jit(solution)/shard_map/all_to_all | solution.py:464
  145.3 1.3 constant_dynamic-update-slice_fusion.11.pull_ref
  146.6 4.4 %all-to-all-done.4.red_ref = f32[8,8,128]{2,1,0:T(8,128)S(1)} async-done(((f32[8,8,128]{2,1,0:T(8,128)}), f32[8,8,128]{2,1,0:T(8,128)S(1)}, u32[]{:S(2)}, u32[]{:S(2)}) %all-to-all-start.4) | async-done | bytes 32800 | tf_op jit(solution)/shard_map/all_to_all | solution.py:464
  152.8 2.1 %shard_map.56 = f32[200,100]{1,0:T(8,128)} custom-call(s32[1]{0:T(128)} %bitcast.refs_0_.stripe_ref, f32[200,100]{1,0:T(8,128)S(1)} %copy-done.33, f32[8,8,128]{2,1,0:T(8,128)S(1)} %all-to-all-done.4.red_ref, bf16[192,768]{1,0:T(8,128)(2,1)S(1)} %copy-done.6, bf16[384,128]{1,0:T(8,128)(2,1)} %constant_dynamic-update-slice_fusion.11.pull_ref), custom_call_target="tpu_custom_call" | custom-call | tf_op jit(solution)/shard_map/pallas_call | solution.py:471
  (124 shorter events, 35.8 us)
Async XLA Ops:
  18.1 23.6 %collective-permute-start = (bf16[2,3,104,128]{3,2,1,0:T(8,128)(2,1)}, bf16[2,3,104,128]{3,2,1,0:T(8,128)(2,1)}, u32[]{:S(2)}, u32[]{:S(2)}) collective-permute-start(bf16[2,3,104,128]{3,2,1,0:T(8,128)(2,1)} %get-tuple-element.28), channel_id=1, source_target_pairs={{0,1},{1,2},{2,3},{3,4},{4,5},{5,6},{6,7},{8,9},{9,10},{10,11},{11... | collective-permute-start | bytes 479240 | tf_op jit(solution)/shard_map/ppermute | solution.py:459
  20.0 21.7 %collective-permute-start.1 = (bf16[2,3,104,128]{3,2,1,0:T(8,128)(2,1)}, bf16[2,3,104,128]{3,2,1,0:T(8,128)(2,1)}, u32[]{:S(2)}, u32[]{:S(2)}) collective-permute-start(bf16[2,3,104,128]{3,2,1,0:T(8,128)(2,1)} %get-tuple-element.29), channel_id=1, source_target_pairs={{1,0},{2,1},{3,2},{4,3},{5,4},{6,5},{7,6},{9,8},{10,9},{11,10},{12... | collective-permute-start | bytes 479240 | tf_op jit(solution)/shard_map/ppermute | solution.py:460
  21.9 19.8 %all-to-all-start = ((f32[8,8,128]{2,1,0:T(8,128)}), f32[8,8,128]{2,1,0:T(8,128)}, u32[]{:S(2)}, u32[]{:S(2)}) async-start(f32[8,8,128]{2,1,0:T(8,128)} %broadcast_in_dim.34), calls=%async_computation | async-start | bytes 65536 | tf_op jit(solution)/shard_map/all_to_all | solution.py:464
  29.9 2.6 %copy-start.34 = (bf16[61,61]{1,0:T(8,128)(2,1)S(1)}, bf16[61,61]{1,0:T(8,128)(2,1)}, u32[]{:S(2)}) copy-start(bf16[61,61]{1,0:T(8,128)(2,1)} %param.5) | copy-start | bytes 22330
  40.4 1.3 copy-start
  41.7 1.0 copy-start.2
  42.7 0.9 copy-start.12
  44.4 1.0 copy-start.28
  45.4 1.0 copy-start.30
  55.7 17.1 %collective-permute-start.2 = (f32[2,2,104,128]{3,2,1,0:T(8,128)}, f32[2,2,104,128]{3,2,1,0:T(8,128)}, u32[]{:S(2)}, u32[]{:S(2)}) collective-permute-start(f32[2,2,104,128]{3,2,1,0:T(8,128)} %get-tuple-element.37), channel_id=1, source_target_pairs={{0,1},{1,2},{2,3},{3,4},{4,5},{5,6},{6,7},{8,9},{9,10},{10,11},{11... | collective-permute-start | bytes 638984 | tf_op jit(solution)/shard_map/ppermute | solution.py:459
  58.8 14.1 %collective-permute-start.3 = (f32[2,2,104,128]{3,2,1,0:T(8,128)}, f32[2,2,104,128]{3,2,1,0:T(8,128)}, u32[]{:S(2)}, u32[]{:S(2)}) collective-permute-start(f32[2,2,104,128]{3,2,1,0:T(8,128)} %get-tuple-element.38), channel_id=1, source_target_pairs={{1,0},{2,1},{3,2},{4,3},{5,4},{6,5},{7,6},{9,8},{10,9},{11,10},{12... | collective-permute-start | bytes 638984 | tf_op jit(solution)/shard_map/ppermute | solution.py:460
  60.7 12.1 %all-to-all-start.1 = ((f32[8,8,128]{2,1,0:T(8,128)}), f32[8,8,128]{2,1,0:T(8,128)}, u32[]{:S(2)}, u32[]{:S(2)}) async-start(f32[8,8,128]{2,1,0:T(8,128)} %broadcast_in_dim.42), calls=%async_computation.1 | async-start | bytes 65536 | tf_op jit(solution)/shard_map/all_to_all | solution.py:464
  72.9 1.0 copy-start.3
  73.8 1.0 copy-start.8
  74.8 0.9 copy-start.13
  76.5 1.0 copy-start.24
  86.3 14.0 %collective-permute-start.4 = (f32[2,2,104,128]{3,2,1,0:T(8,128)}, f32[2,2,104,128]{3,2,1,0:T(8,128)}, u32[]{:S(2)}, u32[]{:S(2)}) collective-permute-start(f32[2,2,104,128]{3,2,1,0:T(8,128)} %get-tuple-element.42), channel_id=1, source_target_pairs={{0,1},{1,2},{2,3},{3,4},{4,5},{5,6},{6,7},{8,9},{9,10},{10,11},{11... | collective-permute-start | bytes 638984 | tf_op jit(solution)/shard_map/ppermute | solution.py:459
  88.6 11.6 %collective-permute-start.5 = (f32[2,2,104,128]{3,2,1,0:T(8,128)}, f32[2,2,104,128]{3,2,1,0:T(8,128)}, u32[]{:S(2)}, u32[]{:S(2)}) collective-permute-start(f32[2,2,104,128]{3,2,1,0:T(8,128)} %get-tuple-element.43), channel_id=1, source_target_pairs={{1,0},{2,1},{3,2},{4,3},{5,4},{6,5},{7,6},{9,8},{10,9},{11,10},{12... | collective-permute-start | bytes 638984 | tf_op jit(solution)/shard_map/ppermute | solution.py:460
  90.5 9.7 %all-to-all-start.2 = ((f32[8,8,128]{2,1,0:T(8,128)}), f32[8,8,128]{2,1,0:T(8,128)}, u32[]{:S(2)}, u32[]{:S(2)}) async-start(f32[8,8,128]{2,1,0:T(8,128)} %broadcast_in_dim.44), calls=%async_computation.2 | async-start | bytes 65536 | tf_op jit(solution)/shard_map/all_to_all | solution.py:464
  100.2 1.0 copy-start.4
  101.2 1.0 copy-start.9
  102.1 0.9 copy-start.14
  103.9 1.0 copy-start.26
  113.6 14.4 %collective-permute-start.6 = (f32[2,2,104,128]{3,2,1,0:T(8,128)}, f32[2,2,104,128]{3,2,1,0:T(8,128)}, u32[]{:S(2)}, u32[]{:S(2)}) collective-permute-start(f32[2,2,104,128]{3,2,1,0:T(8,128)} %get-tuple-element.46), channel_id=1, source_target_pairs={{0,1},{1,2},{2,3},{3,4},{4,5},{5,6},{6,7},{8,9},{9,10},{10,11},{11... | collective-permute-start | bytes 638984 | tf_op jit(solution)/shard_map/ppermute | solution.py:459
  115.9 12.1 %collective-permute-start.7 = (f32[2,2,104,128]{3,2,1,0:T(8,128)}, f32[2,2,104,128]{3,2,1,0:T(8,128)}, u32[]{:S(2)}, u32[]{:S(2)}) collective-permute-start(f32[2,2,104,128]{3,2,1,0:T(8,128)} %get-tuple-element.47), channel_id=1, source_target_pairs={{1,0},{2,1},{3,2},{4,3},{5,4},{6,5},{7,6},{9,8},{10,9},{11,10},{12... | collective-permute-start | bytes 638984 | tf_op jit(solution)/shard_map/ppermute | solution.py:460
  117.9 10.2 %all-to-all-start.3 = ((f32[8,8,128]{2,1,0:T(8,128)}), f32[8,8,128]{2,1,0:T(8,128)}, u32[]{:S(2)}, u32[]{:S(2)}) async-start(f32[8,8,128]{2,1,0:T(8,128)} %broadcast_in_dim.45), calls=%async_computation.3 | async-start | bytes 65536 | tf_op jit(solution)/shard_map/all_to_all | solution.py:464
  128.1 1.0 copy-start.5
  129.0 1.0 copy-start.10
  130.0 0.9 copy-start.15
  131.7 1.0 copy-start.22
  141.9 9.0 %all-to-all-start.4 = ((f32[8,8,128]{2,1,0:T(8,128)}), f32[8,8,128]{2,1,0:T(8,128)S(1)}, u32[]{:S(2)}, u32[]{:S(2)}) async-start(f32[8,8,128]{2,1,0:T(8,128)} %broadcast_in_dim.46), calls=%async_computation.4 | async-start | bytes 65536 | tf_op jit(solution)/shard_map/all_to_all | solution.py:464
  150.9 1.0 copy-start.6
  (17 other events, 12.9 us)

commit v3 on v2

--- a/solution.py
+++ b/solution.py
@@ -147,7 +147,7 @@
             pltpu.VMEM((TAPS_PAD * 8, LANES), f32),
             pltpu.VMEM(((TAPS_PAD + PER - 1) * LANES, LANES), f32),
         ],
-        compiler_params=pltpu.CompilerParams(vmem_limit_bytes=32 * 1024 * 1024),
+        compiler_params=pltpu.CompilerParams(vmem_limit_bytes=10 * 1024 * 1024),
     )(taps)
 
 
@@ -246,7 +246,7 @@
 
 
 def start_kernel(
-    sizes, both_ref,
+    sizes, stripe_ref, both_ref,
     own_out, mask_out, left_out, right_out, red_out, rows_out, cells_out, plane_ref, wide_ref,
 ):
     planes, depth, half, cols, crow, ncx = sizes
@@ -465,9 +465,9 @@
 
     vmem = pl.BlockSpec(memory_space=pltpu.VMEM)
     smem = pl.BlockSpec(memory_space=pltpu.SMEM)
-    params = pltpu.CompilerParams(vmem_limit_bytes=48 * 1024 * 1024)
-
     def call(kernel, out_shape, args, scratch=()):
+        held = sum(math.prod(a.shape) * jnp.dtype(a.dtype).itemsize for a in scratch)
+        params = pltpu.CompilerParams(vmem_limit_bytes=held + 4 * 1024 * 1024)
         return pl.pallas_call(
             kernel,
             out_shape=out_shape,
@@ -527,10 +527,13 @@
             tiles, mask_tiles, halo, halo, few,
             array((PAIR, depth, PER * 2 * ncx), bf16), array((PAIR, PER * ncx, depth), bf16),
         ],
-        [both],
+        [stripe, both],
         [pltpu.VMEM((2, PHASES, depth, LANES), f32), pltpu.VMEM((2, planes * PHASES, LANES), f32)],
     )
     fwd, adj = bands(psf)
+    tables = (rows_table, pull_table, back_table, inside, in_row, in_cell, fwd, adj)
+    own, mask, red, end_table, tables = lax.optimization_barrier((own, mask, red, end_table, tables))
+    rows_table = tables[0]
 
     height = round_up(blocks * depth, 16)
     scratch = [
@@ -548,7 +551,7 @@
         last = step == ITERS - 1
         from_left, from_right = shift(to_right, to_left)
         args = [stripe, own, from_left, from_right, share(red), mask]
-        args += [rows_table, pull_table, back_table, inside, in_row, in_cell, fwd, adj]
+        args += tables
         kernel = functools.partial(step_kernel, sizes, first, last)
         if last:
             row_scratch = pltpu.VMEM((planes * PHASES, LANES), f32)

time: 157 us -> 113 us (0.72)
  blocking collectives: 11.1 us -> 62.9 us
  local copies, waits for them, and re-layouts: 32.8 us -> 0.84 us
  starting transfers between devices: 39.9 us -> 11.5 us
  waiting for transfers between devices: 18 us -> 0.02 us
  Pallas kernels: 40.8 us -> 31.3 us
  other arithmetic: 10.7 us -> 4.16 us
    all_to_all x0 -> x5, blocking collectives: none -> 51.8 us  [share(): lax.all_to_all(jnp.broadcast_to(red, (scans,) + red.shape), 'scan', 0, 0)]
    unnamed x72 -> x2, local copies, waits for them, and re-layouts: 29.7 us -> 0.01 us
    all_to_all x5 -> x0, starting transfers between devices: 25.1 us -> none  [share(): lax.all_to_all(jnp.broadcast_to(red, (scans,) + red.shape), 'scan', 0, 0)]
    all_to_all x5 -> x0, waiting for transfers between devices: 18 us -> none  [share(): lax.all_to_all(jnp.broadcast_to(red, (scans,) + red.shape), 'scan', 0, 0)]
    pallas_call x6, Pallas kernels: 35.7 us -> 26.3 us  [call(): pl.pallas_call(kernel, out_shape=out_shape, in_specs=[smem if a is stripe...]
    unnamed x20, other arithmetic: 6.44 us -> 1.66 us
    ppermute x4, starting transfers between devices: 9.66 us -> 6.3 us  [shift(): lax.ppermute(to_right, 'scan', forward)]
    broadcast_in_dim x5, local copies, waits for them, and re-layouts: 3.07 us -> 0.02 us  [share(): jnp.broadcast_to(red, (scans,) + red.shape)]
  transfers between devices with their start and end apart: 13 -> 8, of which waited for: 4 -> 0; matrix products, arithmetic and copies ran while one was open for 8% -> 3% of each run, Pallas kernels for 3% -> 4%
where the time goes in v3:
time: 113 us; the launch traced here: 112 us
  blocking collectives  62.9 us (56%)
  Pallas kernels  31.3 us (28%)
  starting transfers between devices  11.5 us (10%)
  other arithmetic  4.16 us (4%)
    all_to_all x5, blocking collectives, share(): lax.all_to_all(jnp.broadcast_to(red, (scans,) + red.shape), 'scan', 0, 0)  51.8 us
    pallas_call x6, Pallas kernels, call(): pl.pallas_call(kernel, out_shape=out_shape, in_specs=[smem if a is stripe...  26.3 us
    all_gather x1, blocking collectives, per_device(): both = lax.all_gather(both, 'stripe', axis=0, tiled=True)  11.1 us
    ppermute x4, starting transfers between devices, shift(): lax.ppermute(to_right, 'scan', forward)  6.3 us
    ppermute x4, starting transfers between devices, shift(): lax.ppermute(to_left, 'scan', backward)  5.17 us
    pallas_call x1, Pallas kernels, bands(): pl.pallas_call(bands_kernel, out_shape=[table, table], scratch_shapes=[pl...  5.04 us
  transfers between devices with their start and end apart: 8, of which 0 were waited for; matrix products, arithmetic and copies ran while one was open for 3% of the time, Pallas kernels for 4%

profile of v3, /device:TPU:0, one launch (start us, length us, event | category | flops | bytes accessed | tf_op | source)
XLA Modules:
  0.0 112.3 jit_solution(695275099101418155)
XLA Ops:
  0.6 0.9 convert_element_type.74
  1.5 0.8 fusion.18
  2.4 11.1 %all_gather.3.both_ref = bf16[800,256]{1,0:T(8,128)(2,1)S(1)} all-gather(bf16[200,256]{1,0:T(8,128)(2,1)S(1)} %fusion.18), channel_id=1, replica_groups=mesh['stripe'=4,'scan'=8] {'stripe'}, dimensions={0}, use_global_device_ids=true | all-gather | bytes 512000 | tf_op jit(solution)/shard_map/all_gather | solution.py:519
  13.5 1.1 %shard_map.50 = (f32[2,4,104,128]{3,2,1,0:T(8,128)S(1)}, bf16[2,5,104,128]{3,2,1,0:T(8,128)(2,1)S(1)}, bf16[2,3,104,128]{3,2,1,0:T(8,128)(2,1)S(1)}, bf16[2,3,10...) custom-call(s32[1]{0:T(128)} %bitcast.stripe_ref.refs_0_, ...), custom_call_target="tpu_custom_call" | custom-call | tf_op jit(solution)/shard_map/pallas_call | solution.py:471
  14.6 1.3 %collective-permute-start = (bf16[2,3,104,128]{3,2,1,0:T(8,128)(2,1)S(1)}, bf16[2,3,104,128]{3,2,1,0:T(8,128)(2,1)S(1)}, u32[]{:S(2)}, u32[]{:S(2)}) collective-permute-start(bf16[2,3,104,128]{3,2,1,0:T(8,128)(2,1)S(1)} %get-tuple-element.47), channel_id=1, source_target_pairs={{0,1},{1,2},{2,3},{3,4},{4,5},{5,6},{6,7},{8,9},{9,10},{10,11},{11... | collective-permute-start | bytes 479240 | tf_op jit(solution)/shard_map/ppermute | solution.py:459
  15.9 1.3 %collective-permute-start.1 = (bf16[2,3,104,128]{3,2,1,0:T(8,128)(2,1)S(1)}, bf16[2,3,104,128]{3,2,1,0:T(8,128)(2,1)S(1)}, u32[]{:S(2)}, u32[]{:S(2)}) collective-permute-start(bf16[2,3,104,128]{3,2,1,0:T(8,128)(2,1)S(1)} %get-tuple-element.48), channel_id=1, source_target_pairs={{1,0},{2,1},{3,2},{4,3},{5,4},{6,5},{7,6},{9,8},{10,9},{11,10},{12... | collective-permute-start | bytes 479240 | tf_op jit(solution)/shard_map/ppermute | solution.py:460
  17.4 0.8 rev.3
  18.2 0.2 fusion.65
  19.3 0.4 convolution_multiply_fusion
  19.9 0.2 fusion.24
  20.0 0.2 fusion.23
  20.2 0.2 fusion.25
  20.4 0.2 fusion.19
  20.6 0.2 fusion.20
  20.8 0.2 fusion.17.refs_7_
  21.3 5.0 %shard_map.51 = (bf16[3,2432,128]{2,1,0:T(8,128)(2,1)S(1)}, bf16[3,2432,128]{2,1,0:T(8,128)(2,1)S(1)}) custom-call(bf16[2,64,64]{2,1,0:T(8,128)(2,1)S(1)} %fusion.72.taps_ref), custom_call_target="tpu_custom_call" | custom-call | tf_op jit(solution)/shard_map/pallas_call | solution.py:143
  26.4 13.4 %all_to_all.25.refs_4_ = f32[8,8,128]{2,1,0:T(8,128)S(1)} all-to-all(f32[8,8,128]{2,1,0:T(8,128)S(1)} %broadcast_in_dim.41), channel_id=1, replica_groups=mesh['stripe'=4,'scan'=8] {'scan'}, dimensions={0} | all-to-all | bytes 65536 | tf_op jit(solution)/shard_map/all_to_all | solution.py:464
  39.8 5.9 %shard_map.52 = (f32[2,4,104,128]{3,2,1,0:T(8,128)S(1)}, f32[2,2,104,128]{3,2,1,0:T(8,128)S(1)}, f32[2,2,104,128]{3,2,1,0:T(8,128)S(1)}, f32[8,128]{1,0:T(8,128)S(1)}, bf16[2,5,104,128]{3,2,1,0:T(8,128)(2,1)S(1)}) custom-call(s32[1]{0:T(128)} %bitcast.stripe_ref.refs_0_, f32[2,4,104,128]{3,2,1,0:T(8,128)S(1)} %get-tuple-element.46.refs_1_, ...), custom_call_target="tpu_custom_call" | custom-call | tf_op jit(solution)/shard_map/pallas_call | solution.py:471
  45.7 1.7 %collective-permute-start.2 = (f32[2,2,104,128]{3,2,1,0:T(8,128)S(1)}, f32[2,2,104,128]{3,2,1,0:T(8,128)S(1)}, u32[]{:S(2)}, u32[]{:S(2)}) collective-permute-start(f32[2,2,104,128]{3,2,1,0:T(8,128)S(1)} %get-tuple-element.60), channel_id=1, source_target_pairs={{0,1},{1,2},{2,3},{3,4},{4,5},{5,6},{6,7},{8,9},{9,10},{10,11},{11... | collective-permute-start | bytes 638984 | tf_op jit(solution)/shard_map/ppermute | solution.py:459
  47.3 1.3 %collective-permute-start.3 = (f32[2,2,104,128]{3,2,1,0:T(8,128)S(1)}, f32[2,2,104,128]{3,2,1,0:T(8,128)S(1)}, u32[]{:S(2)}, u32[]{:S(2)}) collective-permute-start(f32[2,2,104,128]{3,2,1,0:T(8,128)S(1)} %get-tuple-element.61), channel_id=1, source_target_pairs={{1,0},{2,1},{3,2},{4,3},{5,4},{6,5},{7,6},{9,8},{10,9},{11,10},{12... | collective-permute-start | bytes 638984 | tf_op jit(solution)/shard_map/ppermute | solution.py:460
  48.6 10.1 %all_to_all.26.refs_4_ = f32[8,8,128]{2,1,0:T(8,128)S(1)} all-to-all(f32[8,8,128]{2,1,0:T(8,128)S(1)} %broadcast_in_dim.42), channel_id=1, replica_groups=mesh['stripe'=4,'scan'=8] {'scan'}, dimensions={0} | all-to-all | bytes 65536 | tf_op jit(solution)/shard_map/all_to_all | solution.py:464
  58.7 5.9 %shard_map.53 = (f32[2,4,104,128]{3,2,1,0:T(8,128)S(1)}, f32[2,2,104,128]{3,2,1,0:T(8,128)S(1)}, f32[2,2,104,128]{3,2,1,0:T(8,128)S(1)}, f32[8,128]{1,0:T(8,128)S(1)}) custom-call(s32[1]{0:T(128)} %bitcast.stripe_ref.refs_0_, f32[2,4,104,128]{3,2,1,0:T(8,128)S(1)} %get-tuple-element.59.refs_1_, f32[2,2,104,128]{3,2,1,0:T(8,128)S(1)} %collective-permute-done.2.refs_2_, ...), custom_call_target="tpu_custom_call" | custom-call | tf_op jit(solution)/shard_map/pallas_call | solution.py:471
  64.6 1.7 %collective-permute-start.4 = (f32[2,2,104,128]{3,2,1,0:T(8,128)S(1)}, f32[2,2,104,128]{3,2,1,0:T(8,128)S(1)}, u32[]{:S(2)}, u32[]{:S(2)}) collective-permute-start(f32[2,2,104,128]{3,2,1,0:T(8,128)S(1)} %get-tuple-element.65), channel_id=1, source_target_pairs={{0,1},{1,2},{2,3},{3,4},{4,5},{5,6},{6,7},{8,9},{9,10},{10,11},{11... | collective-permute-start | bytes 638984 | tf_op jit(solution)/shard_map/ppermute | solution.py:459
  66.3 1.3 %collective-permute-start.5 = (f32[2,2,104,128]{3,2,1,0:T(8,128)S(1)}, f32[2,2,104,128]{3,2,1,0:T(8,128)S(1)}, u32[]{:S(2)}, u32[]{:S(2)}) collective-permute-start(f32[2,2,104,128]{3,2,1,0:T(8,128)S(1)} %get-tuple-element.66), channel_id=1, source_target_pairs={{1,0},{2,1},{3,2},{4,3},{5,4},{6,5},{7,6},{9,8},{10,9},{11,10},{12... | collective-permute-start | bytes 638984 | tf_op jit(solution)/shard_map/ppermute | solution.py:460
  67.6 10.1 %all_to_all.27.refs_4_ = f32[8,8,128]{2,1,0:T(8,128)S(1)} all-to-all(f32[8,8,128]{2,1,0:T(8,128)S(1)} %broadcast_in_dim.44), channel_id=1, replica_groups=mesh['stripe'=4,'scan'=8] {'scan'}, dimensions={0} | all-to-all | bytes 65536 | tf_op jit(solution)/shard_map/all_to_all | solution.py:464
  77.7 5.8 %shard_map.54 = (f32[2,4,104,128]{3,2,1,0:T(8,128)S(1)}, f32[2,2,104,128]{3,2,1,0:T(8,128)S(1)}, f32[2,2,104,128]{3,2,1,0:T(8,128)S(1)}, f32[8,128]{1,0:T(8,128)S(1)}) custom-call(s32[1]{0:T(128)} %bitcast.stripe_ref.refs_0_, f32[2,4,104,128]{3,2,1,0:T(8,128)S(1)} %get-tuple-element.64.refs_1_, f32[2,2,104,128]{3,2,1,0:T(8,128)S(1)} %collective-permute-done.4.refs_2_, ...), custom_call_target="tpu_custom_call" | custom-call | tf_op jit(solution)/shard_map/pallas_call | solution.py:471
  83.5 1.7 %collective-permute-start.6 = (f32[2,2,104,128]{3,2,1,0:T(8,128)S(1)}, f32[2,2,104,128]{3,2,1,0:T(8,128)S(1)}, u32[]{:S(2)}, u32[]{:S(2)}) collective-permute-start(f32[2,2,104,128]{3,2,1,0:T(8,128)S(1)} %get-tuple-element.69), channel_id=1, source_target_pairs={{0,1},{1,2},{2,3},{3,4},{4,5},{5,6},{6,7},{8,9},{9,10},{10,11},{11... | collective-permute-start | bytes 638984 | tf_op jit(solution)/shard_map/ppermute | solution.py:459
  85.2 1.3 %collective-permute-start.7 = (f32[2,2,104,128]{3,2,1,0:T(8,128)S(1)}, f32[2,2,104,128]{3,2,1,0:T(8,128)S(1)}, u32[]{:S(2)}, u32[]{:S(2)}) collective-permute-start(f32[2,2,104,128]{3,2,1,0:T(8,128)S(1)} %get-tuple-element.70), channel_id=1, source_target_pairs={{1,0},{2,1},{3,2},{4,3},{5,4},{6,5},{7,6},{9,8},{10,9},{11,10},{12... | collective-permute-start | bytes 638984 | tf_op jit(solution)/shard_map/ppermute | solution.py:460
  86.5 10.1 %all_to_all.28.refs_4_ = f32[8,8,128]{2,1,0:T(8,128)S(1)} all-to-all(f32[8,8,128]{2,1,0:T(8,128)S(1)} %broadcast_in_dim.45), channel_id=1, replica_groups=mesh['stripe'=4,'scan'=8] {'scan'}, dimensions={0} | all-to-all | bytes 65536 | tf_op jit(solution)/shard_map/all_to_all | solution.py:464
  96.6 6.3 %shard_map.55 = (f32[200,100]{1,0:T(8,128)S(1)}, f32[200,100]{1,0:T(8,128)}, f32[8,128]{1,0:T(8,128)S(1)}) custom-call(s32[1]{0:T(128)} %bitcast.stripe_ref.refs_0_, f32[2,4,104,128]{3,2,1,0:T(8,128)S(1)} %get-tuple-element.68.refs_1_, f32[2,2,104,128]{3,2,1,0:T(8,128)S(1)} %collective-permute-done.6.refs_2_, ...), custom_call_target="tpu_custom_call" | custom-call | tf_op jit(solution)/shard_map/pallas_call | solution.py:471
  102.9 8.1 %all_to_all.29.red_ref = f32[8,8,128]{2,1,0:T(8,128)S(1)} all-to-all(f32[8,8,128]{2,1,0:T(8,128)S(1)} %broadcast_in_dim.46), channel_id=1, replica_groups=mesh['stripe'=4,'scan'=8] {'scan'}, dimensions={0} | all-to-all | bytes 65536 | tf_op jit(solution)/shard_map/all_to_all | solution.py:464
  111.0 1.3 %shard_map.56 = f32[200,100]{1,0:T(8,128)} custom-call(s32[1]{0:T(128)} %bitcast.stripe_ref.refs_0_, f32[200,100]{1,0:T(8,128)S(1)} %get-tuple-element.73.v_ref, f32[8,8,128]{2,1,0:T(8,128)S(1)} %all_to_all.29.red_ref, bf16[192,768]{1,0:T(8,128)(2,1)S(1)} %constant_dynamic-update-slice_fusion.6.refs_6_.rows_ref, ...), custom_call_target="tpu_custom_call" | custom-call | tf_op jit(solution)/shard_map/pallas_call | solution.py:471
  (49 shorter events, 1.4 us)
Async XLA Ops:
  14.6 25.2 %collective-permute-start = (bf16[2,3,104,128]{3,2,1,0:T(8,128)(2,1)S(1)}, bf16[2,3,104,128]{3,2,1,0:T(8,128)(2,1)S(1)}, u32[]{:S(2)}, u32[]{:S(2)}) collective-permute-start(bf16[2,3,104,128]{3,2,1,0:T(8,128)(2,1)S(1)} %get-tuple-element.47), channel_id=1, source_target_pairs={{0,1},{1,2},{2,3},{3,4},{4,5},{5,6},{6,7},{8,9},{9,10},{10,11},{11... | collective-permute-start | bytes 479240 | tf_op jit(solution)/shard_map/ppermute | solution.py:459
  15.9 23.9 %collective-permute-start.1 = (bf16[2,3,104,128]{3,2,1,0:T(8,128)(2,1)S(1)}, bf16[2,3,104,128]{3,2,1,0:T(8,128)(2,1)S(1)}, u32[]{:S(2)}, u32[]{:S(2)}) collective-permute-start(bf16[2,3,104,128]{3,2,1,0:T(8,128)(2,1)S(1)} %get-tuple-element.48), channel_id=1, source_target_pairs={{1,0},{2,1},{3,2},{4,3},{5,4},{6,5},{7,6},{9,8},{10,9},{11,10},{12... | collective-permute-start | bytes 479240 | tf_op jit(solution)/shard_map/ppermute | solution.py:460
  19.9 1.4 %copy-start = (bf16[61,61]{1,0:T(8,128)(2,1)S(1)}, bf16[61,61]{1,0:T(8,128)(2,1)}, u32[]{:S(2)}) copy-start(bf16[61,61]{1,0:T(8,128)(2,1)} %param.5) | copy-start | bytes 22330
  45.7 13.1 %collective-permute-start.2 = (f32[2,2,104,128]{3,2,1,0:T(8,128)S(1)}, f32[2,2,104,128]{3,2,1,0:T(8,128)S(1)}, u32[]{:S(2)}, u32[]{:S(2)}) collective-permute-start(f32[2,2,104,128]{3,2,1,0:T(8,128)S(1)} %get-tuple-element.60), channel_id=1, source_target_pairs={{0,1},{1,2},{2,3},{3,4},{4,5},{5,6},{6,7},{8,9},{9,10},{10,11},{11... | collective-permute-start | bytes 638984 | tf_op jit(solution)/shard_map/ppermute | solution.py:459
  47.3 11.4 %collective-permute-start.3 = (f32[2,2,104,128]{3,2,1,0:T(8,128)S(1)}, f32[2,2,104,128]{3,2,1,0:T(8,128)S(1)}, u32[]{:S(2)}, u32[]{:S(2)}) collective-permute-start(f32[2,2,104,128]{3,2,1,0:T(8,128)S(1)} %get-tuple-element.61), channel_id=1, source_target_pairs={{1,0},{2,1},{3,2},{4,3},{5,4},{6,5},{7,6},{9,8},{10,9},{11,10},{12... | collective-permute-start | bytes 638984 | tf_op jit(solution)/shard_map/ppermute | solution.py:460
  64.6 13.1 %collective-permute-start.4 = (f32[2,2,104,128]{3,2,1,0:T(8,128)S(1)}, f32[2,2,104,128]{3,2,1,0:T(8,128)S(1)}, u32[]{:S(2)}, u32[]{:S(2)}) collective-permute-start(f32[2,2,104,128]{3,2,1,0:T(8,128)S(1)} %get-tuple-element.65), channel_id=1, source_target_pairs={{0,1},{1,2},{2,3},{3,4},{4,5},{5,6},{6,7},{8,9},{9,10},{10,11},{11... | collective-permute-start | bytes 638984 | tf_op jit(solution)/shard_map/ppermute | solution.py:459
  66.3 11.4 %collective-permute-start.5 = (f32[2,2,104,128]{3,2,1,0:T(8,128)S(1)}, f32[2,2,104,128]{3,2,1,0:T(8,128)S(1)}, u32[]{:S(2)}, u32[]{:S(2)}) collective-permute-start(f32[2,2,104,128]{3,2,1,0:T(8,128)S(1)} %get-tuple-element.66), channel_id=1, source_target_pairs={{1,0},{2,1},{3,2},{4,3},{5,4},{6,5},{7,6},{9,8},{10,9},{11,10},{12... | collective-permute-start | bytes 638984 | tf_op jit(solution)/shard_map/ppermute | solution.py:460
  83.5 13.1 %collective-permute-start.6 = (f32[2,2,104,128]{3,2,1,0:T(8,128)S(1)}, f32[2,2,104,128]{3,2,1,0:T(8,128)S(1)}, u32[]{:S(2)}, u32[]{:S(2)}) collective-permute-start(f32[2,2,104,128]{3,2,1,0:T(8,128)S(1)} %get-tuple-element.69), channel_id=1, source_target_pairs={{0,1},{1,2},{2,3},{3,4},{4,5},{5,6},{6,7},{8,9},{9,10},{10,11},{11... | collective-permute-start | bytes 638984 | tf_op jit(solution)/shard_map/ppermute | solution.py:459
  85.2 11.4 %collective-permute-start.7 = (f32[2,2,104,128]{3,2,1,0:T(8,128)S(1)}, f32[2,2,104,128]{3,2,1,0:T(8,128)S(1)}, u32[]{:S(2)}, u32[]{:S(2)}) collective-permute-start(f32[2,2,104,128]{3,2,1,0:T(8,128)S(1)} %get-tuple-element.70), channel_id=1, source_target_pairs={{1,0},{2,1},{3,2},{4,3},{5,4},{6,5},{7,6},{9,8},{10,9},{11,10},{12... | collective-permute-start | bytes 638984 | tf_op jit(solution)/shard_map/ppermute | solution.py:460

commit v4 on v3

--- a/solution.py
+++ b/solution.py
@@ -460,8 +460,19 @@
             lax.ppermute(to_left, "scan", backward),
         )
 
+    near = 1
+    while near * near * 4 <= scans and scans % (near * 2) == 0:
+        near *= 2
+    far = scans // near
+    near_groups = [[f * near + i for i in range(near)] for f in range(far)]
+    far_groups = [[f * near + i for f in range(far)] for i in range(near)]
+
     def share(red):
-        return lax.all_to_all(jnp.broadcast_to(red, (scans,) + red.shape), "scan", 0, 0)
+        held = jnp.broadcast_to(red, (near,) + red.shape)
+        held = lax.all_to_all(held, "scan", 0, 0, axis_index_groups=near_groups)
+        held = jnp.broadcast_to(held, (far,) + held.shape)
+        held = lax.all_to_all(held, "scan", 0, 0, axis_index_groups=far_groups)
+        return held.reshape((scans,) + red.shape)
 
     vmem = pl.BlockSpec(memory_space=pltpu.VMEM)
     smem = pl.BlockSpec(memory_space=pltpu.SMEM)

time: 113 us -> 131 us (1.16)
  blocking collectives: 62.9 us -> 82.2 us
    all_to_all x5 -> x10, blocking collectives: 51.8 us -> 71.1 us  [the longest x5 45.4 us: share(): held = lax.all_to_all(held, 'scan', 0, 0, axis_index_groups=far_groups)]
where the time goes in v4:
time: 131 us
  blocking collectives  82.2 us (63%)
  Pallas kernels  31.3 us (24%)
  starting transfers between devices  10.4 us (8%)
  other arithmetic  4.16 us (3%)
    all_to_all x5, blocking collectives, share(): held = lax.all_to_all(held, 'scan', 0, 0, axis_index_groups=far_groups)  45.4 us
    pallas_call x6, Pallas kernels, call(): pl.pallas_call(kernel, out_shape=out_shape, in_specs=[smem if a is stripe...  26.3 us
    all_to_all x5, blocking collectives, share(): held = lax.all_to_all(held, 'scan', 0, 0, axis_index_groups=near_groups)  25.7 us
    all_gather x1, blocking collectives, per_device(): both = lax.all_gather(both, 'stripe', axis=0, tiled=True)  11.1 us
    ppermute x4, starting transfers between devices, shift(): lax.ppermute(to_right, 'scan', forward)  5.27 us
    ppermute x4, starting transfers between devices, shift(): lax.ppermute(to_left, 'scan', backward)  5.17 us
    pallas_call x1, Pallas kernels, bands(): pl.pallas_call(bands_kernel, out_shape=[table, table], scratch_shapes=[pl...  5.04 us
  transfers between devices with their start and end apart: 8, of which 0 were waited for; matrix products, arithmetic and copies ran while one was open for 3% of the time, Pallas kernels for 4%

profile of v4, /device:TPU:0, one launch (start us, length us, event | category | flops | bytes accessed | tf_op | source)
XLA Modules:
  0.0 130.6 jit_solution(18234761867379606560)
XLA Ops:
  0.6 0.9 convert_element_type.74
  1.5 0.8 fusion.18
  2.4 11.1 %all_gather.3.both_ref = bf16[800,256]{1,0:T(8,128)(2,1)S(1)} all-gather(bf16[200,256]{1,0:T(8,128)(2,1)S(1)} %fusion.18), channel_id=1, replica_groups=mesh['stripe'=4,'scan'=8] {'stripe'}, dimensions={0}, use_global_device_ids=true | all-gather | bytes 512000 | tf_op jit(solution)/shard_map/all_gather | solution.py:530
  13.5 1.1 shard_map.50
  14.6 1.3 collective-permute-start
  15.9 1.3 collective-permute-start.1
  17.4 0.8 rev.3
  18.2 0.2 fusion.65
  19.3 0.4 convolution_multiply_fusion
  20.8 0.2 fusion.17.refs_7_
  21.3 5.0 %shard_map.51 = (bf16[3,2432,128]{2,1,0:T(8,128)(2,1)S(1)}, bf16[3,2432,128]{2,1,0:T(8,128)(2,1)S(1)}) custom-call(bf16[2,64,64]{2,1,0:T(8,128)(2,1)S(1)} %fusion.72.taps_ref), custom_call_target="tpu_custom_call" | custom-call | tf_op jit(solution)/shard_map/pallas_call | solution.py:143
  26.4 6.1 %all_to_all.50 = f32[2,8,128]{2,1,0:T(8,128)S(1)} all-to-all(f32[2,8,128]{2,1,0:T(8,128)S(1)} %broadcast_in_dim.52), channel_id=1, replica_groups={{0,1},{2,3},{4,5},{6,7},{8,9},{10,11},{12,13},{14,15},{16,17},{18,19},{..., dimensions={0} | all-to-all | bytes 16384 | tf_op jit(solution)/shard_map/all_to_all | solution.py:472
  32.5 10.9 %all_to_all.51 = f32[4,2,8,128]{3,2,1,0:T(8,128)S(1)} all-to-all(f32[4,2,8,128]{3,2,1,0:T(8,128)S(1)} %broadcast_in_dim.53), channel_id=1, replica_groups={{0,2,4,6},{1,3,5,7},{8,10,12,14},{9,11,13,15},{16,18,20,22},{17,19,21,2..., dimensions={0} | all-to-all | bytes 65536 | tf_op jit(solution)/shard_map/all_to_all | solution.py:474
  43.4 5.9 %shard_map.52 = (f32[2,4,104,128]{3,2,1,0:T(8,128)S(1)}, f32[2,2,104,128]{3,2,1,0:T(8,128)S(1)}, f32[2,2,104,128]{3,2,1,0:T(8,128)S(1)}, f32[8,128]{1,0:T(8,128)S(1)}, bf16[2,5,104,128]{3,2,1,0:T(8,128)(2,1)S(1)}) custom-call(s32[1]{0:T(128)} %bitcast.stripe_ref.refs_0_, f32[2,4,104,128]{3,2,1,0:T(8,128)S(1)} %get-tuple-element.46.refs_1_, ...), custom_call_target="tpu_custom_call" | custom-call | tf_op jit(solution)/shard_map/pallas_call | solution.py:482
  49.3 1.3 %collective-permute-start.2 = (f32[2,2,104,128]{3,2,1,0:T(8,128)S(1)}, f32[2,2,104,128]{3,2,1,0:T(8,128)S(1)}, u32[]{:S(2)}, u32[]{:S(2)}) collective-permute-start(f32[2,2,104,128]{3,2,1,0:T(8,128)S(1)} %get-tuple-element.60), channel_id=1, source_target_pairs={{0,1},{1,2},{2,3},{3,4},{4,5},{5,6},{6,7},{8,9},{9,10},{10,11},{11... | collective-permute-start | bytes 638984 | tf_op jit(solution)/shard_map/ppermute | solution.py:459
  50.6 1.3 collective-permute-start.3
  51.9 5.3 %all_to_all.52 = f32[2,8,128]{2,1,0:T(8,128)S(1)} all-to-all(f32[2,8,128]{2,1,0:T(8,128)S(1)} %broadcast_in_dim.96), channel_id=1, replica_groups={{0,1},{2,3},{4,5},{6,7},{8,9},{10,11},{12,13},{14,15},{16,17},{18,19},{..., dimensions={0} | all-to-all | bytes 16384 | tf_op jit(solution)/shard_map/all_to_all | solution.py:472
  57.2 8.8 %all_to_all.53 = f32[4,2,8,128]{3,2,1,0:T(8,128)S(1)} all-to-all(f32[4,2,8,128]{3,2,1,0:T(8,128)S(1)} %broadcast_in_dim.97), channel_id=1, replica_groups={{0,2,4,6},{1,3,5,7},{8,10,12,14},{9,11,13,15},{16,18,20,22},{17,19,21,2..., dimensions={0} | all-to-all | bytes 65536 | tf_op jit(solution)/shard_map/all_to_all | solution.py:474
  66.1 5.9 %shard_map.53 = (f32[2,4,104,128]{3,2,1,0:T(8,128)S(1)}, f32[2,2,104,128]{3,2,1,0:T(8,128)S(1)}, f32[2,2,104,128]{3,2,1,0:T(8,128)S(1)}, f32[8,128]{1,0:T(8,128)S(1)}) custom-call(s32[1]{0:T(128)} %bitcast.stripe_ref.refs_0_, f32[2,4,104,128]{3,2,1,0:T(8,128)S(1)} %get-tuple-element.59.refs_1_, f32[2,2,104,128]{3,2,1,0:T(8,128)S(1)} %collective-permute-done.2.refs_2_, ...), custom_call_target="tpu_custom_call" | custom-call | tf_op jit(solution)/shard_map/pallas_call | solution.py:482
  71.9 1.3 %collective-permute-start.4 = (f32[2,2,104,128]{3,2,1,0:T(8,128)S(1)}, f32[2,2,104,128]{3,2,1,0:T(8,128)S(1)}, u32[]{:S(2)}, u32[]{:S(2)}) collective-permute-start(f32[2,2,104,128]{3,2,1,0:T(8,128)S(1)} %get-tuple-element.65), channel_id=1, source_target_pairs={{0,1},{1,2},{2,3},{3,4},{4,5},{5,6},{6,7},{8,9},{9,10},{10,11},{11... | collective-permute-start | bytes 638984 | tf_op jit(solution)/shard_map/ppermute | solution.py:459
  73.2 1.3 collective-permute-start.5
  74.6 5.3 %all_to_all.54 = f32[2,8,128]{2,1,0:T(8,128)S(1)} all-to-all(f32[2,8,128]{2,1,0:T(8,128)S(1)} %broadcast_in_dim.98), channel_id=1, replica_groups={{0,1},{2,3},{4,5},{6,7},{8,9},{10,11},{12,13},{14,15},{16,17},{18,19},{..., dimensions={0} | all-to-all | bytes 16384 | tf_op jit(solution)/shard_map/all_to_all | solution.py:472
  79.9 8.8 %all_to_all.55 = f32[4,2,8,128]{3,2,1,0:T(8,128)S(1)} all-to-all(f32[4,2,8,128]{3,2,1,0:T(8,128)S(1)} %broadcast_in_dim.99), channel_id=1, replica_groups={{0,2,4,6},{1,3,5,7},{8,10,12,14},{9,11,13,15},{16,18,20,22},{17,19,21,2..., dimensions={0} | all-to-all | bytes 65536 | tf_op jit(solution)/shard_map/all_to_all | solution.py:474
  88.7 5.8 %shard_map.54 = (f32[2,4,104,128]{3,2,1,0:T(8,128)S(1)}, f32[2,2,104,128]{3,2,1,0:T(8,128)S(1)}, f32[2,2,104,128]{3,2,1,0:T(8,128)S(1)}, f32[8,128]{1,0:T(8,128)S(1)}) custom-call(s32[1]{0:T(128)} %bitcast.stripe_ref.refs_0_, f32[2,4,104,128]{3,2,1,0:T(8,128)S(1)} %get-tuple-element.64.refs_1_, f32[2,2,104,128]{3,2,1,0:T(8,128)S(1)} %collective-permute-done.4.refs_2_, ...), custom_call_target="tpu_custom_call" | custom-call | tf_op jit(solution)/shard_map/pallas_call | solution.py:482
  94.5 1.3 %collective-permute-start.6 = (f32[2,2,104,128]{3,2,1,0:T(8,128)S(1)}, f32[2,2,104,128]{3,2,1,0:T(8,128)S(1)}, u32[]{:S(2)}, u32[]{:S(2)}) collective-permute-start(f32[2,2,104,128]{3,2,1,0:T(8,128)S(1)} %get-tuple-element.69), channel_id=1, source_target_pairs={{0,1},{1,2},{2,3},{3,4},{4,5},{5,6},{6,7},{8,9},{9,10},{10,11},{11... | collective-permute-start | bytes 638984 | tf_op jit(solution)/shard_map/ppermute | solution.py:459
  95.9 1.3 collective-permute-start.7
  97.2 5.3 %all_to_all.56 = f32[2,8,128]{2,1,0:T(8,128)S(1)} all-to-all(f32[2,8,128]{2,1,0:T(8,128)S(1)} %broadcast_in_dim.100), channel_id=1, replica_groups={{0,1},{2,3},{4,5},{6,7},{8,9},{10,11},{12,13},{14,15},{16,17},{18,19},{..., dimensions={0} | all-to-all | bytes 16384 | tf_op jit(solution)/shard_map/all_to_all | solution.py:472
  102.5 8.8 %all_to_all.57 = f32[4,2,8,128]{3,2,1,0:T(8,128)S(1)} all-to-all(f32[4,2,8,128]{3,2,1,0:T(8,128)S(1)} %broadcast_in_dim.101), channel_id=1, replica_groups={{0,2,4,6},{1,3,5,7},{8,10,12,14},{9,11,13,15},{16,18,20,22},{17,19,21,2..., dimensions={0} | all-to-all | bytes 65536 | tf_op jit(solution)/shard_map/all_to_all | solution.py:474
  111.3 6.3 %shard_map.55 = (f32[200,100]{1,0:T(8,128)S(1)}, f32[200,100]{1,0:T(8,128)}, f32[8,128]{1,0:T(8,128)S(1)}) custom-call(s32[1]{0:T(128)} %bitcast.stripe_ref.refs_0_, f32[2,4,104,128]{3,2,1,0:T(8,128)S(1)} %get-tuple-element.68.refs_1_, f32[2,2,104,128]{3,2,1,0:T(8,128)S(1)} %collective-permute-done.6.refs_2_, ...), custom_call_target="tpu_custom_call" | custom-call | tf_op jit(solution)/shard_map/pallas_call | solution.py:482
  117.6 3.7 %all_to_all.58 = f32[2,8,128]{2,1,0:T(8,128)S(1)} all-to-all(f32[2,8,128]{2,1,0:T(8,128)S(1)} %broadcast_in_dim.102), channel_id=1, replica_groups={{0,1},{2,3},{4,5},{6,7},{8,9},{10,11},{12,13},{14,15},{16,17},{18,19},{..., dimensions={0} | all-to-all | bytes 16384 | tf_op jit(solution)/shard_map/all_to_all | solution.py:472
  121.3 8.0 %all_to_all.59 = f32[4,2,8,128]{3,2,1,0:T(8,128)S(1)} all-to-all(f32[4,2,8,128]{3,2,1,0:T(8,128)S(1)} %broadcast_in_dim.103), channel_id=1, replica_groups={{0,2,4,6},{1,3,5,7},{8,10,12,14},{9,11,13,15},{16,18,20,22},{17,19,21,2..., dimensions={0} | all-to-all | bytes 65536 | tf_op jit(solution)/shard_map/all_to_all | solution.py:474
  129.3 1.3 shard_map.56
  (59 shorter events, 2.3 us)
Async XLA Ops:
  14.6 28.8 %collective-permute-start = (bf16[2,3,104,128]{3,2,1,0:T(8,128)(2,1)S(1)}, bf16[2,3,104,128]{3,2,1,0:T(8,128)(2,1)S(1)}, u32[]{:S(2)}, u32[]{:S(2)}) collective-permute-start(bf16[2,3,104,128]{3,2,1,0:T(8,128)(2,1)S(1)} %get-tuple-element.47), channel_id=1, source_target_pairs={{0,1},{1,2},{2,3},{3,4},{4,5},{5,6},{6,7},{8,9},{9,10},{10,11},{11... | collective-permute-start | bytes 479240 | tf_op jit(solution)/shard_map/ppermute | solution.py:459
  15.9 27.5 %collective-permute-start.1 = (bf16[2,3,104,128]{3,2,1,0:T(8,128)(2,1)S(1)}, bf16[2,3,104,128]{3,2,1,0:T(8,128)(2,1)S(1)}, u32[]{:S(2)}, u32[]{:S(2)}) collective-permute-start(bf16[2,3,104,128]{3,2,1,0:T(8,128)(2,1)S(1)} %get-tuple-element.48), channel_id=1, source_target_pairs={{1,0},{2,1},{3,2},{4,3},{5,4},{6,5},{7,6},{9,8},{10,9},{11,10},{12... | collective-permute-start | bytes 479240 | tf_op jit(solution)/shard_map/ppermute | solution.py:460
  19.9 1.4 %copy-start = (bf16[61,61]{1,0:T(8,128)(2,1)S(1)}, bf16[61,61]{1,0:T(8,128)(2,1)}, u32[]{:S(2)}) copy-start(bf16[61,61]{1,0:T(8,128)(2,1)} %param.5) | copy-start | bytes 22330
  49.3 16.8 %collective-permute-start.2 = (f32[2,2,104,128]{3,2,1,0:T(8,128)S(1)}, f32[2,2,104,128]{3,2,1,0:T(8,128)S(1)}, u32[]{:S(2)}, u32[]{:S(2)}) collective-permute-start(f32[2,2,104,128]{3,2,1,0:T(8,128)S(1)} %get-tuple-element.60), channel_id=1, source_target_pairs={{0,1},{1,2},{2,3},{3,4},{4,5},{5,6},{6,7},{8,9},{9,10},{10,11},{11... | collective-permute-start | bytes 638984 | tf_op jit(solution)/shard_map/ppermute | solution.py:459
  50.6 15.5 %collective-permute-start.3 = (f32[2,2,104,128]{3,2,1,0:T(8,128)S(1)}, f32[2,2,104,128]{3,2,1,0:T(8,128)S(1)}, u32[]{:S(2)}, u32[]{:S(2)}) collective-permute-start(f32[2,2,104,128]{3,2,1,0:T(8,128)S(1)} %get-tuple-element.61), channel_id=1, source_target_pairs={{1,0},{2,1},{3,2},{4,3},{5,4},{6,5},{7,6},{9,8},{10,9},{11,10},{12... | collective-permute-start | bytes 638984 | tf_op jit(solution)/shard_map/ppermute | solution.py:460
  71.9 16.8 %collective-permute-start.4 = (f32[2,2,104,128]{3,2,1,0:T(8,128)S(1)}, f32[2,2,104,128]{3,2,1,0:T(8,128)S(1)}, u32[]{:S(2)}, u32[]{:S(2)}) collective-permute-start(f32[2,2,104,128]{3,2,1,0:T(8,128)S(1)} %get-tuple-element.65), channel_id=1, source_target_pairs={{0,1},{1,2},{2,3},{3,4},{4,5},{5,6},{6,7},{8,9},{9,10},{10,11},{11... | collective-permute-start | bytes 638984 | tf_op jit(solution)/shard_map/ppermute | solution.py:459
  73.2 15.5 %collective-permute-start.5 = (f32[2,2,104,128]{3,2,1,0:T(8,128)S(1)}, f32[2,2,104,128]{3,2,1,0:T(8,128)S(1)}, u32[]{:S(2)}, u32[]{:S(2)}) collective-permute-start(f32[2,2,104,128]{3,2,1,0:T(8,128)S(1)} %get-tuple-element.66), channel_id=1, source_target_pairs={{1,0},{2,1},{3,2},{4,3},{5,4},{6,5},{7,6},{9,8},{10,9},{11,10},{12... | collective-permute-start | bytes 638984 | tf_op jit(solution)/shard_map/ppermute | solution.py:460
  94.5 16.8 %collective-permute-start.6 = (f32[2,2,104,128]{3,2,1,0:T(8,128)S(1)}, f32[2,2,104,128]{3,2,1,0:T(8,128)S(1)}, u32[]{:S(2)}, u32[]{:S(2)}) collective-permute-start(f32[2,2,104,128]{3,2,1,0:T(8,128)S(1)} %get-tuple-element.69), channel_id=1, source_target_pairs={{0,1},{1,2},{2,3},{3,4},{4,5},{5,6},{6,7},{8,9},{9,10},{10,11},{11... | collective-permute-start | bytes 638984 | tf_op jit(solution)/shard_map/ppermute | solution.py:459
  95.9 15.5 %collective-permute-start.7 = (f32[2,2,104,128]{3,2,1,0:T(8,128)S(1)}, f32[2,2,104,128]{3,2,1,0:T(8,128)S(1)}, u32[]{:S(2)}, u32[]{:S(2)}) collective-permute-start(f32[2,2,104,128]{3,2,1,0:T(8,128)S(1)} %get-tuple-element.70), channel_id=1, source_target_pairs={{1,0},{2,1},{3,2},{4,3},{5,4},{6,5},{7,6},{9,8},{10,9},{11,10},{12... | collective-permute-start | bytes 638984 | tf_op jit(solution)/shard_map/ppermute | solution.py:460

commit v5 on v3

v5 whole, which is shorter than its diff:
```python
import functools
import math

import jax
import jax.numpy as jnp
from jax import lax
from jax.experimental import pallas as pl
from jax.experimental.pallas import tpu as pltpu
from jax.sharding import PartitionSpec as P

TAPS = 61
RIM = 30
COARSE = 25
SIGMA = 40
ITERS = 4

back_ratio = 0.6
resist_gain = 3.0
resist_level = 1.5
step_length = 0.5

PHASES = 8
SPAN = 32
LANES = 128
PER = LANES // SPAN
PAIR = PHASES // PER
REACH = 3
TAPS_PAD = 64
FIRST_SHIFT = -(-RIM // PHASES)
SHIFTS = 2 * FIRST_SHIFT + 1
BEFORE = FIRST_SHIFT * PHASES - RIM + PER
SLOTS = SHIFTS * PHASES + PER
EDGE = 8
HALO = 2 * RIM
HALO_BLOCKS = 2
SPARE = HALO_BLOCKS * SPAN - HALO


f32 = jnp.float32
bf16 = jnp.bfloat16
highest = lax.Precision.HIGHEST


def round_up(value, unit):
    return -(-value // unit) * unit


def iota2(shape, dim):
    return lax.broadcasted_iota(jnp.int32, shape, dim)


def dot(left, right, precision=None):
    return lax.dot_general(
        left, right, (((1,), (0,)), ((), ())), precision=precision, preferred_element_type=f32
    )


def dot_t(left, right):
    return lax.dot_general(left, right, (((1,), (1,)), ((), ())), preferred_element_type=f32)


def split(value, parts):
    pieces = []
    for _ in range(parts):
        piece = value.astype(bf16)
        pieces.append(piece)
        value = value - piece.astype(f32)
    return pieces


def one_side(value, axis):
    a, b, c = split(value, 3)
    return jnp.concatenate([a, b, c, a, b, a], axis=axis)


def other_side(value, axis):
    a, b, c = split(value, 3)
    return jnp.concatenate([a, a, a, b, b, c], axis=axis)


def roll(value, shift):
    shift %= LANES
    return pltpu.roll(value, shift, 1) if shift else value


def place(shape):
    return iota2(shape, 1) % SPAN


def group(shape):
    return iota2(shape, 1) // SPAN


def bands_kernel(taps_ref, fwd_ref, adj_ref, base_ref, rows_ref):
    lane = iota2((TAPS_PAD, LANES), 1)
    tap = iota2((TAPS_PAD, LANES), 0)
    owned = [(group((SPAN, LANES)) == k).astype(f32).astype(bf16) for k in range(PER)]
    margin = PER - 1
    for which, (out_ref, offset) in enumerate(((fwd_ref, SPARE), (adj_ref, 0))):
        taps = taps_ref[which]
        for k in range(8):
            hot = (((k - offset - lane) & (LANES - 1)) == tap).astype(f32).astype(bf16)
            base_ref[pl.ds(k, TAPS_PAD, stride=8), :] = dot(taps, hot)
        for a in range(margin):
            rows_ref[pl.ds(a * LANES, LANES), :] = jnp.zeros((LANES, LANES), bf16)

        def turn(step, carry):
            base = base_ref[pl.ds(pl.multiple_of(step * 8, 8), 8), :]
            first = pl.multiple_of((step + margin) * LANES, LANES)
            turned = [roll(base, 8 * g) for g in range(LANES // 8)]
            rows_ref[pl.ds(first, LANES), :] = jnp.concatenate(turned, axis=0).astype(bf16)
            return carry

        lax.fori_loop(0, TAPS_PAD, turn, 0, unroll=8)
        for g in range(REACH):
            for a in list(range(BEFORE)) + list(range(BEFORE + TAPS_PAD, SLOTS)):
                out_ref[g, pl.ds(a * SPAN, SPAN), :] = jnp.zeros((SPAN, LANES), bf16)

        def join(step, carry):
            for g in range(REACH):
                value = None
                for k in reversed(range(PER)):
                    first = pl.multiple_of((step + margin - k) * LANES, LANES)
                    part = rows_ref[pl.ds(first + SPAN * ((g + k) % PER), SPAN), :]
                    part = part * owned[k]
                    value = part if value is None else value + part
                slot = pl.multiple_of((step + BEFORE) * SPAN, SPAN)
                out_ref[g, pl.ds(slot, SPAN), :] = value
            return carry

        lax.fori_loop(0, TAPS_PAD, join, 0, unroll=4)


def bands(psf):
    taps = jnp.stack([psf, psf[::-1, ::-1]])
    extra = TAPS_PAD - TAPS
    taps = jnp.pad(taps, ((0, 0), (0, extra), (0, extra)))
    table = jax.ShapeDtypeStruct((REACH, SLOTS * SPAN, LANES), bf16)
    return pl.pallas_call(
        bands_kernel,
        out_shape=[table, table],
        scratch_shapes=[
            pltpu.VMEM((TAPS_PAD * 8, LANES), f32),
            pltpu.VMEM(((TAPS_PAD + PER - 1) * LANES, LANES), bf16),
        ],
        compiler_params=pltpu.CompilerParams(vmem_limit_bytes=10 * 1024 * 1024),
    )(taps)


def correlate(field, blocks, depth, line_ref, band_ref, part_ref, acc_ref):
    height = blocks * depth
    for n in range(PAIR):
        for g in range(REACH):
            wide = jnp.concatenate([field(n, g + b) for b in range(blocks)], axis=0)
            rest = line_ref.shape[0] - height
            if rest:
                wide = jnp.concatenate([wide, jnp.zeros((rest, LANES), f32)], axis=0)
            tile = n * REACH + g
            line_ref[:, tile * LANES:(tile + 1) * LANES] = wide.astype(bf16)
    for m in range(SHIFTS):
        table = jnp.concatenate(
            [
                jnp.concatenate(
                    [
                        band_ref[g, pl.ds((m * PHASES + PER * (1 + source - n)) * SPAN, LANES), :]
                        for source in range(PAIR) for g in range(REACH)
                    ],
                    axis=0,
                )
                for n in range(PAIR)
            ],
            axis=1,
        )
        product = dot(line_ref[...], table)
        for n in range(PAIR):
            part_ref[n, m, pl.ds(EDGE, line_ref.shape[0]), :] = product[:, n * LANES:(n + 1) * LANES]
    for n in range(PAIR):
        for b in range(blocks):
            total = None
            for m in range(SHIFTS):
                first = EDGE + b * depth + m - FIRST_SHIFT
                piece = part_ref[n, m, pl.ds(first, depth), :]
                total = piece if total is None else total + piece
            acc_ref[n, b, pl.ds(0, depth), :] = total


def in_rows(n, depth, ncx):
    shape = (depth, PER * 2 * ncx)
    column = iota2(shape, 1)
    row = iota2(shape, 0) * PHASES + n * PER + column // (2 * ncx)
    cell = column % ncx
    return ((row >= cell * COARSE) & (row < cell * COARSE + COARSE)).astype(f32).astype(bf16)


def in_cells(n, depth, ncx):
    shape = (PER * ncx, depth)
    line = iota2(shape, 0)
    row = iota2(shape, 1) * PHASES + n * PER + line // ncx
    cell = line % ncx
    return ((row >= cell * COARSE) & (row < cell * COARSE + COARSE)).astype(f32).astype(bf16)


def over_rows(strips, ncx, blocks):
    owner = jnp.concatenate([group((ncx, LANES))] * blocks, axis=1)
    pieces = [piece.astype(f32) for piece in split(strips[:ncx], 2)]
    return jnp.concatenate(
        [jnp.where(owner == k, piece, 0.0).astype(bf16) for k in range(PER) for piece in pieces], axis=0
    )


def cell_rows(products, ncx, blocks):
    owner = jnp.concatenate([group((ncx, LANES))] * blocks, axis=1)
    value = products[:ncx]
    for k in range(1, PER):
        value = jnp.where(owner == k, products[k * ncx:(k + 1) * ncx], value)
    return value


def by_columns(first, crow, value, half):
    shape = (8, value.shape[1])
    lane = iota2(shape, 1)
    at = lane // LANES * SPAN + lane % SPAN - first
    owner = iota2(shape, 0)
    hit = (at >= owner * COARSE) & (at < owner * COARSE + COARSE) & (owner < crow)
    picked = hit.astype(f32).astype(bf16)
    rest = half - value.shape[0]
    if rest:
        value = jnp.concatenate([value, jnp.zeros((rest, value.shape[1]), f32)], axis=0)
    return dot_t(
        jnp.concatenate([picked] * 3, axis=1), jnp.concatenate(split(value, 3), axis=1)
    )


def coarse(red_ref, rows_ref, pull_ref, back_ref, half):
    red = red_ref[...].reshape(red_ref.shape[0] * 8, 2 * half)
    mixed = dot_t(rows_ref[...], one_side(red, 1))
    pull = dot(one_side(mixed[:half], 1), pull_ref[...])
    if back_ref is None:
        return pull
    levels = jnp.concatenate([mixed[half:2 * half], mixed[2 * half:]], axis=1)
    return pull, dot(one_side(levels, 1), back_ref[...])


def start_kernel(
    sizes, place_ref, *refs
):
    planes, depth, half, cols, crow, ncx = sizes
    pieces, refs = refs[:-9], refs[-9:]
    own_out, mask_out, a_out, b_out, red_out, rows_out, cells_out, plane_ref, wide_ref = refs
    owner = group((depth, LANES))
    even = place_ref[1] == 0
    for part in range(2):
        for k, piece in enumerate(pieces):
            rows = piece.shape[0]
            first = pl.multiple_of(place_ref[2 + k] * rows, 8)
            wide_ref[part, pl.ds(first, rows), :] = piece[:, part * LANES:(part + 1) * LANES].astype(f32)
        for r in range(PHASES):
            value = wide_ref[part, pl.ds(r, planes, stride=PHASES), :]
            rest = jnp.zeros((depth - planes, LANES), f32)
            plane_ref[part, r] = jnp.concatenate([value, rest], axis=0)

    def tile(part, n, first):
        value = None
        for k in reversed(range(PER)):
            turned = roll(plane_ref[part, n * PER + k], SPAN * k - first)
            value = turned if value is None else jnp.where(owner <= k, turned, value)
        return value

    sums = None
    blocks = own_out.shape[1]
    for n in range(PAIR):
        rows_out[n] = in_rows(n, depth, ncx)
        cells_out[n] = in_cells(n, depth, ncx)
        tiles = []
        for b in range(blocks):
            tiles.append(tile(0, n, SPAN * b))
            own_out[n, b] = tiles[-1]
        for b in range(mask_out.shape[1]):
            mask_out[n, b] = tile(1, n, SPAN * b - RIM).astype(bf16)
        for t in range(HALO_BLOCKS):
            to_right = tile(0, n, cols - (HALO_BLOCKS - t) * SPAN)
            to_left = tile(0, n, SPAN * (blocks - 1 + t) - cols)
            a_out[n, t] = jnp.where(even, to_right, to_left).astype(bf16)
            b_out[n, t] = jnp.where(even, to_left, to_right).astype(bf16)
        to_right = tile(1, n, cols - RIM)
        to_left = tile(1, n, SPAN * (mask_out.shape[1] - 1) - RIM - cols)
        a_out[n, HALO_BLOCKS] = jnp.where(even, to_right, to_left).astype(bf16)
        b_out[n, HALO_BLOCKS] = jnp.where(even, to_left, to_right).astype(bf16)
        part = dot(cells_out[n], jnp.concatenate(tiles, axis=1).astype(bf16))
        sums = part if sums is None else sums + part
    red_out[...] = jnp.zeros_like(red_out)
    red_out[:, :half] = by_columns(0, crow, cell_rows(sums, ncx, blocks), half)


def step_kernel(sizes, first, last, *refs):
    planes, depth, half, cols, crow, ncx = sizes
    place_ref, own_ref, from_a_ref, from_b_ref, red_ref, mask_ref = refs[:6]
    rows_ref, pull_ref, back_ref, inside_ref, in_row_ref, in_cell_ref, fwd_ref, adj_ref = refs[6:14]
    refs = refs[14:]
    if last:
        v_out, resist_out, red_out = refs[:3]
        x_ref, e_ref, line_ref, tile_line_ref, acc_ref, part_ref, row_ref = refs[3:]
    else:
        v_out, a_out, b_out, red_out = refs[:4]
        refs = refs[4:]
        if first:
            mask_out, refs = refs[0], refs[1:]
        x_ref, e_ref, line_ref, tile_line_ref, acc_ref, part_ref = refs
    wide_blocks = x_ref.shape[1]
    blocks = acc_ref.shape[1]
    tile_blocks = own_ref.shape[1]
    at = place((depth, LANES))
    even = place_ref[1] == 0

    def from_left(n, t):
        return jnp.where(even, from_b_ref[n, t].astype(f32), from_a_ref[n, t].astype(f32))

    def from_right(n, t):
        return jnp.where(even, from_a_ref[n, t].astype(f32), from_b_ref[n, t].astype(f32))

    filled = iota2((depth, LANES), 0) < planes

    ends = part_ref.shape[2] - EDGE
    for n in range(PAIR):
        for m in range(SHIFTS):
            part_ref[n, m, pl.ds(0, EDGE), :] = jnp.zeros((EDGE, LANES), f32)
            part_ref[n, m, pl.ds(ends, EDGE), :] = jnp.zeros((EDGE, LANES), f32)
        e_ref[n, blocks] = jnp.zeros(e_ref.shape[2:], f32)
        if last:
            for b in range(blocks):
                e_ref[n, b, pl.ds(0, EDGE), :] = jnp.zeros((EDGE, LANES), f32)
                e_ref[n, b, pl.ds(EDGE + depth, EDGE), :] = jnp.zeros((EDGE, LANES), f32)

    pull, back = coarse(red_ref, rows_ref, pull_ref, back_ref, half)
    pull = over_rows(pull, ncx, wide_blocks)
    back = over_rows(back, ncx, blocks)

    tail = cols - SPAN * (tile_blocks - 1)
    for n in range(PAIR):
        pulled = dot(in_row_ref[n], pull)
        for b in range(wide_blocks):
            if b < HALO_BLOCKS:
                value = from_left(n, b)
            elif b < HALO_BLOCKS + tile_blocks:
                value = own_ref[n, b - HALO_BLOCKS]
                if b == HALO_BLOCKS + tile_blocks - 1:
                    value = jnp.where(at < tail, value, from_right(n, 0))
            else:
                value = from_right(n, 1)
            value = value - pulled[:, b * LANES:(b + 1) * LANES]
            x_ref[n, b, pl.ds(0, depth), :] = value.astype(bf16).astype(f32)

    correlate(
        lambda n, b: x_ref[n, b, pl.ds(0, depth), :],
        blocks, depth, line_ref, fwd_ref, part_ref, acc_ref,
    )
    lead = EDGE if last else 0

    sums = None
    for n in range(PAIR):
        raised = dot(in_row_ref[n], back)
        rounded = []
        for b in range(blocks):
            mask = mask_ref[n, b]
            if first:
                mask = mask.astype(f32)
                if b == 0:
                    mask = jnp.where(at < RIM, from_left(n, HALO_BLOCKS), mask)
                if b == blocks - 1:
                    edge = RIM + cols - SPAN * (blocks - 1)
                    mask = jnp.where(at < edge, mask, from_right(n, HALO_BLOCKS))
                mask_out[n, b] = mask.astype(bf16)
            exposure = acc_ref[n, b, pl.ds(0, depth), :] + raised[:, b * LANES:(b + 1) * LANES]
            resist = 1.0 / (1.0 + jnp.exp(-resist_gain * (exposure - resist_level)))
            error = (resist - mask.astype(f32)) * resist_gain * resist * (1.0 - resist)
            error = jnp.where(filled, error * inside_ref[b:b + 1, :], 0.0).astype(bf16)
            rounded.append(error)
            e_ref[n, b, pl.ds(lead, depth), :] = error.astype(f32)
            if last:
                acc_ref[n, b, pl.ds(0, depth), :] = resist
        part = dot(in_cell_ref[n], jnp.concatenate(rounded, axis=1))
        sums = part if sums is None else sums + part
    red_out[:, half:] = by_columns(RIM, crow, cell_rows(sums, ncx, blocks), half)

    if last:
        part = v_out.shape[0] // PHASES
        height = round_up(part, 8)
        window = round_up(part + 2 * FIRST_SHIFT, 8)
        start = place_ref[0] * part
        lane = iota2((height, LANES), 1)

        def to_rows(tile, origin, count):
            for r in range(PHASES):
                n, k = divmod(r, PER)
                value = None
                for b in reversed(range(count)):
                    turned = roll(tile(n, b), SPAN * (b - k) - origin)
                    if value is None:
                        value = turned
                    else:
                        value = jnp.where(lane < SPAN * (b + 1) - origin, turned, value)
                row_ref[pl.ds(r, part, stride=PHASES), :] = value[:part]

        to_rows(lambda n, b: acc_ref[n, b, pl.ds(start, height), :], RIM, blocks)
        resist_out[...] = row_ref[:, :cols]
        correlate(
            lambda n, b: e_ref[n, b, pl.ds(start + EDGE - FIRST_SHIFT, window), :],
            tile_blocks, window, tile_line_ref, adj_ref, part_ref, acc_ref,
        )
        to_rows(
            lambda n, b: x_ref[n, HALO_BLOCKS + b, pl.ds(start, height), :]
            - step_length * acc_ref[n, b, pl.ds(FIRST_SHIFT, height), :],
            0, tile_blocks,
        )
        v_out[...] = row_ref[:, :cols]
        red_out[:, :half] = jnp.zeros((8, half), f32)
        return

    correlate(
        lambda n, b: e_ref[n, b], tile_blocks, depth, tile_line_ref, adj_ref, part_ref, acc_ref
    )

    cells = None
    for n in range(PAIR):
        fresh = []
        for b in range(tile_blocks):
            value = x_ref[n, HALO_BLOCKS + b, pl.ds(0, depth), :] - step_length * acc_ref[
                n, b, pl.ds(0, depth), :
            ]
            value = jnp.where(filled, value, 0.0)
            fresh.append(value)
            v_out[n, b] = value
        for piece in split(jnp.concatenate(fresh, axis=1), 2):
            part = dot(in_cell_ref[n], piece)
            cells = part if cells is None else cells + part

        def moved(begin):
            b, step = divmod(begin, SPAN)
            low = roll(fresh[b], -step) if 0 <= b < tile_blocks else None
            high = roll(fresh[b + 1], SPAN - step) if step and 0 <= b + 1 < tile_blocks else None
            if low is None or high is None:
                return high if low is None else low
            return jnp.where(at < SPAN - step, low, high)

        for t in range(HALO_BLOCKS):
            to_right = moved(cols - (HALO_BLOCKS - t) * SPAN)
            to_left = moved(SPAN * (tile_blocks - 1 + t) - cols)
            a_out[n, t] = jnp.where(even, to_right, to_left)
            b_out[n, t] = jnp.where(even, to_left, to_right)
    red_out[:, :half] = by_columns(0, crow, cell_rows(cells, ncx, tile_blocks), half)


def end_kernel(sizes, place_ref, v_ref, red_ref, rows_ref, pull_ref, out_ref):
    planes, depth, half, cols, crow, ncx = sizes
    pull = coarse(red_ref, rows_ref, pull_ref, None, half)
    pull = jnp.concatenate(split(pull, 2), axis=0)
    rows = v_ref.shape[0]
    row = iota2((rows, 2 * half), 0) + place_ref[0] * rows
    cell = iota2((rows, 2 * half), 1)
    cell = jnp.where(cell >= half, cell - half, cell)
    table = ((row >= cell * COARSE) & (row < cell * COARSE + COARSE)).astype(f32).astype(bf16)
    pulled = dot(table, pull)
    out_ref[...] = v_ref[...] - pulled[:, :cols]


def gauss(rows_at, cols_at, ok):
    dist = (rows_at - cols_at).astype(f32)
    table = jnp.exp(-dist * dist / (2.0 * SIGMA * SIGMA)) / (math.sqrt(2.0 * math.pi) * SIGMA)
    return jnp.where(ok, table, 0.0)


def cell_of(column):
    cell = (column.astype(f32) * (1.0 / COARSE)).astype(jnp.int32)
    cell = jnp.where(cell * COARSE > column, cell - 1, cell)
    return jnp.where((cell + 1) * COARSE <= column, cell + 1, cell)


def tables_kernel(sizes, ncy, place_ref, rows_out, pull_out, back_out, end_out, inside_out):
    planes, depth, half, cols, crow, ncx = sizes
    first_column = place_ref[0] * cols
    blocks = inside_out.shape[0]
    columns_all = ncy * COARSE

    def of_cells(shape, first):
        cell, other = iota2(shape, 0), iota2(shape, 1) - first
        return gauss(cell, other, (cell < ncx) & (other >= 0) & (other < ncx))

    gxs = of_cells((half, 2 * half), half)
    gxc = of_cells((half, 2 * half), 0)
    twice = dot(of_cells((half, half), 0), gxs, highest)
    rows_out[...] = other_side(jnp.concatenate([gxs, gxc, twice], axis=0), 1)

    def columns(shape, first):
        lane = iota2(shape, 1)
        at = first_column + first + lane // LANES * SPAN + lane % SPAN
        return cell_of(jnp.maximum(at, 0)), (at >= 0) & (at < columns_all)

    def held(shape):
        line = iota2(shape, 0)
        return (line // 8) * crow + line % 8, line % 8 < crow

    lines = pull_out.shape[0] // 6

    def by_column(width, first):
        cell, held_ok = held((lines, width))
        at, ok = columns((lines, width), first)
        return gauss(cell, at, held_ok & ok)

    pull_scale = step_length * back_ratio / (COARSE * COARSE)
    pull_out[...] = other_side(pull_scale * by_column(pull_out.shape[1], -HALO_BLOCKS * SPAN), 0)
    shape = (lines, LANES)
    cell, held_ok = held(shape)
    at = first_column + iota2(shape, 1)
    end = gauss(cell, cell_of(at), held_ok & (iota2(shape, 1) < cols))
    end_out[...] = other_side(pull_scale * end, 0)
    width = back_out.shape[1]
    level = back_ratio / (COARSE * COARSE) * by_column(width, -RIM)
    cell, held_ok = held((lines, ncy))
    near = gauss(cell, iota2((lines, ncy), 1), held_ok)
    at, ok = columns((ncy, width), -RIM)
    again = dot(near, gauss(iota2((ncy, width), 0), at, ok), highest)
    back_out[...] = other_side(
        jnp.concatenate([level, -back_ratio * pull_scale * again], axis=0), 0
    )
    _, ok = columns((1, blocks * LANES), -RIM)
    ok = ok.astype(f32)
    for b in range(blocks):
        inside_out[b:b + 1, :] = ok[:, b * LANES:(b + 1) * LANES]


def per_device(dose, target, psf):
    rows, cols = dose.shape
    stripes = lax.axis_size("stripe")
    scans = lax.axis_size("scan")
    stripe = lax.axis_index("stripe")
    scan = lax.axis_index("scan")
    if stripes & (stripes - 1):
        partners = [[(i, (i + k) % stripes) for i in range(stripes)] for k in range(1, stripes)]
        sources = [(stripe - k) % stripes for k in range(1, stripes)]
    else:
        partners = [[(i, i ^ k) for i in range(stripes)] for k in range(1, stripes)]
        sources = [stripe ^ k for k in range(1, stripes)]
    place = jnp.stack([stripe, scan % 2, stripe, *sources]).astype(jnp.int32)
    planes = rows * stripes // PHASES
    depth = round_up(planes + FIRST_SHIFT, 8)
    ncx = rows * stripes // COARSE
    crow = cols // COARSE
    ncy = crow * scans
    half = round_up(ncx, LANES // 2)
    sizes = (planes, depth, half, cols, crow, ncx)
    tile_blocks = -(-cols // SPAN)
    blocks = -(-(cols + 2 * RIM) // SPAN)
    wide_blocks = blocks + REACH - 1

    swap_a = [(i, i + 1 - 2 * (i % 2)) for i in range(scans) if 0 <= i + 1 - 2 * (i % 2) < scans]
    swap_b = [(i, i - 1 + 2 * (i % 2)) for i in range(scans) if 0 <= i - 1 + 2 * (i % 2) < scans]

    def swap(to_a, to_b):
        return lax.ppermute(to_a, "scan", swap_a), lax.ppermute(to_b, "scan", swap_b)

    def share(red):
        return lax.all_to_all(jnp.broadcast_to(red, (scans,) + red.shape), "scan", 0, 0)

    vmem = pl.BlockSpec(memory_space=pltpu.VMEM)
    smem = pl.BlockSpec(memory_space=pltpu.SMEM)
    def call(kernel, out_shape, args, scratch=()):
        held = sum(math.prod(a.shape) * jnp.dtype(a.dtype).itemsize for a in scratch)
        params = pltpu.CompilerParams(vmem_limit_bytes=held + 4 * 1024 * 1024)
        return pl.pallas_call(
            kernel,
            out_shape=out_shape,
            in_specs=[smem if a.ndim == 1 else vmem for a in args],
            scratch_shapes=list(scratch),
            compiler_params=params,
        )(*args)

    def array(shape, dtype=f32):
        return jax.ShapeDtypeStruct(shape, dtype)

    both = jnp.pad(dose, ((0, 0), (0, 2 * LANES - cols))) + jnp.pad(
        target.astype(bf16), ((0, 0), (LANES, LANES - cols))
    )
    pieces = [both] + [lax.ppermute(both, "stripe", pairs) for pairs in partners]

    lines = 6 * 8 * scans
    rows_table, pull_table, back_table, end_table, inside = call(
        functools.partial(tables_kernel, sizes, ncy),
        [
            array((3 * half, 12 * half), bf16), array((lines, wide_blocks * LANES), bf16),
            array((2 * lines, blocks * LANES), bf16), array((lines, LANES), bf16),
            array((blocks, LANES)),
        ],
        [scan.reshape(1).astype(jnp.int32)],
    )
    fwd, adj = bands(psf)

    few = array((8, 2 * half))
    halo = array((PAIR, HALO_BLOCKS + 1, depth, LANES), bf16)
    mask_tiles = array((PAIR, blocks, depth, LANES), bf16)
    tiles = array((PAIR, tile_blocks, depth, LANES))
    own, mask, to_a, to_b, red, in_row, in_cell = call(
        functools.partial(start_kernel, sizes),
        [
            tiles, mask_tiles, halo, halo, few,
            array((PAIR, depth, PER * 2 * ncx), bf16), array((PAIR, PER * ncx, depth), bf16),
        ],
        [place, *pieces],
        [pltpu.VMEM((2, PHASES, depth, LANES), f32), pltpu.VMEM((2, planes * PHASES, LANES), f32)],
    )
    tables = (rows_table, pull_table, back_table, inside, in_row, in_cell, fwd, adj)
    own, mask, red, end_table, tables = lax.optimization_barrier((own, mask, red, end_table, tables))
    rows_table = tables[0]

    height = round_up(blocks * depth, 16)
    def step_scratch(last):
        return [
            pltpu.VMEM((PAIR, wide_blocks, depth + EDGE, LANES), f32),
            pltpu.VMEM((PAIR, blocks + 1, depth + 2 * EDGE * last, LANES), f32),
        ] + scratch

    window = round_up(rows // PHASES + 2 * FIRST_SHIFT, 8)
    tile_height = round_up(tile_blocks * depth, 16)
    scratch = [
        pltpu.VMEM((height, PAIR * REACH * LANES), bf16),
        pltpu.VMEM((tile_height, PAIR * REACH * LANES), bf16),
        pltpu.VMEM((PAIR, blocks, depth + EDGE, LANES), f32),
        pltpu.VMEM((PAIR, SHIFTS, height + 2 * EDGE, LANES), f32),
    ]
    packed = array((PAIR, HALO_BLOCKS, depth, LANES))
    tile = array((rows, cols))
    for step in range(ITERS):
        first = step == 0
        last = step == ITERS - 1
        from_a, from_b = swap(to_a, to_b)
        args = [place, own, from_a, from_b, share(red), mask]
        args += tables
        kernel = functools.partial(step_kernel, sizes, first, last)
        if last:
            some = step_scratch(True)
            some[3] = pltpu.VMEM((round_up(tile_blocks * window, 16), PAIR * REACH * LANES), bf16)
            some.append(pltpu.VMEM((rows, LANES), f32))
            v, resist, red = call(kernel, [tile, tile, few], args, some)
        elif first:
            own, to_a, to_b, red, mask = call(
                kernel, [tiles, packed, packed, few, mask_tiles], args, step_scratch(False)
            )
        else:
            own, to_a, to_b, red = call(
                kernel, [tiles, packed, packed, few], args, step_scratch(False)
            )

    updated = call(
        functools.partial(end_kernel, sizes),
        tile,
        [place, v, share(red), rows_table, end_table],
    )
    return resist, updated


def solution(mesh):
    in_specs = (P("stripe", "scan"), P("stripe", "scan"), P())
    out_specs = (P("stripe", "scan"), P("stripe", "scan"))
    return jax.shard_map(
        per_device, mesh=mesh, in_specs=in_specs, out_specs=out_specs, check_vma=False
    )
```

time: 113 us -> 100 us (0.88)
  blocking collectives: 62.9 us -> 51.1 us
  starting transfers between devices: 11.5 us -> 7.4 us
  waiting for transfers between devices: 0.02 us -> 3.21 us
  Pallas kernels: 31.3 us -> 34 us
  other arithmetic: 4.16 us -> 2.47 us
    all_gather x1 -> x0, blocking collectives: 11.1 us -> none  [per_device(): both = lax.all_gather(both, 'stripe', axis=0, tiled=True)]
    ppermute x8 -> x11, starting transfers between devices: 11.5 us -> 7.4 us  [the longest x3 4.6 us: per_device(): lax.ppermute(both, 'stripe', pairs)]
    ppermute x8 -> x11, waiting for transfers between devices: 0.02 us -> 3.21 us  [the longest x3 3.19 us: per_device(): lax.ppermute(both, 'stripe', pairs)]
    pallas_call x6 -> x7, Pallas kernels: 26.3 us -> 29 us  [call(): pl.pallas_call(kernel, out_shape=out_shape, in_specs=[smem if a.ndim == 1...]
    unnamed x20 -> x0, other arithmetic: 1.66 us -> none
    concatenate x5 -> x0, other arithmetic: 1.23 us -> none  [the longest x1 0.83 us: per_device(): jnp.concatenate([jnp.pad(dose, fill), jnp.pad(target.astype(bf16), fill)]...]
  transfers between devices with their start and end apart: 8 -> 11, of which waited for: 0 -> 3; matrix products, arithmetic and copies ran while one was open for 3% -> 2% of each run, Pallas kernels for 4% -> 6%
where the time goes in v5:
time: 100 us; the launch traced here: 99.9 us
  blocking collectives  51.1 us (51%)
  Pallas kernels  34 us (34%)
  starting transfers between devices  7.4 us (7%)
  waiting for transfers between devices  3.21 us (3%)
  other arithmetic  2.47 us (2%)
    all_to_all x5, blocking collectives, share(): lax.all_to_all(jnp.broadcast_to(red, (scans,) + red.shape), 'scan', 0, 0)  51.1 us
    pallas_call x7, Pallas kernels, call(): pl.pallas_call(kernel, out_shape=out_shape, in_specs=[smem if a.ndim == 1...  29 us
    pallas_call x1, Pallas kernels, bands(): pl.pallas_call(bands_kernel, out_shape=[table, table], scratch_shapes=[pl...  4.96 us
    ppermute x3, starting transfers between devices, per_device(): lax.ppermute(both, 'stripe', pairs)  4.6 us
    ppermute x3, waiting for transfers between devices, per_device(): lax.ppermute(both, 'stripe', pairs)  3.19 us
    ppermute x4, starting transfers between devices, swap(): lax.ppermute(to_b, 'scan', swap_b)  2.76 us
  transfers between devices with their start and end apart: 11, of which 3 were waited for; matrix products, arithmetic and copies ran while one was open for 2% of the time, Pallas kernels for 6%

profile of v5, /device:TPU:0, one launch (start us, length us, event | category | flops | bytes accessed | tf_op | source)
XLA Modules:
  0.0 99.9 jit_solution(5858967293601372020)
XLA Ops:
  0.6 0.9 convert_element_type.9
  1.5 0.8 pad_add_fusion.refs_0_
  2.4 4.0 %collective-permute-start.2 = (bf16[200,256]{1,0:T(8,128)(2,1)S(1)}, bf16[200,256]{1,0:T(8,128)(2,1)S(1)}, u32[]{:S(2)}, u32[]{:S(2)}) collective-permute-start(bf16[200,256]{1,0:T(8,128)(2,1)S(1)} %pad_add_fusion.refs_0_), channel_id=1, source_target_pairs={{0,24},{8,16},{16,8},{24,0},{1,25},{9,17},{17,9},{25,1},{2,26},{10... | collective-permute-start | bytes 307208 | tf_op jit(solution)/shard_map/ppermute | solution.py:583
  6.3 0.5 collective-permute-start.1
  6.8 0.1 collective-permute-start
  7.0 0.8 rev.3
  7.8 0.6 shard_map.51
  8.4 0.1 stack.33.place_ref.refs_0_
  8.5 1.1 %collective-permute-done.2.refs_3_ = bf16[200,256]{1,0:T(8,128)(2,1)S(1)} collective-permute-done((bf16[200,256]{1,0:T(8,128)(2,1)S(1)}, bf16[200,256]{1,0:T(8,128)(2,1)S(1)}, u32[]{:S(2)}, u32[]{:S(2)}) %collective-permute-start.2) | collective-permute-done | bytes 102432 | tf_op jit(solution)/shard_map/ppermute | solution.py:583
  9.6 1.8 %collective-permute-done.1.refs_2_ = bf16[200,256]{1,0:T(8,128)(2,1)S(1)} collective-permute-done((bf16[200,256]{1,0:T(8,128)(2,1)S(1)}, bf16[200,256]{1,0:T(8,128)(2,1)S(1)}, u32[]{:S(2)}, u32[]{:S(2)}) %collective-permute-start.1) | collective-permute-done | bytes 102432 | tf_op jit(solution)/shard_map/ppermute | solution.py:583
  11.4 0.3 collective-permute-done.refs_1_
  11.7 1.7 %shard_map.50 = (f32[2,4,104,128]{3,2,1,0:T(8,128)S(1)}, bf16[2,5,104,128]{3,2,1,0:T(8,128)(2,1)S(1)}, bf16[2,3,104,128]{3,2,1,0:T(8,128)(2,1)S(1)}, bf16[2,3,10...) custom-call(s32[6]{0:T(128)S(1)} %stack.33.place_ref.refs_0_, ...), custom_call_target="tpu_custom_call" | custom-call | tf_op jit(solution)/shard_map/pallas_call | solution.py:569
  13.4 0.0 collective-permute-start.3
  13.5 0.7 collective-permute-start.4
  14.1 0.7 fusion.5.taps_ref
  14.9 5.0 %shard_map.52 = (bf16[3,2432,128]{2,1,0:T(8,128)(2,1)S(1)}, bf16[3,2432,128]{2,1,0:T(8,128)(2,1)S(1)}) custom-call(bf16[2,64,64]{2,1,0:T(8,128)(2,1)S(1)} %fusion.5.taps_ref), custom_call_target="tpu_custom_call" | custom-call | tf_op jit(solution)/shard_map/pallas_call | solution.py:139
  19.9 12.2 %all_to_all.25.refs_4_ = f32[8,8,128]{2,1,0:T(8,128)S(1)} all-to-all(f32[8,8,128]{2,1,0:T(8,128)S(1)} %broadcast_in_dim.15), channel_id=1, replica_groups=mesh['stripe'=4,'scan'=8] {'scan'}, dimensions={0} | all-to-all | bytes 65536 | tf_op jit(solution)/shard_map/all_to_all | solution.py:562
  32.1 6.4 %shard_map.53 = (f32[2,4,104,128]{3,2,1,0:T(8,128)S(1)}, f32[2,2,104,128]{3,2,1,0:T(8,128)S(1)}, f32[2,2,104,128]{3,2,1,0:T(8,128)S(1)}, f32[8,128]{1,0:T(8,128)S(1)}, bf16[2,5,104,128]{3,2,1,0:T(8,128)(2,1)S(1)}) custom-call(s32[6]{0:T(128)S(1)} %stack.33.place_ref.refs_0_, f32[2,4,104,128]{3,2,1,0:T(8,128)S(1)} %get-tuple-element.56.refs_1_, ...), custom_call_target="tpu_custom_call" | custom-call | tf_op jit(solution)/shard_map/pallas_call | solution.py:569
  38.5 0.7 collective-permute-start.6
  39.2 10.3 %all_to_all.26.refs_4_ = f32[8,8,128]{2,1,0:T(8,128)S(1)} all-to-all(f32[8,8,128]{2,1,0:T(8,128)S(1)} %broadcast_in_dim.16), channel_id=1, replica_groups=mesh['stripe'=4,'scan'=8] {'scan'}, dimensions={0} | all-to-all | bytes 65536 | tf_op jit(solution)/shard_map/all_to_all | solution.py:562
  49.5 0.0 collective-permute-done.5.refs_2_
  49.5 0.0 collective-permute-done.6.refs_3_
  49.5 6.4 %shard_map.54 = (f32[2,4,104,128]{3,2,1,0:T(8,128)S(1)}, f32[2,2,104,128]{3,2,1,0:T(8,128)S(1)}, f32[2,2,104,128]{3,2,1,0:T(8,128)S(1)}, f32[8,128]{1,0:T(8,128)S(1)}) custom-call(s32[6]{0:T(128)S(1)} %stack.33.place_ref.refs_0_, f32[2,4,104,128]{3,2,1,0:T(8,128)S(1)} %get-tuple-element.69.refs_1_, f32[2,2,104,128]{3,2,1,0:T(8,128)S(1)} %collective-permute-done.5.refs_2_, ...), custom_call_target="tpu_custom_call" | custom-call | tf_op jit(solution)/shard_map/pallas_call | solution.py:569
  55.9 0.0 collective-permute-start.7
  55.9 0.7 collective-permute-start.8
  56.6 10.3 %all_to_all.27.refs_4_ = f32[8,8,128]{2,1,0:T(8,128)S(1)} all-to-all(f32[8,8,128]{2,1,0:T(8,128)S(1)} %broadcast_in_dim.17), channel_id=1, replica_groups=mesh['stripe'=4,'scan'=8] {'scan'}, dimensions={0} | all-to-all | bytes 65536 | tf_op jit(solution)/shard_map/all_to_all | solution.py:562
  66.9 6.4 %shard_map.55 = (f32[2,4,104,128]{3,2,1,0:T(8,128)S(1)}, f32[2,2,104,128]{3,2,1,0:T(8,128)S(1)}, f32[2,2,104,128]{3,2,1,0:T(8,128)S(1)}, f32[8,128]{1,0:T(8,128)S(1)}) custom-call(s32[6]{0:T(128)S(1)} %stack.33.place_ref.refs_0_, f32[2,4,104,128]{3,2,1,0:T(8,128)S(1)} %get-tuple-element.74.refs_1_, f32[2,2,104,128]{3,2,1,0:T(8,128)S(1)} %collective-permute-done.7.refs_2_, ...), custom_call_target="tpu_custom_call" | custom-call | tf_op jit(solution)/shard_map/pallas_call | solution.py:569
  73.3 0.7 collective-permute-start.10
  74.0 10.3 %all_to_all.28.refs_4_ = f32[8,8,128]{2,1,0:T(8,128)S(1)} all-to-all(f32[8,8,128]{2,1,0:T(8,128)S(1)} %broadcast_in_dim.18), channel_id=1, replica_groups=mesh['stripe'=4,'scan'=8] {'scan'}, dimensions={0} | all-to-all | bytes 65536 | tf_op jit(solution)/shard_map/all_to_all | solution.py:562
  84.3 5.7 %shard_map.56 = (f32[200,100]{1,0:T(8,128)S(1)}, f32[200,100]{1,0:T(8,128)}, f32[8,128]{1,0:T(8,128)S(1)}) custom-call(s32[6]{0:T(128)S(1)} %stack.33.place_ref.refs_0_, f32[2,4,104,128]{3,2,1,0:T(8,128)S(1)} %get-tuple-element.78.refs_1_, f32[2,2,104,128]{3,2,1,0:T(8,128)S(1)} %collective-permute-done.9.refs_2_, ...), custom_call_target="tpu_custom_call" | custom-call | tf_op jit(solution)/shard_map/pallas_call | solution.py:569
  90.0 8.1 %all_to_all.29.red_ref = f32[8,8,128]{2,1,0:T(8,128)S(1)} all-to-all(f32[8,8,128]{2,1,0:T(8,128)S(1)} %broadcast_in_dim.19), channel_id=1, replica_groups=mesh['stripe'=4,'scan'=8] {'scan'}, dimensions={0} | all-to-all | bytes 65536 | tf_op jit(solution)/shard_map/all_to_all | solution.py:562
  98.1 1.8 %shard_map.57 = f32[200,100]{1,0:T(8,128)} custom-call(s32[6]{0:T(128)S(1)} %stack.33.place_ref.refs_0_, f32[200,100]{1,0:T(8,128)S(1)} %get-tuple-element.83.v_ref, f32[8,8,128]{2,1,0:T(8,128)S(1)} %all_to_all.29.red_ref, bf16[192,768]{1,0:T(8,128)(2,1)S(1)} %get-tuple-element.61.refs_6_.rows_ref, bf16[384,128]{1,0:T(8,128)(2,1)S(1)} %get-tuple-element.85.pull_ref), custom_call_target="tpu_custom_call" | custom-call | tf_op jit(solution)/shard_map/pallas_call | solution.py:569
  (13 shorter events, 0.0 us)
Async XLA Ops:
  2.4 7.2 %collective-permute-start.2 = (bf16[200,256]{1,0:T(8,128)(2,1)S(1)}, bf16[200,256]{1,0:T(8,128)(2,1)S(1)}, u32[]{:S(2)}, u32[]{:S(2)}) collective-permute-start(bf16[200,256]{1,0:T(8,128)(2,1)S(1)} %pad_add_fusion.refs_0_), channel_id=1, source_target_pairs={{0,24},{8,16},{16,8},{24,0},{1,25},{9,17},{17,9},{25,1},{2,26},{10... | collective-permute-start | bytes 307208 | tf_op jit(solution)/shard_map/ppermute | solution.py:583
  6.3 5.1 %collective-permute-start.1 = (bf16[200,256]{1,0:T(8,128)(2,1)S(1)}, bf16[200,256]{1,0:T(8,128)(2,1)S(1)}, u32[]{:S(2)}, u32[]{:S(2)}) collective-permute-start(bf16[200,256]{1,0:T(8,128)(2,1)S(1)} %pad_add_fusion.refs_0_), channel_id=1, source_target_pairs={{0,16},{8,24},{16,0},{24,8},{1,17},{9,25},{17,1},{25,9},{2,18},{10... | collective-permute-start | bytes 307208 | tf_op jit(solution)/shard_map/ppermute | solution.py:583
  6.8 4.9 %collective-permute-start = (bf16[200,256]{1,0:T(8,128)(2,1)S(1)}, bf16[200,256]{1,0:T(8,128)(2,1)S(1)}, u32[]{:S(2)}, u32[]{:S(2)}) collective-permute-start(bf16[200,256]{1,0:T(8,128)(2,1)S(1)} %pad_add_fusion.refs_0_), channel_id=1, source_target_pairs={{0,8},{8,0},{16,24},{24,16},{1,9},{9,1},{17,25},{25,17},{2,10},{10... | collective-permute-start | bytes 307208 | tf_op jit(solution)/shard_map/ppermute | solution.py:583
  13.4 18.6 %collective-permute-start.3 = (bf16[2,3,104,128]{3,2,1,0:T(8,128)(2,1)S(1)}, bf16[2,3,104,128]{3,2,1,0:T(8,128)(2,1)S(1)}, u32[]{:S(2)}, u32[]{:S(2)}) collective-permute-start(bf16[2,3,104,128]{3,2,1,0:T(8,128)(2,1)S(1)} %get-tuple-element.57), channel_id=1, source_target_pairs={{0,1},{1,0},{2,3},{3,2},{4,5},{5,4},{6,7},{7,6},{8,9},{9,8},{10,11... | collective-permute-start | bytes 479240 | tf_op jit(solution)/shard_map/ppermute | solution.py:559
  13.5 18.6 %collective-permute-start.4 = (bf16[2,3,104,128]{3,2,1,0:T(8,128)(2,1)S(1)}, bf16[2,3,104,128]{3,2,1,0:T(8,128)(2,1)S(1)}, u32[]{:S(2)}, u32[]{:S(2)}) collective-permute-start(bf16[2,3,104,128]{3,2,1,0:T(8,128)(2,1)S(1)} %get-tuple-element.58), channel_id=1, source_target_pairs={{1,2},{2,1},{3,4},{4,3},{5,6},{6,5},{9,10},{10,9},{11,12},{12,11},... | collective-permute-start | bytes 479240 | tf_op jit(solution)/shard_map/ppermute | solution.py:559
  38.5 11.0 %collective-permute-start.5 = (f32[2,2,104,128]{3,2,1,0:T(8,128)S(1)}, f32[2,2,104,128]{3,2,1,0:T(8,128)S(1)}, u32[]{:S(2)}, u32[]{:S(2)}) collective-permute-start(f32[2,2,104,128]{3,2,1,0:T(8,128)S(1)} %get-tuple-element.70), channel_id=1, source_target_pairs={{0,1},{1,0},{2,3},{3,2},{4,5},{5,4},{6,7},{7,6},{8,9},{9,8},{10,11... | collective-permute-start | bytes 638984 | tf_op jit(solution)/shard_map/ppermute | solution.py:559
  38.5 11.0 %collective-permute-start.6 = (f32[2,2,104,128]{3,2,1,0:T(8,128)S(1)}, f32[2,2,104,128]{3,2,1,0:T(8,128)S(1)}, u32[]{:S(2)}, u32[]{:S(2)}) collective-permute-start(f32[2,2,104,128]{3,2,1,0:T(8,128)S(1)} %get-tuple-element.71), channel_id=1, source_target_pairs={{1,2},{2,1},{3,4},{4,3},{5,6},{6,5},{9,10},{10,9},{11,12},{12,11},... | collective-permute-start | bytes 638984 | tf_op jit(solution)/shard_map/ppermute | solution.py:559
  55.9 11.0 %collective-permute-start.7 = (f32[2,2,104,128]{3,2,1,0:T(8,128)S(1)}, f32[2,2,104,128]{3,2,1,0:T(8,128)S(1)}, u32[]{:S(2)}, u32[]{:S(2)}) collective-permute-start(f32[2,2,104,128]{3,2,1,0:T(8,128)S(1)} %get-tuple-element.75), channel_id=1, source_target_pairs={{0,1},{1,0},{2,3},{3,2},{4,5},{5,4},{6,7},{7,6},{8,9},{9,8},{10,11... | collective-permute-start | bytes 638984 | tf_op jit(solution)/shard_map/ppermute | solution.py:559
  55.9 11.0 %collective-permute-start.8 = (f32[2,2,104,128]{3,2,1,0:T(8,128)S(1)}, f32[2,2,104,128]{3,2,1,0:T(8,128)S(1)}, u32[]{:S(2)}, u32[]{:S(2)}) collective-permute-start(f32[2,2,104,128]{3,2,1,0:T(8,128)S(1)} %get-tuple-element.76), channel_id=1, source_target_pairs={{1,2},{2,1},{3,4},{4,3},{5,6},{6,5},{9,10},{10,9},{11,12},{12,11},... | collective-permute-start | bytes 638984 | tf_op jit(solution)/shard_map/ppermute | solution.py:559
  73.3 11.0 %collective-permute-start.9 = (f32[2,2,104,128]{3,2,1,0:T(8,128)S(1)}, f32[2,2,104,128]{3,2,1,0:T(8,128)S(1)}, u32[]{:S(2)}, u32[]{:S(2)}) collective-permute-start(f32[2,2,104,128]{3,2,1,0:T(8,128)S(1)} %get-tuple-element.79), channel_id=1, source_target_pairs={{0,1},{1,0},{2,3},{3,2},{4,5},{5,4},{6,7},{7,6},{8,9},{9,8},{10,11... | collective-permute-start | bytes 638984 | tf_op jit(solution)/shard_map/ppermute | solution.py:559
  73.3 11.0 %collective-permute-start.10 = (f32[2,2,104,128]{3,2,1,0:T(8,128)S(1)}, f32[2,2,104,128]{3,2,1,0:T(8,128)S(1)}, u32[]{:S(2)}, u32[]{:S(2)}) collective-permute-start(f32[2,2,104,128]{3,2,1,0:T(8,128)S(1)} %get-tuple-element.80), channel_id=1, source_target_pairs={{1,2},{2,1},{3,4},{4,3},{5,6},{6,5},{9,10},{10,9},{11,12},{12,11},... | collective-permute-start | bytes 638984 | tf_op jit(solution)/shard_map/ppermute | solution.py:559

commit v6 on v5

--- a/solution.py
+++ b/solution.py
@@ -91,60 +91,63 @@
     return iota2(shape, 1) // SPAN
 
 
-def bands_kernel(taps_ref, fwd_ref, adj_ref, base_ref, rows_ref):
+def bands_kernel(offset, flip, psf_ref, out_ref, taps_ref, base_ref, rows_ref):
     lane = iota2((TAPS_PAD, LANES), 1)
     tap = iota2((TAPS_PAD, LANES), 0)
     owned = [(group((SPAN, LANES)) == k).astype(f32).astype(bf16) for k in range(PER)]
     margin = PER - 1
-    for which, (out_ref, offset) in enumerate(((fwd_ref, SPARE), (adj_ref, 0))):
-        taps = taps_ref[which]
-        for k in range(8):
-            hot = (((k - offset - lane) & (LANES - 1)) == tap).astype(f32).astype(bf16)
-            base_ref[pl.ds(k, TAPS_PAD, stride=8), :] = dot(taps, hot)
-        for a in range(margin):
-            rows_ref[pl.ds(a * LANES, LANES), :] = jnp.zeros((LANES, LANES), bf16)
-
-        def turn(step, carry):
-            base = base_ref[pl.ds(pl.multiple_of(step * 8, 8), 8), :]
-            first = pl.multiple_of((step + margin) * LANES, LANES)
-            turned = [roll(base, 8 * g) for g in range(LANES // 8)]
-            rows_ref[pl.ds(first, LANES), :] = jnp.concatenate(turned, axis=0).astype(bf16)
-            return carry
-
-        lax.fori_loop(0, TAPS_PAD, turn, 0, unroll=8)
+    taps_ref[...] = jnp.zeros_like(taps_ref)
+    taps_ref[:TAPS, :TAPS] = psf_ref[...].astype(f32)
+    taps = taps_ref[:, :TAPS_PAD].astype(bf16)
+    if flip:
+        tap = TAPS - 1 - tap
+        shape = (TAPS_PAD, TAPS_PAD)
+        turned = (iota2(shape, 0) + iota2(shape, 1) == TAPS - 1).astype(f32).astype(bf16)
+        taps = dot(turned, taps).astype(bf16)
+    for k in range(8):
+        hot = (((k - offset - lane) & (LANES - 1)) == tap).astype(f32).astype(bf16)
+        base_ref[pl.ds(k, TAPS_PAD, stride=8), :] = dot(taps, hot)
+    for a in range(margin):
+        rows_ref[pl.ds(a * LANES, LANES), :] = jnp.zeros((LANES, LANES), bf16)
+
+    def turn(step, carry):
+        base = base_ref[pl.ds(pl.multiple_of(step * 8, 8), 8), :]
+        first = pl.multiple_of((step + margin) * LANES, LANES)
+        turned = [roll(base, 8 * g) for g in range(LANES // 8)]
+        rows_ref[pl.ds(first, LANES), :] = jnp.concatenate(turned, axis=0).astype(bf16)
+        return carry
+
+    lax.fori_loop(0, TAPS_PAD, turn, 0, unroll=8)
+    for g in range(REACH):
+        for a in list(range(BEFORE)) + list(range(BEFORE + TAPS_PAD, SLOTS)):
+            out_ref[g, pl.ds(a * SPAN, SPAN), :] = jnp.zeros((SPAN, LANES), bf16)
+
+    def join(step, carry):
         for g in range(REACH):
-            for a in list(range(BEFORE)) + list(range(BEFORE + TAPS_PAD, SLOTS)):
-                out_ref[g, pl.ds(a * SPAN, SPAN), :] = jnp.zeros((SPAN, LANES), bf16)
-
-        def join(step, carry):
-            for g in range(REACH):
-                value = None
-                for k in reversed(range(PER)):
-                    first = pl.multiple_of((step + margin - k) * LANES, LANES)
-                    part = rows_ref[pl.ds(first + SPAN * ((g + k) % PER), SPAN), :]
-                    part = part * owned[k]
-                    value = part if value is None else value + part
-                slot = pl.multiple_of((step + BEFORE) * SPAN, SPAN)
-                out_ref[g, pl.ds(slot, SPAN), :] = value
-            return carry
-
-        lax.fori_loop(0, TAPS_PAD, join, 0, unroll=4)
-
-
-def bands(psf):
-    taps = jnp.stack([psf, psf[::-1, ::-1]])
-    extra = TAPS_PAD - TAPS
-    taps = jnp.pad(taps, ((0, 0), (0, extra), (0, extra)))
-    table = jax.ShapeDtypeStruct((REACH, SLOTS * SPAN, LANES), bf16)
+            value = None
+            for k in reversed(range(PER)):
+                first = pl.multiple_of((step + margin - k) * LANES, LANES)
+                part = rows_ref[pl.ds(first + SPAN * ((g + k) % PER), SPAN), :]
+                part = part * owned[k]
+                value = part if value is None else value + part
+            slot = pl.multiple_of((step + BEFORE) * SPAN, SPAN)
+            out_ref[g, pl.ds(slot, SPAN), :] = value
+        return carry
+
+    lax.fori_loop(0, TAPS_PAD, join, 0, unroll=4)
+
+
+def bands(psf, offset, flip):
     return pl.pallas_call(
-        bands_kernel,
-        out_shape=[table, table],
+        functools.partial(bands_kernel, offset, flip),
+        out_shape=jax.ShapeDtypeStruct((REACH, SLOTS * SPAN, LANES), bf16),
         scratch_shapes=[
+            pltpu.VMEM((TAPS_PAD, LANES), f32),
             pltpu.VMEM((TAPS_PAD * 8, LANES), f32),
             pltpu.VMEM(((TAPS_PAD + PER - 1) * LANES, LANES), bf16),
         ],
         compiler_params=pltpu.CompilerParams(vmem_limit_bytes=10 * 1024 * 1024),
-    )(taps)
+    )(psf)
 
 
 def correlate(field, blocks, depth, line_ref, band_ref, part_ref, acc_ref):
@@ -231,8 +234,8 @@
     )
 
 
-def coarse(red_ref, rows_ref, pull_ref, back_ref, half):
-    red = red_ref[...].reshape(red_ref.shape[0] * 8, 2 * half)
+def coarse(red_refs, rows_ref, pull_ref, back_ref, half):
+    red = jnp.concatenate([ref[...].reshape(-1, 2 * half) for ref in red_refs], axis=0)
     mixed = dot_t(rows_ref[...], one_side(red, 1))
     pull = dot(one_side(mixed[:half], 1), pull_ref[...])
     if back_ref is None:
@@ -245,7 +248,7 @@
     sizes, place_ref, *refs
 ):
     planes, depth, half, cols, crow, ncx = sizes
-    pieces, refs = refs[:-9], refs[-9:]
+    pieces, refs = refs[1:-9], refs[-9:]
     own_out, mask_out, a_out, b_out, red_out, rows_out, cells_out, plane_ref, wide_ref = refs
     owner = group((depth, LANES))
     even = place_ref[1] == 0
@@ -292,11 +295,11 @@
     red_out[:, :half] = by_columns(0, crow, cell_rows(sums, ncx, blocks), half)
 
 
-def step_kernel(sizes, first, last, *refs):
+def step_kernel(sizes, count, first, last, *refs):
     planes, depth, half, cols, crow, ncx = sizes
-    place_ref, own_ref, from_a_ref, from_b_ref, red_ref, mask_ref = refs[:6]
-    rows_ref, pull_ref, back_ref, inside_ref, in_row_ref, in_cell_ref, fwd_ref, adj_ref = refs[6:14]
-    refs = refs[14:]
+    place_ref, own_ref, from_a_ref, from_b_ref, mask_ref = refs[:5]
+    rows_ref, pull_ref, back_ref, inside_ref, in_row_ref, in_cell_ref, fwd_ref, adj_ref = refs[5:13]
+    red_refs, refs = refs[13:13 + count], refs[13 + count:]
     if last:
         v_out, resist_out, red_out = refs[:3]
         x_ref, e_ref, line_ref, tile_line_ref, acc_ref, part_ref, row_ref = refs[3:]
@@ -331,7 +334,7 @@
                 e_ref[n, b, pl.ds(0, EDGE), :] = jnp.zeros((EDGE, LANES), f32)
                 e_ref[n, b, pl.ds(EDGE + depth, EDGE), :] = jnp.zeros((EDGE, LANES), f32)
 
-    pull, back = coarse(red_ref, rows_ref, pull_ref, back_ref, half)
+    pull, back = coarse(red_refs, rows_ref, pull_ref, back_ref, half)
     pull = over_rows(pull, ncx, wide_blocks)
     back = over_rows(back, ncx, blocks)
 
@@ -450,9 +453,10 @@
     red_out[:, :half] = by_columns(0, crow, cell_rows(cells, ncx, tile_blocks), half)
 
 
-def end_kernel(sizes, place_ref, v_ref, red_ref, rows_ref, pull_ref, out_ref):
+def end_kernel(sizes, place_ref, v_ref, rows_ref, pull_ref, *refs):
+    red_refs, out_ref = refs[:-1], refs[-1]
     planes, depth, half, cols, crow, ncx = sizes
-    pull = coarse(red_ref, rows_ref, pull_ref, None, half)
+    pull = coarse(red_refs, rows_ref, pull_ref, None, half)
     pull = jnp.concatenate(split(pull, 2), axis=0)
     rows = v_ref.shape[0]
     row = iota2((rows, 2 * half), 0) + place_ref[0] * rows
@@ -497,7 +501,7 @@
 
     def held(shape):
         line = iota2(shape, 0)
-        return (line // 8) * crow + line % 8, line % 8 < crow
+        return ((line // 8) ^ place_ref[1]) * crow + line % 8, line % 8 < crow
 
     lines = pull_out.shape[0] // 6
 
@@ -558,8 +562,13 @@
     def swap(to_a, to_b):
         return lax.ppermute(to_a, "scan", swap_a), lax.ppermute(to_b, "scan", swap_b)
 
+    swapped = scans <= 8 and not scans & (scans - 1)
+
     def share(red):
-        return lax.all_to_all(jnp.broadcast_to(red, (scans,) + red.shape), "scan", 0, 0)
+        if not swapped:
+            return [lax.all_to_all(jnp.broadcast_to(red, (scans,) + red.shape), "scan", 0, 0)]
+        pairs = [[(i, i ^ k) for i in range(scans)] for k in range(1, scans)]
+        return [red] + [lax.ppermute(red, "scan", pair) for pair in pairs]
 
     vmem = pl.BlockSpec(memory_space=pltpu.VMEM)
     smem = pl.BlockSpec(memory_space=pltpu.SMEM)
@@ -590,9 +599,9 @@
             array((2 * lines, blocks * LANES), bf16), array((lines, LANES), bf16),
             array((blocks, LANES)),
         ],
-        [scan.reshape(1).astype(jnp.int32)],
-    )
-    fwd, adj = bands(psf)
+        [jnp.stack([scan, scan if swapped else jnp.zeros_like(scan)]).astype(jnp.int32)],
+    )
+    fwd = bands(psf, SPARE, False)
 
     few = array((8, 2 * half))
     halo = array((PAIR, HALO_BLOCKS + 1, depth, LANES), bf16)
@@ -604,12 +613,11 @@
             tiles, mask_tiles, halo, halo, few,
             array((PAIR, depth, PER * 2 * ncx), bf16), array((PAIR, PER * ncx, depth), bf16),
         ],
-        [place, *pieces],
+        [place, fwd, *pieces],
         [pltpu.VMEM((2, PHASES, depth, LANES), f32), pltpu.VMEM((2, planes * PHASES, LANES), f32)],
     )
-    tables = (rows_table, pull_table, back_table, inside, in_row, in_cell, fwd, adj)
-    own, mask, red, end_table, tables = lax.optimization_barrier((own, mask, red, end_table, tables))
-    rows_table = tables[0]
+    adj = bands(psf, 0, True)
+    tables = [rows_table, pull_table, back_table, inside, in_row, in_cell, fwd, adj]
 
     height = round_up(blocks * depth, 16)
     def step_scratch(last):
@@ -632,9 +640,9 @@
         first = step == 0
         last = step == ITERS - 1
         from_a, from_b = swap(to_a, to_b)
-        args = [place, own, from_a, from_b, share(red), mask]
-        args += tables
-        kernel = functools.partial(step_kernel, sizes, first, last)
+        shared = share(red)
+        args = [place, own, from_a, from_b, mask, *tables, *shared]
+        kernel = functools.partial(step_kernel, sizes, len(shared), first, last)
         if last:
             some = step_scratch(True)
             some[3] = pltpu.VMEM((round_up(tile_blocks * window, 16), PAIR * REACH * LANES), bf16)
@@ -652,7 +660,7 @@
     updated = call(
         functools.partial(end_kernel, sizes),
         tile,
-        [place, v, share(red), rows_table, end_table],
+        [place, v, rows_table, end_table, *share(red)],
     )
     return resist, updated
 

time: 100 us -> 110 us (1.10)
  blocking collectives: 51.1 us -> 0 us
  starting transfers between devices: 7.4 us -> 51.9 us
  waiting for transfers between devices: 3.21 us -> 19.6 us
    all_to_all x5 -> x0, blocking collectives: 51.1 us -> none  [share(): lax.all_to_all(jnp.broadcast_to(red, (scans,) + red.shape), 'scan', 0, 0)]
    ppermute x0 -> x35, starting transfers between devices: none -> 43.9 us  [share(): return [red] + [lax.ppermute(red, 'scan', pair) for pair in pairs]]
    ppermute x0 -> x35, waiting for transfers between devices: none -> 18.1 us  [share(): return [red] + [lax.ppermute(red, 'scan', pair) for pair in pairs]]
    ppermute x3, waiting for transfers between devices: 3.19 us -> 1.43 us  [per_device(): lax.ppermute(both, 'stripe', pairs)]
    pallas_call x1 -> x2, Pallas kernels: 4.96 us -> 5.04 us  [bands(): pl.pallas_call(functools.partial(bands_kernel, offset, flip), out_shape=j...]
  transfers between devices with their start and end apart: 11 -> 46, of which waited for: 3 -> 18; matrix products, arithmetic and copies ran while one was open for 2% -> 0% of each run, Pallas kernels for 6% -> 6%
where the time goes in v6:
time: 110 us
  starting transfers between devices  51.9 us (47%)
  Pallas kernels  34.7 us (32%)
  waiting for transfers between devices  19.6 us (18%)
  other arithmetic  1.8 us (2%)
    ppermute x35, starting transfers between devices, share(): return [red] + [lax.ppermute(red, 'scan', pair) for pair in pairs]  43.9 us
    pallas_call x7, Pallas kernels, call(): pl.pallas_call(kernel, out_shape=out_shape, in_specs=[smem if a.ndim == 1...  29.6 us
    ppermute x35, waiting for transfers between devices, share(): return [red] + [lax.ppermute(red, 'scan', pair) for pair in pairs]  18.1 us
    pallas_call x2, Pallas kernels, bands(): pl.pallas_call(functools.partial(bands_kernel, offset, flip), out_shape=j...  5.04 us
    ppermute x3, starting transfers between devices, per_device(): lax.ppermute(both, 'stripe', pairs)  4.6 us
    ppermute x4, starting transfers between devices, swap(): lax.ppermute(to_b, 'scan', swap_b)  3.13 us
  transfers between devices with their start and end apart: 46, of which 18 were waited for; matrix products, arithmetic and copies ran while one was open for 0% of the time, Pallas kernels for 6%

profile of v6, /device:TPU:0, one launch (start us, length us, event | category | flops | bytes accessed | tf_op | source)
XLA Modules:
  0.0 109.5 jit_solution(4300069615918725584)
XLA Ops:
  2.4 4.0 %collective-permute-start.2 = (bf16[200,256]{1,0:T(8,128)(2,1)S(1)}, bf16[200,256]{1,0:T(8,128)(2,1)S(1)}, u32[]{:S(2)}, u32[]{:S(2)}) collective-permute-start(bf16[200,256]{1,0:T(8,128)(2,1)S(1)} %pad_add_fusion.refs_1_), channel_id=1, source_target_pairs={{0,24},{8,16},{16,8},{24,0},{1,25},{9,17},{17,9},{25,1},{2,26},{10... | collective-permute-start | bytes 307208 | tf_op jit(solution)/shard_map/ppermute | solution.py:592
  7.7 2.5 %shard_map.50.refs_0_.refs_11_ = bf16[3,2432,128]{2,1,0:T(8,128)(2,1)S(1)} custom-call(bf16[61,61]{1,0:T(8,128)(2,1)S(1)} %copy-done), custom_call_target="tpu_custom_call" | custom-call | tf_op jit(solution)/shard_map/pallas_call | solution.py:141
  11.7 1.7 %shard_map.51 = (f32[2,4,104,128]{3,2,1,0:T(8,128)S(1)}, bf16[2,5,104,128]{3,2,1,0:T(8,128)(2,1)S(1)}, bf16[2,3,104,128]{3,2,1,0:T(8,128)(2,1)S(1)}, bf16[2,3,10...) custom-call(s32[6]{0:T(128)S(1)} %stack.31.place_ref.refs_0_, ...), custom_call_target="tpu_custom_call" | custom-call | tf_op jit(solution)/shard_map/pallas_call | solution.py:578
  14.1 3.8 %collective-permute-start.11 = (f32[8,128]{1,0:T(8,128)S(1)}, f32[8,128]{1,0:T(8,128)S(1)}, u32[]{:S(2)}, u32[]{:S(2)}) collective-permute-start(f32[8,128]{1,0:T(8,128)S(1)} %get-tuple-element.40.refs_13_), channel_id=1, source_target_pairs={{0,7},{1,6},{2,5},{3,4},{4,3},{5,2},{6,1},{7,0},{8,15},{9,14},{10,... | collective-permute-start | bytes 12296 | tf_op jit(solution)/shard_map/ppermute | solution.py:571
  17.9 2.7 %collective-permute-start.10 = (f32[8,128]{1,0:T(8,128)S(1)}, f32[8,128]{1,0:T(8,128)S(1)}, u32[]{:S(2)}, u32[]{:S(2)}) collective-permute-start(f32[8,128]{1,0:T(8,128)S(1)} %get-tuple-element.40.refs_13_), channel_id=1, source_target_pairs={{0,6},{1,7},{2,4},{3,5},{4,2},{5,3},{6,0},{7,1},{8,14},{9,15},{10,... | collective-permute-start | bytes 12296 | tf_op jit(solution)/shard_map/ppermute | solution.py:571
  20.6 2.2 %collective-permute-start.8 = (f32[8,128]{1,0:T(8,128)S(1)}, f32[8,128]{1,0:T(8,128)S(1)}, u32[]{:S(2)}, u32[]{:S(2)}) collective-permute-start(f32[8,128]{1,0:T(8,128)S(1)} %get-tuple-element.40.refs_13_), channel_id=1, source_target_pairs={{0,4},{1,5},{2,6},{3,7},{4,0},{5,1},{6,2},{7,3},{8,12},{9,13},{10,... | collective-permute-start | bytes 12296 | tf_op jit(solution)/shard_map/ppermute | solution.py:571
  23.3 1.2 %collective-permute-done.9.refs_18_ = f32[8,128]{1,0:T(8,128)S(1)} collective-permute-done((f32[8,128]{1,0:T(8,128)S(1)}, f32[8,128]{1,0:T(8,128)S(1)}, u32[]{:S(2)}, u32[]{:S(2)}) %collective-permute-start.9) | collective-permute-done | bytes 4128 | tf_op jit(solution)/shard_map/ppermute | solution.py:571
  26.0 2.6 %shard_map.53.refs_12_ = bf16[3,2432,128]{2,1,0:T(8,128)(2,1)S(1)} custom-call(bf16[61,61]{1,0:T(8,128)(2,1)S(1)} %copy-done.1), custom_call_target="tpu_custom_call" | custom-call | tf_op jit(solution)/shard_map/pallas_call | solution.py:141
  28.6 1.2 %shard_map.52 = (bf16[192,768]{1,0:T(8,128)(2,1)S(1)}, bf16[384,896]{1,0:T(8,128)(2,1)S(1)}, bf16[768,640]{1,0:T(8,128)(2,1)S(1)}, bf16[384,128]{1,0:T(8,128)(2,1)S(1)}, f32[5,128]{1,0:T(8,128)S(1)}) custom-call(s32[2]{0:T(128)S(1)} %pad_add_fusion.1.place_ref), custom_call_target="tpu_custom_call" | custom-call | tf_op jit(solution)/shard_map/pallas_call | solution.py:578
  29.9 6.4 %shard_map.54 = (f32[2,4,104,128]{3,2,1,0:T(8,128)S(1)}, f32[2,2,104,128]{3,2,1,0:T(8,128)S(1)}, f32[2,2,104,128]{3,2,1,0:T(8,128)S(1)}, f32[8,128]{1,0:T(8,128)S(1)}, bf16[2,5,104,128]{3,2,1,0:T(8,128)(2,1)S(1)}) custom-call(s32[6]{0:T(128)S(1)} %stack.31.place_ref.refs_0_, f32[2,4,104,128]{3,2,1,0:T(8,128)S(1)} %get-tuple-element.30.refs_1_, ...), custom_call_target="tpu_custom_call" | custom-call | tf_op jit(solution)/shard_map/pallas_call | solution.py:578
  37.3 3.0 %collective-permute-start.20 = (f32[8,128]{1,0:T(8,128)S(1)}, f32[8,128]{1,0:T(8,128)S(1)}, u32[]{:S(2)}, u32[]{:S(2)}) collective-permute-start(f32[8,128]{1,0:T(8,128)S(1)} %get-tuple-element.45.refs_13_), channel_id=1, source_target_pairs={{0,7},{1,6},{2,5},{3,4},{4,3},{5,2},{6,1},{7,0},{8,15},{9,14},{10,... | collective-permute-start | bytes 12296 | tf_op jit(solution)/shard_map/ppermute | solution.py:571
  40.3 4.2 %collective-permute-start.19 = (f32[8,128]{1,0:T(8,128)S(1)}, f32[8,128]{1,0:T(8,128)S(1)}, u32[]{:S(2)}, u32[]{:S(2)}) collective-permute-start(f32[8,128]{1,0:T(8,128)S(1)} %get-tuple-element.45.refs_13_), channel_id=1, source_target_pairs={{0,6},{1,7},{2,4},{3,5},{4,2},{5,3},{6,0},{7,1},{8,14},{9,15},{10,... | collective-permute-start | bytes 12296 | tf_op jit(solution)/shard_map/ppermute | solution.py:571
  46.1 2.3 %collective-permute-done.18.refs_18_ = f32[8,128]{1,0:T(8,128)S(1)} collective-permute-done((f32[8,128]{1,0:T(8,128)S(1)}, f32[8,128]{1,0:T(8,128)S(1)}, u32[]{:S(2)}, u32[]{:S(2)}) %collective-permute-start.18) | collective-permute-done | bytes 4128 | tf_op jit(solution)/shard_map/ppermute | solution.py:571
  49.2 2.8 %collective-permute-done.15.refs_15_ = f32[8,128]{1,0:T(8,128)S(1)} collective-permute-done((f32[8,128]{1,0:T(8,128)S(1)}, f32[8,128]{1,0:T(8,128)S(1)}, u32[]{:S(2)}, u32[]{:S(2)}) %collective-permute-start.15) | collective-permute-done | bytes 4128 | tf_op jit(solution)/shard_map/ppermute | solution.py:571
  52.0 6.4 %shard_map.55 = (f32[2,4,104,128]{3,2,1,0:T(8,128)S(1)}, f32[2,2,104,128]{3,2,1,0:T(8,128)S(1)}, f32[2,2,104,128]{3,2,1,0:T(8,128)S(1)}, f32[8,128]{1,0:T(8,128)S(1)}) custom-call(s32[6]{0:T(128)S(1)} %stack.31.place_ref.refs_0_, f32[2,4,104,128]{3,2,1,0:T(8,128)S(1)} %get-tuple-element.41.refs_1_, f32[2,2,104,128]{3,2,1,0:T(8,128)S(1)} %collective-permute-done.12.refs_2_, ...), custom_call_target="tpu_custom_call" | custom-call | tf_op jit(solution)/shard_map/pallas_call | solution.py:578
  59.1 1.7 %collective-permute-start.29 = (f32[8,128]{1,0:T(8,128)S(1)}, f32[8,128]{1,0:T(8,128)S(1)}, u32[]{:S(2)}, u32[]{:S(2)}) collective-permute-start(f32[8,128]{1,0:T(8,128)S(1)} %get-tuple-element.49.refs_13_), channel_id=1, source_target_pairs={{0,7},{1,6},{2,5},{3,4},{4,3},{5,2},{6,1},{7,0},{8,15},{9,14},{10,... | collective-permute-start | bytes 12296 | tf_op jit(solution)/shard_map/ppermute | solution.py:571
  60.8 3.6 %collective-permute-start.28 = (f32[8,128]{1,0:T(8,128)S(1)}, f32[8,128]{1,0:T(8,128)S(1)}, u32[]{:S(2)}, u32[]{:S(2)}) collective-permute-start(f32[8,128]{1,0:T(8,128)S(1)} %get-tuple-element.49.refs_13_), channel_id=1, source_target_pairs={{0,6},{1,7},{2,4},{3,5},{4,2},{5,3},{6,0},{7,1},{8,14},{9,15},{10,... | collective-permute-start | bytes 12296 | tf_op jit(solution)/shard_map/ppermute | solution.py:571
  64.5 2.3 %collective-permute-start.26 = (f32[8,128]{1,0:T(8,128)S(1)}, f32[8,128]{1,0:T(8,128)S(1)}, u32[]{:S(2)}, u32[]{:S(2)}) collective-permute-start(f32[8,128]{1,0:T(8,128)S(1)} %get-tuple-element.49.refs_13_), channel_id=1, source_target_pairs={{0,4},{1,5},{2,6},{3,7},{4,0},{5,1},{6,2},{7,3},{8,12},{9,13},{10,... | collective-permute-start | bytes 12296 | tf_op jit(solution)/shard_map/ppermute | solution.py:571
  66.8 1.6 %collective-permute-done.27.refs_18_ = f32[8,128]{1,0:T(8,128)S(1)} collective-permute-done((f32[8,128]{1,0:T(8,128)S(1)}, f32[8,128]{1,0:T(8,128)S(1)}, u32[]{:S(2)}, u32[]{:S(2)}) %collective-permute-start.27) | collective-permute-done | bytes 4128 | tf_op jit(solution)/shard_map/ppermute | solution.py:571
  69.8 2.2 %collective-permute-done.24.refs_15_ = f32[8,128]{1,0:T(8,128)S(1)} collective-permute-done((f32[8,128]{1,0:T(8,128)S(1)}, f32[8,128]{1,0:T(8,128)S(1)}, u32[]{:S(2)}, u32[]{:S(2)}) %collective-permute-start.24) | collective-permute-done | bytes 4128 | tf_op jit(solution)/shard_map/ppermute | solution.py:571
  72.0 6.4 %shard_map.56 = (f32[2,4,104,128]{3,2,1,0:T(8,128)S(1)}, f32[2,2,104,128]{3,2,1,0:T(8,128)S(1)}, f32[2,2,104,128]{3,2,1,0:T(8,128)S(1)}, f32[8,128]{1,0:T(8,128)S(1)}) custom-call(s32[6]{0:T(128)S(1)} %stack.31.place_ref.refs_0_, f32[2,4,104,128]{3,2,1,0:T(8,128)S(1)} %get-tuple-element.46.refs_1_, f32[2,2,104,128]{3,2,1,0:T(8,128)S(1)} %collective-permute-done.21.refs_2_, ...), custom_call_target="tpu_custom_call" | custom-call | tf_op jit(solution)/shard_map/pallas_call | solution.py:578
  79.3 1.8 %collective-permute-start.38 = (f32[8,128]{1,0:T(8,128)S(1)}, f32[8,128]{1,0:T(8,128)S(1)}, u32[]{:S(2)}, u32[]{:S(2)}) collective-permute-start(f32[8,128]{1,0:T(8,128)S(1)} %get-tuple-element.53.refs_13_), channel_id=1, source_target_pairs={{0,7},{1,6},{2,5},{3,4},{4,3},{5,2},{6,1},{7,0},{8,15},{9,14},{10,... | collective-permute-start | bytes 12296 | tf_op jit(solution)/shard_map/ppermute | solution.py:571
  81.2 3.5 %collective-permute-start.37 = (f32[8,128]{1,0:T(8,128)S(1)}, f32[8,128]{1,0:T(8,128)S(1)}, u32[]{:S(2)}, u32[]{:S(2)}) collective-permute-start(f32[8,128]{1,0:T(8,128)S(1)} %get-tuple-element.53.refs_13_), channel_id=1, source_target_pairs={{0,6},{1,7},{2,4},{3,5},{4,2},{5,3},{6,0},{7,1},{8,14},{9,15},{10,... | collective-permute-start | bytes 12296 | tf_op jit(solution)/shard_map/ppermute | solution.py:571
  84.7 2.1 %collective-permute-start.35 = (f32[8,128]{1,0:T(8,128)S(1)}, f32[8,128]{1,0:T(8,128)S(1)}, u32[]{:S(2)}, u32[]{:S(2)}) collective-permute-start(f32[8,128]{1,0:T(8,128)S(1)} %get-tuple-element.53.refs_13_), channel_id=1, source_target_pairs={{0,4},{1,5},{2,6},{3,7},{4,0},{5,1},{6,2},{7,3},{8,12},{9,13},{10,... | collective-permute-start | bytes 12296 | tf_op jit(solution)/shard_map/ppermute | solution.py:571
  86.7 1.8 %collective-permute-done.36.refs_18_ = f32[8,128]{1,0:T(8,128)S(1)} collective-permute-done((f32[8,128]{1,0:T(8,128)S(1)}, f32[8,128]{1,0:T(8,128)S(1)}, u32[]{:S(2)}, u32[]{:S(2)}) %collective-permute-start.36) | collective-permute-done | bytes 4128 | tf_op jit(solution)/shard_map/ppermute | solution.py:571
  89.8 2.4 %collective-permute-done.33.refs_15_ = f32[8,128]{1,0:T(8,128)S(1)} collective-permute-done((f32[8,128]{1,0:T(8,128)S(1)}, f32[8,128]{1,0:T(8,128)S(1)}, u32[]{:S(2)}, u32[]{:S(2)}) %collective-permute-start.33) | collective-permute-done | bytes 4128 | tf_op jit(solution)/shard_map/ppermute | solution.py:571
  92.2 5.7 %shard_map.57 = (f32[200,100]{1,0:T(8,128)S(1)}, f32[200,100]{1,0:T(8,128)}, f32[8,128]{1,0:T(8,128)S(1)}) custom-call(s32[6]{0:T(128)S(1)} %stack.31.place_ref.refs_0_, f32[2,4,104,128]{3,2,1,0:T(8,128)S(1)} %get-tuple-element.50.refs_1_, f32[2,2,104,128]{3,2,1,0:T(8,128)S(1)} %collective-permute-done.30.refs_2_, ...), custom_call_target="tpu_custom_call" | custom-call | tf_op jit(solution)/shard_map/pallas_call | solution.py:578
  97.9 1.2 %collective-permute-start.45 = (f32[8,128]{1,0:T(8,128)S(1)}, f32[8,128]{1,0:T(8,128)S(1)}, u32[]{:S(2)}, u32[]{:S(2)}) collective-permute-start(f32[8,128]{1,0:T(8,128)S(1)} %get-tuple-element.57.refs_0_), channel_id=1, source_target_pairs={{0,7},{1,6},{2,5},{3,4},{4,3},{5,2},{6,1},{7,0},{8,15},{9,14},{10,... | collective-permute-start | bytes 12296 | tf_op jit(solution)/shard_map/ppermute | solution.py:571
  100.3 3.8 %collective-permute-start.42 = (f32[8,128]{1,0:T(8,128)S(1)}, f32[8,128]{1,0:T(8,128)S(1)}, u32[]{:S(2)}, u32[]{:S(2)}) collective-permute-start(f32[8,128]{1,0:T(8,128)S(1)} %get-tuple-element.57.refs_0_), channel_id=1, source_target_pairs={{0,4},{1,5},{2,6},{3,7},{4,0},{5,1},{6,2},{7,3},{8,12},{9,13},{10,... | collective-permute-start | bytes 12296 | tf_op jit(solution)/shard_map/ppermute | solution.py:571
  104.7 1.3 %collective-permute-start.39 = (f32[8,128]{1,0:T(8,128)S(1)}, f32[8,128]{1,0:T(8,128)S(1)}, u32[]{:S(2)}, u32[]{:S(2)}) collective-permute-start(f32[8,128]{1,0:T(8,128)S(1)} %get-tuple-element.57.refs_0_), channel_id=1, source_target_pairs={{0,1},{1,0},{2,3},{3,2},{4,5},{5,4},{6,7},{7,6},{8,9},{9,8},{10,11... | collective-permute-start | bytes 12296 | tf_op jit(solution)/shard_map/ppermute | solution.py:571
  106.0 1.2 %collective-permute-done.41.refs_3_ = f32[8,128]{1,0:T(8,128)S(1)} collective-permute-done((f32[8,128]{1,0:T(8,128)S(1)}, f32[8,128]{1,0:T(8,128)S(1)}, u32[]{:S(2)}, u32[]{:S(2)}) %collective-permute-start.41) | collective-permute-done | bytes 4128 | tf_op jit(solution)/shard_map/ppermute | solution.py:571
  107.7 1.8 %shard_map.58 = f32[200,100]{1,0:T(8,128)} custom-call(s32[6]{0:T(128)S(1)} %stack.31.place_ref.refs_0_, f32[200,100]{1,0:T(8,128)S(1)} %get-tuple-element.55.v_ref, bf16[192,768]{1,0:T(8,128)(2,1)S(1)} %get-tuple-element.34.refs_5_.rows_ref, bf16[384,128]{1,0:T(8,128)(2,1)S(1)} %get-tuple-element.56.pull_ref, f32[8,128]{1,0:T(8,128)S(1)} %get-tuple-element.57.refs_0_, ...), custom_call_target="tpu_custom_call" | custom-call | tf_op jit(solution)/shard_map/pallas_call | solution.py:578
  (77 shorter events, 17.5 us)
Async XLA Ops:
  2.4 7.9 %collective-permute-start.2 = (bf16[200,256]{1,0:T(8,128)(2,1)S(1)}, bf16[200,256]{1,0:T(8,128)(2,1)S(1)}, u32[]{:S(2)}, u32[]{:S(2)}) collective-permute-start(bf16[200,256]{1,0:T(8,128)(2,1)S(1)} %pad_add_fusion.refs_1_), channel_id=1, source_target_pairs={{0,24},{8,16},{16,8},{24,0},{1,25},{9,17},{17,9},{25,1},{2,26},{10... | collective-permute-start | bytes 307208 | tf_op jit(solution)/shard_map/ppermute | solution.py:592
  6.3 5.1 %collective-permute-start.1 = (bf16[200,256]{1,0:T(8,128)(2,1)S(1)}, bf16[200,256]{1,0:T(8,128)(2,1)S(1)}, u32[]{:S(2)}, u32[]{:S(2)}) collective-permute-start(bf16[200,256]{1,0:T(8,128)(2,1)S(1)} %pad_add_fusion.refs_1_), channel_id=1, source_target_pairs={{0,16},{8,24},{16,0},{24,8},{1,17},{9,25},{17,1},{25,9},{2,18},{10... | collective-permute-start | bytes 307208 | tf_op jit(solution)/shard_map/ppermute | solution.py:592
  6.8 4.9 %collective-permute-start = (bf16[200,256]{1,0:T(8,128)(2,1)S(1)}, bf16[200,256]{1,0:T(8,128)(2,1)S(1)}, u32[]{:S(2)}, u32[]{:S(2)}) collective-permute-start(bf16[200,256]{1,0:T(8,128)(2,1)S(1)} %pad_add_fusion.refs_1_), channel_id=1, source_target_pairs={{0,8},{8,0},{16,24},{24,16},{1,9},{9,1},{17,25},{25,17},{2,10},{10... | collective-permute-start | bytes 307208 | tf_op jit(solution)/shard_map/ppermute | solution.py:592
  13.4 16.4 %collective-permute-start.3 = (bf16[2,3,104,128]{3,2,1,0:T(8,128)(2,1)S(1)}, bf16[2,3,104,128]{3,2,1,0:T(8,128)(2,1)S(1)}, u32[]{:S(2)}, u32[]{:S(2)}) collective-permute-start(bf16[2,3,104,128]{3,2,1,0:T(8,128)(2,1)S(1)} %get-tuple-element.31), channel_id=1, source_target_pairs={{0,1},{1,0},{2,3},{3,2},{4,5},{5,4},{6,7},{7,6},{8,9},{9,8},{10,11... | collective-permute-start | bytes 479240 | tf_op jit(solution)/shard_map/ppermute | solution.py:563
  13.5 16.4 %collective-permute-start.4 = (bf16[2,3,104,128]{3,2,1,0:T(8,128)(2,1)S(1)}, bf16[2,3,104,128]{3,2,1,0:T(8,128)(2,1)S(1)}, u32[]{:S(2)}, u32[]{:S(2)}) collective-permute-start(bf16[2,3,104,128]{3,2,1,0:T(8,128)(2,1)S(1)} %get-tuple-element.32), channel_id=1, source_target_pairs={{1,2},{2,1},{3,4},{4,3},{5,6},{6,5},{9,10},{10,9},{11,12},{12,11},... | collective-permute-start | bytes 479240 | tf_op jit(solution)/shard_map/ppermute | solution.py:563
  14.1 6.4 %collective-permute-start.11 = (f32[8,128]{1,0:T(8,128)S(1)}, f32[8,128]{1,0:T(8,128)S(1)}, u32[]{:S(2)}, u32[]{:S(2)}) collective-permute-start(f32[8,128]{1,0:T(8,128)S(1)} %get-tuple-element.40.refs_13_), channel_id=1, source_target_pairs={{0,7},{1,6},{2,5},{3,4},{4,3},{5,2},{6,1},{7,0},{8,15},{9,14},{10,... | collective-permute-start | bytes 12296 | tf_op jit(solution)/shard_map/ppermute | solution.py:571
  17.9 5.4 %collective-permute-start.10 = (f32[8,128]{1,0:T(8,128)S(1)}, f32[8,128]{1,0:T(8,128)S(1)}, u32[]{:S(2)}, u32[]{:S(2)}) collective-permute-start(f32[8,128]{1,0:T(8,128)S(1)} %get-tuple-element.40.refs_13_), channel_id=1, source_target_pairs={{0,6},{1,7},{2,4},{3,5},{4,2},{5,3},{6,0},{7,1},{8,14},{9,15},{10,... | collective-permute-start | bytes 12296 | tf_op jit(solution)/shard_map/ppermute | solution.py:571
  20.6 3.9 %collective-permute-start.9 = (f32[8,128]{1,0:T(8,128)S(1)}, f32[8,128]{1,0:T(8,128)S(1)}, u32[]{:S(2)}, u32[]{:S(2)}) collective-permute-start(f32[8,128]{1,0:T(8,128)S(1)} %get-tuple-element.40.refs_13_), channel_id=1, source_target_pairs={{0,5},{1,4},{2,7},{3,6},{4,1},{5,0},{6,3},{7,2},{8,13},{9,12},{10,... | collective-permute-start | bytes 12296 | tf_op jit(solution)/shard_map/ppermute | solution.py:571
  20.6 5.0 %collective-permute-start.8 = (f32[8,128]{1,0:T(8,128)S(1)}, f32[8,128]{1,0:T(8,128)S(1)}, u32[]{:S(2)}, u32[]{:S(2)}) collective-permute-start(f32[8,128]{1,0:T(8,128)S(1)} %get-tuple-element.40.refs_13_), channel_id=1, source_target_pairs={{0,4},{1,5},{2,6},{3,7},{4,0},{5,1},{6,2},{7,3},{8,12},{9,13},{10,... | collective-permute-start | bytes 12296 | tf_op jit(solution)/shard_map/ppermute | solution.py:571
  23.3 6.5 %collective-permute-start.7 = (f32[8,128]{1,0:T(8,128)S(1)}, f32[8,128]{1,0:T(8,128)S(1)}, u32[]{:S(2)}, u32[]{:S(2)}) collective-permute-start(f32[8,128]{1,0:T(8,128)S(1)} %get-tuple-element.40.refs_13_), channel_id=1, source_target_pairs={{0,3},{1,2},{2,1},{3,0},{4,7},{5,6},{6,5},{7,4},{8,11},{9,10},{10,... | collective-permute-start | bytes 12296 | tf_op jit(solution)/shard_map/ppermute | solution.py:571
  24.5 5.3 %collective-permute-start.6 = (f32[8,128]{1,0:T(8,128)S(1)}, f32[8,128]{1,0:T(8,128)S(1)}, u32[]{:S(2)}, u32[]{:S(2)}) collective-permute-start(f32[8,128]{1,0:T(8,128)S(1)} %get-tuple-element.40.refs_13_), channel_id=1, source_target_pairs={{0,2},{1,3},{2,0},{3,1},{4,6},{5,7},{6,4},{7,5},{8,10},{9,11},{10,... | collective-permute-start | bytes 12296 | tf_op jit(solution)/shard_map/ppermute | solution.py:571
  25.6 4.2 %collective-permute-start.5 = (f32[8,128]{1,0:T(8,128)S(1)}, f32[8,128]{1,0:T(8,128)S(1)}, u32[]{:S(2)}, u32[]{:S(2)}) collective-permute-start(f32[8,128]{1,0:T(8,128)S(1)} %get-tuple-element.40.refs_13_), channel_id=1, source_target_pairs={{0,1},{1,0},{2,3},{3,2},{4,5},{5,4},{6,7},{7,6},{8,9},{9,8},{10,11... | collective-permute-start | bytes 12296 | tf_op jit(solution)/shard_map/ppermute | solution.py:571
  36.3 15.7 %collective-permute-start.12 = (f32[2,2,104,128]{3,2,1,0:T(8,128)S(1)}, f32[2,2,104,128]{3,2,1,0:T(8,128)S(1)}, u32[]{:S(2)}, u32[]{:S(2)}) collective-permute-start(f32[2,2,104,128]{3,2,1,0:T(8,128)S(1)} %get-tuple-element.42), channel_id=1, source_target_pairs={{0,1},{1,0},{2,3},{3,2},{4,5},{5,4},{6,7},{7,6},{8,9},{9,8},{10,11... | collective-permute-start | bytes 638984 | tf_op jit(solution)/shard_map/ppermute | solution.py:563
  36.5 15.6 %collective-permute-start.13 = (f32[2,2,104,128]{3,2,1,0:T(8,128)S(1)}, f32[2,2,104,128]{3,2,1,0:T(8,128)S(1)}, u32[]{:S(2)}, u32[]{:S(2)}) collective-permute-start(f32[2,2,104,128]{3,2,1,0:T(8,128)S(1)} %get-tuple-element.43), channel_id=1, source_target_pairs={{1,2},{2,1},{3,4},{4,3},{5,6},{6,5},{9,10},{10,9},{11,12},{12,11},... | collective-permute-start | bytes 638984 | tf_op jit(solution)/shard_map/ppermute | solution.py:563
  37.3 7.2 %collective-permute-start.20 = (f32[8,128]{1,0:T(8,128)S(1)}, f32[8,128]{1,0:T(8,128)S(1)}, u32[]{:S(2)}, u32[]{:S(2)}) collective-permute-start(f32[8,128]{1,0:T(8,128)S(1)} %get-tuple-element.45.refs_13_), channel_id=1, source_target_pairs={{0,7},{1,6},{2,5},{3,4},{4,3},{5,2},{6,1},{7,0},{8,15},{9,14},{10,... | collective-permute-start | bytes 12296 | tf_op jit(solution)/shard_map/ppermute | solution.py:571
  40.3 5.8 %collective-permute-start.19 = (f32[8,128]{1,0:T(8,128)S(1)}, f32[8,128]{1,0:T(8,128)S(1)}, u32[]{:S(2)}, u32[]{:S(2)}) collective-permute-start(f32[8,128]{1,0:T(8,128)S(1)} %get-tuple-element.45.refs_13_), channel_id=1, source_target_pairs={{0,6},{1,7},{2,4},{3,5},{4,2},{5,3},{6,0},{7,1},{8,14},{9,15},{10,... | collective-permute-start | bytes 12296 | tf_op jit(solution)/shard_map/ppermute | solution.py:571
  44.5 3.9 %collective-permute-start.18 = (f32[8,128]{1,0:T(8,128)S(1)}, f32[8,128]{1,0:T(8,128)S(1)}, u32[]{:S(2)}, u32[]{:S(2)}) collective-permute-start(f32[8,128]{1,0:T(8,128)S(1)} %get-tuple-element.45.refs_13_), channel_id=1, source_target_pairs={{0,5},{1,4},{2,7},{3,6},{4,1},{5,0},{6,3},{7,2},{8,13},{9,12},{10,... | collective-permute-start | bytes 12296 | tf_op jit(solution)/shard_map/ppermute | solution.py:571
  44.5 4.5 %collective-permute-start.17 = (f32[8,128]{1,0:T(8,128)S(1)}, f32[8,128]{1,0:T(8,128)S(1)}, u32[]{:S(2)}, u32[]{:S(2)}) collective-permute-start(f32[8,128]{1,0:T(8,128)S(1)} %get-tuple-element.45.refs_13_), channel_id=1, source_target_pairs={{0,4},{1,5},{2,6},{3,7},{4,0},{5,1},{6,2},{7,3},{8,12},{9,13},{10,... | collective-permute-start | bytes 12296 | tf_op jit(solution)/shard_map/ppermute | solution.py:571
  58.4 13.6 %collective-permute-start.21 = (f32[2,2,104,128]{3,2,1,0:T(8,128)S(1)}, f32[2,2,104,128]{3,2,1,0:T(8,128)S(1)}, u32[]{:S(2)}, u32[]{:S(2)}) collective-permute-start(f32[2,2,104,128]{3,2,1,0:T(8,128)S(1)} %get-tuple-element.47), channel_id=1, source_target_pairs={{0,1},{1,0},{2,3},{3,2},{4,5},{5,4},{6,7},{7,6},{8,9},{9,8},{10,11... | collective-permute-start | bytes 638984 | tf_op jit(solution)/shard_map/ppermute | solution.py:563
  58.4 13.6 %collective-permute-start.22 = (f32[2,2,104,128]{3,2,1,0:T(8,128)S(1)}, f32[2,2,104,128]{3,2,1,0:T(8,128)S(1)}, u32[]{:S(2)}, u32[]{:S(2)}) collective-permute-start(f32[2,2,104,128]{3,2,1,0:T(8,128)S(1)} %get-tuple-element.48), channel_id=1, source_target_pairs={{1,2},{2,1},{3,4},{4,3},{5,6},{6,5},{9,10},{10,9},{11,12},{12,11},... | collective-permute-start | bytes 638984 | tf_op jit(solution)/shard_map/ppermute | solution.py:563
  59.1 5.3 %collective-permute-start.29 = (f32[8,128]{1,0:T(8,128)S(1)}, f32[8,128]{1,0:T(8,128)S(1)}, u32[]{:S(2)}, u32[]{:S(2)}) collective-permute-start(f32[8,128]{1,0:T(8,128)S(1)} %get-tuple-element.49.refs_13_), channel_id=1, source_target_pairs={{0,7},{1,6},{2,5},{3,4},{4,3},{5,2},{6,1},{7,0},{8,15},{9,14},{10,... | collective-permute-start | bytes 12296 | tf_op jit(solution)/shard_map/ppermute | solution.py:571
  60.8 5.9 %collective-permute-start.28 = (f32[8,128]{1,0:T(8,128)S(1)}, f32[8,128]{1,0:T(8,128)S(1)}, u32[]{:S(2)}, u32[]{:S(2)}) collective-permute-start(f32[8,128]{1,0:T(8,128)S(1)} %get-tuple-element.49.refs_13_), channel_id=1, source_target_pairs={{0,6},{1,7},{2,4},{3,5},{4,2},{5,3},{6,0},{7,1},{8,14},{9,15},{10,... | collective-permute-start | bytes 12296 | tf_op jit(solution)/shard_map/ppermute | solution.py:571
  64.5 4.5 %collective-permute-start.26 = (f32[8,128]{1,0:T(8,128)S(1)}, f32[8,128]{1,0:T(8,128)S(1)}, u32[]{:S(2)}, u32[]{:S(2)}) collective-permute-start(f32[8,128]{1,0:T(8,128)S(1)} %get-tuple-element.49.refs_13_), channel_id=1, source_target_pairs={{0,4},{1,5},{2,6},{3,7},{4,0},{5,1},{6,2},{7,3},{8,12},{9,13},{10,... | collective-permute-start | bytes 12296 | tf_op jit(solution)/shard_map/ppermute | solution.py:571
  78.4 13.8 %collective-permute-start.30 = (f32[2,2,104,128]{3,2,1,0:T(8,128)S(1)}, f32[2,2,104,128]{3,2,1,0:T(8,128)S(1)}, u32[]{:S(2)}, u32[]{:S(2)}) collective-permute-start(f32[2,2,104,128]{3,2,1,0:T(8,128)S(1)} %get-tuple-element.51), channel_id=1, source_target_pairs={{0,1},{1,0},{2,3},{3,2},{4,5},{5,4},{6,7},{7,6},{8,9},{9,8},{10,11... | collective-permute-start | bytes 638984 | tf_op jit(solution)/shard_map/ppermute | solution.py:563
  78.4 13.8 %collective-permute-start.31 = (f32[2,2,104,128]{3,2,1,0:T(8,128)S(1)}, f32[2,2,104,128]{3,2,1,0:T(8,128)S(1)}, u32[]{:S(2)}, u32[]{:S(2)}) collective-permute-start(f32[2,2,104,128]{3,2,1,0:T(8,128)S(1)} %get-tuple-element.52), channel_id=1, source_target_pairs={{1,2},{2,1},{3,4},{4,3},{5,6},{6,5},{9,10},{10,9},{11,12},{12,11},... | collective-permute-start | bytes 638984 | tf_op jit(solution)/shard_map/ppermute | solution.py:563
  79.3 5.3 %collective-permute-start.38 = (f32[8,128]{1,0:T(8,128)S(1)}, f32[8,128]{1,0:T(8,128)S(1)}, u32[]{:S(2)}, u32[]{:S(2)}) collective-permute-start(f32[8,128]{1,0:T(8,128)S(1)} %get-tuple-element.53.refs_13_), channel_id=1, source_target_pairs={{0,7},{1,6},{2,5},{3,4},{4,3},{5,2},{6,1},{7,0},{8,15},{9,14},{10,... | collective-permute-start | bytes 12296 | tf_op jit(solution)/shard_map/ppermute | solution.py:571
  81.2 5.6 %collective-permute-start.37 = (f32[8,128]{1,0:T(8,128)S(1)}, f32[8,128]{1,0:T(8,128)S(1)}, u32[]{:S(2)}, u32[]{:S(2)}) collective-permute-start(f32[8,128]{1,0:T(8,128)S(1)} %get-tuple-element.53.refs_13_), channel_id=1, source_target_pairs={{0,6},{1,7},{2,4},{3,5},{4,2},{5,3},{6,0},{7,1},{8,14},{9,15},{10,... | collective-permute-start | bytes 12296 | tf_op jit(solution)/shard_map/ppermute | solution.py:571
  84.7 4.5 %collective-permute-start.35 = (f32[8,128]{1,0:T(8,128)S(1)}, f32[8,128]{1,0:T(8,128)S(1)}, u32[]{:S(2)}, u32[]{:S(2)}) collective-permute-start(f32[8,128]{1,0:T(8,128)S(1)} %get-tuple-element.53.refs_13_), channel_id=1, source_target_pairs={{0,4},{1,5},{2,6},{3,7},{4,0},{5,1},{6,2},{7,3},{8,12},{9,13},{10,... | collective-permute-start | bytes 12296 | tf_op jit(solution)/shard_map/ppermute | solution.py:571
  97.9 6.2 %collective-permute-start.45 = (f32[8,128]{1,0:T(8,128)S(1)}, f32[8,128]{1,0:T(8,128)S(1)}, u32[]{:S(2)}, u32[]{:S(2)}) collective-permute-start(f32[8,128]{1,0:T(8,128)S(1)} %get-tuple-element.57.refs_0_), channel_id=1, source_target_pairs={{0,7},{1,6},{2,5},{3,4},{4,3},{5,2},{6,1},{7,0},{8,15},{9,14},{10,... | collective-permute-start | bytes 12296 | tf_op jit(solution)/shard_map/ppermute | solution.py:571
  99.1 5.5 %collective-permute-start.44 = (f32[8,128]{1,0:T(8,128)S(1)}, f32[8,128]{1,0:T(8,128)S(1)}, u32[]{:S(2)}, u32[]{:S(2)}) collective-permute-start(f32[8,128]{1,0:T(8,128)S(1)} %get-tuple-element.57.refs_0_), channel_id=1, source_target_pairs={{0,6},{1,7},{2,4},{3,5},{4,2},{5,3},{6,0},{7,1},{8,14},{9,15},{10,... | collective-permute-start | bytes 12296 | tf_op jit(solution)/shard_map/ppermute | solution.py:571
  100.3 5.7 %collective-permute-start.43 = (f32[8,128]{1,0:T(8,128)S(1)}, f32[8,128]{1,0:T(8,128)S(1)}, u32[]{:S(2)}, u32[]{:S(2)}) collective-permute-start(f32[8,128]{1,0:T(8,128)S(1)} %get-tuple-element.57.refs_0_), channel_id=1, source_target_pairs={{0,5},{1,4},{2,7},{3,6},{4,1},{5,0},{6,3},{7,2},{8,13},{9,12},{10,... | collective-permute-start | bytes 12296 | tf_op jit(solution)/shard_map/ppermute | solution.py:571
  100.3 5.7 %collective-permute-start.42 = (f32[8,128]{1,0:T(8,128)S(1)}, f32[8,128]{1,0:T(8,128)S(1)}, u32[]{:S(2)}, u32[]{:S(2)}) collective-permute-start(f32[8,128]{1,0:T(8,128)S(1)} %get-tuple-element.57.refs_0_), channel_id=1, source_target_pairs={{0,4},{1,5},{2,6},{3,7},{4,0},{5,1},{6,2},{7,3},{8,12},{9,13},{10,... | collective-permute-start | bytes 12296 | tf_op jit(solution)/shard_map/ppermute | solution.py:571
  (16 other events, 65.8 us)

commit v7 on v6

--- a/solution.py
+++ b/solution.py
@@ -154,7 +154,7 @@
     height = blocks * depth
     for n in range(PAIR):
         for g in range(REACH):
-            wide = jnp.concatenate([field(n, g + b) for b in range(blocks)], axis=0)
+            wide = field(n, g)
             rest = line_ref.shape[0] - height
             if rest:
                 wide = jnp.concatenate([wide, jnp.zeros((rest, LANES), f32)], axis=0)
@@ -187,6 +187,12 @@
             acc_ref[n, b, pl.ds(0, depth), :] = total
 
 
+def stacked(ref, n, g, blocks, first, depth):
+    if ref.shape[2] == depth:
+        return ref[n, g:g + blocks].reshape(blocks * depth, LANES)
+    return jnp.concatenate([ref[n, g + b, pl.ds(first, depth), :] for b in range(blocks)], axis=0)
+
+
 def in_rows(n, depth, ncx):
     shape = (depth, PER * 2 * ncx)
     column = iota2(shape, 1)
@@ -234,8 +240,8 @@
     )
 
 
-def coarse(red_refs, rows_ref, pull_ref, back_ref, half):
-    red = jnp.concatenate([ref[...].reshape(-1, 2 * half) for ref in red_refs], axis=0)
+def coarse(red_pieces, rows_ref, pull_ref, back_ref, half):
+    red = jnp.concatenate([piece.reshape(-1, 2 * half) for piece in red_pieces], axis=0)
     mixed = dot_t(rows_ref[...], one_side(red, 1))
     pull = dot(one_side(mixed[:half], 1), pull_ref[...])
     if back_ref is None:
@@ -269,6 +275,11 @@
             value = turned if value is None else jnp.where(owner <= k, turned, value)
         return value
 
+    def put(n, t, to_right, to_left):
+        lines = pl.ds((n * (HALO_BLOCKS + 1) + t) * depth, depth)
+        a_out[lines, :] = jnp.where(even, to_right, to_left)
+        b_out[lines, :] = jnp.where(even, to_left, to_right)
+
     sums = None
     blocks = own_out.shape[1]
     for n in range(PAIR):
@@ -283,16 +294,16 @@
         for t in range(HALO_BLOCKS):
             to_right = tile(0, n, cols - (HALO_BLOCKS - t) * SPAN)
             to_left = tile(0, n, SPAN * (blocks - 1 + t) - cols)
-            a_out[n, t] = jnp.where(even, to_right, to_left).astype(bf16)
-            b_out[n, t] = jnp.where(even, to_left, to_right).astype(bf16)
+            put(n, t, to_right, to_left)
         to_right = tile(1, n, cols - RIM)
         to_left = tile(1, n, SPAN * (mask_out.shape[1] - 1) - RIM - cols)
-        a_out[n, HALO_BLOCKS] = jnp.where(even, to_right, to_left).astype(bf16)
-        b_out[n, HALO_BLOCKS] = jnp.where(even, to_left, to_right).astype(bf16)
+        put(n, HALO_BLOCKS, to_right, to_left)
         part = dot(cells_out[n], jnp.concatenate(tiles, axis=1).astype(bf16))
         sums = part if sums is None else sums + part
     red_out[...] = jnp.zeros_like(red_out)
     red_out[:, :half] = by_columns(0, crow, cell_rows(sums, ncx, blocks), half)
+    if a_out.shape != b_out.shape:
+        a_out[pl.ds(b_out.shape[0], 8), :] = red_out[...]
 
 
 def step_kernel(sizes, count, first, last, *refs):
@@ -314,12 +325,15 @@
     tile_blocks = own_ref.shape[1]
     at = place((depth, LANES))
     even = place_ref[1] == 0
+    halo_tiles = from_b_ref.shape[0] // (PAIR * depth)
 
     def from_left(n, t):
-        return jnp.where(even, from_b_ref[n, t].astype(f32), from_a_ref[n, t].astype(f32))
+        lines = pl.ds((n * halo_tiles + t) * depth, depth)
+        return jnp.where(even, from_b_ref[lines, :], from_a_ref[lines, :])
 
     def from_right(n, t):
-        return jnp.where(even, from_a_ref[n, t].astype(f32), from_b_ref[n, t].astype(f32))
+        lines = pl.ds((n * halo_tiles + t) * depth, depth)
+        return jnp.where(even, from_a_ref[lines, :], from_b_ref[lines, :])
 
     filled = iota2((depth, LANES), 0) < planes
 
@@ -334,7 +348,10 @@
                 e_ref[n, b, pl.ds(0, EDGE), :] = jnp.zeros((EDGE, LANES), f32)
                 e_ref[n, b, pl.ds(EDGE + depth, EDGE), :] = jnp.zeros((EDGE, LANES), f32)
 
-    pull, back = coarse(red_refs, rows_ref, pull_ref, back_ref, half)
+    pieces = [ref[...] for ref in red_refs]
+    if from_a_ref.shape != from_b_ref.shape:
+        pieces.insert(1, from_a_ref[pl.ds(from_b_ref.shape[0], 8), :])
+    pull, back = coarse(pieces, rows_ref, pull_ref, back_ref, half)
     pull = over_rows(pull, ncx, wide_blocks)
     back = over_rows(back, ncx, blocks)
 
@@ -354,7 +371,7 @@
             x_ref[n, b, pl.ds(0, depth), :] = value.astype(bf16).astype(f32)
 
     correlate(
-        lambda n, b: x_ref[n, b, pl.ds(0, depth), :],
+        lambda n, g: stacked(x_ref, n, g, blocks, 0, depth),
         blocks, depth, line_ref, fwd_ref, part_ref, acc_ref,
     )
     lead = EDGE if last else 0
@@ -407,7 +424,7 @@
         to_rows(lambda n, b: acc_ref[n, b, pl.ds(start, height), :], RIM, blocks)
         resist_out[...] = row_ref[:, :cols]
         correlate(
-            lambda n, b: e_ref[n, b, pl.ds(start + EDGE - FIRST_SHIFT, window), :],
+            lambda n, g: stacked(e_ref, n, g, tile_blocks, start + EDGE - FIRST_SHIFT, window),
             tile_blocks, window, tile_line_ref, adj_ref, part_ref, acc_ref,
         )
         to_rows(
@@ -420,7 +437,8 @@
         return
 
     correlate(
-        lambda n, b: e_ref[n, b], tile_blocks, depth, tile_line_ref, adj_ref, part_ref, acc_ref
+        lambda n, g: stacked(e_ref, n, g, tile_blocks, 0, depth),
+        tile_blocks, depth, tile_line_ref, adj_ref, part_ref, acc_ref,
     )
 
     cells = None
@@ -448,15 +466,18 @@
         for t in range(HALO_BLOCKS):
             to_right = moved(cols - (HALO_BLOCKS - t) * SPAN)
             to_left = moved(SPAN * (tile_blocks - 1 + t) - cols)
-            a_out[n, t] = jnp.where(even, to_right, to_left)
-            b_out[n, t] = jnp.where(even, to_left, to_right)
+            lines = pl.ds((n * HALO_BLOCKS + t) * depth, depth)
+            a_out[lines, :] = jnp.where(even, to_right, to_left)
+            b_out[lines, :] = jnp.where(even, to_left, to_right)
     red_out[:, :half] = by_columns(0, crow, cell_rows(cells, ncx, tile_blocks), half)
+    if a_out.shape != b_out.shape:
+        a_out[pl.ds(b_out.shape[0], 8), :] = red_out[...]
 
 
 def end_kernel(sizes, place_ref, v_ref, rows_ref, pull_ref, *refs):
     red_refs, out_ref = refs[:-1], refs[-1]
     planes, depth, half, cols, crow, ncx = sizes
-    pull = coarse(red_refs, rows_ref, pull_ref, None, half)
+    pull = coarse([ref[...] for ref in red_refs], rows_ref, pull_ref, None, half)
     pull = jnp.concatenate(split(pull, 2), axis=0)
     rows = v_ref.shape[0]
     row = iota2((rows, 2 * half), 0) + place_ref[0] * rows
@@ -562,13 +583,16 @@
     def swap(to_a, to_b):
         return lax.ppermute(to_a, "scan", swap_a), lax.ppermute(to_b, "scan", swap_b)
 
-    swapped = scans <= 8 and not scans & (scans - 1)
+    swapped = scans <= 8 and not scans & (scans - 1) and 2 * round_up(ncx, LANES // 2) == LANES
+
+    def spread_pairs(red, other):
+        pair = jnp.concatenate([red, other], axis=0)
+        return [
+            lax.ppermute(pair, "scan", [(i, i ^ k) for i in range(scans)]) for k in range(2, scans, 2)
+        ]
 
     def share(red):
-        if not swapped:
-            return [lax.all_to_all(jnp.broadcast_to(red, (scans,) + red.shape), "scan", 0, 0)]
-        pairs = [[(i, i ^ k) for i in range(scans)] for k in range(1, scans)]
-        return [red] + [lax.ppermute(red, "scan", pair) for pair in pairs]
+        return [lax.all_to_all(jnp.broadcast_to(red, (scans,) + red.shape), "scan", 0, 0)]
 
     vmem = pl.BlockSpec(memory_space=pltpu.VMEM)
     smem = pl.BlockSpec(memory_space=pltpu.SMEM)
@@ -604,13 +628,17 @@
     fwd = bands(psf, SPARE, False)
 
     few = array((8, 2 * half))
-    halo = array((PAIR, HALO_BLOCKS + 1, depth, LANES), bf16)
+
+    def halos(count):
+        lines = PAIR * count * depth
+        return [array((lines + 8 * swapped, LANES)), array((lines, LANES))]
+
     mask_tiles = array((PAIR, blocks, depth, LANES), bf16)
     tiles = array((PAIR, tile_blocks, depth, LANES))
     own, mask, to_a, to_b, red, in_row, in_cell = call(
         functools.partial(start_kernel, sizes),
         [
-            tiles, mask_tiles, halo, halo, few,
+            tiles, mask_tiles, *halos(HALO_BLOCKS + 1), few,
             array((PAIR, depth, PER * 2 * ncx), bf16), array((PAIR, PER * ncx, depth), bf16),
         ],
         [place, fwd, *pieces],
@@ -622,7 +650,7 @@
     height = round_up(blocks * depth, 16)
     def step_scratch(last):
         return [
-            pltpu.VMEM((PAIR, wide_blocks, depth + EDGE, LANES), f32),
+            pltpu.VMEM((PAIR, wide_blocks, depth + EDGE * last, LANES), f32),
             pltpu.VMEM((PAIR, blocks + 1, depth + 2 * EDGE * last, LANES), f32),
         ] + scratch
 
@@ -634,13 +662,12 @@
         pltpu.VMEM((PAIR, blocks, depth + EDGE, LANES), f32),
         pltpu.VMEM((PAIR, SHIFTS, height + 2 * EDGE, LANES), f32),
     ]
-    packed = array((PAIR, HALO_BLOCKS, depth, LANES))
     tile = array((rows, cols))
     for step in range(ITERS):
         first = step == 0
         last = step == ITERS - 1
         from_a, from_b = swap(to_a, to_b)
-        shared = share(red)
+        shared = [red] + spread_pairs(red, from_a[from_b.shape[0]:]) if swapped else share(red)
         args = [place, own, from_a, from_b, mask, *tables, *shared]
         kernel = functools.partial(step_kernel, sizes, len(shared), first, last)
         if last:
@@ -650,17 +677,22 @@
             v, resist, red = call(kernel, [tile, tile, few], args, some)
         elif first:
             own, to_a, to_b, red, mask = call(
-                kernel, [tiles, packed, packed, few, mask_tiles], args, step_scratch(False)
+                kernel, [tiles, *halos(HALO_BLOCKS), few, mask_tiles], args, step_scratch(False)
             )
         else:
             own, to_a, to_b, red = call(
-                kernel, [tiles, packed, packed, few], args, step_scratch(False)
+                kernel, [tiles, *halos(HALO_BLOCKS), few], args, step_scratch(False)
             )
 
+    if swapped:
+        other = lax.ppermute(red, "scan", swap_a)
+        shared = [red, other] + spread_pairs(red, other)
+    else:
+        shared = share(red)
     updated = call(
         functools.partial(end_kernel, sizes),
         tile,
-        [place, v, rows_table, end_table, *share(red)],
+        [place, v, rows_table, end_table, *shared],
     )
     return resist, updated
 

time: 110 us -> 89.9 us (0.82)
  starting transfers between devices: 51.9 us -> 31.8 us
    ppermute x35 -> x16, starting transfers between devices: 43.9 us -> 23.9 us  [the longest x15 23.9 us: spread_pairs(): lax.ppermute(pair, 'scan', [(i, i ^ k) for i in range(scans)])]
    ppermute x4, waiting for transfers between devices: 0.01 us -> 2.91 us  [swap(): lax.ppermute(to_a, 'scan', swap_a)]
    ppermute x35 -> x16, waiting for transfers between devices: 18.1 us -> 15.2 us  [the longest x15 14.1 us: spread_pairs(): lax.ppermute(pair, 'scan', [(i, i ^ k) for i in range(scans)])]
  transfers between devices with their start and end apart: 46 -> 27, of which waited for: 18 -> 17; matrix products, arithmetic and copies ran while one was open for 0% -> 0% of each run, Pallas kernels for 6% -> 7%
where the time goes in v7:
time: 89.9 us; the launch traced here: 89.6 us
  Pallas kernels  34.8 us (39%)
  starting transfers between devices  31.8 us (35%)
  waiting for transfers between devices  19.6 us (22%)
  other arithmetic  1.82 us (2%)
    pallas_call x7, Pallas kernels, call(): pl.pallas_call(kernel, out_shape=out_shape, in_specs=[smem if a.ndim == 1...  29.8 us
    ppermute x15, starting transfers between devices, spread_pairs(): lax.ppermute(pair, 'scan', [(i, i ^ k) for i in range(scans)])  23.9 us
    ppermute x15, waiting for transfers between devices, spread_pairs(): lax.ppermute(pair, 'scan', [(i, i ^ k) for i in range(scans)])  14.1 us
    pallas_call x2, Pallas kernels, bands(): pl.pallas_call(functools.partial(bands_kernel, offset, flip), out_shape=j...  5.04 us
    ppermute x3, starting transfers between devices, per_device(): lax.ppermute(both, 'stripe', pairs)  4.6 us
    ppermute x4, starting transfers between devices, swap(): lax.ppermute(to_b, 'scan', swap_b)  3.17 us
    ppermute x4, waiting for transfers between devices, swap(): lax.ppermute(to_a, 'scan', swap_a)  2.91 us
  transfers between devices with their start and end apart: 27, of which 17 were waited for; matrix products, arithmetic and copies ran while one was open for 0% of the time, Pallas kernels for 7%

profile of v7, /device:TPU:0, one launch (start us, length us, event | category | flops | bytes accessed | tf_op | source)
XLA Modules:
  0.0 89.6 jit_solution(17636637213014285048)
XLA Ops:
  0.6 0.9 %convert_element_type.7 = bf16[200,100]{1,0:T(8,128)(2,1)S(1)} convert(s32[200,100]{1,0:T(8,128)} %param.4) | non-fusion elementwise | flops 20000 | bytes 120000 | tf_op jit(solution)/shard_map/convert_element_type | solution.py:614
  1.5 0.8 pad_add_fusion.refs_1_
  2.4 4.0 %collective-permute-start.2 = (bf16[200,256]{1,0:T(8,128)(2,1)S(1)}, bf16[200,256]{1,0:T(8,128)(2,1)S(1)}, u32[]{:S(2)}, u32[]{:S(2)}) collective-permute-start(bf16[200,256]{1,0:T(8,128)(2,1)S(1)} %pad_add_fusion.refs_1_), channel_id=1, source_target_pairs={{0,24},{8,16},{16,8},{24,0},{1,25},{9,17},{17,9},{25,1},{2,26},{10... | collective-permute-start | bytes 307208 | tf_op jit(solution)/shard_map/ppermute | solution.py:616
  7.0 0.7 copy-done
  7.7 2.5 %shard_map.50.refs_0_.refs_11_ = bf16[3,2432,128]{2,1,0:T(8,128)(2,1)S(1)} custom-call(bf16[61,61]{1,0:T(8,128)(2,1)S(1)} %copy-done), custom_call_target="tpu_custom_call" | custom-call | tf_op jit(solution)/shard_map/pallas_call | solution.py:141
  10.3 1.1 %collective-permute-done.1.refs_3_ = bf16[200,256]{1,0:T(8,128)(2,1)S(1)} collective-permute-done((bf16[200,256]{1,0:T(8,128)(2,1)S(1)}, bf16[200,256]{1,0:T(8,128)(2,1)S(1)}, u32[]{:S(2)}, u32[]{:S(2)}) %collective-permute-start.1) | collective-permute-done | bytes 102432 | tf_op jit(solution)/shard_map/ppermute | solution.py:616
  11.7 2.0 %shard_map.51 = (f32[2,4,104,128]{3,2,1,0:T(8,128)S(1)}, bf16[2,5,104,128]{3,2,1,0:T(8,128)(2,1)S(1)}, f32[632,128]{1,0:T(8,128)S(1)}, f32[624,128]{1,0:T(8,128)...) custom-call(s32[6]{0:T(128)S(1)} %stack.31.place_ref.refs_0_, ...), custom_call_target="tpu_custom_call" | custom-call | tf_op jit(solution)/shard_map/pallas_call | solution.py:602
  14.5 0.9 %collective-permute-done.3.refs_2_ = f32[632,128]{1,0:T(8,128)S(1)} collective-permute-done((f32[632,128]{1,0:T(8,128)S(1)}, f32[632,128]{1,0:T(8,128)S(1)}, u32[]{:S(2)}, u32[]{:S(2)}) %collective-permute-start.3) | collective-permute-done | bytes 323616 | tf_op jit(solution)/shard_map/ppermute | solution.py:584
  15.4 4.5 %collective-permute-start.7 = (f32[16,128]{1,0:T(8,128)S(1)}, f32[16,128]{1,0:T(8,128)S(1)}, u32[]{:S(2)}, u32[]{:S(2)}) collective-permute-start(f32[16,128]{1,0:T(8,128)S(1)} %pad_maximum_fusion), channel_id=1, source_target_pairs={{0,6},{1,7},{2,4},{3,5},{4,2},{5,3},{6,0},{7,1},{8,14},{9,15},{10,... | collective-permute-start | bytes 24584 | tf_op jit(solution)/shard_map/ppermute | solution.py:591
  20.7 2.6 %shard_map.53.refs_12_ = bf16[3,2432,128]{2,1,0:T(8,128)(2,1)S(1)} custom-call(bf16[61,61]{1,0:T(8,128)(2,1)S(1)} %copy-done.1), custom_call_target="tpu_custom_call" | custom-call | tf_op jit(solution)/shard_map/pallas_call | solution.py:141
  23.3 1.2 %shard_map.52 = (bf16[192,768]{1,0:T(8,128)(2,1)S(1)}, bf16[384,896]{1,0:T(8,128)(2,1)S(1)}, bf16[768,640]{1,0:T(8,128)(2,1)S(1)}, bf16[384,128]{1,0:T(8,128)(2,1)S(1)}, f32[5,128]{1,0:T(8,128)S(1)}) custom-call(s32[2]{0:T(128)S(1)} %pad_add_fusion.1.place_ref), custom_call_target="tpu_custom_call" | custom-call | tf_op jit(solution)/shard_map/pallas_call | solution.py:602
  24.4 0.7 collective-permute-done.7.refs_16_
  25.1 6.4 %shard_map.54 = (f32[2,4,104,128]{3,2,1,0:T(8,128)S(1)}, f32[424,128]{1,0:T(8,128)S(1)}, f32[416,128]{1,0:T(8,128)S(1)}, f32[8,128]{1,0:T(8,128)S(1)}, bf16[2,5,104,128]{3,2,1,0:T(8,128)(2,1)S(1)}) custom-call(s32[6]{0:T(128)S(1)} %stack.31.place_ref.refs_0_, f32[2,4,104,128]{3,2,1,0:T(8,128)S(1)} %get-tuple-element.30.refs_1_, ...), custom_call_target="tpu_custom_call" | custom-call | tf_op jit(solution)/shard_map/pallas_call | solution.py:602
  31.6 0.9 collective-permute-start.9
  33.1 3.9 %collective-permute-start.12 = (f32[16,128]{1,0:T(8,128)S(1)}, f32[16,128]{1,0:T(8,128)S(1)}, u32[]{:S(2)}, u32[]{:S(2)}) collective-permute-start(f32[16,128]{1,0:T(8,128)S(1)} %pad_maximum_fusion.1), channel_id=1, source_target_pairs={{0,6},{1,7},{2,4},{3,5},{4,2},{5,3},{6,0},{7,1},{8,14},{9,15},{10,... | collective-permute-start | bytes 24584 | tf_op jit(solution)/shard_map/ppermute | solution.py:591
  37.6 3.0 %collective-permute-done.12.refs_16_ = f32[16,128]{1,0:T(8,128)S(1)} collective-permute-done((f32[16,128]{1,0:T(8,128)S(1)}, f32[16,128]{1,0:T(8,128)S(1)}, u32[]{:S(2)}, u32[]{:S(2)}) %collective-permute-start.12) | collective-permute-done | bytes 8224 | tf_op jit(solution)/shard_map/ppermute | solution.py:591
  40.6 0.9 collective-permute-done.11.refs_15_
  41.5 6.4 %shard_map.55 = (f32[2,4,104,128]{3,2,1,0:T(8,128)S(1)}, f32[424,128]{1,0:T(8,128)S(1)}, f32[416,128]{1,0:T(8,128)S(1)}, f32[8,128]{1,0:T(8,128)S(1)}) custom-call(s32[6]{0:T(128)S(1)} %stack.31.place_ref.refs_0_, f32[2,4,104,128]{3,2,1,0:T(8,128)S(1)} %get-tuple-element.41.refs_1_, f32[424,128]{1,0:T(8,128)S(1)} %collective-permute-done.8.refs_2_, ...), custom_call_target="tpu_custom_call" | custom-call | tf_op jit(solution)/shard_map/pallas_call | solution.py:602
  48.6 0.8 collective-permute-done.13.refs_2_
  49.4 4.1 %collective-permute-start.17 = (f32[16,128]{1,0:T(8,128)S(1)}, f32[16,128]{1,0:T(8,128)S(1)}, u32[]{:S(2)}, u32[]{:S(2)}) collective-permute-start(f32[16,128]{1,0:T(8,128)S(1)} %pad_maximum_fusion.2), channel_id=1, source_target_pairs={{0,6},{1,7},{2,4},{3,5},{4,2},{5,3},{6,0},{7,1},{8,14},{9,15},{10,... | collective-permute-start | bytes 24584 | tf_op jit(solution)/shard_map/ppermute | solution.py:591
  54.2 3.3 %collective-permute-done.17.refs_16_ = f32[16,128]{1,0:T(8,128)S(1)} collective-permute-done((f32[16,128]{1,0:T(8,128)S(1)}, f32[16,128]{1,0:T(8,128)S(1)}, u32[]{:S(2)}, u32[]{:S(2)}) %collective-permute-start.17) | collective-permute-done | bytes 8224 | tf_op jit(solution)/shard_map/ppermute | solution.py:591
  58.1 6.4 %shard_map.56 = (f32[2,4,104,128]{3,2,1,0:T(8,128)S(1)}, f32[424,128]{1,0:T(8,128)S(1)}, f32[416,128]{1,0:T(8,128)S(1)}, f32[8,128]{1,0:T(8,128)S(1)}) custom-call(s32[6]{0:T(128)S(1)} %stack.31.place_ref.refs_0_, f32[2,4,104,128]{3,2,1,0:T(8,128)S(1)} %get-tuple-element.46.refs_1_, f32[424,128]{1,0:T(8,128)S(1)} %collective-permute-done.13.refs_2_, ...), custom_call_target="tpu_custom_call" | custom-call | tf_op jit(solution)/shard_map/pallas_call | solution.py:602
  64.5 0.9 %collective-permute-start.19 = (f32[416,128]{1,0:T(8,128)S(1)}, f32[416,128]{1,0:T(8,128)S(1)}, u32[]{:S(2)}, u32[]{:S(2)}) collective-permute-start(f32[416,128]{1,0:T(8,128)S(1)} %get-tuple-element.52), channel_id=1, source_target_pairs={{1,2},{2,1},{3,4},{4,3},{5,6},{6,5},{9,10},{10,9},{11,12},{12,11},... | collective-permute-start | bytes 638984 | tf_op jit(solution)/shard_map/ppermute | solution.py:584
  66.0 4.3 %collective-permute-start.22 = (f32[16,128]{1,0:T(8,128)S(1)}, f32[16,128]{1,0:T(8,128)S(1)}, u32[]{:S(2)}, u32[]{:S(2)}) collective-permute-start(f32[16,128]{1,0:T(8,128)S(1)} %pad_maximum_fusion.3), channel_id=1, source_target_pairs={{0,6},{1,7},{2,4},{3,5},{4,2},{5,3},{6,0},{7,1},{8,14},{9,15},{10,... | collective-permute-start | bytes 24584 | tf_op jit(solution)/shard_map/ppermute | solution.py:591
  71.0 3.2 %collective-permute-done.22.refs_16_ = f32[16,128]{1,0:T(8,128)S(1)} collective-permute-done((f32[16,128]{1,0:T(8,128)S(1)}, f32[16,128]{1,0:T(8,128)S(1)}, u32[]{:S(2)}, u32[]{:S(2)}) %collective-permute-start.22) | collective-permute-done | bytes 8224 | tf_op jit(solution)/shard_map/ppermute | solution.py:591
  74.1 0.7 collective-permute-done.21.refs_15_
  74.9 5.7 %shard_map.57 = (f32[200,100]{1,0:T(8,128)S(1)}, f32[200,100]{1,0:T(8,128)}, f32[8,128]{1,0:T(8,128)S(1)}) custom-call(s32[6]{0:T(128)S(1)} %stack.31.place_ref.refs_0_, f32[2,4,104,128]{3,2,1,0:T(8,128)S(1)} %get-tuple-element.50.refs_1_, f32[424,128]{1,0:T(8,128)S(1)} %collective-permute-done.18.refs_2_, f32[416,128]{1,0:T(8,128)S(1)} %collective-permute-done.19.refs_3_, ...), custom_call_target="tpu_custom_call" | custom-call | tf_op jit(solution)/shard_map/pallas_call | solution.py:602
  80.5 1.2 %collective-permute-done.23.refs_1_ = f32[8,128]{1,0:T(8,128)S(1)} collective-permute-done((f32[8,128]{1,0:T(8,128)S(1)}, f32[8,128]{1,0:T(8,128)S(1)}, u32[]{:S(2)}, u32[]{:S(2)}) %collective-permute-start.23) | collective-permute-done | bytes 4128 | tf_op jit(solution)/shard_map/ppermute | solution.py:688
  81.7 1.5 %collective-permute-start.26 = (f32[16,128]{1,0:T(8,128)S(1)}, f32[16,128]{1,0:T(8,128)S(1)}, u32[]{:S(2)}, u32[]{:S(2)}) collective-permute-start(f32[16,128]{1,0:T(8,128)S(1)} %constant_dynamic-update-slice_fusion), channel_id=1, source_target_pairs={{0,6},{1,7},{2,4},{3,5},{4,2},{5,3},{6,0},{7,1},{8,14},{9,15},{10,... | collective-permute-start | bytes 24584 | tf_op jit(solution)/shard_map/ppermute | solution.py:591
  83.7 2.4 %collective-permute-start.24 = (f32[16,128]{1,0:T(8,128)S(1)}, f32[16,128]{1,0:T(8,128)S(1)}, u32[]{:S(2)}, u32[]{:S(2)}) collective-permute-start(f32[16,128]{1,0:T(8,128)S(1)} %constant_dynamic-update-slice_fusion), channel_id=1, source_target_pairs={{0,2},{1,3},{2,0},{3,1},{4,6},{5,7},{6,4},{7,5},{8,10},{9,11},{10,... | collective-permute-start | bytes 24584 | tf_op jit(solution)/shard_map/ppermute | solution.py:591
  86.1 1.1 %collective-permute-done.26.refs_4_ = f32[16,128]{1,0:T(8,128)S(1)} collective-permute-done((f32[16,128]{1,0:T(8,128)S(1)}, f32[16,128]{1,0:T(8,128)S(1)}, u32[]{:S(2)}, u32[]{:S(2)}) %collective-permute-start.26) | collective-permute-done | bytes 8224 | tf_op jit(solution)/shard_map/ppermute | solution.py:591
  87.8 1.8 %shard_map.58 = f32[200,100]{1,0:T(8,128)} custom-call(s32[6]{0:T(128)S(1)} %stack.31.place_ref.refs_0_, f32[200,100]{1,0:T(8,128)S(1)} %get-tuple-element.55.v_ref, bf16[192,768]{1,0:T(8,128)(2,1)S(1)} %get-tuple-element.34.refs_5_.rows_ref, bf16[384,128]{1,0:T(8,128)(2,1)S(1)} %get-tuple-element.56.pull_ref, f32[8,128]{1,0:T(8,128)S(1)} %get-tuple-element.57.refs_0_, ...), custom_call_target="tpu_custom_call" | custom-call | tf_op jit(solution)/shard_map/pallas_call | solution.py:602
  (49 shorter events, 8.2 us)
Async XLA Ops:
  2.4 7.9 %collective-permute-start.2 = (bf16[200,256]{1,0:T(8,128)(2,1)S(1)}, bf16[200,256]{1,0:T(8,128)(2,1)S(1)}, u32[]{:S(2)}, u32[]{:S(2)}) collective-permute-start(bf16[200,256]{1,0:T(8,128)(2,1)S(1)} %pad_add_fusion.refs_1_), channel_id=1, source_target_pairs={{0,24},{8,16},{16,8},{24,0},{1,25},{9,17},{17,9},{25,1},{2,26},{10... | collective-permute-start | bytes 307208 | tf_op jit(solution)/shard_map/ppermute | solution.py:616
  6.3 5.1 %collective-permute-start.1 = (bf16[200,256]{1,0:T(8,128)(2,1)S(1)}, bf16[200,256]{1,0:T(8,128)(2,1)S(1)}, u32[]{:S(2)}, u32[]{:S(2)}) collective-permute-start(bf16[200,256]{1,0:T(8,128)(2,1)S(1)} %pad_add_fusion.refs_1_), channel_id=1, source_target_pairs={{0,16},{8,24},{16,0},{24,8},{1,17},{9,25},{17,1},{25,9},{2,18},{10... | collective-permute-start | bytes 307208 | tf_op jit(solution)/shard_map/ppermute | solution.py:616
  6.8 4.9 %collective-permute-start = (bf16[200,256]{1,0:T(8,128)(2,1)S(1)}, bf16[200,256]{1,0:T(8,128)(2,1)S(1)}, u32[]{:S(2)}, u32[]{:S(2)}) collective-permute-start(bf16[200,256]{1,0:T(8,128)(2,1)S(1)} %pad_add_fusion.refs_1_), channel_id=1, source_target_pairs={{0,8},{8,0},{16,24},{24,16},{1,9},{9,1},{17,25},{25,17},{2,10},{10... | collective-permute-start | bytes 307208 | tf_op jit(solution)/shard_map/ppermute | solution.py:616
  7.0 0.7 copy-start
  7.7 13.0 %copy-start.1 = (bf16[61,61]{1,0:T(8,128)(2,1)S(1)}, bf16[61,61]{1,0:T(8,128)(2,1)}, u32[]{:S(2)}) copy-start(bf16[61,61]{1,0:T(8,128)(2,1)} %psf_ref.3) | copy-start | bytes 22330
  13.7 1.7 %collective-permute-start.3 = (f32[632,128]{1,0:T(8,128)S(1)}, f32[632,128]{1,0:T(8,128)S(1)}, u32[]{:S(2)}, u32[]{:S(2)}) collective-permute-start(f32[632,128]{1,0:T(8,128)S(1)} %get-tuple-element.31), channel_id=1, source_target_pairs={{0,1},{1,0},{2,3},{3,2},{4,5},{5,4},{6,7},{7,6},{8,9},{9,8},{10,11... | collective-permute-start | bytes 970760 | tf_op jit(solution)/shard_map/ppermute | solution.py:584
  13.8 10.6 %collective-permute-start.4 = (f32[624,128]{1,0:T(8,128)S(1)}, f32[624,128]{1,0:T(8,128)S(1)}, u32[]{:S(2)}, u32[]{:S(2)}) collective-permute-start(f32[624,128]{1,0:T(8,128)S(1)} %get-tuple-element.32), channel_id=1, source_target_pairs={{1,2},{2,1},{3,4},{4,3},{5,6},{6,5},{9,10},{10,9},{11,12},{12,11},... | collective-permute-start | bytes 958472 | tf_op jit(solution)/shard_map/ppermute | solution.py:584
  15.4 9.7 %collective-permute-start.7 = (f32[16,128]{1,0:T(8,128)S(1)}, f32[16,128]{1,0:T(8,128)S(1)}, u32[]{:S(2)}, u32[]{:S(2)}) collective-permute-start(f32[16,128]{1,0:T(8,128)S(1)} %pad_maximum_fusion), channel_id=1, source_target_pairs={{0,6},{1,7},{2,4},{3,5},{4,2},{5,3},{6,0},{7,1},{8,14},{9,15},{10,... | collective-permute-start | bytes 24584 | tf_op jit(solution)/shard_map/ppermute | solution.py:591
  20.0 5.2 %collective-permute-start.6 = (f32[16,128]{1,0:T(8,128)S(1)}, f32[16,128]{1,0:T(8,128)S(1)}, u32[]{:S(2)}, u32[]{:S(2)}) collective-permute-start(f32[16,128]{1,0:T(8,128)S(1)} %pad_maximum_fusion), channel_id=1, source_target_pairs={{0,4},{1,5},{2,6},{3,7},{4,0},{5,1},{6,2},{7,3},{8,12},{9,13},{10,... | collective-permute-start | bytes 24584 | tf_op jit(solution)/shard_map/ppermute | solution.py:591
  20.0 5.2 %collective-permute-start.5 = (f32[16,128]{1,0:T(8,128)S(1)}, f32[16,128]{1,0:T(8,128)S(1)}, u32[]{:S(2)}, u32[]{:S(2)}) collective-permute-start(f32[16,128]{1,0:T(8,128)S(1)} %pad_maximum_fusion), channel_id=1, source_target_pairs={{0,2},{1,3},{2,0},{3,1},{4,6},{5,7},{6,4},{7,5},{8,10},{9,11},{10,... | collective-permute-start | bytes 24584 | tf_op jit(solution)/shard_map/ppermute | solution.py:591
  31.6 1.5 %collective-permute-start.8 = (f32[424,128]{1,0:T(8,128)S(1)}, f32[424,128]{1,0:T(8,128)S(1)}, u32[]{:S(2)}, u32[]{:S(2)}) collective-permute-start(f32[424,128]{1,0:T(8,128)S(1)} %get-tuple-element.42), channel_id=1, source_target_pairs={{0,1},{1,0},{2,3},{3,2},{4,5},{5,4},{6,7},{7,6},{8,9},{9,8},{10,11... | collective-permute-start | bytes 651272 | tf_op jit(solution)/shard_map/ppermute | solution.py:584
  31.6 6.0 %collective-permute-start.9 = (f32[416,128]{1,0:T(8,128)S(1)}, f32[416,128]{1,0:T(8,128)S(1)}, u32[]{:S(2)}, u32[]{:S(2)}) collective-permute-start(f32[416,128]{1,0:T(8,128)S(1)} %get-tuple-element.43), channel_id=1, source_target_pairs={{1,2},{2,1},{3,4},{4,3},{5,6},{6,5},{9,10},{10,9},{11,12},{12,11},... | collective-permute-start | bytes 638984 | tf_op jit(solution)/shard_map/ppermute | solution.py:584
  33.1 7.6 %collective-permute-start.12 = (f32[16,128]{1,0:T(8,128)S(1)}, f32[16,128]{1,0:T(8,128)S(1)}, u32[]{:S(2)}, u32[]{:S(2)}) collective-permute-start(f32[16,128]{1,0:T(8,128)S(1)} %pad_maximum_fusion.1), channel_id=1, source_target_pairs={{0,6},{1,7},{2,4},{3,5},{4,2},{5,3},{6,0},{7,1},{8,14},{9,15},{10,... | collective-permute-start | bytes 24584 | tf_op jit(solution)/shard_map/ppermute | solution.py:591
  37.0 4.5 %collective-permute-start.11 = (f32[16,128]{1,0:T(8,128)S(1)}, f32[16,128]{1,0:T(8,128)S(1)}, u32[]{:S(2)}, u32[]{:S(2)}) collective-permute-start(f32[16,128]{1,0:T(8,128)S(1)} %pad_maximum_fusion.1), channel_id=1, source_target_pairs={{0,4},{1,5},{2,6},{3,7},{4,0},{5,1},{6,2},{7,3},{8,12},{9,13},{10,... | collective-permute-start | bytes 24584 | tf_op jit(solution)/shard_map/ppermute | solution.py:591
  37.4 4.1 %collective-permute-start.10 = (f32[16,128]{1,0:T(8,128)S(1)}, f32[16,128]{1,0:T(8,128)S(1)}, u32[]{:S(2)}, u32[]{:S(2)}) collective-permute-start(f32[16,128]{1,0:T(8,128)S(1)} %pad_maximum_fusion.1), channel_id=1, source_target_pairs={{0,2},{1,3},{2,0},{3,1},{4,6},{5,7},{6,4},{7,5},{8,10},{9,11},{10,... | collective-permute-start | bytes 24584 | tf_op jit(solution)/shard_map/ppermute | solution.py:591
  47.9 1.5 %collective-permute-start.13 = (f32[424,128]{1,0:T(8,128)S(1)}, f32[424,128]{1,0:T(8,128)S(1)}, u32[]{:S(2)}, u32[]{:S(2)}) collective-permute-start(f32[424,128]{1,0:T(8,128)S(1)} %get-tuple-element.47), channel_id=1, source_target_pairs={{0,1},{1,0},{2,3},{3,2},{4,5},{5,4},{6,7},{7,6},{8,9},{9,8},{10,11... | collective-permute-start | bytes 651272 | tf_op jit(solution)/shard_map/ppermute | solution.py:584
  47.9 6.3 %collective-permute-start.14 = (f32[416,128]{1,0:T(8,128)S(1)}, f32[416,128]{1,0:T(8,128)S(1)}, u32[]{:S(2)}, u32[]{:S(2)}) collective-permute-start(f32[416,128]{1,0:T(8,128)S(1)} %get-tuple-element.48), channel_id=1, source_target_pairs={{1,2},{2,1},{3,4},{4,3},{5,6},{6,5},{9,10},{10,9},{11,12},{12,11},... | collective-permute-start | bytes 638984 | tf_op jit(solution)/shard_map/ppermute | solution.py:584
  49.4 8.1 %collective-permute-start.17 = (f32[16,128]{1,0:T(8,128)S(1)}, f32[16,128]{1,0:T(8,128)S(1)}, u32[]{:S(2)}, u32[]{:S(2)}) collective-permute-start(f32[16,128]{1,0:T(8,128)S(1)} %pad_maximum_fusion.2), channel_id=1, source_target_pairs={{0,6},{1,7},{2,4},{3,5},{4,2},{5,3},{6,0},{7,1},{8,14},{9,15},{10,... | collective-permute-start | bytes 24584 | tf_op jit(solution)/shard_map/ppermute | solution.py:591
  53.5 4.5 %collective-permute-start.16 = (f32[16,128]{1,0:T(8,128)S(1)}, f32[16,128]{1,0:T(8,128)S(1)}, u32[]{:S(2)}, u32[]{:S(2)}) collective-permute-start(f32[16,128]{1,0:T(8,128)S(1)} %pad_maximum_fusion.2), channel_id=1, source_target_pairs={{0,4},{1,5},{2,6},{3,7},{4,0},{5,1},{6,2},{7,3},{8,12},{9,13},{10,... | collective-permute-start | bytes 24584 | tf_op jit(solution)/shard_map/ppermute | solution.py:591
  53.5 4.5 %collective-permute-start.15 = (f32[16,128]{1,0:T(8,128)S(1)}, f32[16,128]{1,0:T(8,128)S(1)}, u32[]{:S(2)}, u32[]{:S(2)}) collective-permute-start(f32[16,128]{1,0:T(8,128)S(1)} %pad_maximum_fusion.2), channel_id=1, source_target_pairs={{0,2},{1,3},{2,0},{3,1},{4,6},{5,7},{6,4},{7,5},{8,10},{9,11},{10,... | collective-permute-start | bytes 24584 | tf_op jit(solution)/shard_map/ppermute | solution.py:591
  64.5 1.5 %collective-permute-start.18 = (f32[424,128]{1,0:T(8,128)S(1)}, f32[424,128]{1,0:T(8,128)S(1)}, u32[]{:S(2)}, u32[]{:S(2)}) collective-permute-start(f32[424,128]{1,0:T(8,128)S(1)} %get-tuple-element.51), channel_id=1, source_target_pairs={{0,1},{1,0},{2,3},{3,2},{4,5},{5,4},{6,7},{7,6},{8,9},{9,8},{10,11... | collective-permute-start | bytes 651272 | tf_op jit(solution)/shard_map/ppermute | solution.py:584
  64.5 6.5 %collective-permute-start.19 = (f32[416,128]{1,0:T(8,128)S(1)}, f32[416,128]{1,0:T(8,128)S(1)}, u32[]{:S(2)}, u32[]{:S(2)}) collective-permute-start(f32[416,128]{1,0:T(8,128)S(1)} %get-tuple-element.52), channel_id=1, source_target_pairs={{1,2},{2,1},{3,4},{4,3},{5,6},{6,5},{9,10},{10,9},{11,12},{12,11},... | collective-permute-start | bytes 638984 | tf_op jit(solution)/shard_map/ppermute | solution.py:584
  66.0 8.2 %collective-permute-start.22 = (f32[16,128]{1,0:T(8,128)S(1)}, f32[16,128]{1,0:T(8,128)S(1)}, u32[]{:S(2)}, u32[]{:S(2)}) collective-permute-start(f32[16,128]{1,0:T(8,128)S(1)} %pad_maximum_fusion.3), channel_id=1, source_target_pairs={{0,6},{1,7},{2,4},{3,5},{4,2},{5,3},{6,0},{7,1},{8,14},{9,15},{10,... | collective-permute-start | bytes 24584 | tf_op jit(solution)/shard_map/ppermute | solution.py:591
  70.3 4.5 %collective-permute-start.21 = (f32[16,128]{1,0:T(8,128)S(1)}, f32[16,128]{1,0:T(8,128)S(1)}, u32[]{:S(2)}, u32[]{:S(2)}) collective-permute-start(f32[16,128]{1,0:T(8,128)S(1)} %pad_maximum_fusion.3), channel_id=1, source_target_pairs={{0,4},{1,5},{2,6},{3,7},{4,0},{5,1},{6,2},{7,3},{8,12},{9,13},{10,... | collective-permute-start | bytes 24584 | tf_op jit(solution)/shard_map/ppermute | solution.py:591
  70.3 4.5 %collective-permute-start.20 = (f32[16,128]{1,0:T(8,128)S(1)}, f32[16,128]{1,0:T(8,128)S(1)}, u32[]{:S(2)}, u32[]{:S(2)}) collective-permute-start(f32[16,128]{1,0:T(8,128)S(1)} %pad_maximum_fusion.3), channel_id=1, source_target_pairs={{0,2},{1,3},{2,0},{3,1},{4,6},{5,7},{6,4},{7,5},{8,10},{9,11},{10,... | collective-permute-start | bytes 24584 | tf_op jit(solution)/shard_map/ppermute | solution.py:591
  80.5 1.2 %collective-permute-start.23 = (f32[8,128]{1,0:T(8,128)S(1)}, f32[8,128]{1,0:T(8,128)S(1)}, u32[]{:S(2)}, u32[]{:S(2)}) collective-permute-start(f32[8,128]{1,0:T(8,128)S(1)} %get-tuple-element.57.refs_0_), channel_id=1, source_target_pairs={{0,1},{1,0},{2,3},{3,2},{4,5},{5,4},{6,7},{7,6},{8,9},{9,8},{10,11... | collective-permute-start | bytes 12296 | tf_op jit(solution)/shard_map/ppermute | solution.py:688
  81.7 5.5 %collective-permute-start.26 = (f32[16,128]{1,0:T(8,128)S(1)}, f32[16,128]{1,0:T(8,128)S(1)}, u32[]{:S(2)}, u32[]{:S(2)}) collective-permute-start(f32[16,128]{1,0:T(8,128)S(1)} %constant_dynamic-update-slice_fusion), channel_id=1, source_target_pairs={{0,6},{1,7},{2,4},{3,5},{4,2},{5,3},{6,0},{7,1},{8,14},{9,15},{10,... | collective-permute-start | bytes 24584 | tf_op jit(solution)/shard_map/ppermute | solution.py:591
  83.2 4.6 %collective-permute-start.25 = (f32[16,128]{1,0:T(8,128)S(1)}, f32[16,128]{1,0:T(8,128)S(1)}, u32[]{:S(2)}, u32[]{:S(2)}) collective-permute-start(f32[16,128]{1,0:T(8,128)S(1)} %constant_dynamic-update-slice_fusion), channel_id=1, source_target_pairs={{0,4},{1,5},{2,6},{3,7},{4,0},{5,1},{6,2},{7,3},{8,12},{9,13},{10,... | collective-permute-start | bytes 24584 | tf_op jit(solution)/shard_map/ppermute | solution.py:591
  83.7 4.1 %collective-permute-start.24 = (f32[16,128]{1,0:T(8,128)S(1)}, f32[16,128]{1,0:T(8,128)S(1)}, u32[]{:S(2)}, u32[]{:S(2)}) collective-permute-start(f32[16,128]{1,0:T(8,128)S(1)} %constant_dynamic-update-slice_fusion), channel_id=1, source_target_pairs={{0,2},{1,3},{2,0},{3,1},{4,6},{5,7},{6,4},{7,5},{8,10},{9,11},{10,... | collective-permute-start | bytes 24584 | tf_op jit(solution)/shard_map/ppermute | solution.py:591

commit v8 on v7

--- a/solution.py
+++ b/solution.py
@@ -250,18 +250,26 @@
     return pull, dot(one_side(levels, 1), back_ref[...])
 
 
+def both_kernel(dose_ref, target_ref, out_ref):
+    cols = dose_ref.shape[1]
+    out_ref[...] = jnp.zeros_like(out_ref)
+    out_ref[:, :cols] = dose_ref[...]
+    out_ref[:, LANES:LANES + cols] = target_ref[...].astype(f32).astype(bf16)
+
+
 def start_kernel(
-    sizes, place_ref, *refs
+    sizes, partner, *refs
 ):
     planes, depth, half, cols, crow, ncx = sizes
-    pieces, refs = refs[1:-9], refs[-9:]
+    pieces, refs = refs[2:-9], refs[-9:]
     own_out, mask_out, a_out, b_out, red_out, rows_out, cells_out, plane_ref, wide_ref = refs
     owner = group((depth, LANES))
-    even = place_ref[1] == 0
+    stripe = lax.axis_index("stripe")
+    even = lax.axis_index("scan") % 2 == 0
     for part in range(2):
         for k, piece in enumerate(pieces):
             rows = piece.shape[0]
-            first = pl.multiple_of(place_ref[2 + k] * rows, 8)
+            first = pl.multiple_of(partner(stripe, k) * rows, 8)
             wide_ref[part, pl.ds(first, rows), :] = piece[:, part * LANES:(part + 1) * LANES].astype(f32)
         for r in range(PHASES):
             value = wide_ref[part, pl.ds(r, planes, stride=PHASES), :]
@@ -308,15 +316,15 @@
 
 def step_kernel(sizes, count, first, last, *refs):
     planes, depth, half, cols, crow, ncx = sizes
-    place_ref, own_ref, from_a_ref, from_b_ref, mask_ref = refs[:5]
-    rows_ref, pull_ref, back_ref, inside_ref, in_row_ref, in_cell_ref, fwd_ref, adj_ref = refs[5:13]
-    red_refs, refs = refs[13:13 + count], refs[13 + count:]
+    own_ref, from_a_ref, from_b_ref, mask_ref = refs[:4]
+    rows_ref, pull_ref, back_ref, inside_ref, in_row_ref, in_cell_ref, fwd_ref = refs[4:11]
+    red_refs, refs = refs[11:11 + count], refs[11 + count:]
     if last:
-        v_out, resist_out, red_out = refs[:3]
-        x_ref, e_ref, line_ref, tile_line_ref, acc_ref, part_ref, row_ref = refs[3:]
+        e_out, x_out, resist_out, red_out = refs[:4]
+        x_ref, e_ref, line_ref, acc_ref, part_ref = refs[4:]
     else:
-        v_out, a_out, b_out, red_out = refs[:4]
-        refs = refs[4:]
+        adj_ref, v_out, a_out, b_out, red_out = refs[:5]
+        refs = refs[5:]
         if first:
             mask_out, refs = refs[0], refs[1:]
         x_ref, e_ref, line_ref, tile_line_ref, acc_ref, part_ref = refs
@@ -324,7 +332,7 @@
     blocks = acc_ref.shape[1]
     tile_blocks = own_ref.shape[1]
     at = place((depth, LANES))
-    even = place_ref[1] == 0
+    even = lax.axis_index("scan") % 2 == 0
     halo_tiles = from_b_ref.shape[0] // (PAIR * depth)
 
     def from_left(n, t):
@@ -403,36 +411,15 @@
     red_out[:, half:] = by_columns(RIM, crow, cell_rows(sums, ncx, blocks), half)
 
     if last:
-        part = v_out.shape[0] // PHASES
-        height = round_up(part, 8)
-        window = round_up(part + 2 * FIRST_SHIFT, 8)
-        start = place_ref[0] * part
-        lane = iota2((height, LANES), 1)
-
-        def to_rows(tile, origin, count):
-            for r in range(PHASES):
-                n, k = divmod(r, PER)
-                value = None
-                for b in reversed(range(count)):
-                    turned = roll(tile(n, b), SPAN * (b - k) - origin)
-                    if value is None:
-                        value = turned
-                    else:
-                        value = jnp.where(lane < SPAN * (b + 1) - origin, turned, value)
-                row_ref[pl.ds(r, part, stride=PHASES), :] = value[:part]
-
-        to_rows(lambda n, b: acc_ref[n, b, pl.ds(start, height), :], RIM, blocks)
-        resist_out[...] = row_ref[:, :cols]
-        correlate(
-            lambda n, g: stacked(e_ref, n, g, tile_blocks, start + EDGE - FIRST_SHIFT, window),
-            tile_blocks, window, tile_line_ref, adj_ref, part_ref, acc_ref,
-        )
-        to_rows(
-            lambda n, b: x_ref[n, HALO_BLOCKS + b, pl.ds(start, height), :]
-            - step_length * acc_ref[n, b, pl.ds(FIRST_SHIFT, height), :],
-            0, tile_blocks,
-        )
-        v_out[...] = row_ref[:, :cols]
+        height = x_out.shape[2]
+        start = lax.axis_index("stripe") * (planes // lax.axis_size("stripe"))
+        for n in range(PAIR):
+            for b in range(blocks):
+                e_out[n, b] = e_ref[n, b, pl.ds(start + EDGE - FIRST_SHIFT, e_out.shape[2]), :]
+                resist_out[n, b] = acc_ref[n, b, pl.ds(start, height), :]
+            e_out[n, blocks] = jnp.zeros(e_out.shape[2:], f32)
+            for b in range(tile_blocks):
+                x_out[n, b] = x_ref[n, HALO_BLOCKS + b, pl.ds(start, height), :]
         red_out[:, :half] = jnp.zeros((8, half), f32)
         return
 
@@ -474,13 +461,53 @@
         a_out[pl.ds(b_out.shape[0], 8), :] = red_out[...]
 
 
-def end_kernel(sizes, place_ref, v_ref, rows_ref, pull_ref, *refs):
+def finish_kernel(
+    e_ref, x_ref, r_ref, adj_ref, v_out, resist_out, line_ref, acc_ref, part_ref, row_ref
+):
+    blocks = x_ref.shape[1]
+    window = e_ref.shape[2]
+    height = x_ref.shape[2]
+    part = v_out.shape[0] // PHASES
+    cols = v_out.shape[1]
+    lane = iota2((height, LANES), 1)
+
+    def to_rows(tile, origin, count):
+        for r in range(PHASES):
+            n, k = divmod(r, PER)
+            value = None
+            for b in reversed(range(count)):
+                turned = roll(tile(n, b), SPAN * (b - k) - origin)
+                if value is None:
+                    value = turned
+                else:
+                    value = jnp.where(lane < SPAN * (b + 1) - origin, turned, value)
+            row_ref[pl.ds(r, part, stride=PHASES), :] = value[:part]
+
+    to_rows(lambda n, b: r_ref[n, b], RIM, r_ref.shape[1])
+    resist_out[...] = row_ref[:, :cols]
+    ends = part_ref.shape[2] - EDGE
+    for n in range(PAIR):
+        for m in range(SHIFTS):
+            part_ref[n, m, pl.ds(0, EDGE), :] = jnp.zeros((EDGE, LANES), f32)
+            part_ref[n, m, pl.ds(ends, EDGE), :] = jnp.zeros((EDGE, LANES), f32)
+    correlate(
+        lambda n, g: stacked(e_ref, n, g, blocks, 0, window),
+        blocks, window, line_ref, adj_ref, part_ref, acc_ref,
+    )
+    to_rows(
+        lambda n, b: x_ref[n, b] - step_length * acc_ref[n, b, pl.ds(FIRST_SHIFT, height), :],
+        0, blocks,
+    )
+    v_out[...] = row_ref[:, :cols]
+
+
+def end_kernel(sizes, v_ref, rows_ref, pull_ref, *refs):
     red_refs, out_ref = refs[:-1], refs[-1]
     planes, depth, half, cols, crow, ncx = sizes
     pull = coarse([ref[...] for ref in red_refs], rows_ref, pull_ref, None, half)
     pull = jnp.concatenate(split(pull, 2), axis=0)
     rows = v_ref.shape[0]
-    row = iota2((rows, 2 * half), 0) + place_ref[0] * rows
+    row = iota2((rows, 2 * half), 0) + lax.axis_index("stripe") * rows
     cell = iota2((rows, 2 * half), 1)
     cell = jnp.where(cell >= half, cell - half, cell)
     table = ((row >= cell * COARSE) & (row < cell * COARSE + COARSE)).astype(f32).astype(bf16)
@@ -500,9 +527,11 @@
     return jnp.where((cell + 1) * COARSE <= column, cell + 1, cell)
 
 
-def tables_kernel(sizes, ncy, place_ref, rows_out, pull_out, back_out, end_out, inside_out):
+def tables_kernel(sizes, ncy, swapped, rows_out, pull_out, back_out, end_out, inside_out):
     planes, depth, half, cols, crow, ncx = sizes
-    first_column = place_ref[0] * cols
+    scan = lax.axis_index("scan")
+    first_column = scan * cols
+    turn = scan if swapped else 0
     blocks = inside_out.shape[0]
     columns_all = ncy * COARSE
 
@@ -522,7 +551,7 @@
 
     def held(shape):
         line = iota2(shape, 0)
-        return ((line // 8) ^ place_ref[1]) * crow + line % 8, line % 8 < crow
+        return ((line // 8) ^ turn) * crow + line % 8, line % 8 < crow
 
     lines = pull_out.shape[0] // 6
 
@@ -557,15 +586,16 @@
     rows, cols = dose.shape
     stripes = lax.axis_size("stripe")
     scans = lax.axis_size("scan")
-    stripe = lax.axis_index("stripe")
-    scan = lax.axis_index("scan")
     if stripes & (stripes - 1):
         partners = [[(i, (i + k) % stripes) for i in range(stripes)] for k in range(1, stripes)]
-        sources = [(stripe - k) % stripes for k in range(1, stripes)]
     else:
         partners = [[(i, i ^ k) for i in range(stripes)] for k in range(1, stripes)]
-        sources = [stripe ^ k for k in range(1, stripes)]
-    place = jnp.stack([stripe, scan % 2, stripe, *sources]).astype(jnp.int32)
+
+    def partner(stripe, k):
+        if stripes & (stripes - 1):
+            return lax.rem(stripe + (stripes - k), stripes)
+        return stripe ^ k
+
     planes = rows * stripes // PHASES
     depth = round_up(planes + FIRST_SHIFT, 8)
     ncx = rows * stripes // COARSE
@@ -595,14 +625,13 @@
         return [lax.all_to_all(jnp.broadcast_to(red, (scans,) + red.shape), "scan", 0, 0)]
 
     vmem = pl.BlockSpec(memory_space=pltpu.VMEM)
-    smem = pl.BlockSpec(memory_space=pltpu.SMEM)
     def call(kernel, out_shape, args, scratch=()):
         held = sum(math.prod(a.shape) * jnp.dtype(a.dtype).itemsize for a in scratch)
         params = pltpu.CompilerParams(vmem_limit_bytes=held + 4 * 1024 * 1024)
         return pl.pallas_call(
             kernel,
             out_shape=out_shape,
-            in_specs=[smem if a.ndim == 1 else vmem for a in args],
+            in_specs=[vmem] * len(args),
             scratch_shapes=list(scratch),
             compiler_params=params,
         )(*args)
@@ -610,20 +639,18 @@
     def array(shape, dtype=f32):
         return jax.ShapeDtypeStruct(shape, dtype)
 
-    both = jnp.pad(dose, ((0, 0), (0, 2 * LANES - cols))) + jnp.pad(
-        target.astype(bf16), ((0, 0), (LANES, LANES - cols))
-    )
+    both = call(both_kernel, array((rows, 2 * LANES), bf16), [dose, target])
     pieces = [both] + [lax.ppermute(both, "stripe", pairs) for pairs in partners]
 
     lines = 6 * 8 * scans
     rows_table, pull_table, back_table, end_table, inside = call(
-        functools.partial(tables_kernel, sizes, ncy),
+        functools.partial(tables_kernel, sizes, ncy, swapped),
         [
             array((3 * half, 12 * half), bf16), array((lines, wide_blocks * LANES), bf16),
             array((2 * lines, blocks * LANES), bf16), array((lines, LANES), bf16),
             array((blocks, LANES)),
         ],
-        [jnp.stack([scan, scan if swapped else jnp.zeros_like(scan)]).astype(jnp.int32)],
+        [],
     )
     fwd = bands(psf, SPARE, False)
 
@@ -636,46 +663,54 @@
     mask_tiles = array((PAIR, blocks, depth, LANES), bf16)
     tiles = array((PAIR, tile_blocks, depth, LANES))
     own, mask, to_a, to_b, red, in_row, in_cell = call(
-        functools.partial(start_kernel, sizes),
+        functools.partial(start_kernel, sizes, partner),
         [
             tiles, mask_tiles, *halos(HALO_BLOCKS + 1), few,
             array((PAIR, depth, PER * 2 * ncx), bf16), array((PAIR, PER * ncx, depth), bf16),
         ],
-        [place, fwd, *pieces],
+        [fwd, rows_table, *pieces],
         [pltpu.VMEM((2, PHASES, depth, LANES), f32), pltpu.VMEM((2, planes * PHASES, LANES), f32)],
     )
     adj = bands(psf, 0, True)
-    tables = [rows_table, pull_table, back_table, inside, in_row, in_cell, fwd, adj]
+    tables = [rows_table, pull_table, back_table, inside, in_row, in_cell, fwd]
 
     height = round_up(blocks * depth, 16)
+    tile_height = round_up(tile_blocks * depth, 16)
+    line = PAIR * REACH * LANES
+
+    def products(height):
+        return pltpu.VMEM((PAIR, SHIFTS, height + 2 * EDGE, LANES), f32)
+
     def step_scratch(last):
-        return [
+        scratch = [
             pltpu.VMEM((PAIR, wide_blocks, depth + EDGE * last, LANES), f32),
             pltpu.VMEM((PAIR, blocks + 1, depth + 2 * EDGE * last, LANES), f32),
-        ] + scratch
-
-    window = round_up(rows // PHASES + 2 * FIRST_SHIFT, 8)
-    tile_height = round_up(tile_blocks * depth, 16)
-    scratch = [
-        pltpu.VMEM((height, PAIR * REACH * LANES), bf16),
-        pltpu.VMEM((tile_height, PAIR * REACH * LANES), bf16),
-        pltpu.VMEM((PAIR, blocks, depth + EDGE, LANES), f32),
-        pltpu.VMEM((PAIR, SHIFTS, height + 2 * EDGE, LANES), f32),
-    ]
+            pltpu.VMEM((height, line), bf16),
+        ]
+        if not last:
+            scratch.append(pltpu.VMEM((tile_height, line), bf16))
+        return scratch + [pltpu.VMEM((PAIR, blocks, depth + EDGE, LANES), f32), products(height)]
+
+    own_planes = rows // PHASES
+    own_depth = round_up(own_planes, 8)
+    window = round_up(own_planes + 2 * FIRST_SHIFT, 8)
     tile = array((rows, cols))
     for step in range(ITERS):
         first = step == 0
         last = step == ITERS - 1
         from_a, from_b = swap(to_a, to_b)
         shared = [red] + spread_pairs(red, from_a[from_b.shape[0]:]) if swapped else share(red)
-        args = [place, own, from_a, from_b, mask, *tables, *shared]
+        args = [own, from_a, from_b, mask, *tables, *shared]
         kernel = functools.partial(step_kernel, sizes, len(shared), first, last)
         if last:
-            some = step_scratch(True)
-            some[3] = pltpu.VMEM((round_up(tile_blocks * window, 16), PAIR * REACH * LANES), bf16)
-            some.append(pltpu.VMEM((rows, LANES), f32))
-            v, resist, red = call(kernel, [tile, tile, few], args, some)
-        elif first:
+            shape = [
+                array((PAIR, blocks + 1, window, LANES)), array((PAIR, tile_blocks, own_depth, LANES)),
+                array((PAIR, blocks, own_depth, LANES)), few,
+            ]
+            error, current, resist, red = call(kernel, shape, args, step_scratch(True))
+            continue
+        args.append(adj)
+        if first:
             own, to_a, to_b, red, mask = call(
                 kernel, [tiles, *halos(HALO_BLOCKS), few, mask_tiles], args, step_scratch(False)
             )
@@ -684,6 +719,18 @@
                 kernel, [tiles, *halos(HALO_BLOCKS), few], args, step_scratch(False)
             )
 
+    last_height = round_up(tile_blocks * window, 16)
+    v, resist = call(
+        finish_kernel,
+        [tile, tile],
+        [error, current, resist, adj],
+        [
+            pltpu.VMEM((last_height, line), bf16),
+            pltpu.VMEM((PAIR, tile_blocks, window, LANES), f32),
+            products(last_height),
+            pltpu.VMEM((rows, LANES), f32),
+        ],
+    )
     if swapped:
         other = lax.ppermute(red, "scan", swap_a)
         shared = [red, other] + spread_pairs(red, other)
@@ -692,7 +739,7 @@
     updated = call(
         functools.partial(end_kernel, sizes),
         tile,
-        [place, v, rows_table, end_table, *shared],
+        [v, rows_table, end_table, *shared],
     )
     return resist, updated
 

time: 89.9 us -> 85.3 us (0.949)
  Pallas kernels: 34.8 us -> 31.5 us
  other arithmetic: 1.82 us -> 0.02 us
  local copies, waits for them, and re-layouts: 0.82 us -> 2.42 us
  waiting for transfers between devices: 19.6 us -> 18.7 us
    pallas_call x7 -> x9, Pallas kernels: 29.8 us -> 26.5 us  [call(): pl.pallas_call(kernel, out_shape=out_shape, in_specs=[vmem] * len(args),...]
    unnamed x5 -> x9, local copies, waits for them, and re-layouts: 0.72 us -> 2.41 us
    convert_element_type x1 -> x0, other arithmetic: 0.9 us -> none  [per_device(): target.astype(bf16)]
  transfers between devices with their start and end apart: 27 -> 27, of which waited for: 17 -> 16; matrix products, arithmetic and copies ran while one was open for 0% -> 0% of each run, Pallas kernels for 7% -> 8%
where the time goes in v8:
time: 85.3 us; the launch traced here: 85 us
  starting transfers between devices  31.6 us (37%)
  Pallas kernels  31.5 us (37%)
  waiting for transfers between devices  18.7 us (22%)
  local copies, waits for them, and re-layouts  2.42 us (3%)
    pallas_call x9, Pallas kernels, call(): pl.pallas_call(kernel, out_shape=out_shape, in_specs=[vmem] * len(args),...  26.5 us
    ppermute x15, starting transfers between devices, spread_pairs(): lax.ppermute(pair, 'scan', [(i, i ^ k) for i in range(scans)])  23.7 us
    ppermute x15, waiting for transfers between devices, spread_pairs(): lax.ppermute(pair, 'scan', [(i, i ^ k) for i in range(scans)])  13.7 us
    pallas_call x2, Pallas kernels, bands(): pl.pallas_call(functools.partial(bands_kernel, offset, flip), out_shape=j...  5.04 us
    ppermute x3, starting transfers between devices, per_device(): lax.ppermute(both, 'stripe', pairs)  4.6 us
    ppermute x4, starting transfers between devices, swap(): lax.ppermute(to_b, 'scan', swap_b)  3.17 us
    ppermute x4, waiting for transfers between devices, swap(): lax.ppermute(to_a, 'scan', swap_a)  2.91 us
    unnamed x9, local copies, waits for them, and re-layouts  2.41 us
  transfers between devices with their start and end apart: 27, of which 16 were waited for; matrix products, arithmetic and copies ran while one was open for 0% of the time, Pallas kernels for 8%

profile of v8, /device:TPU:0, one launch (start us, length us, event | category | flops | bytes accessed | tf_op | source)
XLA Modules:
  0.0 85.0 jit_solution(15947285853232931075)
XLA Ops:
  0.6 0.9 %copy-done = s32[200,100]{1,0:T(8,128)S(1)} copy-done((s32[200,100]{1,0:T(8,128)S(1)}, s32[200,100]{1,0:T(8,128)}, u32[]{:S(2)}) %copy-start) | copy-done | bytes 80024
  1.5 0.8 copy-done.3
  2.4 4.0 %collective-permute-start.2 = (bf16[200,256]{1,0:T(8,128)(2,1)S(1)}, bf16[200,256]{1,0:T(8,128)(2,1)S(1)}, u32[]{:S(2)}, u32[]{:S(2)}) collective-permute-start(bf16[200,256]{1,0:T(8,128)(2,1)S(1)} %shard_map.52.refs_2_), channel_id=1, source_target_pairs={{0,24},{8,16},{16,8},{24,0},{1,25},{9,17},{17,9},{25,1},{2,26},{10... | collective-permute-start | bytes 307208 | tf_op jit(solution)/shard_map/ppermute | solution.py:643
  7.6 0.7 copy-done.1
  8.3 2.5 %shard_map.50.refs_0_.refs_10_ = bf16[3,2432,128]{2,1,0:T(8,128)(2,1)S(1)} custom-call(bf16[61,61]{1,0:T(8,128)(2,1)S(1)} %copy-done.1), custom_call_target="tpu_custom_call" | custom-call | tf_op jit(solution)/shard_map/pallas_call | solution.py:141
  11.7 1.5 %shard_map.53 = (f32[2,4,104,128]{3,2,1,0:T(8,128)S(1)}, bf16[2,5,104,128]{3,2,1,0:T(8,128)(2,1)S(1)}, f32[632,128]{1,0:T(8,128)S(1)}, f32[624,128]{1,0:T(8,128)...) custom-call(bf16[3,2432,128]{2,1,0:T(8,128)(2,1)S(1)} %shard_map.50.refs_0_.refs_10_,, ...), custom_call_target="tpu_custom_call" | custom-call | tf_op jit(solution)/shard_map/pallas_call | solution.py:631
  13.3 0.7 collective-permute-start.4
  14.0 0.9 %collective-permute-done.3.refs_1_ = f32[632,128]{1,0:T(8,128)S(1)} collective-permute-done((f32[632,128]{1,0:T(8,128)S(1)}, f32[632,128]{1,0:T(8,128)S(1)}, u32[]{:S(2)}, u32[]{:S(2)}) %collective-permute-start.3) | collective-permute-done | bytes 323616 | tf_op jit(solution)/shard_map/ppermute | solution.py:614
  14.9 4.5 %collective-permute-start.7 = (f32[16,128]{1,0:T(8,128)S(1)}, f32[16,128]{1,0:T(8,128)S(1)}, u32[]{:S(2)}, u32[]{:S(2)}) collective-permute-start(f32[16,128]{1,0:T(8,128)S(1)} %pad_maximum_fusion), channel_id=1, source_target_pairs={{0,6},{1,7},{2,4},{3,5},{4,2},{5,3},{6,0},{7,1},{8,14},{9,15},{10,... | collective-permute-start | bytes 24584 | tf_op jit(solution)/shard_map/ppermute | solution.py:621
  20.1 2.6 %shard_map.54.refs_15_.adj_ref = bf16[3,2432,128]{2,1,0:T(8,128)(2,1)S(1)} custom-call(bf16[61,61]{1,0:T(8,128)(2,1)S(1)} %copy-done.2), custom_call_target="tpu_custom_call" | custom-call | tf_op jit(solution)/shard_map/pallas_call | solution.py:141
  22.7 1.9 %collective-permute-done.7.refs_14_ = f32[16,128]{1,0:T(8,128)S(1)} collective-permute-done((f32[16,128]{1,0:T(8,128)S(1)}, f32[16,128]{1,0:T(8,128)S(1)}, u32[]{:S(2)}, u32[]{:S(2)}) %collective-permute-start.7) | collective-permute-done | bytes 8224 | tf_op jit(solution)/shard_map/ppermute | solution.py:621
  24.6 5.9 %shard_map.55 = (f32[2,4,104,128]{3,2,1,0:T(8,128)S(1)}, f32[424,128]{1,0:T(8,128)S(1)}, f32[416,128]{1,0:T(8,128)S(1)}, f32[8,128]{1,0:T(8,128)S(1)}, bf16[2,5,104,128]{3,2,1,0:T(8,128)(2,1)S(1)}) custom-call(f32[2,4,104,128]{3,2,1,0:T(8,128)S(1)} %get-tuple-element.34.refs_0_, f32[632,128]{1,0:T(8,128)S(1)} %collective-permute-done.3.refs_1_, ...), custom_call_target="tpu_custom_call" | custom-call | tf_op jit(solution)/shard_map/pallas_call | solution.py:631
  30.5 0.9 %collective-permute-start.9 = (f32[416,128]{1,0:T(8,128)S(1)}, f32[416,128]{1,0:T(8,128)S(1)}, u32[]{:S(2)}, u32[]{:S(2)}) collective-permute-start(f32[416,128]{1,0:T(8,128)S(1)} %get-tuple-element.46), channel_id=1, source_target_pairs={{1,2},{2,1},{3,4},{4,3},{5,6},{6,5},{9,10},{10,9},{11,12},{12,11},... | collective-permute-start | bytes 638984 | tf_op jit(solution)/shard_map/ppermute | solution.py:614
  32.0 3.7 %collective-permute-start.12 = (f32[16,128]{1,0:T(8,128)S(1)}, f32[16,128]{1,0:T(8,128)S(1)}, u32[]{:S(2)}, u32[]{:S(2)}) collective-permute-start(f32[16,128]{1,0:T(8,128)S(1)} %pad_maximum_fusion.1), channel_id=1, source_target_pairs={{0,6},{1,7},{2,4},{3,5},{4,2},{5,3},{6,0},{7,1},{8,14},{9,15},{10,... | collective-permute-start | bytes 24584 | tf_op jit(solution)/shard_map/ppermute | solution.py:621
  36.4 3.1 %collective-permute-done.12.refs_14_ = f32[16,128]{1,0:T(8,128)S(1)} collective-permute-done((f32[16,128]{1,0:T(8,128)S(1)}, f32[16,128]{1,0:T(8,128)S(1)}, u32[]{:S(2)}, u32[]{:S(2)}) %collective-permute-start.12) | collective-permute-done | bytes 8224 | tf_op jit(solution)/shard_map/ppermute | solution.py:621
  39.6 0.7 collective-permute-done.11.refs_13_
  40.2 5.9 %shard_map.56 = (f32[2,4,104,128]{3,2,1,0:T(8,128)S(1)}, f32[424,128]{1,0:T(8,128)S(1)}, f32[416,128]{1,0:T(8,128)S(1)}, f32[8,128]{1,0:T(8,128)S(1)}) custom-call(f32[2,4,104,128]{3,2,1,0:T(8,128)S(1)} %get-tuple-element.44.refs_0_, f32[424,128]{1,0:T(8,128)S(1)} %collective-permute-done.8.refs_1_, f32[416,128]{1,0:T(8,128)S(1)} %collective-permute-done.9.refs_2_, ...), custom_call_target="tpu_custom_call" | custom-call | tf_op jit(solution)/shard_map/pallas_call | solution.py:631
  46.1 0.7 collective-permute-start.14
  46.8 0.8 collective-permute-done.13.refs_1_
  47.6 4.1 %collective-permute-start.17 = (f32[16,128]{1,0:T(8,128)S(1)}, f32[16,128]{1,0:T(8,128)S(1)}, u32[]{:S(2)}, u32[]{:S(2)}) collective-permute-start(f32[16,128]{1,0:T(8,128)S(1)} %pad_maximum_fusion.2), channel_id=1, source_target_pairs={{0,6},{1,7},{2,4},{3,5},{4,2},{5,3},{6,0},{7,1},{8,14},{9,15},{10,... | collective-permute-start | bytes 24584 | tf_op jit(solution)/shard_map/ppermute | solution.py:621
  52.4 3.3 %collective-permute-done.17.refs_14_ = f32[16,128]{1,0:T(8,128)S(1)} collective-permute-done((f32[16,128]{1,0:T(8,128)S(1)}, f32[16,128]{1,0:T(8,128)S(1)}, u32[]{:S(2)}, u32[]{:S(2)}) %collective-permute-start.17) | collective-permute-done | bytes 8224 | tf_op jit(solution)/shard_map/ppermute | solution.py:621
  56.3 5.9 %shard_map.57 = (f32[2,4,104,128]{3,2,1,0:T(8,128)S(1)}, f32[424,128]{1,0:T(8,128)S(1)}, f32[416,128]{1,0:T(8,128)S(1)}, f32[8,128]{1,0:T(8,128)S(1)}) custom-call(f32[2,4,104,128]{3,2,1,0:T(8,128)S(1)} %get-tuple-element.49.refs_0_, f32[424,128]{1,0:T(8,128)S(1)} %collective-permute-done.13.refs_1_, f32[416,128]{1,0:T(8,128)S(1)} %collective-permute-done.14.refs_2_, ...), custom_call_target="tpu_custom_call" | custom-call | tf_op jit(solution)/shard_map/pallas_call | solution.py:631
  62.2 0.9 %collective-permute-start.19 = (f32[416,128]{1,0:T(8,128)S(1)}, f32[416,128]{1,0:T(8,128)S(1)}, u32[]{:S(2)}, u32[]{:S(2)}) collective-permute-start(f32[416,128]{1,0:T(8,128)S(1)} %get-tuple-element.55), channel_id=1, source_target_pairs={{1,2},{2,1},{3,4},{4,3},{5,6},{6,5},{9,10},{10,9},{11,12},{12,11},... | collective-permute-start | bytes 638984 | tf_op jit(solution)/shard_map/ppermute | solution.py:614
  63.7 4.3 %collective-permute-start.22 = (f32[16,128]{1,0:T(8,128)S(1)}, f32[16,128]{1,0:T(8,128)S(1)}, u32[]{:S(2)}, u32[]{:S(2)}) collective-permute-start(f32[16,128]{1,0:T(8,128)S(1)} %pad_maximum_fusion.3), channel_id=1, source_target_pairs={{0,6},{1,7},{2,4},{3,5},{4,2},{5,3},{6,0},{7,1},{8,14},{9,15},{10,... | collective-permute-start | bytes 24584 | tf_op jit(solution)/shard_map/ppermute | solution.py:621
  68.7 3.2 %collective-permute-done.22.refs_14_ = f32[16,128]{1,0:T(8,128)S(1)} collective-permute-done((f32[16,128]{1,0:T(8,128)S(1)}, f32[16,128]{1,0:T(8,128)S(1)}, u32[]{:S(2)}, u32[]{:S(2)}) %collective-permute-start.22) | collective-permute-done | bytes 8224 | tf_op jit(solution)/shard_map/ppermute | solution.py:621
  71.9 0.7 collective-permute-done.21.refs_13_
  72.6 3.9 %shard_map.58 = (f32[2,6,40,128]{3,2,1,0:T(8,128)S(1)}, f32[2,4,32,128]{3,2,1,0:T(8,128)S(1)}, f32[2,5,32,128]{3,2,1,0:T(8,128)S(1)}, f32[8,128]{1,0:T(8,128)S(1)}) custom-call(f32[2,4,104,128]{3,2,1,0:T(8,128)S(1)} %get-tuple-element.53.refs_0_, f32[424,128]{1,0:T(8,128)S(1)} %collective-permute-done.18.refs_1_, ...), custom_call_target="tpu_custom_call" | custom-call | tf_op jit(solution)/shard_map/pallas_call | solution.py:631
  76.5 1.2 %collective-permute-done.23.refs_1_ = f32[8,128]{1,0:T(8,128)S(1)} collective-permute-done((f32[8,128]{1,0:T(8,128)S(1)}, f32[8,128]{1,0:T(8,128)S(1)}, u32[]{:S(2)}, u32[]{:S(2)}) %collective-permute-start.23) | collective-permute-done | bytes 4128 | tf_op jit(solution)/shard_map/ppermute | solution.py:735
  77.6 1.5 %collective-permute-start.26 = (f32[16,128]{1,0:T(8,128)S(1)}, f32[16,128]{1,0:T(8,128)S(1)}, u32[]{:S(2)}, u32[]{:S(2)}) collective-permute-start(f32[16,128]{1,0:T(8,128)S(1)} %constant_dynamic-update-slice_fusion), channel_id=1, source_target_pairs={{0,6},{1,7},{2,4},{3,5},{4,2},{5,3},{6,0},{7,1},{8,14},{9,15},{10,... | collective-permute-start | bytes 24584 | tf_op jit(solution)/shard_map/ppermute | solution.py:621
  79.7 2.4 %collective-permute-start.24 = (f32[16,128]{1,0:T(8,128)S(1)}, f32[16,128]{1,0:T(8,128)S(1)}, u32[]{:S(2)}, u32[]{:S(2)}) collective-permute-start(f32[16,128]{1,0:T(8,128)S(1)} %constant_dynamic-update-slice_fusion), channel_id=1, source_target_pairs={{0,2},{1,3},{2,0},{3,1},{4,6},{5,7},{6,4},{7,5},{8,10},{9,11},{10,... | collective-permute-start | bytes 24584 | tf_op jit(solution)/shard_map/ppermute | solution.py:621
  82.0 1.6 %shard_map.59 = (f32[200,100]{1,0:T(8,128)S(1)}, f32[200,100]{1,0:T(8,128)}) custom-call(f32[2,6,40,128]{3,2,1,0:T(8,128)S(1)} %get-tuple-element.57.e_ref, f32[2,4,32,128]{3,2,1,0:T(8,128)S(1)} %get-tuple-element.58.x_ref, f32[2,5,32,128]{3,2,1,0:T(8,128)S(1)} %get-tuple-element.59.r_ref, bf16[3,2432,128]{2,1,0:T(8,128)(2,1)S(1)} %shard_map.54.refs_15_.adj_ref), custom_call_target="tpu_custom_call" | custom-call | tf_op jit(solution)/shard_map/pallas_call | solution.py:631
  83.7 1.2 %shard_map.60 = f32[200,100]{1,0:T(8,128)} custom-call(f32[200,100]{1,0:T(8,128)S(1)} %get-tuple-element.61.v_ref, bf16[192,768]{1,0:T(8,128)(2,1)S(1)} %get-tuple-element.33.refs_1_.refs_4_.rows_ref, bf16[384,128]{1,0:T(8,128)(2,1)S(1)} %get-tuple-element.62.pull_ref, f32[8,128]{1,0:T(8,128)S(1)} %get-tuple-element.63.refs_0_, ...), custom_call_target="tpu_custom_call" | custom-call | tf_op jit(solution)/shard_map/pallas_call | solution.py:631
  (51 shorter events, 7.5 us)
Async XLA Ops:
  0.6 0.9 %copy-start = (s32[200,100]{1,0:T(8,128)S(1)}, s32[200,100]{1,0:T(8,128)}, u32[]{:S(2)}) copy-start(s32[200,100]{1,0:T(8,128)} %target_ref.1) | copy-start | bytes 240004
  1.5 0.8 copy-start.3
  2.4 8.4 %collective-permute-start.2 = (bf16[200,256]{1,0:T(8,128)(2,1)S(1)}, bf16[200,256]{1,0:T(8,128)(2,1)S(1)}, u32[]{:S(2)}, u32[]{:S(2)}) collective-permute-start(bf16[200,256]{1,0:T(8,128)(2,1)S(1)} %shard_map.52.refs_2_), channel_id=1, source_target_pairs={{0,24},{8,16},{16,8},{24,0},{1,25},{9,17},{17,9},{25,1},{2,26},{10... | collective-permute-start | bytes 307208 | tf_op jit(solution)/shard_map/ppermute | solution.py:643
  6.3 5.1 %collective-permute-start.1 = (bf16[200,256]{1,0:T(8,128)(2,1)S(1)}, bf16[200,256]{1,0:T(8,128)(2,1)S(1)}, u32[]{:S(2)}, u32[]{:S(2)}) collective-permute-start(bf16[200,256]{1,0:T(8,128)(2,1)S(1)} %shard_map.52.refs_2_), channel_id=1, source_target_pairs={{0,16},{8,24},{16,0},{24,8},{1,17},{9,25},{17,1},{25,9},{2,18},{10... | collective-permute-start | bytes 307208 | tf_op jit(solution)/shard_map/ppermute | solution.py:643
  6.8 4.9 %collective-permute-start = (bf16[200,256]{1,0:T(8,128)(2,1)S(1)}, bf16[200,256]{1,0:T(8,128)(2,1)S(1)}, u32[]{:S(2)}, u32[]{:S(2)}) collective-permute-start(bf16[200,256]{1,0:T(8,128)(2,1)S(1)} %shard_map.52.refs_2_), channel_id=1, source_target_pairs={{0,8},{8,0},{16,24},{24,16},{1,9},{9,1},{17,25},{25,17},{2,10},{10... | collective-permute-start | bytes 307208 | tf_op jit(solution)/shard_map/ppermute | solution.py:643
  7.6 0.7 copy-start.1
  8.3 11.8 %copy-start.2 = (bf16[61,61]{1,0:T(8,128)(2,1)S(1)}, bf16[61,61]{1,0:T(8,128)(2,1)}, u32[]{:S(2)}) copy-start(bf16[61,61]{1,0:T(8,128)(2,1)} %psf_ref.3) | copy-start | bytes 22330
  13.2 1.7 %collective-permute-start.3 = (f32[632,128]{1,0:T(8,128)S(1)}, f32[632,128]{1,0:T(8,128)S(1)}, u32[]{:S(2)}, u32[]{:S(2)}) collective-permute-start(f32[632,128]{1,0:T(8,128)S(1)} %get-tuple-element.35), channel_id=1, source_target_pairs={{0,1},{1,0},{2,3},{3,2},{4,5},{5,4},{6,7},{7,6},{8,9},{9,8},{10,11... | collective-permute-start | bytes 970760 | tf_op jit(solution)/shard_map/ppermute | solution.py:614
  13.3 9.4 %collective-permute-start.4 = (f32[624,128]{1,0:T(8,128)S(1)}, f32[624,128]{1,0:T(8,128)S(1)}, u32[]{:S(2)}, u32[]{:S(2)}) collective-permute-start(f32[624,128]{1,0:T(8,128)S(1)} %get-tuple-element.36), channel_id=1, source_target_pairs={{1,2},{2,1},{3,4},{4,3},{5,6},{6,5},{9,10},{10,9},{11,12},{12,11},... | collective-permute-start | bytes 958472 | tf_op jit(solution)/shard_map/ppermute | solution.py:614
  14.9 9.7 %collective-permute-start.7 = (f32[16,128]{1,0:T(8,128)S(1)}, f32[16,128]{1,0:T(8,128)S(1)}, u32[]{:S(2)}, u32[]{:S(2)}) collective-permute-start(f32[16,128]{1,0:T(8,128)S(1)} %pad_maximum_fusion), channel_id=1, source_target_pairs={{0,6},{1,7},{2,4},{3,5},{4,2},{5,3},{6,0},{7,1},{8,14},{9,15},{10,... | collective-permute-start | bytes 24584 | tf_op jit(solution)/shard_map/ppermute | solution.py:621
  19.4 5.2 %collective-permute-start.6 = (f32[16,128]{1,0:T(8,128)S(1)}, f32[16,128]{1,0:T(8,128)S(1)}, u32[]{:S(2)}, u32[]{:S(2)}) collective-permute-start(f32[16,128]{1,0:T(8,128)S(1)} %pad_maximum_fusion), channel_id=1, source_target_pairs={{0,4},{1,5},{2,6},{3,7},{4,0},{5,1},{6,2},{7,3},{8,12},{9,13},{10,... | collective-permute-start | bytes 24584 | tf_op jit(solution)/shard_map/ppermute | solution.py:621
  19.4 5.2 %collective-permute-start.5 = (f32[16,128]{1,0:T(8,128)S(1)}, f32[16,128]{1,0:T(8,128)S(1)}, u32[]{:S(2)}, u32[]{:S(2)}) collective-permute-start(f32[16,128]{1,0:T(8,128)S(1)} %pad_maximum_fusion), channel_id=1, source_target_pairs={{0,2},{1,3},{2,0},{3,1},{4,6},{5,7},{6,4},{7,5},{8,10},{9,11},{10,... | collective-permute-start | bytes 24584 | tf_op jit(solution)/shard_map/ppermute | solution.py:621
  30.5 1.5 %collective-permute-start.8 = (f32[424,128]{1,0:T(8,128)S(1)}, f32[424,128]{1,0:T(8,128)S(1)}, u32[]{:S(2)}, u32[]{:S(2)}) collective-permute-start(f32[424,128]{1,0:T(8,128)S(1)} %get-tuple-element.45), channel_id=1, source_target_pairs={{0,1},{1,0},{2,3},{3,2},{4,5},{5,4},{6,7},{7,6},{8,9},{9,8},{10,11... | collective-permute-start | bytes 651272 | tf_op jit(solution)/shard_map/ppermute | solution.py:614
  30.5 5.9 %collective-permute-start.9 = (f32[416,128]{1,0:T(8,128)S(1)}, f32[416,128]{1,0:T(8,128)S(1)}, u32[]{:S(2)}, u32[]{:S(2)}) collective-permute-start(f32[416,128]{1,0:T(8,128)S(1)} %get-tuple-element.46), channel_id=1, source_target_pairs={{1,2},{2,1},{3,4},{4,3},{5,6},{6,5},{9,10},{10,9},{11,12},{12,11},... | collective-permute-start | bytes 638984 | tf_op jit(solution)/shard_map/ppermute | solution.py:614
  32.0 7.5 %collective-permute-start.12 = (f32[16,128]{1,0:T(8,128)S(1)}, f32[16,128]{1,0:T(8,128)S(1)}, u32[]{:S(2)}, u32[]{:S(2)}) collective-permute-start(f32[16,128]{1,0:T(8,128)S(1)} %pad_maximum_fusion.1), channel_id=1, source_target_pairs={{0,6},{1,7},{2,4},{3,5},{4,2},{5,3},{6,0},{7,1},{8,14},{9,15},{10,... | collective-permute-start | bytes 24584 | tf_op jit(solution)/shard_map/ppermute | solution.py:621
  35.7 4.5 %collective-permute-start.11 = (f32[16,128]{1,0:T(8,128)S(1)}, f32[16,128]{1,0:T(8,128)S(1)}, u32[]{:S(2)}, u32[]{:S(2)}) collective-permute-start(f32[16,128]{1,0:T(8,128)S(1)} %pad_maximum_fusion.1), channel_id=1, source_target_pairs={{0,4},{1,5},{2,6},{3,7},{4,0},{5,1},{6,2},{7,3},{8,12},{9,13},{10,... | collective-permute-start | bytes 24584 | tf_op jit(solution)/shard_map/ppermute | solution.py:621
  36.3 3.9 %collective-permute-start.10 = (f32[16,128]{1,0:T(8,128)S(1)}, f32[16,128]{1,0:T(8,128)S(1)}, u32[]{:S(2)}, u32[]{:S(2)}) collective-permute-start(f32[16,128]{1,0:T(8,128)S(1)} %pad_maximum_fusion.1), channel_id=1, source_target_pairs={{0,2},{1,3},{2,0},{3,1},{4,6},{5,7},{6,4},{7,5},{8,10},{9,11},{10,... | collective-permute-start | bytes 24584 | tf_op jit(solution)/shard_map/ppermute | solution.py:621
  46.1 1.5 %collective-permute-start.13 = (f32[424,128]{1,0:T(8,128)S(1)}, f32[424,128]{1,0:T(8,128)S(1)}, u32[]{:S(2)}, u32[]{:S(2)}) collective-permute-start(f32[424,128]{1,0:T(8,128)S(1)} %get-tuple-element.50), channel_id=1, source_target_pairs={{0,1},{1,0},{2,3},{3,2},{4,5},{5,4},{6,7},{7,6},{8,9},{9,8},{10,11... | collective-permute-start | bytes 651272 | tf_op jit(solution)/shard_map/ppermute | solution.py:614
  46.1 6.3 %collective-permute-start.14 = (f32[416,128]{1,0:T(8,128)S(1)}, f32[416,128]{1,0:T(8,128)S(1)}, u32[]{:S(2)}, u32[]{:S(2)}) collective-permute-start(f32[416,128]{1,0:T(8,128)S(1)} %get-tuple-element.51), channel_id=1, source_target_pairs={{1,2},{2,1},{3,4},{4,3},{5,6},{6,5},{9,10},{10,9},{11,12},{12,11},... | collective-permute-start | bytes 638984 | tf_op jit(solution)/shard_map/ppermute | solution.py:614
  47.6 8.1 %collective-permute-start.17 = (f32[16,128]{1,0:T(8,128)S(1)}, f32[16,128]{1,0:T(8,128)S(1)}, u32[]{:S(2)}, u32[]{:S(2)}) collective-permute-start(f32[16,128]{1,0:T(8,128)S(1)} %pad_maximum_fusion.2), channel_id=1, source_target_pairs={{0,6},{1,7},{2,4},{3,5},{4,2},{5,3},{6,0},{7,1},{8,14},{9,15},{10,... | collective-permute-start | bytes 24584 | tf_op jit(solution)/shard_map/ppermute | solution.py:621
  51.8 4.5 %collective-permute-start.16 = (f32[16,128]{1,0:T(8,128)S(1)}, f32[16,128]{1,0:T(8,128)S(1)}, u32[]{:S(2)}, u32[]{:S(2)}) collective-permute-start(f32[16,128]{1,0:T(8,128)S(1)} %pad_maximum_fusion.2), channel_id=1, source_target_pairs={{0,4},{1,5},{2,6},{3,7},{4,0},{5,1},{6,2},{7,3},{8,12},{9,13},{10,... | collective-permute-start | bytes 24584 | tf_op jit(solution)/shard_map/ppermute | solution.py:621
  51.8 4.5 %collective-permute-start.15 = (f32[16,128]{1,0:T(8,128)S(1)}, f32[16,128]{1,0:T(8,128)S(1)}, u32[]{:S(2)}, u32[]{:S(2)}) collective-permute-start(f32[16,128]{1,0:T(8,128)S(1)} %pad_maximum_fusion.2), channel_id=1, source_target_pairs={{0,2},{1,3},{2,0},{3,1},{4,6},{5,7},{6,4},{7,5},{8,10},{9,11},{10,... | collective-permute-start | bytes 24584 | tf_op jit(solution)/shard_map/ppermute | solution.py:621
  62.2 1.5 %collective-permute-start.18 = (f32[424,128]{1,0:T(8,128)S(1)}, f32[424,128]{1,0:T(8,128)S(1)}, u32[]{:S(2)}, u32[]{:S(2)}) collective-permute-start(f32[424,128]{1,0:T(8,128)S(1)} %get-tuple-element.54), channel_id=1, source_target_pairs={{0,1},{1,0},{2,3},{3,2},{4,5},{5,4},{6,7},{7,6},{8,9},{9,8},{10,11... | collective-permute-start | bytes 651272 | tf_op jit(solution)/shard_map/ppermute | solution.py:614
  62.2 6.5 %collective-permute-start.19 = (f32[416,128]{1,0:T(8,128)S(1)}, f32[416,128]{1,0:T(8,128)S(1)}, u32[]{:S(2)}, u32[]{:S(2)}) collective-permute-start(f32[416,128]{1,0:T(8,128)S(1)} %get-tuple-element.55), channel_id=1, source_target_pairs={{1,2},{2,1},{3,4},{4,3},{5,6},{6,5},{9,10},{10,9},{11,12},{12,11},... | collective-permute-start | bytes 638984 | tf_op jit(solution)/shard_map/ppermute | solution.py:614
  63.7 8.2 %collective-permute-start.22 = (f32[16,128]{1,0:T(8,128)S(1)}, f32[16,128]{1,0:T(8,128)S(1)}, u32[]{:S(2)}, u32[]{:S(2)}) collective-permute-start(f32[16,128]{1,0:T(8,128)S(1)} %pad_maximum_fusion.3), channel_id=1, source_target_pairs={{0,6},{1,7},{2,4},{3,5},{4,2},{5,3},{6,0},{7,1},{8,14},{9,15},{10,... | collective-permute-start | bytes 24584 | tf_op jit(solution)/shard_map/ppermute | solution.py:621
  68.0 4.5 %collective-permute-start.21 = (f32[16,128]{1,0:T(8,128)S(1)}, f32[16,128]{1,0:T(8,128)S(1)}, u32[]{:S(2)}, u32[]{:S(2)}) collective-permute-start(f32[16,128]{1,0:T(8,128)S(1)} %pad_maximum_fusion.3), channel_id=1, source_target_pairs={{0,4},{1,5},{2,6},{3,7},{4,0},{5,1},{6,2},{7,3},{8,12},{9,13},{10,... | collective-permute-start | bytes 24584 | tf_op jit(solution)/shard_map/ppermute | solution.py:621
  68.0 4.5 %collective-permute-start.20 = (f32[16,128]{1,0:T(8,128)S(1)}, f32[16,128]{1,0:T(8,128)S(1)}, u32[]{:S(2)}, u32[]{:S(2)}) collective-permute-start(f32[16,128]{1,0:T(8,128)S(1)} %pad_maximum_fusion.3), channel_id=1, source_target_pairs={{0,2},{1,3},{2,0},{3,1},{4,6},{5,7},{6,4},{7,5},{8,10},{9,11},{10,... | collective-permute-start | bytes 24584 | tf_op jit(solution)/shard_map/ppermute | solution.py:621
  76.4 1.2 %collective-permute-start.23 = (f32[8,128]{1,0:T(8,128)S(1)}, f32[8,128]{1,0:T(8,128)S(1)}, u32[]{:S(2)}, u32[]{:S(2)}) collective-permute-start(f32[8,128]{1,0:T(8,128)S(1)} %get-tuple-element.63.refs_0_), channel_id=1, source_target_pairs={{0,1},{1,0},{2,3},{3,2},{4,5},{5,4},{6,7},{7,6},{8,9},{9,8},{10,11... | collective-permute-start | bytes 12296 | tf_op jit(solution)/shard_map/ppermute | solution.py:735
  77.6 5.9 %collective-permute-start.26 = (f32[16,128]{1,0:T(8,128)S(1)}, f32[16,128]{1,0:T(8,128)S(1)}, u32[]{:S(2)}, u32[]{:S(2)}) collective-permute-start(f32[16,128]{1,0:T(8,128)S(1)} %constant_dynamic-update-slice_fusion), channel_id=1, source_target_pairs={{0,6},{1,7},{2,4},{3,5},{4,2},{5,3},{6,0},{7,1},{8,14},{9,15},{10,... | collective-permute-start | bytes 24584 | tf_op jit(solution)/shard_map/ppermute | solution.py:621
  79.1 4.6 %collective-permute-start.25 = (f32[16,128]{1,0:T(8,128)S(1)}, f32[16,128]{1,0:T(8,128)S(1)}, u32[]{:S(2)}, u32[]{:S(2)}) collective-permute-start(f32[16,128]{1,0:T(8,128)S(1)} %constant_dynamic-update-slice_fusion), channel_id=1, source_target_pairs={{0,4},{1,5},{2,6},{3,7},{4,0},{5,1},{6,2},{7,3},{8,12},{9,13},{10,... | collective-permute-start | bytes 24584 | tf_op jit(solution)/shard_map/ppermute | solution.py:621
  79.7 4.1 %collective-permute-start.24 = (f32[16,128]{1,0:T(8,128)S(1)}, f32[16,128]{1,0:T(8,128)S(1)}, u32[]{:S(2)}, u32[]{:S(2)}) collective-permute-start(f32[16,128]{1,0:T(8,128)S(1)} %constant_dynamic-update-slice_fusion), channel_id=1, source_target_pairs={{0,2},{1,3},{2,0},{3,1},{4,6},{5,7},{6,4},{7,5},{8,10},{9,11},{10,... | collective-permute-start | bytes 24584 | tf_op jit(solution)/shard_map/ppermute | solution.py:621

commit v9 on v8

--- a/solution.py
+++ b/solution.py
@@ -314,18 +314,20 @@
         a_out[pl.ds(b_out.shape[0], 8), :] = red_out[...]
 
 
-def step_kernel(sizes, count, first, last, *refs):
+def step_kernel(sizes, count, first_step, last, *refs):
     planes, depth, half, cols, crow, ncx = sizes
     own_ref, from_a_ref, from_b_ref, mask_ref = refs[:4]
     rows_ref, pull_ref, back_ref, inside_ref, in_row_ref, in_cell_ref, fwd_ref = refs[4:11]
     red_refs, refs = refs[11:11 + count], refs[11 + count:]
+    if not first_step:
+        halo_ref, refs = refs[0], refs[1:]
     if last:
         e_out, x_out, resist_out, red_out = refs[:4]
         x_ref, e_ref, line_ref, acc_ref, part_ref = refs[4:]
     else:
-        adj_ref, v_out, a_out, b_out, red_out = refs[:5]
-        refs = refs[5:]
-        if first:
+        adj_ref, v_out, a_out, b_out, red_out, halo_out = refs[:6]
+        refs = refs[6:]
+        if first_step:
             mask_out, refs = refs[0], refs[1:]
         x_ref, e_ref, line_ref, tile_line_ref, acc_ref, part_ref = refs
     wide_blocks = x_ref.shape[1]
@@ -333,17 +335,21 @@
     tile_blocks = own_ref.shape[1]
     at = place((depth, LANES))
     even = lax.axis_index("scan") % 2 == 0
-    halo_tiles = from_b_ref.shape[0] // (PAIR * depth)
+    filled = iota2((depth, LANES), 0) < planes
+    halo_lines = from_b_ref.shape[0]
+    halo_tiles = halo_lines // (PAIR * depth)
+    from_a = from_a_ref[...].astype(f32)
+    from_b = from_b_ref[...].astype(f32)
 
     def from_left(n, t):
-        lines = pl.ds((n * halo_tiles + t) * depth, depth)
-        return jnp.where(even, from_b_ref[lines, :], from_a_ref[lines, :])
+        first = (n * halo_tiles + t) * depth
+        value = jnp.where(even, from_b[first:first + depth], from_a[first:first + depth])
+        return value if first_step or t >= HALO_BLOCKS else halo_ref[n, t] - value
 
     def from_right(n, t):
-        lines = pl.ds((n * halo_tiles + t) * depth, depth)
-        return jnp.where(even, from_a_ref[lines, :], from_b_ref[lines, :])
-
-    filled = iota2((depth, LANES), 0) < planes
+        first = (n * halo_tiles + t) * depth
+        value = jnp.where(even, from_a[first:first + depth], from_b[first:first + depth])
+        return value if first_step or t >= HALO_BLOCKS else halo_ref[n, HALO_BLOCKS + t] - value
 
     ends = part_ref.shape[2] - EDGE
     for n in range(PAIR):
@@ -358,7 +364,11 @@
 
     pieces = [ref[...] for ref in red_refs]
     if from_a_ref.shape != from_b_ref.shape:
-        pieces.insert(1, from_a_ref[pl.ds(from_b_ref.shape[0], 8), :])
+        other = from_a[halo_lines:halo_lines + 8]
+        if not first_step:
+            for k in range(1, 3):
+                other += from_a[halo_lines + 8 * k:halo_lines + 8 * k + 8]
+        pieces.insert(1, other)
     pull, back = coarse(pieces, rows_ref, pull_ref, back_ref, half)
     pull = over_rows(pull, ncx, wide_blocks)
     back = over_rows(back, ncx, blocks)
@@ -376,7 +386,12 @@
             else:
                 value = from_right(n, 1)
             value = value - pulled[:, b * LANES:(b + 1) * LANES]
-            x_ref[n, b, pl.ds(0, depth), :] = value.astype(bf16).astype(f32)
+            value = value.astype(bf16).astype(f32)
+            x_ref[n, b, pl.ds(0, depth), :] = value
+            if not last and b < HALO_BLOCKS:
+                halo_out[n, b] = value
+            elif not last and b >= wide_blocks - HALO_BLOCKS:
+                halo_out[n, b - wide_blocks + 2 * HALO_BLOCKS] = value
 
     correlate(
         lambda n, g: stacked(x_ref, n, g, blocks, 0, depth),
@@ -390,7 +405,7 @@
         rounded = []
         for b in range(blocks):
             mask = mask_ref[n, b]
-            if first:
+            if first_step:
                 mask = mask.astype(f32)
                 if b == 0:
                     mask = jnp.where(at < RIM, from_left(n, HALO_BLOCKS), mask)
@@ -429,13 +444,16 @@
     )
 
     cells = None
+    to_a = []
+    to_b = []
     for n in range(PAIR):
         fresh = []
+        moves = []
         for b in range(tile_blocks):
-            value = x_ref[n, HALO_BLOCKS + b, pl.ds(0, depth), :] - step_length * acc_ref[
-                n, b, pl.ds(0, depth), :
-            ]
-            value = jnp.where(filled, value, 0.0)
+            move = step_length * acc_ref[n, b, pl.ds(0, depth), :]
+            move = jnp.where(filled, move, 0.0)
+            value = x_ref[n, HALO_BLOCKS + b, pl.ds(0, depth), :] - move
+            moves.append(move)
             fresh.append(value)
             v_out[n, b] = value
         for piece in split(jnp.concatenate(fresh, axis=1), 2):
@@ -444,8 +462,8 @@
 
         def moved(begin):
             b, step = divmod(begin, SPAN)
-            low = roll(fresh[b], -step) if 0 <= b < tile_blocks else None
-            high = roll(fresh[b + 1], SPAN - step) if step and 0 <= b + 1 < tile_blocks else None
+            low = roll(moves[b], -step) if 0 <= b < tile_blocks else None
+            high = roll(moves[b + 1], SPAN - step) if step and 0 <= b + 1 < tile_blocks else None
             if low is None or high is None:
                 return high if low is None else low
             return jnp.where(at < SPAN - step, low, high)
@@ -453,12 +471,16 @@
         for t in range(HALO_BLOCKS):
             to_right = moved(cols - (HALO_BLOCKS - t) * SPAN)
             to_left = moved(SPAN * (tile_blocks - 1 + t) - cols)
-            lines = pl.ds((n * HALO_BLOCKS + t) * depth, depth)
-            a_out[lines, :] = jnp.where(even, to_right, to_left)
-            b_out[lines, :] = jnp.where(even, to_left, to_right)
-    red_out[:, :half] = by_columns(0, crow, cell_rows(cells, ncx, tile_blocks), half)
-    if a_out.shape != b_out.shape:
-        a_out[pl.ds(b_out.shape[0], 8), :] = red_out[...]
+            to_a.append(jnp.where(even, to_right, to_left))
+            to_b.append(jnp.where(even, to_left, to_right))
+    b_out[...] = jnp.concatenate(to_b, axis=0).astype(bf16)
+    cells = by_columns(0, crow, cell_rows(cells, ncx, tile_blocks), half)
+    red_out[:, :half] = cells
+    rest = a_out.shape[0] - b_out.shape[0]
+    if rest:
+        to_a += [piece.astype(f32) for piece in split(red_out[...], 3)]
+        to_a.append(jnp.zeros((rest - 24, LANES), f32))
+    a_out[...] = jnp.concatenate(to_a, axis=0).astype(bf16)
 
 
 def finish_kernel(
@@ -660,6 +682,10 @@
         lines = PAIR * count * depth
         return [array((lines + 8 * swapped, LANES)), array((lines, LANES))]
 
+    lines = round_up(PAIR * HALO_BLOCKS * depth, 16)
+    moves = [array((lines + 32 * swapped, LANES), bf16), array((lines, LANES), bf16)]
+    halo_shape = array((PAIR, 2 * HALO_BLOCKS, depth, LANES))
+
     mask_tiles = array((PAIR, blocks, depth, LANES), bf16)
     tiles = array((PAIR, tile_blocks, depth, LANES))
     own, mask, to_a, to_b, red, in_row, in_cell = call(
@@ -699,8 +725,16 @@
         first = step == 0
         last = step == ITERS - 1
         from_a, from_b = swap(to_a, to_b)
-        shared = [red] + spread_pairs(red, from_a[from_b.shape[0]:]) if swapped else share(red)
+        if swapped:
+            other = from_a[from_b.shape[0]:].astype(f32)
+            if not first:
+                other = other[:8] + other[8:16] + other[16:24]
+            shared = [red] + spread_pairs(red, other)
+        else:
+            shared = share(red)
         args = [own, from_a, from_b, mask, *tables, *shared]
+        if not first:
+            args.append(held)
         kernel = functools.partial(step_kernel, sizes, len(shared), first, last)
         if last:
             shape = [
@@ -711,12 +745,12 @@
             continue
         args.append(adj)
         if first:
-            own, to_a, to_b, red, mask = call(
-                kernel, [tiles, *halos(HALO_BLOCKS), few, mask_tiles], args, step_scratch(False)
+            own, to_a, to_b, red, held, mask = call(
+                kernel, [tiles, *moves, few, halo_shape, mask_tiles], args, step_scratch(False)
             )
         else:
-            own, to_a, to_b, red = call(
-                kernel, [tiles, *halos(HALO_BLOCKS), few], args, step_scratch(False)
+            own, to_a, to_b, red, held = call(
+                kernel, [tiles, *moves, few, halo_shape], args, step_scratch(False)
             )
 
     last_height = round_up(tile_blocks * window, 16)

time: 85.3 us -> 85.3 us (level)
    unnamed x9 -> x7, local copies, waits for them, and re-layouts: 2.41 us -> 2.41 us
where the time goes in v9:
time: 85.3 us; the launch traced here: 85 us
  starting transfers between devices  32 us (38%)
  Pallas kernels  31.4 us (37%)
  waiting for transfers between devices  18.4 us (22%)
  local copies, waits for them, and re-layouts  2.41 us (3%)
    pallas_call x9, Pallas kernels, call(): pl.pallas_call(kernel, out_shape=out_shape, in_specs=[vmem] * len(args),...  26.3 us
    ppermute x15, starting transfers between devices, spread_pairs(): lax.ppermute(pair, 'scan', [(i, i ^ k) for i in range(scans)])  24.1 us
    ppermute x15, waiting for transfers between devices, spread_pairs(): lax.ppermute(pair, 'scan', [(i, i ^ k) for i in range(scans)])  13.8 us
    pallas_call x2, Pallas kernels, bands(): pl.pallas_call(functools.partial(bands_kernel, offset, flip), out_shape=j...  5.04 us
    ppermute x3, starting transfers between devices, per_device(): lax.ppermute(both, 'stripe', pairs)  4.6 us
    ppermute x4, starting transfers between devices, swap(): lax.ppermute(to_b, 'scan', swap_b)  3.08 us
    ppermute x4, waiting for transfers between devices, swap(): lax.ppermute(to_a, 'scan', swap_a)  2.47 us
    unnamed x7, local copies, waits for them, and re-layouts  2.41 us
  transfers between devices with their start and end apart: 27, of which 16 were waited for; matrix products, arithmetic and copies ran while one was open for 0% of the time, Pallas kernels for 8%

profile of v9, /device:TPU:0, one launch (start us, length us, event | category | flops | bytes accessed | tf_op | source)
XLA Modules:
  0.0 85.0 jit_solution(6908899511727209511)
XLA Ops:
  0.6 0.9 %copy-done = s32[200,100]{1,0:T(8,128)S(1)} copy-done((s32[200,100]{1,0:T(8,128)S(1)}, s32[200,100]{1,0:T(8,128)}, u32[]{:S(2)}) %copy-start) | copy-done | bytes 80024
  1.5 0.8 copy-done.2
  2.4 4.0 %collective-permute-start.2 = (bf16[200,256]{1,0:T(8,128)(2,1)S(1)}, bf16[200,256]{1,0:T(8,128)(2,1)S(1)}, u32[]{:S(2)}, u32[]{:S(2)}) collective-permute-start(bf16[200,256]{1,0:T(8,128)(2,1)S(1)} %shard_map.52.refs_2_), channel_id=1, source_target_pairs={{0,24},{8,16},{16,8},{24,0},{1,25},{9,17},{17,9},{25,1},{2,26},{10... | collective-permute-start | bytes 307208 | tf_op jit(solution)/shard_map/ppermute | solution.py:665
  7.6 0.7 copy-done.1
  8.3 2.5 %shard_map.50.refs_0_.refs_10_ = bf16[3,2432,128]{2,1,0:T(8,128)(2,1)S(1)} custom-call(bf16[61,61]{1,0:T(8,128)(2,1)S(1)} %copy-done.1), custom_call_target="tpu_custom_call" | custom-call | tf_op jit(solution)/shard_map/pallas_call | solution.py:141
  11.7 1.5 %shard_map.53 = (f32[2,4,104,128]{3,2,1,0:T(8,128)S(1)}, bf16[2,5,104,128]{3,2,1,0:T(8,128)(2,1)S(1)}, f32[632,128]{1,0:T(8,128)S(1)}, f32[624,128]{1,0:T(8,128)...) custom-call(bf16[3,2432,128]{2,1,0:T(8,128)(2,1)S(1)} %shard_map.50.refs_0_.refs_10_,, ...), custom_call_target="tpu_custom_call" | custom-call | tf_op jit(solution)/shard_map/pallas_call | solution.py:653
  13.3 0.7 collective-permute-start.4
  14.0 0.9 %collective-permute-done.3.refs_1_ = f32[632,128]{1,0:T(8,128)S(1)} collective-permute-done((f32[632,128]{1,0:T(8,128)S(1)}, f32[632,128]{1,0:T(8,128)S(1)}, u32[]{:S(2)}, u32[]{:S(2)}) %collective-permute-start.3) | collective-permute-done | bytes 323616 | tf_op jit(solution)/shard_map/ppermute | solution.py:636
  14.9 4.5 %collective-permute-start.7 = (f32[16,128]{1,0:T(8,128)S(1)}, f32[16,128]{1,0:T(8,128)S(1)}, u32[]{:S(2)}, u32[]{:S(2)}) collective-permute-start(f32[16,128]{1,0:T(8,128)S(1)} %pad_maximum_fusion), channel_id=1, source_target_pairs={{0,6},{1,7},{2,4},{3,5},{4,2},{5,3},{6,0},{7,1},{8,14},{9,15},{10,... | collective-permute-start | bytes 24584 | tf_op jit(solution)/shard_map/ppermute | solution.py:643
  20.1 2.6 %shard_map.54.refs_15_.refs_16_.adj_ref = bf16[3,2432,128]{2,1,0:T(8,128)(2,1)S(1)} custom-call(bf16[61,61]{1,0:T(8,128)(2,1)S(1)} %copy-done.1), custom_call_target="tpu_custom_call" | custom-call | tf_op jit(solution)/shard_map/pallas_call | solution.py:141
  22.7 2.0 %collective-permute-done.7.refs_14_ = f32[16,128]{1,0:T(8,128)S(1)} collective-permute-done((f32[16,128]{1,0:T(8,128)S(1)}, f32[16,128]{1,0:T(8,128)S(1)}, u32[]{:S(2)}, u32[]{:S(2)}) %collective-permute-start.7) | collective-permute-done | bytes 8224 | tf_op jit(solution)/shard_map/ppermute | solution.py:643
  24.6 5.9 %shard_map.55 = (f32[2,4,104,128]{3,2,1,0:T(8,128)S(1)}, bf16[448,128]{1,0:T(8,128)(2,1)S(1)}, bf16[416,128]{1,0:T(8,128)(2,1)S(1)}, f32[8,128]{1,0:T(8,128)S(1)...) custom-call(f32[2,4,104,128]{3,2,1,0:T(8,128)S(1)} %get-tuple-element.37.refs_0_, ...), custom_call_target="tpu_custom_call" | custom-call | tf_op jit(solution)/shard_map/pallas_call | solution.py:653
  30.5 0.8 collective-permute-start.9
  31.9 3.8 %collective-permute-start.12 = (f32[16,128]{1,0:T(8,128)S(1)}, f32[16,128]{1,0:T(8,128)S(1)}, u32[]{:S(2)}, u32[]{:S(2)}) collective-permute-start(f32[16,128]{1,0:T(8,128)S(1)} %pad_maximum_fusion.1), channel_id=1, source_target_pairs={{0,6},{1,7},{2,4},{3,5},{4,2},{5,3},{6,0},{7,1},{8,14},{9,15},{10,... | collective-permute-start | bytes 24584 | tf_op jit(solution)/shard_map/ppermute | solution.py:643
  36.3 1.9 %collective-permute-done.12.refs_14_ = f32[16,128]{1,0:T(8,128)S(1)} collective-permute-done((f32[16,128]{1,0:T(8,128)S(1)}, f32[16,128]{1,0:T(8,128)S(1)}, u32[]{:S(2)}, u32[]{:S(2)}) %collective-permute-start.12) | collective-permute-done | bytes 8224 | tf_op jit(solution)/shard_map/ppermute | solution.py:643
  38.2 2.0 %collective-permute-done.11.refs_13_ = f32[16,128]{1,0:T(8,128)S(1)} collective-permute-done((f32[16,128]{1,0:T(8,128)S(1)}, f32[16,128]{1,0:T(8,128)S(1)}, u32[]{:S(2)}, u32[]{:S(2)}) %collective-permute-start.11) | collective-permute-done | bytes 8224 | tf_op jit(solution)/shard_map/ppermute | solution.py:643
  40.2 5.9 %shard_map.56 = (f32[2,4,104,128]{3,2,1,0:T(8,128)S(1)}, bf16[448,128]{1,0:T(8,128)(2,1)S(1)}, bf16[416,128]{1,0:T(8,128)(2,1)S(1)}, f32[8,128]{1,0:T(8,128)S(1)}, f32[2,4,104,128]{3,2,1,0:T(8,128)S(1)}) custom-call(f32[2,4,104,128]{3,2,1,0:T(8,128)S(1)} %get-tuple-element.47.refs_0_, bf16[448,128]{1,0:T(8,128)(2,1)S(1)} %collective-permute-done.8.refs_1_, ...), custom_call_target="tpu_custom_call" | custom-call | tf_op jit(solution)/shard_map/pallas_call | solution.py:653
  46.1 0.7 collective-permute-start.14
  47.5 4.3 %collective-permute-start.17 = (f32[16,128]{1,0:T(8,128)S(1)}, f32[16,128]{1,0:T(8,128)S(1)}, u32[]{:S(2)}, u32[]{:S(2)}) collective-permute-start(f32[16,128]{1,0:T(8,128)S(1)} %pad_maximum_fusion.2), channel_id=1, source_target_pairs={{0,6},{1,7},{2,4},{3,5},{4,2},{5,3},{6,0},{7,1},{8,14},{9,15},{10,... | collective-permute-start | bytes 24584 | tf_op jit(solution)/shard_map/ppermute | solution.py:643
  52.4 2.1 %collective-permute-done.17.refs_14_ = f32[16,128]{1,0:T(8,128)S(1)} collective-permute-done((f32[16,128]{1,0:T(8,128)S(1)}, f32[16,128]{1,0:T(8,128)S(1)}, u32[]{:S(2)}, u32[]{:S(2)}) %collective-permute-start.17) | collective-permute-done | bytes 8224 | tf_op jit(solution)/shard_map/ppermute | solution.py:643
  54.5 1.7 %collective-permute-done.16.refs_13_ = f32[16,128]{1,0:T(8,128)S(1)} collective-permute-done((f32[16,128]{1,0:T(8,128)S(1)}, f32[16,128]{1,0:T(8,128)S(1)}, u32[]{:S(2)}, u32[]{:S(2)}) %collective-permute-start.16) | collective-permute-done | bytes 8224 | tf_op jit(solution)/shard_map/ppermute | solution.py:643
  56.3 5.9 %shard_map.57 = (f32[2,4,104,128]{3,2,1,0:T(8,128)S(1)}, bf16[448,128]{1,0:T(8,128)(2,1)S(1)}, bf16[416,128]{1,0:T(8,128)(2,1)S(1)}, f32[8,128]{1,0:T(8,128)S(1)}, f32[2,4,104,128]{3,2,1,0:T(8,128)S(1)}) custom-call(f32[2,4,104,128]{3,2,1,0:T(8,128)S(1)} %get-tuple-element.53.refs_0_, bf16[448,128]{1,0:T(8,128)(2,1)S(1)} %collective-permute-done.13.refs_1_, ...), custom_call_target="tpu_custom_call" | custom-call | tf_op jit(solution)/shard_map/pallas_call | solution.py:653
  62.2 0.9 %collective-permute-start.19 = (bf16[416,128]{1,0:T(8,128)(2,1)S(1)}, bf16[416,128]{1,0:T(8,128)(2,1)S(1)}, u32[]{:S(2)}, u32[]{:S(2)}) collective-permute-start(bf16[416,128]{1,0:T(8,128)(2,1)S(1)} %get-tuple-element.60), channel_id=1, source_target_pairs={{1,2},{2,1},{3,4},{4,3},{5,6},{6,5},{9,10},{10,9},{11,12},{12,11},... | collective-permute-start | bytes 319496 | tf_op jit(solution)/shard_map/ppermute | solution.py:636
  63.5 4.5 %collective-permute-start.22 = (f32[16,128]{1,0:T(8,128)S(1)}, f32[16,128]{1,0:T(8,128)S(1)}, u32[]{:S(2)}, u32[]{:S(2)}) collective-permute-start(f32[16,128]{1,0:T(8,128)S(1)} %pad_maximum_fusion.3), channel_id=1, source_target_pairs={{0,6},{1,7},{2,4},{3,5},{4,2},{5,3},{6,0},{7,1},{8,14},{9,15},{10,... | collective-permute-start | bytes 24584 | tf_op jit(solution)/shard_map/ppermute | solution.py:643
  68.7 2.0 %collective-permute-done.22.refs_14_ = f32[16,128]{1,0:T(8,128)S(1)} collective-permute-done((f32[16,128]{1,0:T(8,128)S(1)}, f32[16,128]{1,0:T(8,128)S(1)}, u32[]{:S(2)}, u32[]{:S(2)}) %collective-permute-start.22) | collective-permute-done | bytes 8224 | tf_op jit(solution)/shard_map/ppermute | solution.py:643
  70.7 1.9 %collective-permute-done.21.refs_13_ = f32[16,128]{1,0:T(8,128)S(1)} collective-permute-done((f32[16,128]{1,0:T(8,128)S(1)}, f32[16,128]{1,0:T(8,128)S(1)}, u32[]{:S(2)}, u32[]{:S(2)}) %collective-permute-start.21) | collective-permute-done | bytes 8224 | tf_op jit(solution)/shard_map/ppermute | solution.py:643
  72.6 3.8 %shard_map.58 = (f32[2,6,40,128]{3,2,1,0:T(8,128)S(1)}, f32[2,4,32,128]{3,2,1,0:T(8,128)S(1)}, f32[2,5,32,128]{3,2,1,0:T(8,128)S(1)}, f32[8,128]{1,0:T(8,128)S(1)}) custom-call(f32[2,4,104,128]{3,2,1,0:T(8,128)S(1)} %get-tuple-element.58.refs_0_, bf16[448,128]{1,0:T(8,128)(2,1)S(1)} %collective-permute-done.18.refs_1_, ...), custom_call_target="tpu_custom_call" | custom-call | tf_op jit(solution)/shard_map/pallas_call | solution.py:653
  76.4 1.2 %collective-permute-done.23.refs_1_ = f32[8,128]{1,0:T(8,128)S(1)} collective-permute-done((f32[8,128]{1,0:T(8,128)S(1)}, f32[8,128]{1,0:T(8,128)S(1)}, u32[]{:S(2)}, u32[]{:S(2)}) %collective-permute-start.23) | collective-permute-done | bytes 4128 | tf_op jit(solution)/shard_map/ppermute | solution.py:769
  77.6 1.5 %collective-permute-start.26 = (f32[16,128]{1,0:T(8,128)S(1)}, f32[16,128]{1,0:T(8,128)S(1)}, u32[]{:S(2)}, u32[]{:S(2)}) collective-permute-start(f32[16,128]{1,0:T(8,128)S(1)} %constant_dynamic-update-slice_fusion), channel_id=1, source_target_pairs={{0,6},{1,7},{2,4},{3,5},{4,2},{5,3},{6,0},{7,1},{8,14},{9,15},{10,... | collective-permute-start | bytes 24584 | tf_op jit(solution)/shard_map/ppermute | solution.py:643
  79.6 2.4 %collective-permute-start.24 = (f32[16,128]{1,0:T(8,128)S(1)}, f32[16,128]{1,0:T(8,128)S(1)}, u32[]{:S(2)}, u32[]{:S(2)}) collective-permute-start(f32[16,128]{1,0:T(8,128)S(1)} %constant_dynamic-update-slice_fusion), channel_id=1, source_target_pairs={{0,2},{1,3},{2,0},{3,1},{4,6},{5,7},{6,4},{7,5},{8,10},{9,11},{10,... | collective-permute-start | bytes 24584 | tf_op jit(solution)/shard_map/ppermute | solution.py:643
  82.0 1.5 %shard_map.59 = (f32[200,100]{1,0:T(8,128)S(1)}, f32[200,100]{1,0:T(8,128)}) custom-call(f32[2,6,40,128]{3,2,1,0:T(8,128)S(1)} %get-tuple-element.63.e_ref, f32[2,4,32,128]{3,2,1,0:T(8,128)S(1)} %get-tuple-element.64.x_ref, f32[2,5,32,128]{3,2,1,0:T(8,128)S(1)} %get-tuple-element.65.r_ref, bf16[3,2432,128]{2,1,0:T(8,128)(2,1)S(1)} %shard_map.54.refs_15_.refs_16_.adj_ref), custom_call_target="tpu_custom_call" | custom-call | tf_op jit(solution)/shard_map/pallas_call | solution.py:653
  83.7 1.2 %shard_map.60 = f32[200,100]{1,0:T(8,128)} custom-call(f32[200,100]{1,0:T(8,128)S(1)} %get-tuple-element.67.v_ref, bf16[192,768]{1,0:T(8,128)(2,1)S(1)} %get-tuple-element.36.refs_1_.refs_4_.rows_ref, bf16[384,128]{1,0:T(8,128)(2,1)S(1)} %get-tuple-element.68.pull_ref, f32[8,128]{1,0:T(8,128)S(1)} %get-tuple-element.69.refs_0_, ...), custom_call_target="tpu_custom_call" | custom-call | tf_op jit(solution)/shard_map/pallas_call | solution.py:653
  (52 shorter events, 7.3 us)
Async XLA Ops:
  0.6 0.9 %copy-start = (s32[200,100]{1,0:T(8,128)S(1)}, s32[200,100]{1,0:T(8,128)}, u32[]{:S(2)}) copy-start(s32[200,100]{1,0:T(8,128)} %target_ref.1) | copy-start | bytes 240004
  1.5 0.8 copy-start.2
  2.4 8.4 %collective-permute-start.2 = (bf16[200,256]{1,0:T(8,128)(2,1)S(1)}, bf16[200,256]{1,0:T(8,128)(2,1)S(1)}, u32[]{:S(2)}, u32[]{:S(2)}) collective-permute-start(bf16[200,256]{1,0:T(8,128)(2,1)S(1)} %shard_map.52.refs_2_), channel_id=1, source_target_pairs={{0,24},{8,16},{16,8},{24,0},{1,25},{9,17},{17,9},{25,1},{2,26},{10... | collective-permute-start | bytes 307208 | tf_op jit(solution)/shard_map/ppermute | solution.py:665
  6.3 5.1 %collective-permute-start.1 = (bf16[200,256]{1,0:T(8,128)(2,1)S(1)}, bf16[200,256]{1,0:T(8,128)(2,1)S(1)}, u32[]{:S(2)}, u32[]{:S(2)}) collective-permute-start(bf16[200,256]{1,0:T(8,128)(2,1)S(1)} %shard_map.52.refs_2_), channel_id=1, source_target_pairs={{0,16},{8,24},{16,0},{24,8},{1,17},{9,25},{17,1},{25,9},{2,18},{10... | collective-permute-start | bytes 307208 | tf_op jit(solution)/shard_map/ppermute | solution.py:665
  6.8 4.9 %collective-permute-start = (bf16[200,256]{1,0:T(8,128)(2,1)S(1)}, bf16[200,256]{1,0:T(8,128)(2,1)S(1)}, u32[]{:S(2)}, u32[]{:S(2)}) collective-permute-start(bf16[200,256]{1,0:T(8,128)(2,1)S(1)} %shard_map.52.refs_2_), channel_id=1, source_target_pairs={{0,8},{8,0},{16,24},{24,16},{1,9},{9,1},{17,25},{25,17},{2,10},{10... | collective-permute-start | bytes 307208 | tf_op jit(solution)/shard_map/ppermute | solution.py:665
  7.6 0.7 copy-start.1
  13.2 1.7 %collective-permute-start.3 = (f32[632,128]{1,0:T(8,128)S(1)}, f32[632,128]{1,0:T(8,128)S(1)}, u32[]{:S(2)}, u32[]{:S(2)}) collective-permute-start(f32[632,128]{1,0:T(8,128)S(1)} %get-tuple-element.38), channel_id=1, source_target_pairs={{0,1},{1,0},{2,3},{3,2},{4,5},{5,4},{6,7},{7,6},{8,9},{9,8},{10,11... | collective-permute-start | bytes 970760 | tf_op jit(solution)/shard_map/ppermute | solution.py:636
  13.3 9.4 %collective-permute-start.4 = (f32[624,128]{1,0:T(8,128)S(1)}, f32[624,128]{1,0:T(8,128)S(1)}, u32[]{:S(2)}, u32[]{:S(2)}) collective-permute-start(f32[624,128]{1,0:T(8,128)S(1)} %get-tuple-element.39), channel_id=1, source_target_pairs={{1,2},{2,1},{3,4},{4,3},{5,6},{6,5},{9,10},{10,9},{11,12},{12,11},... | collective-permute-start | bytes 958472 | tf_op jit(solution)/shard_map/ppermute | solution.py:636
  14.9 9.7 %collective-permute-start.7 = (f32[16,128]{1,0:T(8,128)S(1)}, f32[16,128]{1,0:T(8,128)S(1)}, u32[]{:S(2)}, u32[]{:S(2)}) collective-permute-start(f32[16,128]{1,0:T(8,128)S(1)} %pad_maximum_fusion), channel_id=1, source_target_pairs={{0,6},{1,7},{2,4},{3,5},{4,2},{5,3},{6,0},{7,1},{8,14},{9,15},{10,... | collective-permute-start | bytes 24584 | tf_op jit(solution)/shard_map/ppermute | solution.py:643
  19.4 5.2 %collective-permute-start.6 = (f32[16,128]{1,0:T(8,128)S(1)}, f32[16,128]{1,0:T(8,128)S(1)}, u32[]{:S(2)}, u32[]{:S(2)}) collective-permute-start(f32[16,128]{1,0:T(8,128)S(1)} %pad_maximum_fusion), channel_id=1, source_target_pairs={{0,4},{1,5},{2,6},{3,7},{4,0},{5,1},{6,2},{7,3},{8,12},{9,13},{10,... | collective-permute-start | bytes 24584 | tf_op jit(solution)/shard_map/ppermute | solution.py:643
  19.4 5.2 %collective-permute-start.5 = (f32[16,128]{1,0:T(8,128)S(1)}, f32[16,128]{1,0:T(8,128)S(1)}, u32[]{:S(2)}, u32[]{:S(2)}) collective-permute-start(f32[16,128]{1,0:T(8,128)S(1)} %pad_maximum_fusion), channel_id=1, source_target_pairs={{0,2},{1,3},{2,0},{3,1},{4,6},{5,7},{6,4},{7,5},{8,10},{9,11},{10,... | collective-permute-start | bytes 24584 | tf_op jit(solution)/shard_map/ppermute | solution.py:643
  30.5 1.4 %collective-permute-start.8 = (bf16[448,128]{1,0:T(8,128)(2,1)S(1)}, bf16[448,128]{1,0:T(8,128)(2,1)S(1)}, u32[]{:S(2)}, u32[]{:S(2)}) collective-permute-start(bf16[448,128]{1,0:T(8,128)(2,1)S(1)} %get-tuple-element.48), channel_id=1, source_target_pairs={{0,1},{1,0},{2,3},{3,2},{4,5},{5,4},{6,7},{7,6},{8,9},{9,8},{10,11... | collective-permute-start | bytes 344072 | tf_op jit(solution)/shard_map/ppermute | solution.py:636
  30.5 5.8 %collective-permute-start.9 = (bf16[416,128]{1,0:T(8,128)(2,1)S(1)}, bf16[416,128]{1,0:T(8,128)(2,1)S(1)}, u32[]{:S(2)}, u32[]{:S(2)}) collective-permute-start(bf16[416,128]{1,0:T(8,128)(2,1)S(1)} %get-tuple-element.49), channel_id=1, source_target_pairs={{1,2},{2,1},{3,4},{4,3},{5,6},{6,5},{9,10},{10,9},{11,12},{12,11},... | collective-permute-start | bytes 319496 | tf_op jit(solution)/shard_map/ppermute | solution.py:636
  31.9 6.3 %collective-permute-start.12 = (f32[16,128]{1,0:T(8,128)S(1)}, f32[16,128]{1,0:T(8,128)S(1)}, u32[]{:S(2)}, u32[]{:S(2)}) collective-permute-start(f32[16,128]{1,0:T(8,128)S(1)} %pad_maximum_fusion.1), channel_id=1, source_target_pairs={{0,6},{1,7},{2,4},{3,5},{4,2},{5,3},{6,0},{7,1},{8,14},{9,15},{10,... | collective-permute-start | bytes 24584 | tf_op jit(solution)/shard_map/ppermute | solution.py:643
  35.7 4.5 %collective-permute-start.11 = (f32[16,128]{1,0:T(8,128)S(1)}, f32[16,128]{1,0:T(8,128)S(1)}, u32[]{:S(2)}, u32[]{:S(2)}) collective-permute-start(f32[16,128]{1,0:T(8,128)S(1)} %pad_maximum_fusion.1), channel_id=1, source_target_pairs={{0,4},{1,5},{2,6},{3,7},{4,0},{5,1},{6,2},{7,3},{8,12},{9,13},{10,... | collective-permute-start | bytes 24584 | tf_op jit(solution)/shard_map/ppermute | solution.py:643
  36.3 3.9 %collective-permute-start.10 = (f32[16,128]{1,0:T(8,128)S(1)}, f32[16,128]{1,0:T(8,128)S(1)}, u32[]{:S(2)}, u32[]{:S(2)}) collective-permute-start(f32[16,128]{1,0:T(8,128)S(1)} %pad_maximum_fusion.1), channel_id=1, source_target_pairs={{0,2},{1,3},{2,0},{3,1},{4,6},{5,7},{6,4},{7,5},{8,10},{9,11},{10,... | collective-permute-start | bytes 24584 | tf_op jit(solution)/shard_map/ppermute | solution.py:643
  46.1 1.4 %collective-permute-start.13 = (bf16[448,128]{1,0:T(8,128)(2,1)S(1)}, bf16[448,128]{1,0:T(8,128)(2,1)S(1)}, u32[]{:S(2)}, u32[]{:S(2)}) collective-permute-start(bf16[448,128]{1,0:T(8,128)(2,1)S(1)} %get-tuple-element.54), channel_id=1, source_target_pairs={{0,1},{1,0},{2,3},{3,2},{4,5},{5,4},{6,7},{7,6},{8,9},{9,8},{10,11... | collective-permute-start | bytes 344072 | tf_op jit(solution)/shard_map/ppermute | solution.py:636
  46.1 6.3 %collective-permute-start.14 = (bf16[416,128]{1,0:T(8,128)(2,1)S(1)}, bf16[416,128]{1,0:T(8,128)(2,1)S(1)}, u32[]{:S(2)}, u32[]{:S(2)}) collective-permute-start(bf16[416,128]{1,0:T(8,128)(2,1)S(1)} %get-tuple-element.55), channel_id=1, source_target_pairs={{1,2},{2,1},{3,4},{4,3},{5,6},{6,5},{9,10},{10,9},{11,12},{12,11},... | collective-permute-start | bytes 319496 | tf_op jit(solution)/shard_map/ppermute | solution.py:636
  47.5 7.1 %collective-permute-start.17 = (f32[16,128]{1,0:T(8,128)S(1)}, f32[16,128]{1,0:T(8,128)S(1)}, u32[]{:S(2)}, u32[]{:S(2)}) collective-permute-start(f32[16,128]{1,0:T(8,128)S(1)} %pad_maximum_fusion.2), channel_id=1, source_target_pairs={{0,6},{1,7},{2,4},{3,5},{4,2},{5,3},{6,0},{7,1},{8,14},{9,15},{10,... | collective-permute-start | bytes 24584 | tf_op jit(solution)/shard_map/ppermute | solution.py:643
  51.7 4.5 %collective-permute-start.16 = (f32[16,128]{1,0:T(8,128)S(1)}, f32[16,128]{1,0:T(8,128)S(1)}, u32[]{:S(2)}, u32[]{:S(2)}) collective-permute-start(f32[16,128]{1,0:T(8,128)S(1)} %pad_maximum_fusion.2), channel_id=1, source_target_pairs={{0,4},{1,5},{2,6},{3,7},{4,0},{5,1},{6,2},{7,3},{8,12},{9,13},{10,... | collective-permute-start | bytes 24584 | tf_op jit(solution)/shard_map/ppermute | solution.py:643
  51.7 4.5 %collective-permute-start.15 = (f32[16,128]{1,0:T(8,128)S(1)}, f32[16,128]{1,0:T(8,128)S(1)}, u32[]{:S(2)}, u32[]{:S(2)}) collective-permute-start(f32[16,128]{1,0:T(8,128)S(1)} %pad_maximum_fusion.2), channel_id=1, source_target_pairs={{0,2},{1,3},{2,0},{3,1},{4,6},{5,7},{6,4},{7,5},{8,10},{9,11},{10,... | collective-permute-start | bytes 24584 | tf_op jit(solution)/shard_map/ppermute | solution.py:643
  62.1 1.4 %collective-permute-start.18 = (bf16[448,128]{1,0:T(8,128)(2,1)S(1)}, bf16[448,128]{1,0:T(8,128)(2,1)S(1)}, u32[]{:S(2)}, u32[]{:S(2)}) collective-permute-start(bf16[448,128]{1,0:T(8,128)(2,1)S(1)} %get-tuple-element.59), channel_id=1, source_target_pairs={{0,1},{1,0},{2,3},{3,2},{4,5},{5,4},{6,7},{7,6},{8,9},{9,8},{10,11... | collective-permute-start | bytes 344072 | tf_op jit(solution)/shard_map/ppermute | solution.py:636
  62.2 6.5 %collective-permute-start.19 = (bf16[416,128]{1,0:T(8,128)(2,1)S(1)}, bf16[416,128]{1,0:T(8,128)(2,1)S(1)}, u32[]{:S(2)}, u32[]{:S(2)}) collective-permute-start(bf16[416,128]{1,0:T(8,128)(2,1)S(1)} %get-tuple-element.60), channel_id=1, source_target_pairs={{1,2},{2,1},{3,4},{4,3},{5,6},{6,5},{9,10},{10,9},{11,12},{12,11},... | collective-permute-start | bytes 319496 | tf_op jit(solution)/shard_map/ppermute | solution.py:636
  63.5 7.2 %collective-permute-start.22 = (f32[16,128]{1,0:T(8,128)S(1)}, f32[16,128]{1,0:T(8,128)S(1)}, u32[]{:S(2)}, u32[]{:S(2)}) collective-permute-start(f32[16,128]{1,0:T(8,128)S(1)} %pad_maximum_fusion.3), channel_id=1, source_target_pairs={{0,6},{1,7},{2,4},{3,5},{4,2},{5,3},{6,0},{7,1},{8,14},{9,15},{10,... | collective-permute-start | bytes 24584 | tf_op jit(solution)/shard_map/ppermute | solution.py:643
  68.0 4.5 %collective-permute-start.21 = (f32[16,128]{1,0:T(8,128)S(1)}, f32[16,128]{1,0:T(8,128)S(1)}, u32[]{:S(2)}, u32[]{:S(2)}) collective-permute-start(f32[16,128]{1,0:T(8,128)S(1)} %pad_maximum_fusion.3), channel_id=1, source_target_pairs={{0,4},{1,5},{2,6},{3,7},{4,0},{5,1},{6,2},{7,3},{8,12},{9,13},{10,... | collective-permute-start | bytes 24584 | tf_op jit(solution)/shard_map/ppermute | solution.py:643
  68.0 4.5 %collective-permute-start.20 = (f32[16,128]{1,0:T(8,128)S(1)}, f32[16,128]{1,0:T(8,128)S(1)}, u32[]{:S(2)}, u32[]{:S(2)}) collective-permute-start(f32[16,128]{1,0:T(8,128)S(1)} %pad_maximum_fusion.3), channel_id=1, source_target_pairs={{0,2},{1,3},{2,0},{3,1},{4,6},{5,7},{6,4},{7,5},{8,10},{9,11},{10,... | collective-permute-start | bytes 24584 | tf_op jit(solution)/shard_map/ppermute | solution.py:643
  76.4 1.2 %collective-permute-start.23 = (f32[8,128]{1,0:T(8,128)S(1)}, f32[8,128]{1,0:T(8,128)S(1)}, u32[]{:S(2)}, u32[]{:S(2)}) collective-permute-start(f32[8,128]{1,0:T(8,128)S(1)} %get-tuple-element.69.refs_0_), channel_id=1, source_target_pairs={{0,1},{1,0},{2,3},{3,2},{4,5},{5,4},{6,7},{7,6},{8,9},{9,8},{10,11... | collective-permute-start | bytes 12296 | tf_op jit(solution)/shard_map/ppermute | solution.py:769
  77.6 5.9 %collective-permute-start.26 = (f32[16,128]{1,0:T(8,128)S(1)}, f32[16,128]{1,0:T(8,128)S(1)}, u32[]{:S(2)}, u32[]{:S(2)}) collective-permute-start(f32[16,128]{1,0:T(8,128)S(1)} %constant_dynamic-update-slice_fusion), channel_id=1, source_target_pairs={{0,6},{1,7},{2,4},{3,5},{4,2},{5,3},{6,0},{7,1},{8,14},{9,15},{10,... | collective-permute-start | bytes 24584 | tf_op jit(solution)/shard_map/ppermute | solution.py:643
  79.1 4.6 %collective-permute-start.25 = (f32[16,128]{1,0:T(8,128)S(1)}, f32[16,128]{1,0:T(8,128)S(1)}, u32[]{:S(2)}, u32[]{:S(2)}) collective-permute-start(f32[16,128]{1,0:T(8,128)S(1)} %constant_dynamic-update-slice_fusion), channel_id=1, source_target_pairs={{0,4},{1,5},{2,6},{3,7},{4,0},{5,1},{6,2},{7,3},{8,12},{9,13},{10,... | collective-permute-start | bytes 24584 | tf_op jit(solution)/shard_map/ppermute | solution.py:643
  79.6 4.1 %collective-permute-start.24 = (f32[16,128]{1,0:T(8,128)S(1)}, f32[16,128]{1,0:T(8,128)S(1)}, u32[]{:S(2)}, u32[]{:S(2)}) collective-permute-start(f32[16,128]{1,0:T(8,128)S(1)} %constant_dynamic-update-slice_fusion), channel_id=1, source_target_pairs={{0,2},{1,3},{2,0},{3,1},{4,6},{5,7},{6,4},{7,5},{8,10},{9,11},{10,... | collective-permute-start | bytes 24584 | tf_op jit(solution)/shard_map/ppermute | solution.py:643

commit v10 on v8

--- a/solution.py
+++ b/solution.py
@@ -150,7 +150,7 @@
     )(psf)
 
 
-def correlate(field, blocks, depth, line_ref, band_ref, part_ref, acc_ref):
+def correlate(field, blocks, depth, line_ref, band_ref, part_ref, acc_ref, between=None):
     height = blocks * depth
     for n in range(PAIR):
         for g in range(REACH):
@@ -177,6 +177,7 @@
         product = dot(line_ref[...], table)
         for n in range(PAIR):
             part_ref[n, m, pl.ds(EDGE, line_ref.shape[0]), :] = product[:, n * LANES:(n + 1) * LANES]
+    made = between() if between else None
     for n in range(PAIR):
         for b in range(blocks):
             total = None
@@ -185,6 +186,7 @@
                 piece = part_ref[n, m, pl.ds(first, depth), :]
                 total = piece if total is None else total + piece
             acc_ref[n, b, pl.ds(0, depth), :] = total
+    return made
 
 
 def stacked(ref, n, g, blocks, first, depth):
@@ -246,8 +248,12 @@
     pull = dot(one_side(mixed[:half], 1), pull_ref[...])
     if back_ref is None:
         return pull
-    levels = jnp.concatenate([mixed[half:2 * half], mixed[2 * half:]], axis=1)
-    return pull, dot(one_side(levels, 1), back_ref[...])
+
+    def back():
+        levels = jnp.concatenate([mixed[half:2 * half], mixed[2 * half:]], axis=1)
+        return dot(one_side(levels, 1), back_ref[...])
+
+    return pull, back
 
 
 def both_kernel(dose_ref, target_ref, out_ref):
@@ -359,9 +365,8 @@
     pieces = [ref[...] for ref in red_refs]
     if from_a_ref.shape != from_b_ref.shape:
         pieces.insert(1, from_a_ref[pl.ds(from_b_ref.shape[0], 8), :])
-    pull, back = coarse(pieces, rows_ref, pull_ref, back_ref, half)
+    pull, make_back = coarse(pieces, rows_ref, pull_ref, back_ref, half)
     pull = over_rows(pull, ncx, wide_blocks)
-    back = over_rows(back, ncx, blocks)
 
     tail = cols - SPAN * (tile_blocks - 1)
     for n in range(PAIR):
@@ -378,9 +383,10 @@
             value = value - pulled[:, b * LANES:(b + 1) * LANES]
             x_ref[n, b, pl.ds(0, depth), :] = value.astype(bf16).astype(f32)
 
-    correlate(
+    back = correlate(
         lambda n, g: stacked(x_ref, n, g, blocks, 0, depth),
         blocks, depth, line_ref, fwd_ref, part_ref, acc_ref,
+        lambda: over_rows(make_back(), ncx, blocks),
     )
     lead = EDGE if last else 0
 

time: 85.3 us -> 85.7 us (level)
  no operation moved by 1% of the time
where the time goes in v10:
time: 85.7 us; the launch traced here: 85.3 us
  Pallas kernels  31.7 us (37%)
  starting transfers between devices  31.7 us (37%)
  waiting for transfers between devices  18.7 us (22%)
  local copies, waits for them, and re-layouts  2.42 us (3%)
    pallas_call x9, Pallas kernels, call(): pl.pallas_call(kernel, out_shape=out_shape, in_specs=[vmem] * len(args),...  26.7 us
    ppermute x15, starting transfers between devices, spread_pairs(): lax.ppermute(pair, 'scan', [(i, i ^ k) for i in range(scans)])  23.8 us
    ppermute x15, waiting for transfers between devices, spread_pairs(): lax.ppermute(pair, 'scan', [(i, i ^ k) for i in range(scans)])  13.7 us
    pallas_call x2, Pallas kernels, bands(): pl.pallas_call(functools.partial(bands_kernel, offset, flip), out_shape=j...  5.04 us
    ppermute x3, starting transfers between devices, per_device(): lax.ppermute(both, 'stripe', pairs)  4.6 us
    ppermute x4, starting transfers between devices, swap(): lax.ppermute(to_b, 'scan', swap_b)  3.2 us
    ppermute x4, waiting for transfers between devices, swap(): lax.ppermute(to_a, 'scan', swap_a)  2.91 us
    unnamed x9, local copies, waits for them, and re-layouts  2.41 us
  transfers between devices with their start and end apart: 27, of which 16 were waited for; matrix products, arithmetic and copies ran while one was open for 0% of the time, Pallas kernels for 8%

profile of v10, /device:TPU:0, one launch (start us, length us, event | category | flops | bytes accessed | tf_op | source)
XLA Modules:
  0.0 85.3 jit_solution(13294230917881393831)
XLA Ops:
  0.6 0.9 %copy-done = s32[200,100]{1,0:T(8,128)S(1)} copy-done((s32[200,100]{1,0:T(8,128)S(1)}, s32[200,100]{1,0:T(8,128)}, u32[]{:S(2)}) %copy-start) | copy-done | bytes 80024
  1.5 0.8 copy-done.3
  2.4 4.0 %collective-permute-start.2 = (bf16[200,256]{1,0:T(8,128)(2,1)S(1)}, bf16[200,256]{1,0:T(8,128)(2,1)S(1)}, u32[]{:S(2)}, u32[]{:S(2)}) collective-permute-start(bf16[200,256]{1,0:T(8,128)(2,1)S(1)} %shard_map.52.refs_2_), channel_id=1, source_target_pairs={{0,24},{8,16},{16,8},{24,0},{1,25},{9,17},{17,9},{25,1},{2,26},{10... | collective-permute-start | bytes 307208 | tf_op jit(solution)/shard_map/ppermute | solution.py:649
  7.6 0.7 copy-done.1
  8.3 2.5 %shard_map.50.refs_0_.refs_10_ = bf16[3,2432,128]{2,1,0:T(8,128)(2,1)S(1)} custom-call(bf16[61,61]{1,0:T(8,128)(2,1)S(1)} %copy-done.1), custom_call_target="tpu_custom_call" | custom-call | tf_op jit(solution)/shard_map/pallas_call | solution.py:141
  11.7 1.5 %shard_map.53 = (f32[2,4,104,128]{3,2,1,0:T(8,128)S(1)}, bf16[2,5,104,128]{3,2,1,0:T(8,128)(2,1)S(1)}, f32[632,128]{1,0:T(8,128)S(1)}, f32[624,128]{1,0:T(8,128)...) custom-call(bf16[3,2432,128]{2,1,0:T(8,128)(2,1)S(1)} %shard_map.50.refs_0_.refs_10_,, ...), custom_call_target="tpu_custom_call" | custom-call | tf_op jit(solution)/shard_map/pallas_call | solution.py:637
  13.3 0.7 collective-permute-start.4
  14.0 0.9 %collective-permute-done.3.refs_1_ = f32[632,128]{1,0:T(8,128)S(1)} collective-permute-done((f32[632,128]{1,0:T(8,128)S(1)}, f32[632,128]{1,0:T(8,128)S(1)}, u32[]{:S(2)}, u32[]{:S(2)}) %collective-permute-start.3) | collective-permute-done | bytes 323616 | tf_op jit(solution)/shard_map/ppermute | solution.py:620
  14.9 4.5 %collective-permute-start.7 = (f32[16,128]{1,0:T(8,128)S(1)}, f32[16,128]{1,0:T(8,128)S(1)}, u32[]{:S(2)}, u32[]{:S(2)}) collective-permute-start(f32[16,128]{1,0:T(8,128)S(1)} %pad_maximum_fusion), channel_id=1, source_target_pairs={{0,6},{1,7},{2,4},{3,5},{4,2},{5,3},{6,0},{7,1},{8,14},{9,15},{10,... | collective-permute-start | bytes 24584 | tf_op jit(solution)/shard_map/ppermute | solution.py:627
  20.1 2.6 %shard_map.54.refs_15_.adj_ref = bf16[3,2432,128]{2,1,0:T(8,128)(2,1)S(1)} custom-call(bf16[61,61]{1,0:T(8,128)(2,1)S(1)} %copy-done.2), custom_call_target="tpu_custom_call" | custom-call | tf_op jit(solution)/shard_map/pallas_call | solution.py:141
  22.7 1.9 %collective-permute-done.7.refs_14_ = f32[16,128]{1,0:T(8,128)S(1)} collective-permute-done((f32[16,128]{1,0:T(8,128)S(1)}, f32[16,128]{1,0:T(8,128)S(1)}, u32[]{:S(2)}, u32[]{:S(2)}) %collective-permute-start.7) | collective-permute-done | bytes 8224 | tf_op jit(solution)/shard_map/ppermute | solution.py:627
  24.6 6.0 %shard_map.55 = (f32[2,4,104,128]{3,2,1,0:T(8,128)S(1)}, f32[424,128]{1,0:T(8,128)S(1)}, f32[416,128]{1,0:T(8,128)S(1)}, f32[8,128]{1,0:T(8,128)S(1)}, bf16[2,5,104,128]{3,2,1,0:T(8,128)(2,1)S(1)}) custom-call(f32[2,4,104,128]{3,2,1,0:T(8,128)S(1)} %get-tuple-element.34.refs_0_, f32[632,128]{1,0:T(8,128)S(1)} %collective-permute-done.3.refs_1_, ...), custom_call_target="tpu_custom_call" | custom-call | tf_op jit(solution)/shard_map/pallas_call | solution.py:637
  30.6 0.9 %collective-permute-start.9 = (f32[416,128]{1,0:T(8,128)S(1)}, f32[416,128]{1,0:T(8,128)S(1)}, u32[]{:S(2)}, u32[]{:S(2)}) collective-permute-start(f32[416,128]{1,0:T(8,128)S(1)} %get-tuple-element.46), channel_id=1, source_target_pairs={{1,2},{2,1},{3,4},{4,3},{5,6},{6,5},{9,10},{10,9},{11,12},{12,11},... | collective-permute-start | bytes 638984 | tf_op jit(solution)/shard_map/ppermute | solution.py:620
  32.1 3.7 %collective-permute-start.12 = (f32[16,128]{1,0:T(8,128)S(1)}, f32[16,128]{1,0:T(8,128)S(1)}, u32[]{:S(2)}, u32[]{:S(2)}) collective-permute-start(f32[16,128]{1,0:T(8,128)S(1)} %pad_maximum_fusion.1), channel_id=1, source_target_pairs={{0,6},{1,7},{2,4},{3,5},{4,2},{5,3},{6,0},{7,1},{8,14},{9,15},{10,... | collective-permute-start | bytes 24584 | tf_op jit(solution)/shard_map/ppermute | solution.py:627
  36.5 3.1 %collective-permute-done.12.refs_14_ = f32[16,128]{1,0:T(8,128)S(1)} collective-permute-done((f32[16,128]{1,0:T(8,128)S(1)}, f32[16,128]{1,0:T(8,128)S(1)}, u32[]{:S(2)}, u32[]{:S(2)}) %collective-permute-start.12) | collective-permute-done | bytes 8224 | tf_op jit(solution)/shard_map/ppermute | solution.py:627
  39.7 0.7 collective-permute-done.11.refs_13_
  40.3 5.9 %shard_map.56 = (f32[2,4,104,128]{3,2,1,0:T(8,128)S(1)}, f32[424,128]{1,0:T(8,128)S(1)}, f32[416,128]{1,0:T(8,128)S(1)}, f32[8,128]{1,0:T(8,128)S(1)}) custom-call(f32[2,4,104,128]{3,2,1,0:T(8,128)S(1)} %get-tuple-element.44.refs_0_, f32[424,128]{1,0:T(8,128)S(1)} %collective-permute-done.8.refs_1_, f32[416,128]{1,0:T(8,128)S(1)} %collective-permute-done.9.refs_2_, ...), custom_call_target="tpu_custom_call" | custom-call | tf_op jit(solution)/shard_map/pallas_call | solution.py:637
  46.3 0.7 collective-permute-start.14
  47.0 0.8 collective-permute-done.13.refs_1_
  47.8 4.1 %collective-permute-start.17 = (f32[16,128]{1,0:T(8,128)S(1)}, f32[16,128]{1,0:T(8,128)S(1)}, u32[]{:S(2)}, u32[]{:S(2)}) collective-permute-start(f32[16,128]{1,0:T(8,128)S(1)} %pad_maximum_fusion.2), channel_id=1, source_target_pairs={{0,6},{1,7},{2,4},{3,5},{4,2},{5,3},{6,0},{7,1},{8,14},{9,15},{10,... | collective-permute-start | bytes 24584 | tf_op jit(solution)/shard_map/ppermute | solution.py:627
  52.6 3.3 %collective-permute-done.17.refs_14_ = f32[16,128]{1,0:T(8,128)S(1)} collective-permute-done((f32[16,128]{1,0:T(8,128)S(1)}, f32[16,128]{1,0:T(8,128)S(1)}, u32[]{:S(2)}, u32[]{:S(2)}) %collective-permute-start.17) | collective-permute-done | bytes 8224 | tf_op jit(solution)/shard_map/ppermute | solution.py:627
  56.5 5.9 %shard_map.57 = (f32[2,4,104,128]{3,2,1,0:T(8,128)S(1)}, f32[424,128]{1,0:T(8,128)S(1)}, f32[416,128]{1,0:T(8,128)S(1)}, f32[8,128]{1,0:T(8,128)S(1)}) custom-call(f32[2,4,104,128]{3,2,1,0:T(8,128)S(1)} %get-tuple-element.49.refs_0_, f32[424,128]{1,0:T(8,128)S(1)} %collective-permute-done.13.refs_1_, f32[416,128]{1,0:T(8,128)S(1)} %collective-permute-done.14.refs_2_, ...), custom_call_target="tpu_custom_call" | custom-call | tf_op jit(solution)/shard_map/pallas_call | solution.py:637
  62.4 0.9 %collective-permute-start.19 = (f32[416,128]{1,0:T(8,128)S(1)}, f32[416,128]{1,0:T(8,128)S(1)}, u32[]{:S(2)}, u32[]{:S(2)}) collective-permute-start(f32[416,128]{1,0:T(8,128)S(1)} %get-tuple-element.55), channel_id=1, source_target_pairs={{1,2},{2,1},{3,4},{4,3},{5,6},{6,5},{9,10},{10,9},{11,12},{12,11},... | collective-permute-start | bytes 638984 | tf_op jit(solution)/shard_map/ppermute | solution.py:620
  64.0 4.3 %collective-permute-start.22 = (f32[16,128]{1,0:T(8,128)S(1)}, f32[16,128]{1,0:T(8,128)S(1)}, u32[]{:S(2)}, u32[]{:S(2)}) collective-permute-start(f32[16,128]{1,0:T(8,128)S(1)} %pad_maximum_fusion.3), channel_id=1, source_target_pairs={{0,6},{1,7},{2,4},{3,5},{4,2},{5,3},{6,0},{7,1},{8,14},{9,15},{10,... | collective-permute-start | bytes 24584 | tf_op jit(solution)/shard_map/ppermute | solution.py:627
  69.0 3.2 %collective-permute-done.22.refs_14_ = f32[16,128]{1,0:T(8,128)S(1)} collective-permute-done((f32[16,128]{1,0:T(8,128)S(1)}, f32[16,128]{1,0:T(8,128)S(1)}, u32[]{:S(2)}, u32[]{:S(2)}) %collective-permute-start.22) | collective-permute-done | bytes 8224 | tf_op jit(solution)/shard_map/ppermute | solution.py:627
  72.1 0.7 collective-permute-done.21.refs_13_
  72.8 3.9 %shard_map.58 = (f32[2,6,40,128]{3,2,1,0:T(8,128)S(1)}, f32[2,4,32,128]{3,2,1,0:T(8,128)S(1)}, f32[2,5,32,128]{3,2,1,0:T(8,128)S(1)}, f32[8,128]{1,0:T(8,128)S(1)}) custom-call(f32[2,4,104,128]{3,2,1,0:T(8,128)S(1)} %get-tuple-element.53.refs_0_, f32[424,128]{1,0:T(8,128)S(1)} %collective-permute-done.18.refs_1_, ...), custom_call_target="tpu_custom_call" | custom-call | tf_op jit(solution)/shard_map/pallas_call | solution.py:637
  76.8 1.2 %collective-permute-done.23.refs_1_ = f32[8,128]{1,0:T(8,128)S(1)} collective-permute-done((f32[8,128]{1,0:T(8,128)S(1)}, f32[8,128]{1,0:T(8,128)S(1)}, u32[]{:S(2)}, u32[]{:S(2)}) %collective-permute-start.23) | collective-permute-done | bytes 4128 | tf_op jit(solution)/shard_map/ppermute | solution.py:741
  78.0 1.5 %collective-permute-start.26 = (f32[16,128]{1,0:T(8,128)S(1)}, f32[16,128]{1,0:T(8,128)S(1)}, u32[]{:S(2)}, u32[]{:S(2)}) collective-permute-start(f32[16,128]{1,0:T(8,128)S(1)} %constant_dynamic-update-slice_fusion), channel_id=1, source_target_pairs={{0,6},{1,7},{2,4},{3,5},{4,2},{5,3},{6,0},{7,1},{8,14},{9,15},{10,... | collective-permute-start | bytes 24584 | tf_op jit(solution)/shard_map/ppermute | solution.py:627
  80.0 2.4 %collective-permute-start.24 = (f32[16,128]{1,0:T(8,128)S(1)}, f32[16,128]{1,0:T(8,128)S(1)}, u32[]{:S(2)}, u32[]{:S(2)}) collective-permute-start(f32[16,128]{1,0:T(8,128)S(1)} %constant_dynamic-update-slice_fusion), channel_id=1, source_target_pairs={{0,2},{1,3},{2,0},{3,1},{4,6},{5,7},{6,4},{7,5},{8,10},{9,11},{10,... | collective-permute-start | bytes 24584 | tf_op jit(solution)/shard_map/ppermute | solution.py:627
  82.4 1.6 %shard_map.59 = (f32[200,100]{1,0:T(8,128)S(1)}, f32[200,100]{1,0:T(8,128)}) custom-call(f32[2,6,40,128]{3,2,1,0:T(8,128)S(1)} %get-tuple-element.57.e_ref, f32[2,4,32,128]{3,2,1,0:T(8,128)S(1)} %get-tuple-element.58.x_ref, f32[2,5,32,128]{3,2,1,0:T(8,128)S(1)} %get-tuple-element.59.r_ref, bf16[3,2432,128]{2,1,0:T(8,128)(2,1)S(1)} %shard_map.54.refs_15_.adj_ref), custom_call_target="tpu_custom_call" | custom-call | tf_op jit(solution)/shard_map/pallas_call | solution.py:637
  84.1 1.3 %shard_map.60 = f32[200,100]{1,0:T(8,128)} custom-call(f32[200,100]{1,0:T(8,128)S(1)} %get-tuple-element.61.v_ref, bf16[192,768]{1,0:T(8,128)(2,1)S(1)} %get-tuple-element.33.refs_1_.refs_4_.rows_ref, bf16[384,128]{1,0:T(8,128)(2,1)S(1)} %get-tuple-element.62.pull_ref, f32[8,128]{1,0:T(8,128)S(1)} %get-tuple-element.63.refs_0_, ...), custom_call_target="tpu_custom_call" | custom-call | tf_op jit(solution)/shard_map/pallas_call | solution.py:637
  (51 shorter events, 7.6 us)
Async XLA Ops:
  0.6 0.9 %copy-start = (s32[200,100]{1,0:T(8,128)S(1)}, s32[200,100]{1,0:T(8,128)}, u32[]{:S(2)}) copy-start(s32[200,100]{1,0:T(8,128)} %target_ref.1) | copy-start | bytes 240004
  1.5 0.8 copy-start.3
  2.4 8.4 %collective-permute-start.2 = (bf16[200,256]{1,0:T(8,128)(2,1)S(1)}, bf16[200,256]{1,0:T(8,128)(2,1)S(1)}, u32[]{:S(2)}, u32[]{:S(2)}) collective-permute-start(bf16[200,256]{1,0:T(8,128)(2,1)S(1)} %shard_map.52.refs_2_), channel_id=1, source_target_pairs={{0,24},{8,16},{16,8},{24,0},{1,25},{9,17},{17,9},{25,1},{2,26},{10... | collective-permute-start | bytes 307208 | tf_op jit(solution)/shard_map/ppermute | solution.py:649
  6.3 5.1 %collective-permute-start.1 = (bf16[200,256]{1,0:T(8,128)(2,1)S(1)}, bf16[200,256]{1,0:T(8,128)(2,1)S(1)}, u32[]{:S(2)}, u32[]{:S(2)}) collective-permute-start(bf16[200,256]{1,0:T(8,128)(2,1)S(1)} %shard_map.52.refs_2_), channel_id=1, source_target_pairs={{0,16},{8,24},{16,0},{24,8},{1,17},{9,25},{17,1},{25,9},{2,18},{10... | collective-permute-start | bytes 307208 | tf_op jit(solution)/shard_map/ppermute | solution.py:649
  6.8 4.9 %collective-permute-start = (bf16[200,256]{1,0:T(8,128)(2,1)S(1)}, bf16[200,256]{1,0:T(8,128)(2,1)S(1)}, u32[]{:S(2)}, u32[]{:S(2)}) collective-permute-start(bf16[200,256]{1,0:T(8,128)(2,1)S(1)} %shard_map.52.refs_2_), channel_id=1, source_target_pairs={{0,8},{8,0},{16,24},{24,16},{1,9},{9,1},{17,25},{25,17},{2,10},{10... | collective-permute-start | bytes 307208 | tf_op jit(solution)/shard_map/ppermute | solution.py:649
  7.6 0.7 copy-start.1
  8.3 11.8 %copy-start.2 = (bf16[61,61]{1,0:T(8,128)(2,1)S(1)}, bf16[61,61]{1,0:T(8,128)(2,1)}, u32[]{:S(2)}) copy-start(bf16[61,61]{1,0:T(8,128)(2,1)} %psf_ref.3) | copy-start | bytes 22330
  13.2 1.7 %collective-permute-start.3 = (f32[632,128]{1,0:T(8,128)S(1)}, f32[632,128]{1,0:T(8,128)S(1)}, u32[]{:S(2)}, u32[]{:S(2)}) collective-permute-start(f32[632,128]{1,0:T(8,128)S(1)} %get-tuple-element.35), channel_id=1, source_target_pairs={{0,1},{1,0},{2,3},{3,2},{4,5},{5,4},{6,7},{7,6},{8,9},{9,8},{10,11... | collective-permute-start | bytes 970760 | tf_op jit(solution)/shard_map/ppermute | solution.py:620
  13.3 9.4 %collective-permute-start.4 = (f32[624,128]{1,0:T(8,128)S(1)}, f32[624,128]{1,0:T(8,128)S(1)}, u32[]{:S(2)}, u32[]{:S(2)}) collective-permute-start(f32[624,128]{1,0:T(8,128)S(1)} %get-tuple-element.36), channel_id=1, source_target_pairs={{1,2},{2,1},{3,4},{4,3},{5,6},{6,5},{9,10},{10,9},{11,12},{12,11},... | collective-permute-start | bytes 958472 | tf_op jit(solution)/shard_map/ppermute | solution.py:620
  14.9 9.7 %collective-permute-start.7 = (f32[16,128]{1,0:T(8,128)S(1)}, f32[16,128]{1,0:T(8,128)S(1)}, u32[]{:S(2)}, u32[]{:S(2)}) collective-permute-start(f32[16,128]{1,0:T(8,128)S(1)} %pad_maximum_fusion), channel_id=1, source_target_pairs={{0,6},{1,7},{2,4},{3,5},{4,2},{5,3},{6,0},{7,1},{8,14},{9,15},{10,... | collective-permute-start | bytes 24584 | tf_op jit(solution)/shard_map/ppermute | solution.py:627
  19.4 5.2 %collective-permute-start.6 = (f32[16,128]{1,0:T(8,128)S(1)}, f32[16,128]{1,0:T(8,128)S(1)}, u32[]{:S(2)}, u32[]{:S(2)}) collective-permute-start(f32[16,128]{1,0:T(8,128)S(1)} %pad_maximum_fusion), channel_id=1, source_target_pairs={{0,4},{1,5},{2,6},{3,7},{4,0},{5,1},{6,2},{7,3},{8,12},{9,13},{10,... | collective-permute-start | bytes 24584 | tf_op jit(solution)/shard_map/ppermute | solution.py:627
  19.4 5.2 %collective-permute-start.5 = (f32[16,128]{1,0:T(8,128)S(1)}, f32[16,128]{1,0:T(8,128)S(1)}, u32[]{:S(2)}, u32[]{:S(2)}) collective-permute-start(f32[16,128]{1,0:T(8,128)S(1)} %pad_maximum_fusion), channel_id=1, source_target_pairs={{0,2},{1,3},{2,0},{3,1},{4,6},{5,7},{6,4},{7,5},{8,10},{9,11},{10,... | collective-permute-start | bytes 24584 | tf_op jit(solution)/shard_map/ppermute | solution.py:627
  30.6 1.5 %collective-permute-start.8 = (f32[424,128]{1,0:T(8,128)S(1)}, f32[424,128]{1,0:T(8,128)S(1)}, u32[]{:S(2)}, u32[]{:S(2)}) collective-permute-start(f32[424,128]{1,0:T(8,128)S(1)} %get-tuple-element.45), channel_id=1, source_target_pairs={{0,1},{1,0},{2,3},{3,2},{4,5},{5,4},{6,7},{7,6},{8,9},{9,8},{10,11... | collective-permute-start | bytes 651272 | tf_op jit(solution)/shard_map/ppermute | solution.py:620
  30.6 5.9 %collective-permute-start.9 = (f32[416,128]{1,0:T(8,128)S(1)}, f32[416,128]{1,0:T(8,128)S(1)}, u32[]{:S(2)}, u32[]{:S(2)}) collective-permute-start(f32[416,128]{1,0:T(8,128)S(1)} %get-tuple-element.46), channel_id=1, source_target_pairs={{1,2},{2,1},{3,4},{4,3},{5,6},{6,5},{9,10},{10,9},{11,12},{12,11},... | collective-permute-start | bytes 638984 | tf_op jit(solution)/shard_map/ppermute | solution.py:620
  32.1 7.5 %collective-permute-start.12 = (f32[16,128]{1,0:T(8,128)S(1)}, f32[16,128]{1,0:T(8,128)S(1)}, u32[]{:S(2)}, u32[]{:S(2)}) collective-permute-start(f32[16,128]{1,0:T(8,128)S(1)} %pad_maximum_fusion.1), channel_id=1, source_target_pairs={{0,6},{1,7},{2,4},{3,5},{4,2},{5,3},{6,0},{7,1},{8,14},{9,15},{10,... | collective-permute-start | bytes 24584 | tf_op jit(solution)/shard_map/ppermute | solution.py:627
  35.8 4.5 %collective-permute-start.11 = (f32[16,128]{1,0:T(8,128)S(1)}, f32[16,128]{1,0:T(8,128)S(1)}, u32[]{:S(2)}, u32[]{:S(2)}) collective-permute-start(f32[16,128]{1,0:T(8,128)S(1)} %pad_maximum_fusion.1), channel_id=1, source_target_pairs={{0,4},{1,5},{2,6},{3,7},{4,0},{5,1},{6,2},{7,3},{8,12},{9,13},{10,... | collective-permute-start | bytes 24584 | tf_op jit(solution)/shard_map/ppermute | solution.py:627
  36.4 3.9 %collective-permute-start.10 = (f32[16,128]{1,0:T(8,128)S(1)}, f32[16,128]{1,0:T(8,128)S(1)}, u32[]{:S(2)}, u32[]{:S(2)}) collective-permute-start(f32[16,128]{1,0:T(8,128)S(1)} %pad_maximum_fusion.1), channel_id=1, source_target_pairs={{0,2},{1,3},{2,0},{3,1},{4,6},{5,7},{6,4},{7,5},{8,10},{9,11},{10,... | collective-permute-start | bytes 24584 | tf_op jit(solution)/shard_map/ppermute | solution.py:627
  46.3 1.5 %collective-permute-start.13 = (f32[424,128]{1,0:T(8,128)S(1)}, f32[424,128]{1,0:T(8,128)S(1)}, u32[]{:S(2)}, u32[]{:S(2)}) collective-permute-start(f32[424,128]{1,0:T(8,128)S(1)} %get-tuple-element.50), channel_id=1, source_target_pairs={{0,1},{1,0},{2,3},{3,2},{4,5},{5,4},{6,7},{7,6},{8,9},{9,8},{10,11... | collective-permute-start | bytes 651272 | tf_op jit(solution)/shard_map/ppermute | solution.py:620
  46.3 6.3 %collective-permute-start.14 = (f32[416,128]{1,0:T(8,128)S(1)}, f32[416,128]{1,0:T(8,128)S(1)}, u32[]{:S(2)}, u32[]{:S(2)}) collective-permute-start(f32[416,128]{1,0:T(8,128)S(1)} %get-tuple-element.51), channel_id=1, source_target_pairs={{1,2},{2,1},{3,4},{4,3},{5,6},{6,5},{9,10},{10,9},{11,12},{12,11},... | collective-permute-start | bytes 638984 | tf_op jit(solution)/shard_map/ppermute | solution.py:620
  47.8 8.1 %collective-permute-start.17 = (f32[16,128]{1,0:T(8,128)S(1)}, f32[16,128]{1,0:T(8,128)S(1)}, u32[]{:S(2)}, u32[]{:S(2)}) collective-permute-start(f32[16,128]{1,0:T(8,128)S(1)} %pad_maximum_fusion.2), channel_id=1, source_target_pairs={{0,6},{1,7},{2,4},{3,5},{4,2},{5,3},{6,0},{7,1},{8,14},{9,15},{10,... | collective-permute-start | bytes 24584 | tf_op jit(solution)/shard_map/ppermute | solution.py:627
  51.9 4.5 %collective-permute-start.16 = (f32[16,128]{1,0:T(8,128)S(1)}, f32[16,128]{1,0:T(8,128)S(1)}, u32[]{:S(2)}, u32[]{:S(2)}) collective-permute-start(f32[16,128]{1,0:T(8,128)S(1)} %pad_maximum_fusion.2), channel_id=1, source_target_pairs={{0,4},{1,5},{2,6},{3,7},{4,0},{5,1},{6,2},{7,3},{8,12},{9,13},{10,... | collective-permute-start | bytes 24584 | tf_op jit(solution)/shard_map/ppermute | solution.py:627
  51.9 4.5 %collective-permute-start.15 = (f32[16,128]{1,0:T(8,128)S(1)}, f32[16,128]{1,0:T(8,128)S(1)}, u32[]{:S(2)}, u32[]{:S(2)}) collective-permute-start(f32[16,128]{1,0:T(8,128)S(1)} %pad_maximum_fusion.2), channel_id=1, source_target_pairs={{0,2},{1,3},{2,0},{3,1},{4,6},{5,7},{6,4},{7,5},{8,10},{9,11},{10,... | collective-permute-start | bytes 24584 | tf_op jit(solution)/shard_map/ppermute | solution.py:627
  62.4 1.5 %collective-permute-start.18 = (f32[424,128]{1,0:T(8,128)S(1)}, f32[424,128]{1,0:T(8,128)S(1)}, u32[]{:S(2)}, u32[]{:S(2)}) collective-permute-start(f32[424,128]{1,0:T(8,128)S(1)} %get-tuple-element.54), channel_id=1, source_target_pairs={{0,1},{1,0},{2,3},{3,2},{4,5},{5,4},{6,7},{7,6},{8,9},{9,8},{10,11... | collective-permute-start | bytes 651272 | tf_op jit(solution)/shard_map/ppermute | solution.py:620
  62.4 6.5 %collective-permute-start.19 = (f32[416,128]{1,0:T(8,128)S(1)}, f32[416,128]{1,0:T(8,128)S(1)}, u32[]{:S(2)}, u32[]{:S(2)}) collective-permute-start(f32[416,128]{1,0:T(8,128)S(1)} %get-tuple-element.55), channel_id=1, source_target_pairs={{1,2},{2,1},{3,4},{4,3},{5,6},{6,5},{9,10},{10,9},{11,12},{12,11},... | collective-permute-start | bytes 638984 | tf_op jit(solution)/shard_map/ppermute | solution.py:620
  64.0 8.2 %collective-permute-start.22 = (f32[16,128]{1,0:T(8,128)S(1)}, f32[16,128]{1,0:T(8,128)S(1)}, u32[]{:S(2)}, u32[]{:S(2)}) collective-permute-start(f32[16,128]{1,0:T(8,128)S(1)} %pad_maximum_fusion.3), channel_id=1, source_target_pairs={{0,6},{1,7},{2,4},{3,5},{4,2},{5,3},{6,0},{7,1},{8,14},{9,15},{10,... | collective-permute-start | bytes 24584 | tf_op jit(solution)/shard_map/ppermute | solution.py:627
  68.3 4.5 %collective-permute-start.21 = (f32[16,128]{1,0:T(8,128)S(1)}, f32[16,128]{1,0:T(8,128)S(1)}, u32[]{:S(2)}, u32[]{:S(2)}) collective-permute-start(f32[16,128]{1,0:T(8,128)S(1)} %pad_maximum_fusion.3), channel_id=1, source_target_pairs={{0,4},{1,5},{2,6},{3,7},{4,0},{5,1},{6,2},{7,3},{8,12},{9,13},{10,... | collective-permute-start | bytes 24584 | tf_op jit(solution)/shard_map/ppermute | solution.py:627
  68.3 4.5 %collective-permute-start.20 = (f32[16,128]{1,0:T(8,128)S(1)}, f32[16,128]{1,0:T(8,128)S(1)}, u32[]{:S(2)}, u32[]{:S(2)}) collective-permute-start(f32[16,128]{1,0:T(8,128)S(1)} %pad_maximum_fusion.3), channel_id=1, source_target_pairs={{0,2},{1,3},{2,0},{3,1},{4,6},{5,7},{6,4},{7,5},{8,10},{9,11},{10,... | collective-permute-start | bytes 24584 | tf_op jit(solution)/shard_map/ppermute | solution.py:627
  76.8 1.2 %collective-permute-start.23 = (f32[8,128]{1,0:T(8,128)S(1)}, f32[8,128]{1,0:T(8,128)S(1)}, u32[]{:S(2)}, u32[]{:S(2)}) collective-permute-start(f32[8,128]{1,0:T(8,128)S(1)} %get-tuple-element.63.refs_0_), channel_id=1, source_target_pairs={{0,1},{1,0},{2,3},{3,2},{4,5},{5,4},{6,7},{7,6},{8,9},{9,8},{10,11... | collective-permute-start | bytes 12296 | tf_op jit(solution)/shard_map/ppermute | solution.py:741
  78.0 5.9 %collective-permute-start.26 = (f32[16,128]{1,0:T(8,128)S(1)}, f32[16,128]{1,0:T(8,128)S(1)}, u32[]{:S(2)}, u32[]{:S(2)}) collective-permute-start(f32[16,128]{1,0:T(8,128)S(1)} %constant_dynamic-update-slice_fusion), channel_id=1, source_target_pairs={{0,6},{1,7},{2,4},{3,5},{4,2},{5,3},{6,0},{7,1},{8,14},{9,15},{10,... | collective-permute-start | bytes 24584 | tf_op jit(solution)/shard_map/ppermute | solution.py:627
  79.4 4.6 %collective-permute-start.25 = (f32[16,128]{1,0:T(8,128)S(1)}, f32[16,128]{1,0:T(8,128)S(1)}, u32[]{:S(2)}, u32[]{:S(2)}) collective-permute-start(f32[16,128]{1,0:T(8,128)S(1)} %constant_dynamic-update-slice_fusion), channel_id=1, source_target_pairs={{0,4},{1,5},{2,6},{3,7},{4,0},{5,1},{6,2},{7,3},{8,12},{9,13},{10,... | collective-permute-start | bytes 24584 | tf_op jit(solution)/shard_map/ppermute | solution.py:627
  80.0 4.1 %collective-permute-start.24 = (f32[16,128]{1,0:T(8,128)S(1)}, f32[16,128]{1,0:T(8,128)S(1)}, u32[]{:S(2)}, u32[]{:S(2)}) collective-permute-start(f32[16,128]{1,0:T(8,128)S(1)} %constant_dynamic-update-slice_fusion), channel_id=1, source_target_pairs={{0,2},{1,3},{2,0},{3,1},{4,6},{5,7},{6,4},{7,5},{8,10},{9,11},{10,... | collective-permute-start | bytes 24584 | tf_op jit(solution)/shard_map/ppermute | solution.py:627
